TPU v7x, 32 devices: a whole 2x2x4 slice. The times are simulated.
32 devices in a mesh: group: 4 (over y, x), seq: 8 (over z, core).
Axes of the slice: x: 2, y: 2, z: 4, core: 2. Of those that a mesh axis runs over, the one named last changes fastest.
Arguments:
- features: bfloat16 [4096, 768], P(('group', 'seq')), may hold values from -6 to 6
- tiles: bfloat16 [4096, 1024], P(('group', 'seq')), may hold values from -0.5 to 0.5
- tile_src: int32 [32, 8], P(('group', 'seq')), may hold values from 0 to 3
- tile_count: int32 [32], P(('group', 'seq')), may hold values from 1 to 8, as said below
- node_bucket: int32 [4096], P(('group', 'seq')), may hold values from 0 to 15
- w_qk: bfloat16 [768, 1536], replicated, may hold values from -0.3125 to 0.3125
- w_v: bfloat16 [768, 768], replicated, may hold values from -1.25 to 1.25
- bias_table: float32 [32, 256], replicated, may hold values from -2 to 300
Outputs:
- attended: bfloat16 [4096, 768], P(('group', 'seq'))
Inputs may be any that keep to these rules, and one draw needn't show every extreme that they name: `tile_count`: some row block uses all 8 slots.
All inputs are finite; a program needn't handle non-finite values.
Results may differ from a plain program's by a relative error of at most 0.012.
Values may be sent and summed in bfloat16 or wider, within the bound.
No kernel may reach another device: no remote copies, remote signals or barrier semaphores. Data moves between devices by JAX's collectives and lax.ppermute only.
A program may use at most 64 MiB of HBM per device.

v0:
```python
import math

import jax
import jax.numpy as jnp
from jax import lax
from jax.sharding import PartitionSpec as P

H = 32
HD = 24
NB = 16
TILES = 8


def on_device(features, tiles, tile_src, tile_count, node_bucket, w_qk, w_v, bias_table):
    row_count, feat_width = features.shape
    group_count = lax.axis_size("group")
    seq_count = lax.axis_size("seq")
    live_flag = jnp.arange(TILES) < tile_count[0]
    tile_rows = tiles.reshape(row_count, TILES, row_count)
    sources = tile_src[0]
    gathered = lax.all_gather(features, "group", axis=0, tiled=True)
    chosen = gathered.reshape(group_count, row_count, feat_width)[sources]
    masked = tile_rows * live_flag.astype(jnp.bfloat16)[None, :, None]
    aggregated = features.astype(jnp.float32) + jnp.einsum(
        "rtc,tcd->rd", masked, chosen, preferred_element_type=jnp.float32
    )
    mean_square = jnp.mean(aggregated * aggregated, axis=-1, keepdims=True)
    normed = (aggregated * lax.rsqrt(mean_square + 1e-06)).astype(jnp.bfloat16)
    query_key = jnp.dot(normed, w_qk, preferred_element_type=jnp.float32).astype(jnp.bfloat16)
    values = jnp.dot(normed, w_v, preferred_element_type=jnp.float32).astype(jnp.bfloat16)
    bias_cube = bias_table.reshape(H, NB, NB)
    scale = 1.0 / math.sqrt(HD)
    iota_nb = jnp.arange(NB)
    head_local = H // seq_count
    local_width = head_local * HD
    query_send = query_key[:, :feat_width].reshape(row_count, seq_count, local_width)
    key_send = query_key[:, feat_width:].reshape(row_count, seq_count, local_width)
    value_send = values.reshape(row_count, seq_count, local_width)
    query_all, key_all, value_all = (
        lax.all_to_all(query_send, "seq", split_axis=1, concat_axis=0, tiled=True),
        lax.all_to_all(key_send, "seq", split_axis=1, concat_axis=0, tiled=True),
        lax.all_to_all(value_send, "seq", split_axis=1, concat_axis=0, tiled=True),
    )
    group_rows = seq_count * row_count
    query_all = query_all.reshape(group_rows, head_local, HD)
    key_all = key_all.reshape(group_rows, head_local, HD)
    value_all = value_all.reshape(group_rows, head_local, HD)
    bucket_group = lax.all_gather(node_bucket, "seq", axis=0, tiled=True)
    my_cube = lax.dynamic_slice_in_dim(bias_cube, lax.axis_index("seq") * head_local, head_local, 0)
    key_onehot = (bucket_group[:, None] == iota_nb[None, :]).astype(jnp.float32)
    query_rows_bias = my_cube[:, bucket_group, :]
    query_block = math.gcd(group_rows, 512)

    def attend_queries(block_index):
        offset = block_index * query_block
        query_part = lax.dynamic_slice_in_dim(query_all, offset, query_block, 0)
        bias_part = lax.dynamic_slice_in_dim(query_rows_bias, offset, query_block, 1)
        scores = (
            jnp.einsum("rhd,nhd->hrn", query_part, key_all, preferred_element_type=jnp.float32)
            * scale
        )
        scores = scores + jnp.einsum(
            "hrb,nb->hrn", bias_part, key_onehot, precision=lax.Precision.HIGHEST
        )
        peak = jnp.max(scores, axis=-1, keepdims=True)
        weights = jnp.exp(scores - peak)
        total_weight = jnp.sum(weights, axis=-1)
        mixed = jnp.einsum(
            "hrn,nhd->hrd",
            weights.astype(jnp.bfloat16),
            value_all,
            preferred_element_type=jnp.float32,
        )
        mixed = mixed / total_weight[..., None]
        return mixed.transpose(1, 0, 2).reshape(query_block, local_width).astype(jnp.bfloat16)

    head_rows = lax.map(attend_queries, jnp.arange(group_rows // query_block)).reshape(
        group_rows, local_width
    )
    attended = lax.all_to_all(head_rows, "seq", split_axis=0, concat_axis=1, tiled=True)
    return attended


def solution(mesh):
    in_specs = (
        P(("group", "seq"), None),
        P(("group", "seq"), None),
        P(("group", "seq"), None),
        P(("group", "seq")),
        P(("group", "seq")),
        P(),
        P(),
        P(),
    )
    out_specs = P(("group", "seq"), None)
    return jax.shard_map(
        on_device, mesh=mesh, in_specs=in_specs, out_specs=out_specs, check_vma=False
    )
```

profile of v0, /device:TPU:0, one launch (start us, length us, event | category | flops | bytes accessed | tf_op | source)
XLA Modules:
  0.0 113.5 jit_solution(12108838583794148130)
XLA Ops:
  0.0 0.0 copy-start
  0.0 0.0 copy-start.1
  0.0 14.1 %all_gather.6 = bf16[512,768]{1,0:T(8,128)(2,1)S(1)} all-gather(bf16[128,768]{1,0:T(8,128)(2,1)} %param.10), channel_id=1, replica_groups=mesh['group'=4,'seq'=8] {'group'}, dimensions={0}, use_global_device_ids=true | all-gather | bytes 983040 | tf_op jit(solution)/shard_map/all_gather | solution.py:21
  14.1 0.7 fusion.28
  15.4 1.8 %gather_fusion = bf16[8,128,768]{2,1,0:T(8,128)(2,1)} fusion(bf16[4,128,768]{2,1,0:T(8,128)(2,1)S(1)} %bitcast.88, s32[1024]{0:T(1024)S(1)} %pad_clamp_fusion), kind=kCustom, calls=%fused_computation | custom fusion | bytes 3145760 | tf_op jit(solution)/shard_map/gather | solution.py:22
  17.2 0.0 copy-done.1
  17.2 2.0 %multiply_reduce_fusion = (f32[128]{0:T(128)S(1)}, f32[128,768]{1,0:T(8,128)S(1)}) fusion(bf16[8,128,768]{2,1,0:T(8,128)(2,1)} %gather_fusion, bf16[8]{0:T(256)(128)(2,1)S(1)} %compare_convert_fusion, bf16[128,768]{1,0:T(8,128)(2,1)S(1)} %copy-done.1, bf16[128,1024]{1,0:T(8,128)(2,1)} %param.11), kind=kOutput, calls=%fused_computation.27 | convolution fusion | flops 202243968 | bytes 2425360 | tf_op jit(solution)/shard_map/rtc,tcd->rd/dot_general | solution.py:24
  19.2 0.0 copy-start.4
  19.2 0.0 copy-done
  19.2 0.0 copy-start.5
  19.2 0.5 convolution_convert_fusion
  19.8 0.8 copy.37
  20.6 4.9 %all-to-all-start = ((bf16[128,8,96]{0,2,1:T(8,128)(2,1)}), bf16[128,8,96]{0,2,1:T(8,128)(2,1)S(1)}, u32[]{:S(2)}, u32[]{:S(2)}) async-start(bf16[128,8,96]{0,2,1:T(8,128)(2,1)} %bitcast.5), calls=%async_computation | async-start | bytes 393216 | tf_op jit(solution)/shard_map/all_to_all | solution.py:40
  25.5 0.8 copy.39
  26.3 7.5 %all-to-all-done = bf16[128,8,96]{0,2,1:T(8,128)(2,1)S(1)} async-done(((bf16[128,8,96]{0,2,1:T(8,128)(2,1)}), bf16[128,8,96]{0,2,1:T(8,128)(2,1)S(1)}, u32[]{:S(2)}, u32[]{:S(2)}) %all-to-all-start) | async-done | bytes 196640 | tf_op jit(solution)/shard_map/all_to_all | solution.py:40
  33.8 3.4 %all-to-all-start.1 = ((bf16[128,8,96]{0,2,1:T(8,128)(2,1)}), bf16[128,8,96]{0,2,1:T(8,128)(2,1)S(1)}, u32[]{:S(2)}, u32[]{:S(2)}) async-start(bf16[128,8,96]{0,2,1:T(8,128)(2,1)} %bitcast.8), calls=%async_computation.1 | async-start | bytes 393216 | tf_op jit(solution)/shard_map/all_to_all | solution.py:41
  37.2 1.6 %convolution_convert_fusion.1 = bf16[128,768]{1,0:T(8,128)(2,1)S(1)} fusion(bf16[768,768]{1,0:T(8,128)(2,1)} %param.16, f32[128,768]{1,0:T(8,128)S(1)} %get-tuple-element.112, f32[128]{0:T(128)S(1)} %add_rsqrt_fusion), kind=kOutput, calls=%fused_computation.25 | convolution fusion | flops 151289856 | bytes 1769984 | tf_op jit(solution)/shard_map/dot_general | solution.py:30
  38.9 0.8 copy.43
  39.7 5.8 %all-to-all-done.1 = bf16[128,8,96]{0,2,1:T(8,128)(2,1)S(1)} async-done(((bf16[128,8,96]{0,2,1:T(8,128)(2,1)}), bf16[128,8,96]{0,2,1:T(8,128)(2,1)S(1)}, u32[]{:S(2)}, u32[]{:S(2)}) %all-to-all-start.1) | async-done | bytes 196640 | tf_op jit(solution)/shard_map/all_to_all | solution.py:41
  45.5 3.4 %all-to-all-start.2 = ((bf16[128,8,96]{0,2,1:T(8,128)(2,1)}), bf16[128,8,96]{0,2,1:T(8,128)(2,1)S(1)}, u32[]{:S(2)}, u32[]{:S(2)}) async-start(bf16[128,8,96]{0,2,1:T(8,128)(2,1)} %bitcast.15), calls=%async_computation.2 | async-start | bytes 393216 | tf_op jit(solution)/shard_map/all_to_all | solution.py:42
  48.9 0.0 copy-done.4
  48.9 0.1 copy.41
  49.0 0.1 constant_dynamic-slice_fusion
  49.1 0.2 copy.49
  49.3 0.0 copy-done.5
  49.3 12.1 %all-gather = s32[8,1,128]{2,1,0:T(1,128)S(1)} all-gather(s32[1,1,128]{2,1,0:T(1,128)S(1)} %bitcast.97), channel_id=1, replica_groups=mesh['group'=4,'seq'=8] {'seq'}, dimensions={0}, use_global_device_ids=true | all-gather | bytes 4608 | tf_op jit(solution)/shard_map/all_gather | solution.py:48
  61.4 7.9 %gather_fusion.1 = f32[1024,4,16]{2,1,0:T(4,128)} fusion(f32[4,16,16]{2,0,1:T(4,128)S(1)} %copy.49, s32[1024]{0:T(1024)S(1)} %fusion.27), kind=kCustom, calls=%fused_computation.1 | custom fusion | bytes 528384 | tf_op jit(solution)/shard_map/gather | solution.py:51
  69.2 1.8 %copy.45 = f32[4,1024,16]{1,2,0:T(8,128)S(1)} copy(f32[4,1024,16]{2,0,1:T(4,128)} %bitcast.87) | data formatting | bytes 524288
  71.1 0.1 copy.38
  71.2 0.1 reshape.96
  71.3 0.1 copy.40
  71.3 0.1 reshape.98
  71.4 0.0 all-to-all-done.2
  71.4 0.1 copy.44
  71.5 0.1 reshape.101
  71.6 29.0 %while.11 = (s32[]{:T(128)}, bf16[2,512,96]{1,2,0:T(8,128)(2,1)}, s32[2]{0:T(128)S(1)}, bf16[1024,4,24]{0,2,1:T(8,128)(2,1)S(1)}, bf16[1024,4,24]{0,2,1:T(8,128)...) while((s32[]{:T(128)}, bf16[2,512,96]{1,2,0:T(8,128)(2,1)}, ...), condition=%wide.region_4.5_spmd.clone, body=%wide.region_1.4_spmd.clone.sunk | while | flops 618786816 | bytes 44478704 | solution.py:77
  71.7 0.6 dynamic_slice.29
  72.8 1.3 %fusion.49 = f32[4,512,1024]{2,1,0:T(8,128)S(1)} fusion(bf16[1024,4,24]{0,2,1:T(8,128)(2,1)S(1)} %get-tuple-element.194, bf16[1024,4,24]{0,2,1:T(8,128)(2,1)S(1)} %get-tuple-element.193, s32[]{:T(128)S(6)} %select_n.31), kind=kOutput, calls=%fused_computation.13.clone.1 | convolution fusion | flops 100663296 | bytes 8683524 | tf_op jit(solution)/shard_map/while/body/eval_jaxpr/rhd,nhd->hrn/dot_general | solution.py:59
  74.1 8.1 %fusion.50 = (f32[4,512]{1,0:T(4,128)S(1)}, f32[4,512,1024]{2,1,0:T(8,128)S(1)}) fusion(s32[1024]{0:T(1024)S(1)} %get-tuple-element.197, f32[4,1024,16]{1,2,0:T(8,128)S(1)} %get-tuple-element.195, s32[]{:T(128)S(6)} %select_n.31, f32[4,512,1024]{2,1,0:T(8,128)S(1)} %fusion.49), kind=kOutput, calls=%fused_computation.39.clone.1 | convolution fusion | flops 408975360 | bytes 16920580 | tf_op jit(solution)/shard_map/while/body/eval_jaxpr/hrb,nb->hrn/dot_general | solution.py:62
  82.2 1.9 %fusion.51 = f32[4,512]{1,0:T(4,128)S(1)} fusion(f32[4,512,1024]{2,1,0:T(8,128)S(1)} %get-tuple-element.164, f32[4,512]{1,0:T(4,128)S(1)} %get-tuple-element.165), kind=kLoop, calls=%fused_computation.5.clone.1 | loop fusion | flops 4192256 | bytes 8404992 | tf_op jit(solution)/shard_map/while/body/eval_jaxpr/reduce_sum | solution.py:67
  84.1 0.0 copy-start.2
  84.1 1.3 %fusion.52 = bf16[512,4,24]{0,2,1:T(8,128)(2,1)S(1)} fusion(bf16[1024,4,24]{0,2,1:T(8,128)(2,1)S(1)} %get-tuple-element.196, f32[4,512,1024]{2,1,0:T(8,128)S(1)} %get-tuple-element.164, f32[4,512]{1,0:T(4,128)S(1)} %get-tuple-element.165, f32[512,4]{0,1:T(4,128)S(1)} %bitcast.89), kind=kOutput, calls=%fused_computation.11.clone.1 | convolution fusion | flops 104955904 | bytes 8699904 | tf_op jit(solution)/shard_map/while/body/eval_jaxpr/hrn,nhd->hrd/dot_general | solution.py:68
  85.4 0.0 copy-done.2
  85.5 0.0 copy-start.3
  85.5 0.7 copy-done.3
  86.1 0.6 dynamic_slice.29
  87.3 1.3 %fusion.49 = f32[4,512,1024]{2,1,0:T(8,128)S(1)} fusion(bf16[1024,4,24]{0,2,1:T(8,128)(2,1)S(1)} %get-tuple-element.194, bf16[1024,4,24]{0,2,1:T(8,128)(2,1)S(1)} %get-tuple-element.193, s32[]{:T(128)S(6)} %select_n.31), kind=kOutput, calls=%fused_computation.13.clone.1 | convolution fusion | flops 100663296 | bytes 8683524 | tf_op jit(solution)/shard_map/while/body/eval_jaxpr/rhd,nhd->hrn/dot_general | solution.py:59
  88.6 8.1 %fusion.50 = (f32[4,512]{1,0:T(4,128)S(1)}, f32[4,512,1024]{2,1,0:T(8,128)S(1)}) fusion(s32[1024]{0:T(1024)S(1)} %get-tuple-element.197, f32[4,1024,16]{1,2,0:T(8,128)S(1)} %get-tuple-element.195, s32[]{:T(128)S(6)} %select_n.31, f32[4,512,1024]{2,1,0:T(8,128)S(1)} %fusion.49), kind=kOutput, calls=%fused_computation.39.clone.1 | convolution fusion | flops 408975360 | bytes 16920580 | tf_op jit(solution)/shard_map/while/body/eval_jaxpr/hrb,nb->hrn/dot_general | solution.py:62
  96.7 1.9 %fusion.51 = f32[4,512]{1,0:T(4,128)S(1)} fusion(f32[4,512,1024]{2,1,0:T(8,128)S(1)} %get-tuple-element.164, f32[4,512]{1,0:T(4,128)S(1)} %get-tuple-element.165), kind=kLoop, calls=%fused_computation.5.clone.1 | loop fusion | flops 4192256 | bytes 8404992 | tf_op jit(solution)/shard_map/while/body/eval_jaxpr/reduce_sum | solution.py:67
  98.6 0.0 copy-start.2
  98.6 1.3 %fusion.52 = bf16[512,4,24]{0,2,1:T(8,128)(2,1)S(1)} fusion(bf16[1024,4,24]{0,2,1:T(8,128)(2,1)S(1)} %get-tuple-element.196, f32[4,512,1024]{2,1,0:T(8,128)S(1)} %get-tuple-element.164, f32[4,512]{1,0:T(4,128)S(1)} %get-tuple-element.165, f32[512,4]{0,1:T(4,128)S(1)} %bitcast.89), kind=kOutput, calls=%fused_computation.11.clone.1 | convolution fusion | flops 104955904 | bytes 8699904 | tf_op jit(solution)/shard_map/while/body/eval_jaxpr/hrn,nhd->hrd/dot_general | solution.py:68
  99.9 0.0 copy-done.2
  99.9 0.0 copy-start.3
  100.0 0.7 copy-done.3
  100.6 1.1 copy.46
  101.8 0.1 all_to_all.56
  101.9 10.7 %all_to_all.64 = bf16[8,128,96]{1,2,0:T(8,128)(2,1)S(1)} all-to-all(bf16[8,128,96]{1,2,0:T(8,128)(2,1)S(1)} %copy.47), channel_id=1, replica_groups=mesh['group'=4,'seq'=8] {'seq'}, dimensions={0} | all-to-all | bytes 393216 | tf_op jit(solution)/shard_map/all_to_all | solution.py:80
  112.7 0.8 copy.48
  (10 shorter events, 0.1 us)
Async XLA Ops:
  0.0 19.2 %copy-start = (bf16[768,1536]{1,0:T(8,128)(2,1)S(1)}, bf16[768,1536]{1,0:T(8,128)(2,1)}, u32[]{:S(2)}) copy-start(bf16[768,1536]{1,0:T(8,128)(2,1)} %param.15) | copy-start | bytes 7077892
  0.0 17.2 %copy-start.1 = (bf16[128,768]{1,0:T(8,128)(2,1)S(1)}, bf16[128,768]{1,0:T(8,128)(2,1)}, u32[]{:S(2)}) copy-start(bf16[128,768]{1,0:T(8,128)(2,1)} %param.10) | copy-start | bytes 589828
  19.2 29.7 %copy-start.4 = (f32[32,256]{1,0:T(8,128)S(1)}, f32[32,256]{1,0:T(8,128)}, u32[]{:S(2)}) copy-start(f32[32,256]{1,0:T(8,128)} %param.17) | copy-start | bytes 98308
  19.2 30.1 %copy-start.5 = (s32[128]{0:T(128)S(1)}, s32[128]{0:T(128)}, u32[]{:S(2)}) copy-start(s32[128]{0:T(128)} %param.14) | copy-start | bytes 1540
  20.6 13.2 %all-to-all-start = ((bf16[128,8,96]{0,2,1:T(8,128)(2,1)}), bf16[128,8,96]{0,2,1:T(8,128)(2,1)S(1)}, u32[]{:S(2)}, u32[]{:S(2)}) async-start(bf16[128,8,96]{0,2,1:T(8,128)(2,1)} %bitcast.5), calls=%async_computation | async-start | bytes 393216 | tf_op jit(solution)/shard_map/all_to_all | solution.py:40
  33.8 11.7 %all-to-all-start.1 = ((bf16[128,8,96]{0,2,1:T(8,128)(2,1)}), bf16[128,8,96]{0,2,1:T(8,128)(2,1)S(1)}, u32[]{:S(2)}, u32[]{:S(2)}) async-start(bf16[128,8,96]{0,2,1:T(8,128)(2,1)} %bitcast.8), calls=%async_computation.1 | async-start | bytes 393216 | tf_op jit(solution)/shard_map/all_to_all | solution.py:41
  45.5 25.9 %all-to-all-start.2 = ((bf16[128,8,96]{0,2,1:T(8,128)(2,1)}), bf16[128,8,96]{0,2,1:T(8,128)(2,1)S(1)}, u32[]{:S(2)}, u32[]{:S(2)}) async-start(bf16[128,8,96]{0,2,1:T(8,128)(2,1)} %bitcast.15), calls=%async_computation.2 | async-start | bytes 393216 | tf_op jit(solution)/shard_map/all_to_all | solution.py:42
  84.1 1.4 %copy-start.2 = (bf16[2,512,96]{1,2,0:T(8,128)(2,1)S(1)}, bf16[2,512,96]{1,2,0:T(8,128)(2,1)}, u32[]{:S(2)}) copy-start(bf16[2,512,96]{1,2,0:T(8,128)(2,1)} %get-tuple-element.179) | copy-start | bytes 589828 | tf_op jit(solution)/shard_map/while
  85.5 0.7 copy-start.3
  98.6 1.4 %copy-start.2 = (bf16[2,512,96]{1,2,0:T(8,128)(2,1)S(1)}, bf16[2,512,96]{1,2,0:T(8,128)(2,1)}, u32[]{:S(2)}) copy-start(bf16[2,512,96]{1,2,0:T(8,128)(2,1)} %get-tuple-element.179) | copy-start | bytes 589828 | tf_op jit(solution)/shard_map/while
  99.9 0.7 copy-start.3
where the time goes:
time: 114 us; the launch traced here: 113 us
  blocking collectives  36.9 us (32%)
  matrix products  25.6 us (22%)
  local copies, waits for them, and re-layouts  19.5 us (17%)
  waiting for transfers between devices  13.3 us (12%)
  starting transfers between devices  11.7 us (10%)
  other arithmetic  4.42 us (4%)
  loops' own time  1.24 us (1%)
    dot_general x2, matrix products, attend_queries(): jnp.einsum('hrb,nb->hrn', bias_part, key_onehot, precision=lax.Precision....  16.2 us
    all_gather x1, blocking collectives, on_device(): gathered = lax.all_gather(features, 'group', axis=0, tiled=True)  14.1 us
    all_gather x1, blocking collectives, on_device(): bucket_group = lax.all_gather(node_bucket, 'seq', axis=0, tiled=True)  12.1 us
    all_to_all x1, blocking collectives, on_device(): lax.all_to_all(head_rows, 'seq', split_axis=0, concat_axis=1, tiled=True)  10.7 us
    gather x1, local copies, waits for them, and re-layouts, on_device(): query_rows_bias = my_cube[:, bucket_group, :]  7.87 us
    all_to_all x1, waiting for transfers between devices, on_device(): lax.all_to_all(query_send, 'seq', split_axis=1, concat_axis=0, tiled=True)  7.53 us
    all_to_all x1, waiting for transfers between devices, on_device(): lax.all_to_all(key_send, 'seq', split_axis=1, concat_axis=0, tiled=True)  5.79 us
    all_to_all x1, starting transfers between devices, on_device(): lax.all_to_all(query_send, 'seq', split_axis=1, concat_axis=0, tiled=True)  4.88 us
  transfers between devices with their start and end apart: 3, of which 2 were waited for; matrix products, arithmetic and copies ran while one was open for 12% of the time, Pallas kernels for 0%

commit v1 on v0

v1 whole, which is shorter than its diff:
```python
import functools
import math

import jax
import jax.numpy as jnp
import numpy as np
from jax import lax
from jax.experimental import pallas as pl
from jax.experimental.pallas import tpu as pltpu
from jax.sharding import PartitionSpec as P

H = 32
HD = 24
NB = 16
TILES = 8
LANES = 128
PAD = 32
QUAD = LANES // PAD
NT = (((1,), (1,)), ((), ()))
VMEM_LIMIT = 56 * 1024 * 1024


def vmem():
    return pl.BlockSpec(memory_space=pltpu.VMEM)


def smem():
    return pl.BlockSpec(memory_space=pltpu.SMEM)


def pad_matrix():
    rows = np.arange(16 * HD)
    cols = (rows // HD) * PAD + rows % HD
    sel = np.zeros((16 * HD, 16 * PAD), np.float32)
    sel[rows, cols] = 1.0
    return sel


def prepare_kernel(w_qk_ref, w_v_ref, bias_ref, sel_ref, wq_ref, wk_ref, wv_ref, table_ref):
    width = w_v_ref.shape[1]
    half = 16 * HD
    sel = sel_ref[...]
    for src, base, dst in ((w_qk_ref, 0, wq_ref), (w_qk_ref, width, wk_ref), (w_v_ref, 0, wv_ref)):
        for part in range(width // half):
            block = src[:, base + part * half : base + (part + 1) * half]
            dst[:, part * 512 : (part + 1) * 512] = jnp.dot(
                block, sel, preferred_element_type=jnp.float32
            ).astype(jnp.bfloat16)
    scaled = bias_ref[...] * math.sqrt(HD)
    high = scaled.astype(jnp.bfloat16).astype(jnp.float32)
    rest = scaled - high
    mid = rest.astype(jnp.bfloat16).astype(jnp.float32)
    low = rest - mid
    lane = lax.broadcasted_iota(jnp.int32, scaled.shape, 1) % LANES
    parts = jnp.where(lane < NB, high, jnp.where(lane < 2 * NB, mid, jnp.where(lane < 3 * NB, low, 0.0)))
    table_ref[...] = parts.astype(jnp.bfloat16)


def aggregate_kernel(src_ref, count_ref, feat_ref, gathered_ref, tiles_ref, bucket_ref, out_ref):
    rows, width = feat_ref.shape
    count = count_ref[0]
    picked = []
    masked = []
    for t in range(TILES):
        start = pl.multiple_of(src_ref[0, t] * rows, rows)
        picked.append(gathered_ref[pl.ds(start, rows), :])
        tile = tiles_ref[:, t * rows : (t + 1) * rows]
        masked.append(jnp.where(t < count, tile, jnp.zeros_like(tile)))
    total = feat_ref[...].astype(jnp.float32) + jnp.dot(
        jnp.concatenate(masked, axis=1),
        jnp.concatenate(picked, axis=0),
        preferred_element_type=jnp.float32,
    )
    mean_square = jnp.mean(total * total, axis=-1, keepdims=True)
    out_ref[:rows, :] = (total * lax.rsqrt(mean_square + 1e-06)).astype(jnp.bfloat16)
    bucket = bucket_ref[...].astype(jnp.float32)
    out_ref[rows:, :] = jnp.zeros((out_ref.shape[0] - rows, width), jnp.bfloat16)
    out_ref[rows:, :rows] = jnp.broadcast_to(bucket, (out_ref.shape[0] - rows, rows)).astype(
        jnp.bfloat16
    )


def one_hot_slab(bucket_row):
    n = bucket_row.shape[1]
    index = lax.broadcasted_iota(jnp.int32, (LANES, n), 0)
    wanted = jnp.where(index < 3 * NB, index % NB, -1).astype(jnp.float32)
    hot = jnp.where(wanted == bucket_row, 1.0, 0.0)
    return hot.T.astype(jnp.bfloat16)


def attend_kernel(
    own_ref, all_ref, wq_ref, wk_ref, wv_ref, table_ref, sel_ref, out_ref,
    k_ref, v_ref, hot_ref, q_ref, bias_ref, x0_ref, x1_ref, p0_ref, p1_ref, heads_ref,
):
    rows = out_ref.shape[0]
    blocks = all_ref.shape[0]
    keys = blocks * rows
    wide = k_ref.shape[1]
    quads = H // QUAD
    factor = math.log2(math.e) / math.sqrt(HD)

    for s in range(blocks):
        hot_ref[s * rows : (s + 1) * rows, :] = one_hot_slab(
            all_ref[s, rows : rows + 8, :rows].astype(jnp.float32)[0:1, :]
        )
    hot_q = one_hot_slab(own_ref[rows : rows + 8, :rows].astype(jnp.float32)[0:1, :])[:, :NB]
    q_ref[...] = jnp.dot(
        own_ref[:rows, :], wq_ref[...], preferred_element_type=jnp.float32
    ).astype(jnp.bfloat16)
    bias_ref[...] = jnp.dot(hot_q, table_ref[...], preferred_element_type=jnp.float32).astype(
        jnp.bfloat16
    )

    step = 4 if blocks % 4 == 0 else 1

    def project(i, carry):
        cols = pl.ds(pl.multiple_of(i * 256, 256), 256)
        for w_ref, dst in ((wk_ref, k_ref), (wv_ref, v_ref)):
            for s in range(0, blocks, step):
                block = jnp.concatenate([all_ref[s + j, :rows, :] for j in range(step)], axis=0)
                dst[s * rows : (s + step) * rows, cols] = jnp.dot(
                    block, w_ref[:, cols], preferred_element_type=jnp.float32
                ).astype(jnp.bfloat16)
        return carry

    lax.fori_loop(0, wide // 256, project, 0)

    lane_head = lax.broadcasted_iota(jnp.int32, (rows, LANES), 1) // PAD
    ones = jnp.ones((keys, LANES), jnp.bfloat16)

    def scores(m, x_ref):
        cols = pl.ds(pl.multiple_of(m * LANES, LANES), LANES)
        q = q_ref[:, cols]
        zero = jnp.zeros_like(q)
        left = jnp.concatenate([jnp.where(lane_head == h, q, zero) for h in range(QUAD)], axis=0)
        right = jnp.concatenate(
            [
                bias_ref[:, pl.ds(pl.multiple_of((m * QUAD + h) * LANES, LANES), LANES)]
                for h in range(QUAD)
            ],
            axis=0,
        )
        query = jnp.concatenate([left, right], axis=1)
        for n in range(0, keys, 256):
            key = jnp.concatenate([k_ref[n : n + 256, cols], hot_ref[n : n + 256, :]], axis=1)
            x_ref[:, n : n + 256] = lax.dot_general(
                query, key, NT, preferred_element_type=jnp.float32
            )

    def mix(m, x_ref, p_ref):
        cols = pl.ds(pl.multiple_of(m * LANES, LANES), LANES)
        for r in range(0, QUAD * rows, 16):
            x = x_ref[r : r + 16, :]
            peak = jnp.max(x, axis=-1, keepdims=True)
            p_ref[r : r + 16, :] = jnp.exp2((x - peak) * factor).astype(jnp.bfloat16)
        value = jnp.concatenate([v_ref[:, cols], ones], axis=1)
        mixed = jnp.dot(p_ref[...], value, preferred_element_type=jnp.float32)
        top = mixed[:rows, :LANES]
        total = mixed[:rows, LANES:]
        for h in range(1, QUAD):
            top = jnp.where(lane_head == h, mixed[h * rows : (h + 1) * rows, :LANES], top)
            total = jnp.where(lane_head == h, mixed[h * rows : (h + 1) * rows, LANES:], total)
        heads_ref[:, cols] = (top / total).astype(jnp.bfloat16)

    scores(0, x0_ref)

    def pair(i, carry):
        m = i * 2
        scores(m + 1, x1_ref)
        mix(m, x0_ref, p0_ref)
        scores(jnp.minimum(m + 2, quads - 1), x0_ref)
        mix(m + 1, x1_ref, p1_ref)
        return carry

    lax.fori_loop(0, quads // 2, pair, 0)

    half = 16 * HD
    for part in range(out_ref.shape[1] // half):
        out_ref[:, part * half : (part + 1) * half] = lax.dot_general(
            heads_ref[:, part * 512 : (part + 1) * 512], sel_ref[...], NT,
            preferred_element_type=jnp.float32,
        ).astype(jnp.bfloat16)


def on_device(features, tiles, tile_src, tile_count, node_bucket, w_qk, w_v, bias_table):
    rows, width = features.shape
    seq_count = lax.axis_size("seq")
    wide = H * PAD
    keys = seq_count * rows
    bf16 = jnp.bfloat16
    sel = jnp.asarray(pad_matrix(), bf16)
    params = pltpu.CompilerParams(vmem_limit_bytes=VMEM_LIMIT)

    cube = bias_table.reshape(H, NB, NB).transpose(1, 0, 2)
    cube = jnp.concatenate([cube, cube, cube, jnp.zeros((NB, H, LANES - 3 * NB), jnp.float32)], axis=2)
    cube = cube.reshape(NB, H * LANES)
    shape = jax.ShapeDtypeStruct
    wq, wk, wv, table = pl.pallas_call(
        prepare_kernel,
        out_shape=[shape((width, wide), bf16)] * 3 + [shape((NB, H * LANES), bf16)],
        in_specs=[vmem()] * 4,
        out_specs=[vmem()] * 4,
        compiler_params=params,
        cost_estimate=pl.CostEstimate(flops=2 * width * width * 3 * 512, bytes_accessed=9_000_000, transcendentals=0),
        name="prepare",
    )(w_qk, w_v, cube, sel)

    gathered = lax.all_gather(features, "group", axis=0, tiled=True)
    own = pl.pallas_call(
        aggregate_kernel,
        out_shape=shape((rows + 16, width), bf16),
        in_specs=[smem(), smem()] + [vmem()] * 4,
        out_specs=vmem(),
        compiler_params=params,
        name="aggregate",
    )(tile_src, tile_count, features, gathered, tiles, node_bucket.reshape(1, rows))

    everyone = lax.all_gather(own, "seq", axis=0, tiled=False)
    return pl.pallas_call(
        attend_kernel,
        out_shape=shape((rows, width), bf16),
        in_specs=[vmem()] * 7,
        out_specs=vmem(),
        scratch_shapes=[
            pltpu.VMEM((keys, wide), bf16),
            pltpu.VMEM((keys, wide), bf16),
            pltpu.VMEM((keys, LANES), bf16),
            pltpu.VMEM((rows, wide), bf16),
            pltpu.VMEM((rows, H * LANES), bf16),
            pltpu.VMEM((QUAD * rows, keys), jnp.float32),
            pltpu.VMEM((QUAD * rows, keys), jnp.float32),
            pltpu.VMEM((QUAD * rows, keys), bf16),
            pltpu.VMEM((QUAD * rows, keys), bf16),
            pltpu.VMEM((rows, wide), bf16),
        ],
        compiler_params=params,
        name="attend",
    )(own, everyone, wq, wk, wv, table, sel)


def solution(mesh):
    in_specs = (
        P(("group", "seq"), None),
        P(("group", "seq"), None),
        P(("group", "seq"), None),
        P(("group", "seq")),
        P(("group", "seq")),
        P(),
        P(),
        P(),
    )
    out_specs = P(("group", "seq"), None)
    return jax.shard_map(
        on_device, mesh=mesh, in_specs=in_specs, out_specs=out_specs, check_vma=False
    )
```

time: 114 us -> 74.1 us (0.65)
  matrix products: 25.6 us -> 0 us
  Pallas kernels: 0 us -> 23.7 us
  blocking collectives: 36.9 us -> 15.3 us
  local copies, waits for them, and re-layouts: 19.5 us -> 1.16 us
  between operations: 0.86 us -> 14.1 us
  starting transfers between devices: 11.7 us -> 0.01 us
  waiting for transfers between devices: 13.3 us -> 19.4 us
  other arithmetic: 4.42 us -> 0.2 us
  loops' own time: 1.24 us -> 0 us
    dot_general x9 -> x0, matrix products: 25.6 us -> none  [the longest x2 16.2 us: attend_queries(): jnp.einsum('hrb,nb->hrn', bias_part, key_onehot, precision=lax.Precision....]
    pallas_call x0 -> x3, Pallas kernels: none -> 23.7 us  [the longest x1 15.3 us: on_device(): pl.pallas_call(attend_kernel, out_shape=shape((rows, width), bf16), in_sp...]
    all_gather x0 -> x1, waiting for transfers between devices: none -> 19.4 us  [on_device(): everyone = lax.all_gather(own, 'seq', axis=0, tiled=False)]
    all_to_all x3 -> x0, waiting for transfers between devices: 13.3 us -> none  [the longest x1 7.53 us: on_device(): lax.all_to_all(query_send, 'seq', split_axis=1, concat_axis=0, tiled=True)]
    all_gather x1 -> x0, blocking collectives: 12.1 us -> none  [on_device(): bucket_group = lax.all_gather(node_bucket, 'seq', axis=0, tiled=True)]
    all_to_all x3 -> x0, starting transfers between devices: 11.7 us -> none  [the longest x1 4.88 us: on_device(): lax.all_to_all(query_send, 'seq', split_axis=1, concat_axis=0, tiled=True)]
    all_to_all x1 -> x0, blocking collectives: 10.7 us -> none  [on_device(): lax.all_to_all(head_rows, 'seq', split_axis=0, concat_axis=1, tiled=True)]
    gather x2 -> x0, local copies, waits for them, and re-layouts: 9.67 us -> none  [the longest x1 7.87 us: on_device(): query_rows_bias = my_cube[:, bucket_group, :]]
  transfers between devices with their start and end apart: 3 -> 1, of which waited for: 2 -> 1; matrix products, arithmetic and copies ran while one was open for 12% -> 2% of each run, Pallas kernels for 0% -> 8%
where the time goes in v1:
time: 74.1 us; the launch traced here: 73.8 us
  Pallas kernels  23.7 us (32%)
  waiting for transfers between devices  19.4 us (26%)
  blocking collectives  15.3 us (21%)
  between operations  14.1 us (19%)
  local copies, waits for them, and re-layouts  1.16 us (2%)
    all_gather x1, waiting for transfers between devices, on_device(): everyone = lax.all_gather(own, 'seq', axis=0, tiled=False)  19.4 us
    pallas_call x1, Pallas kernels, on_device(): pl.pallas_call(attend_kernel, out_shape=shape((rows, width), bf16), in_sp...  15.3 us
    all_gather x1, blocking collectives, on_device(): gathered = lax.all_gather(features, 'group', axis=0, tiled=True)  15.3 us
    pallas_call x1, Pallas kernels, on_device(): pl.pallas_call(prepare_kernel, out_shape=[shape((width, wide), bf16)] * 3...  6.01 us
    pallas_call x1, Pallas kernels, on_device(): pl.pallas_call(aggregate_kernel, out_shape=shape((rows + 16, width), bf16...  2.43 us
  transfers between devices with their start and end apart: 1, of which 1 were waited for; matrix products, arithmetic and copies ran while one was open for 2% of the time, Pallas kernels for 8%

profile of v1, /device:TPU:0, one launch (start us, length us, event | category | flops | bytes accessed | tf_op | source)
XLA Modules:
  0.0 73.8 jit_solution(1564328170957613170)
XLA Ops:
  6.5 0.0 copy-start
  6.5 0.0 all-gather.3.cloned.1.call-start
  6.5 15.3 %all_gather.9.gathered_ref = bf16[512,768]{1,0:T(8,128)(2,1)} all-gather(bf16[128,768]{1,0:T(8,128)(2,1)} %feat_ref.1), channel_id=1, replica_groups=mesh['group'=4,'seq'=8] {'group'}, dimensions={0}, use_global_device_ids=true | all-gather | bytes 983040 | tf_op jit(solution)/shard_map/all_gather | solution.py:208
  22.4 2.4 %aggregate.1.own_ref = bf16[144,768]{1,0:T(8,128)(2,1)} custom-call(s32[1,8]{1,0:T(1,128)} %src_ref.1, s32[1]{0:T(128)S(6)} %copy.18.count_ref, bf16[128,768]{1,0:T(8,128)(2,1)} %feat_ref.1, bf16[512,768]{1,0:T(8,128)(2,1)} %all_gather.9.gathered_ref, bf16[128,1024]{1,0:T(8,128)(2,1)} %tiles_ref.1, s32[1,128]{1,0:T(1,128)} %bitcast.13), custom_call_target="tpu_custom_call" | custom-call | tf_op jit(solution)/shard_map/aggregate/pallas_call | solution.py:209
  24.9 0.0 all-gather.3.cloned.1.call-update
  24.9 0.0 copy-done
  24.9 0.1 copy.11
  25.0 0.1 copy.12
  25.2 0.1 pad.3.clone
  25.2 0.2 maximum_maximum_fusion
  25.4 0.9 %copy.17 = f32[2,8,32,128]{3,1,2,0:T(8,128)} copy(f32[2,8,32,128]{3,2,1,0:T(8,128)S(1)} %bitcast.10) | data formatting | bytes 524288
  26.3 6.0 %prepare.1 = (bf16[768,1024]{1,0:T(8,128)(2,1)}, bf16[768,1024]{1,0:T(8,128)(2,1)}, bf16[768,1024]{1,0:T(8,128)(2,1)}, bf16[16,4096]{1,0:T(8,128)(2,1)}) custom-call(bf16[768,1536]{1,0:T(8,128)(2,1)} %w_qk_ref.1, bf16[768,768]{1,0:T(8,128)(2,1)} %w_v_ref.1, f32[16,4096]{1,0:T(8,128)} %bitcast.12, bf16[384,512]{1,0:T(8,128)(2,1)} %constant.4.clone.sel_ref), custom_call_target="tpu_custom_call" | custom-call | flops 1811939328 | bytes 9000000 | tf_op jit(solution)/shard_map/prepare/pallas_call | solution.py:198
  32.3 19.4 %all-gather.3.cloned.1.call-done = bf16[1152,768]{1,0:T(8,128)(2,1)} async-done(((bf16[144,768]{1,0:T(8,128)(2,1)}), bf16[1152,768]{1,0:T(8,128)(2,1)}) %all-gather.3.cloned.1.call-update) | async-done | bytes 1769488 | tf_op jit(solution)/shard_map/all_gather | solution.py:218
  51.7 15.3 %attend.1 = bf16[128,768]{1,0:T(8,128)(2,1)} custom-call(bf16[144,768]{1,0:T(8,128)(2,1)} %aggregate.1.own_ref, bf16[8,144,768]{2,1,0:T(8,128)(2,1)} %bitcast.9, bf16[768,1024]{1,0:T(8,128)(2,1)} %get-tuple-element.9.wq_ref, bf16[768,1024]{1,0:T(8,128)(2,1)} %get-tuple-element.10.wk_ref, bf16[768,1024]{1,0:T(8,128)(2,1)} %get-tuple-element.11.wv_ref, ...), custom_call_target="tpu_custom_call" | custom-call | tf_op jit(solution)/shard_map/attend/pallas_call | solution.py:219
  (1 shorter events, 0.0 us)
Async XLA Ops:
  6.5 18.4 %copy-start = (f32[32,256]{1,0:T(8,128)S(1)}, f32[32,256]{1,0:T(8,128)}, u32[]{:S(2)}) copy-start(f32[32,256]{1,0:T(8,128)} %param.16) | copy-start | bytes 98308
  6.5 45.2 %all-gather.3.cloned.1.call-start = ((), (), s32[]{:S(2)}) async-start(), calls=%async_computation | async-start | bytes 1990656 | tf_op jit(solution)/shard_map/all_gather | solution.py:218
Sparse Core Ops, SparseCore 0:
  25.0 26.6 all-gather.2

commit v2 on v1

v2 whole, which is shorter than its diff:
```python
import math

import jax
import jax.numpy as jnp
import numpy as np
from jax import lax
from jax.experimental import pallas as pl
from jax.experimental.pallas import tpu as pltpu
from jax.sharding import PartitionSpec as P

H = 32
HD = 24
NB = 16
TILES = 8
LANES = 128
PAD = 32
QUAD = LANES // PAD
WIDE = H * PAD
HALF = 16 * HD
HALF_PAD = 16 * PAD
NT = (((1,), (1,)), ((), ()))
MIB = 1024 * 1024
BF16 = jnp.bfloat16
F32 = jnp.float32


def vmem():
    return pl.BlockSpec(memory_space=pltpu.VMEM)


def smem():
    return pl.BlockSpec(memory_space=pltpu.SMEM)


def limit(mib):
    return pltpu.CompilerParams(vmem_limit_bytes=mib * MIB)


def shape(*dims, dtype=BF16):
    return jax.ShapeDtypeStruct(dims, dtype)


def cost(flops, nbytes):
    return pl.CostEstimate(flops=int(flops), bytes_accessed=int(nbytes), transcendentals=0)


def pad_matrix():
    rows = np.arange(HALF)
    cols = (rows // HD) * PAD + rows % HD
    sel = np.zeros((HALF, HALF_PAD), np.float32)
    sel[rows, cols] = 1.0
    return sel


def one_hot_slab(bucket_row):
    n = bucket_row.shape[1]
    index = lax.broadcasted_iota(jnp.int32, (LANES, n), 0)
    wanted = jnp.where(index < 3 * NB, index % NB, -1)
    hot = jnp.where(wanted == bucket_row, 1.0, 0.0)
    return hot.T.astype(BF16)


def prepare_kernel(w_qk_ref, w_v_ref, cube_ref, sel_ref, bucket_ref, wq_ref, wk_ref, wv_ref, bias_ref):
    width = w_v_ref.shape[1]
    sel = sel_ref[...]
    for src, base, dst in ((w_qk_ref, 0, wq_ref), (w_qk_ref, width, wk_ref), (w_v_ref, 0, wv_ref)):
        for part in range(width // HALF):
            block = src[:, base + part * HALF : base + (part + 1) * HALF]
            dst[:, part * HALF_PAD : (part + 1) * HALF_PAD] = jnp.dot(
                block, sel, preferred_element_type=F32
            ).astype(BF16)
    scaled = cube_ref[...] * math.sqrt(HD)
    high = scaled.astype(BF16).astype(F32)
    rest = scaled - high
    mid = rest.astype(BF16).astype(F32)
    low = rest - mid
    lane = lax.broadcasted_iota(jnp.int32, scaled.shape, 1) % LANES
    parts = jnp.where(
        lane < NB, high, jnp.where(lane < 2 * NB, mid, jnp.where(lane < 3 * NB, low, 0.0))
    )
    hot = one_hot_slab(bucket_ref[...])[:, :NB]
    bias_ref[...] = jnp.dot(hot, parts.astype(BF16), preferred_element_type=F32).astype(BF16)


def aggregate_kernel(src_ref, count_ref, me_ref, tiles_ref, *refs):
    feature_refs, out_ref, held = refs[:-2], refs[-2], refs[-1]
    rows = out_ref.shape[0]
    for d, ref in enumerate(feature_refs):
        held[d * rows : (d + 1) * rows, :] = ref[...]
    count = count_ref[0]
    me = me_ref[0]
    picked = []
    masked = []
    for t in range(TILES):
        start = pl.multiple_of((src_ref[0, t] ^ me) * rows, rows)
        picked.append(held[pl.ds(start, rows), :])
        tile = tiles_ref[:, t * rows : (t + 1) * rows]
        masked.append(jnp.where(t < count, tile, jnp.zeros_like(tile)))
    total = feature_refs[0][...].astype(F32) + jnp.dot(
        jnp.concatenate(masked, axis=1),
        jnp.concatenate(picked, axis=0),
        preferred_element_type=F32,
    )
    mean_square = jnp.mean(total * total, axis=-1, keepdims=True)
    out_ref[...] = (total * lax.rsqrt(mean_square + 1e-06)).astype(BF16)


def query_kernel(own_ref, wq_ref, bucket_ref, q_ref, hot_ref):
    rows = own_ref.shape[0]
    q_ref[...] = jnp.dot(own_ref[...], wq_ref[...], preferred_element_type=F32).astype(BF16)
    for s in range(bucket_ref.shape[0]):
        hot_ref[s * rows : (s + 1) * rows, :] = one_hot_slab(bucket_ref[s : s + 1, :])


def project_kernel(first_ref, second_ref, wk_ref, wv_ref, k_ref, v_ref):
    block = jnp.concatenate([first_ref[...], second_ref[...]], axis=0)
    for w_ref, dst in ((wk_ref, k_ref), (wv_ref, v_ref)):
        for n in range(0, WIDE, 256):
            dst[:, n : n + 256] = jnp.dot(
                block, w_ref[:, n : n + 256], preferred_element_type=F32
            ).astype(BF16)


def attend_kernel(q_ref, bias_ref, hot_ref, sel_ref, *refs):
    pairs = (len(refs) - 6) // 2
    k_refs, v_refs = refs[:pairs], refs[pairs : 2 * pairs]
    out_ref, x0_ref, x1_ref, p0_ref, p1_ref, heads_ref = refs[2 * pairs :]
    rows = out_ref.shape[0]
    span = k_refs[0].shape[0]
    quads = H // QUAD
    factor = math.log2(math.e) / math.sqrt(HD)
    lane_head = lax.broadcasted_iota(jnp.int32, (rows, LANES), 1) // PAD
    ones = jnp.ones((span, LANES), BF16)

    def scores(m, x_ref):
        cols = pl.ds(pl.multiple_of(m * LANES, LANES), LANES)
        q = q_ref[:, cols]
        zero = jnp.zeros_like(q)
        left = jnp.concatenate([jnp.where(lane_head == h, q, zero) for h in range(QUAD)], axis=0)
        right = jnp.concatenate(
            [
                bias_ref[:, pl.ds(pl.multiple_of((m * QUAD + h) * LANES, LANES), LANES)]
                for h in range(QUAD)
            ],
            axis=0,
        )
        query = jnp.concatenate([left, right], axis=1)
        for n, k_ref in enumerate(k_refs):
            part = slice(n * span, (n + 1) * span)
            key = jnp.concatenate([k_ref[:, cols], hot_ref[part, :]], axis=1)
            x_ref[:, part] = lax.dot_general(query, key, NT, preferred_element_type=F32)

    def mix(m, x_ref, p_ref):
        cols = pl.ds(pl.multiple_of(m * LANES, LANES), LANES)
        for r in range(0, QUAD * rows, 16):
            x = x_ref[r : r + 16, :]
            peak = jnp.max(x, axis=-1, keepdims=True)
            p_ref[r : r + 16, :] = jnp.exp2((x - peak) * factor).astype(BF16)
        value = jnp.concatenate(
            [jnp.concatenate([v_ref[:, cols], ones], axis=1) for v_ref in v_refs], axis=0
        )
        mixed = jnp.dot(p_ref[...], value, preferred_element_type=F32)
        top = mixed[:rows, :LANES]
        total = mixed[:rows, LANES:]
        for h in range(1, QUAD):
            top = jnp.where(lane_head == h, mixed[h * rows : (h + 1) * rows, :LANES], top)
            total = jnp.where(lane_head == h, mixed[h * rows : (h + 1) * rows, LANES:], total)
        heads_ref[:, cols] = (top / total).astype(BF16)

    scores(0, x0_ref)

    def two(i, carry):
        m = i * 2
        scores(m + 1, x1_ref)
        mix(m, x0_ref, p0_ref)
        scores(jnp.minimum(m + 2, quads - 1), x0_ref)
        mix(m + 1, x1_ref, p1_ref)
        return carry

    lax.fori_loop(0, quads // 2, two, 0)

    for part in range(out_ref.shape[1] // HALF):
        out_ref[:, part * HALF : (part + 1) * HALF] = lax.dot_general(
            heads_ref[:, part * HALF_PAD : (part + 1) * HALF_PAD], sel_ref[...], NT,
            preferred_element_type=F32,
        ).astype(BF16)


def swap(array, axis, distance):
    return lax.ppermute(array, axis, [(i, i ^ distance) for i in range(lax.axis_size(axis))])


def on_device(features, tiles, tile_src, tile_count, node_bucket, w_qk, w_v, bias_table):
    rows, width = features.shape
    groups = lax.axis_size("group")
    seq_count = lax.axis_size("seq")
    keys = seq_count * rows
    sel = jnp.asarray(pad_matrix(), BF16)
    own_bucket = node_bucket.reshape(1, rows)

    blocks = [features] + [swap(features, "group", d) for d in range(1, groups)]
    buckets = own_bucket
    step = 1
    while step < seq_count:
        buckets = jnp.concatenate([buckets, swap(buckets, "seq", step)], axis=0)
        step *= 2

    cube = bias_table.reshape(H, NB, NB).transpose(1, 0, 2)
    cube = jnp.concatenate([cube, cube, cube, jnp.zeros((NB, H, LANES - 3 * NB), F32)], axis=2)
    cube = cube.reshape(NB, H * LANES)
    wq, wk, wv, bias = pl.pallas_call(
        prepare_kernel,
        out_shape=[shape(width, WIDE)] * 3 + [shape(rows, H * LANES)],
        in_specs=[vmem()] * 5,
        out_specs=[vmem()] * 4,
        compiler_params=limit(24),
        cost_estimate=cost(6 * width * width * HALF_PAD, 10_000_000),
        name="prepare",
    )(w_qk, w_v, cube, sel, own_bucket)

    own = pl.pallas_call(
        aggregate_kernel,
        out_shape=shape(rows, width),
        in_specs=[smem()] * 3 + [vmem()] * (1 + groups),
        out_specs=vmem(),
        scratch_shapes=[pltpu.VMEM((groups * rows, width), BF16)],
        compiler_params=limit(24),
        name="aggregate",
    )(tile_src, tile_count, lax.axis_index("group").reshape(1), tiles, *blocks)

    far = [own] + [swap(own, "seq", 2 * d) for d in range(1, seq_count // 2)]
    near = [swap(block, "seq", 1) for block in far]

    q, hot = pl.pallas_call(
        query_kernel,
        out_shape=[shape(rows, WIDE), shape(keys, LANES)],
        in_specs=[vmem()] * 3,
        out_specs=[vmem()] * 2,
        compiler_params=limit(16),
        cost_estimate=cost(2 * rows * width * WIDE, 2_000_000),
        name="query",
    )(own, wq, buckets)
    k_parts = []
    v_parts = []
    for first, second in zip(far, near):
        k, v = pl.pallas_call(
            project_kernel,
            out_shape=[shape(2 * rows, WIDE)] * 2,
            in_specs=[vmem()] * 4,
            out_specs=[vmem()] * 2,
            compiler_params=limit(16),
            cost_estimate=cost(8 * rows * width * WIDE, 4_000_000),
            name="project",
        )(first, second, wk, wv)
        k_parts.append(k)
        v_parts.append(v)

    need = 2 * QUAD * rows * keys * 6 + 4 * keys * WIDE + 2 * keys * LANES
    return pl.pallas_call(
        attend_kernel,
        out_shape=shape(rows, width),
        in_specs=[vmem()] * (4 + 2 * len(k_parts)),
        out_specs=vmem(),
        scratch_shapes=[
            pltpu.VMEM((QUAD * rows, keys), F32),
            pltpu.VMEM((QUAD * rows, keys), F32),
            pltpu.VMEM((QUAD * rows, keys), BF16),
            pltpu.VMEM((QUAD * rows, keys), BF16),
            pltpu.VMEM((rows, WIDE), BF16),
        ],
        compiler_params=limit(need // MIB + 8),
        name="attend",
    )(q, bias, hot, sel, *k_parts, *v_parts)


def solution(mesh):
    in_specs = (
        P(("group", "seq"), None),
        P(("group", "seq"), None),
        P(("group", "seq"), None),
        P(("group", "seq")),
        P(("group", "seq")),
        P(),
        P(),
        P(),
    )
    out_specs = P(("group", "seq"), None)
    return jax.shard_map(
        on_device, mesh=mesh, in_specs=in_specs, out_specs=out_specs, check_vma=False
    )
```

time: 74.1 us -> 48.3 us (0.65)
  blocking collectives: 15.3 us -> 0 us
  starting transfers between devices: 0.01 us -> 14.7 us
  between operations: 14.1 us -> 0.84 us
  Pallas kernels: 23.7 us -> 15.9 us
  waiting for transfers between devices: 19.4 us -> 12.9 us
  local copies, waits for them, and re-layouts: 1.16 us -> 2.9 us
    all_gather x1 -> x0, waiting for transfers between devices: 19.4 us -> none  [on_device(): everyone = lax.all_gather(own, 'seq', axis=0, tiled=False)]
    all_gather x1 -> x0, blocking collectives: 15.3 us -> none  [on_device(): gathered = lax.all_gather(features, 'group', axis=0, tiled=True)]
    ppermute x0 -> x13, starting transfers between devices: none -> 14.7 us  [swap(): lax.ppermute(array, axis, [(i, i ^ distance) for i in range(lax.axis_size...]
    ppermute x0 -> x13, waiting for transfers between devices: none -> 12.9 us  [swap(): lax.ppermute(array, axis, [(i, i ^ distance) for i in range(lax.axis_size...]
    pallas_call x3 -> x8, Pallas kernels: 23.7 us -> 15.9 us  [the longest x1 7.61 us: on_device(): pl.pallas_call(attend_kernel, out_shape=shape(rows, width), in_specs=[vme...]
    unnamed x4 -> x16, local copies, waits for them, and re-layouts: 0.96 us -> 2.69 us
  transfers between devices with their start and end apart: 1 -> 13, of which waited for: 1 -> 3; matrix products, arithmetic and copies ran while one was open for 2% -> 4% of each run, Pallas kernels for 8% -> 15%
where the time goes in v2:
time: 48.3 us; the launch traced here: 48.1 us
  Pallas kernels  15.9 us (33%)
  starting transfers between devices  14.7 us (30%)
  waiting for transfers between devices  12.9 us (27%)
  local copies, waits for them, and re-layouts  2.9 us (6%)
  other arithmetic  0.89 us (2%)
  between operations  0.84 us (2%)
    ppermute x13, starting transfers between devices, swap(): lax.ppermute(array, axis, [(i, i ^ distance) for i in range(lax.axis_size...  14.7 us
    ppermute x13, waiting for transfers between devices, swap(): lax.ppermute(array, axis, [(i, i ^ distance) for i in range(lax.axis_size...  12.9 us
    pallas_call x1, Pallas kernels, on_device(): pl.pallas_call(attend_kernel, out_shape=shape(rows, width), in_specs=[vme...  7.61 us
    pallas_call x4, Pallas kernels, on_device(): pl.pallas_call(project_kernel, out_shape=[shape(2 * rows, WIDE)] * 2, in_...  3.95 us
    pallas_call x1, Pallas kernels, on_device(): pl.pallas_call(prepare_kernel, out_shape=[shape(width, WIDE)] * 3 + [shap...  2.87 us
    unnamed x16, local copies, waits for them, and re-layouts  2.69 us
    pallas_call x1, Pallas kernels, on_device(): pl.pallas_call(aggregate_kernel, out_shape=shape(rows, width), in_specs=[...  1.07 us
  transfers between devices with their start and end apart: 13, of which 3 were waited for; matrix products, arithmetic and copies ran while one was open for 4% of the time, Pallas kernels for 15%

profile of v2, /device:TPU:0, one launch (start us, length us, event | category | flops | bytes accessed | tf_op | source)
XLA Modules:
  0.0 48.1 jit_solution(663552887762574599)
XLA Ops:
  0.0 0.0 copy-start
  0.0 0.0 copy-start.3
  0.0 0.0 copy-start.2
  0.0 0.0 copy-start.4
  0.0 0.0 copy-start.1
  0.0 0.0 copy-start.6
  0.0 0.5 %collective-permute-start.3 = (s32[1,128]{1,0:T(1,128)}, s32[1,128]{1,0:T(1,128)S(1)}, u32[]{:S(2)}, u32[]{:S(2)}) collective-permute-start(s32[1,128]{1,0:T(1,128)} %bitcast.10), channel_id=1, source_target_pairs={{0,1},{1,0},{2,3},{3,2},{4,5},{5,4},{6,7},{7,6},{8,9},{9,8},{10,11... | collective-permute-start | bytes 1544 | tf_op jit(solution)/shard_map/ppermute | solution.py:190
  0.6 2.6 %collective-permute-start.1 = (bf16[128,768]{1,0:T(8,128)(2,1)}, bf16[128,768]{1,0:T(8,128)(2,1)S(1)}, u32[]{:S(2)}, u32[]{:S(2)}) collective-permute-start(bf16[128,768]{1,0:T(8,128)(2,1)} %refs_0_.1), channel_id=1, source_target_pairs={{0,16},{8,24},{16,0},{24,8},{1,17},{9,25},{17,1},{25,9},{2,18},{10... | collective-permute-start | bytes 589832 | tf_op jit(solution)/shard_map/ppermute | solution.py:190
  3.2 1.5 %collective-permute-start = (bf16[128,768]{1,0:T(8,128)(2,1)}, bf16[128,768]{1,0:T(8,128)(2,1)S(1)}, u32[]{:S(2)}, u32[]{:S(2)}) collective-permute-start(bf16[128,768]{1,0:T(8,128)(2,1)} %refs_0_.1), channel_id=1, source_target_pairs={{0,8},{8,0},{16,24},{24,16},{1,9},{9,1},{17,25},{25,17},{2,10},{10... | collective-permute-start | bytes 589832 | tf_op jit(solution)/shard_map/ppermute | solution.py:190
  4.6 0.0 collective-permute-start.2
  4.7 0.9 %copy.11 = f32[32,256]{0,1:T(8,128)S(1)} copy(f32[32,256]{1,0:T(8,128)} %param.16) | data formatting | bytes 65536 | tf_op args[7]
  5.5 0.1 copy.12
  5.7 0.1 pad.12.clone
  5.8 0.0 collective-permute-done.3
  5.8 0.7 %pad_add_fusion.2 = s32[2,128]{1,0:T(2,128)S(1)} fusion(s32[1,128]{1,0:T(1,128)S(1)} %collective-permute-done.3, s32[1,128]{1,0:T(1,128)} %bitcast.11), kind=kLoop, calls=%fused_computation.4 | loop fusion | flops 256 | bytes 2048 | tf_op jit(solution)/shard_map/concatenate | solution.py:205
  6.4 2.0 %collective-permute-start.4 = (s32[2,128]{1,0:T(2,128)S(1)}, s32[2,128]{1,0:T(2,128)S(1)}, u32[]{:S(2)}, u32[]{:S(2)}) collective-permute-start(s32[2,128]{1,0:T(2,128)S(1)} %pad_add_fusion.2), channel_id=1, source_target_pairs={{0,2},{1,3},{2,0},{3,1},{4,6},{5,7},{6,4},{7,5},{8,10},{9,11},{10,... | collective-permute-start | bytes 3080 | tf_op jit(solution)/shard_map/ppermute | solution.py:190
  8.4 0.2 maximum_maximum_fusion
  9.3 0.2 copy.17
  9.5 0.0 collective-permute-done.1.refs_2_
  9.5 1.6 %collective-permute-done.refs_1_ = bf16[128,768]{1,0:T(8,128)(2,1)S(1)} collective-permute-done((bf16[128,768]{1,0:T(8,128)(2,1)}, bf16[128,768]{1,0:T(8,128)(2,1)S(1)}, u32[]{:S(2)}, u32[]{:S(2)}) %collective-permute-start) | collective-permute-done | bytes 196640 | tf_op jit(solution)/shard_map/ppermute | solution.py:190
  11.1 3.2 %collective-permute-done.2.refs_3_ = bf16[128,768]{1,0:T(8,128)(2,1)S(1)} collective-permute-done((bf16[128,768]{1,0:T(8,128)(2,1)}, bf16[128,768]{1,0:T(8,128)(2,1)S(1)}, u32[]{:S(2)}, u32[]{:S(2)}) %collective-permute-start.2) | collective-permute-done | bytes 196640 | tf_op jit(solution)/shard_map/ppermute | solution.py:190
  14.3 0.0 copy-done.2
  14.3 0.0 copy-done.4
  14.3 0.0 copy-done.1
  14.3 1.1 %aggregate.1.own_ref.first_ref = bf16[128,768]{1,0:T(8,128)(2,1)S(1)} custom-call(s32[1,8]{1,0:T(1,128)S(1)} %copy-done.4, s32[1]{0:T(128)S(6)} %copy.18.count_ref, s32[1]{0:T(128)} %bitcast.me_ref, bf16[128,1024]{1,0:T(8,128)(2,1)S(1)} %copy-done.1, bf16[128,768]{1,0:T(8,128)(2,1)S(1)} %copy-done.2, bf16[128,768]{1,0:T(8,128)(2,1)S(1)} %collective-permute-done.refs_1_, ...), custom_call_target="tpu_custom_call" | custom-call | tf_op jit(solution)/shard_map/aggregate/pallas_call | solution.py:221
  15.4 3.9 %collective-permute-start.11 = (bf16[128,768]{1,0:T(8,128)(2,1)S(1)}, bf16[128,768]{1,0:T(8,128)(2,1)S(1)}, u32[]{:S(2)}, u32[]{:S(2)}) collective-permute-start(bf16[128,768]{1,0:T(8,128)(2,1)S(1)} %aggregate.1.own_ref.first_ref), channel_id=1, source_target_pairs={{0,6},{1,7},{2,4},{3,5},{4,2},{5,3},{6,0},{7,1},{8,14},{9,15},{10,... | collective-permute-start | bytes 589832 | tf_op jit(solution)/shard_map/ppermute | solution.py:190
  19.2 0.0 collective-permute-start.9
  19.2 0.0 collective-permute-done.4
  19.2 0.0 copy-done.3
  19.3 3.0 %collective-permute-start.5 = (s32[4,128]{1,0:T(4,128)S(1)}, s32[4,128]{1,0:T(4,128)S(1)}, u32[]{:S(2)}, u32[]{:S(2)}) collective-permute-start(s32[4,128]{1,0:T(4,128)S(1)} %pad_add_fusion.1), channel_id=1, source_target_pairs={{0,4},{1,5},{2,6},{3,7},{4,0},{5,1},{6,2},{7,3},{8,12},{9,13},{10,... | collective-permute-start | bytes 6152 | tf_op jit(solution)/shard_map/ppermute | solution.py:190
  22.2 0.0 collective-permute-start.7
  22.3 0.0 collective-permute-start.6
  22.3 0.0 copy-done
  22.3 0.0 copy-done.6
  22.3 0.0 copy-start.5
  22.3 1.7 %copy-done.5 = bf16[768,1536]{1,0:T(8,128)(2,1)S(1)} copy-done((bf16[768,1536]{1,0:T(8,128)(2,1)S(1)}, bf16[768,1536]{1,0:T(8,128)(2,1)}, u32[]{:S(2)}) %copy-start.5) | copy-done | bytes 2359320
  23.9 2.9 %prepare.1 = (bf16[768,1024]{1,0:T(8,128)(2,1)S(1)}, bf16[768,1024]{1,0:T(8,128)(2,1)S(1)}, bf16[768,1024]{1,0:T(8,128)(2,1)S(1)}, bf16[128,4096]{1,0:T(8,128)(2,1)S(1)}) custom-call(bf16[768,1536]{1,0:T(8,128)(2,1)S(1)} %copy-done.5, bf16[768,768]{1,0:T(8,128)(2,1)S(1)} %copy-done.6, f32[16,4096]{1,0:T(8,128)S(1)} %bitcast.9, bf16[384,512]{1,0:T(8,128)(2,1)S(1)} %copy-done, ...), custom_call_target="tpu_custom_call" | custom-call | flops 1811939328 | bytes 10000000 | tf_op jit(solution)/shard_map/prepare/pallas_call | solution.py:211
  26.8 0.0 collective-permute-done.11.first_ref
  26.8 0.6 %collective-permute-start.12 = (bf16[128,768]{1,0:T(8,128)(2,1)S(1)}, bf16[128,768]{1,0:T(8,128)(2,1)S(1)}, u32[]{:S(2)}, u32[]{:S(2)}) collective-permute-start(bf16[128,768]{1,0:T(8,128)(2,1)S(1)} %collective-permute-done.11.first_ref), channel_id=1, source_target_pairs={{0,1},{1,0},{2,3},{3,2},{4,5},{5,4},{6,7},{7,6},{8,9},{9,8},{10,11... | collective-permute-start | bytes 589832 | tf_op jit(solution)/shard_map/ppermute | solution.py:190
  27.4 8.1 %collective-permute-done.9.first_ref = bf16[128,768]{1,0:T(8,128)(2,1)S(1)} collective-permute-done((bf16[128,768]{1,0:T(8,128)(2,1)S(1)}, bf16[128,768]{1,0:T(8,128)(2,1)S(1)}, u32[]{:S(2)}, u32[]{:S(2)}) %collective-permute-start.9) | collective-permute-done | bytes 196640 | tf_op jit(solution)/shard_map/ppermute | solution.py:190
  35.5 0.0 collective-permute-start.10
  35.5 0.0 collective-permute-done.5
  35.5 0.4 query.1
  35.9 0.0 collective-permute-done.7.first_ref
  35.9 0.6 %collective-permute-start.8 = (bf16[128,768]{1,0:T(8,128)(2,1)S(1)}, bf16[128,768]{1,0:T(8,128)(2,1)S(1)}, u32[]{:S(2)}, u32[]{:S(2)}) collective-permute-start(bf16[128,768]{1,0:T(8,128)(2,1)S(1)} %collective-permute-done.7.first_ref), channel_id=1, source_target_pairs={{0,1},{1,0},{2,3},{3,2},{4,5},{5,4},{6,7},{7,6},{8,9},{9,8},{10,11... | collective-permute-start | bytes 589832 | tf_op jit(solution)/shard_map/ppermute | solution.py:190
  36.5 0.0 collective-permute-done.6.second_ref
  36.5 1.0 %project.4 = (bf16[256,1024]{1,0:T(8,128)(2,1)S(1)}, bf16[256,1024]{1,0:T(8,128)(2,1)S(1)}) custom-call(bf16[128,768]{1,0:T(8,128)(2,1)S(1)} %aggregate.1.own_ref.first_ref, bf16[128,768]{1,0:T(8,128)(2,1)S(1)} %collective-permute-done.6.second_ref, bf16[768,1024]{1,0:T(8,128)(2,1)S(1)} %get-tuple-element.23.wk_ref, ...), custom_call_target="tpu_custom_call" | custom-call | flops 805306368 | bytes 4000000 | tf_op jit(solution)/shard_map/project/pallas_call | solution.py:246
  37.5 0.0 collective-permute-done.12.second_ref
  37.5 1.0 %project.7 = (bf16[256,1024]{1,0:T(8,128)(2,1)S(1)}, bf16[256,1024]{1,0:T(8,128)(2,1)S(1)}) custom-call(bf16[128,768]{1,0:T(8,128)(2,1)S(1)} %collective-permute-done.11.first_ref, bf16[128,768]{1,0:T(8,128)(2,1)S(1)} %collective-permute-done.12.second_ref, bf16[768,1024]{1,0:T(8,128)(2,1)S(1)} %get-tuple-element.23.wk_ref, ...), custom_call_target="tpu_custom_call" | custom-call | flops 805306368 | bytes 4000000 | tf_op jit(solution)/shard_map/project/pallas_call | solution.py:246
  38.5 0.0 collective-permute-done.10.second_ref
  38.5 1.0 %project.6 = (bf16[256,1024]{1,0:T(8,128)(2,1)S(1)}, bf16[256,1024]{1,0:T(8,128)(2,1)S(1)}) custom-call(bf16[128,768]{1,0:T(8,128)(2,1)S(1)} %collective-permute-done.9.first_ref, bf16[128,768]{1,0:T(8,128)(2,1)S(1)} %collective-permute-done.10.second_ref, bf16[768,1024]{1,0:T(8,128)(2,1)S(1)} %get-tuple-element.23.wk_ref, ...), custom_call_target="tpu_custom_call" | custom-call | flops 805306368 | bytes 4000000 | tf_op jit(solution)/shard_map/project/pallas_call | solution.py:246
  39.5 0.0 collective-permute-done.8.second_ref
  39.5 1.0 %project.5 = (bf16[256,1024]{1,0:T(8,128)(2,1)S(1)}, bf16[256,1024]{1,0:T(8,128)(2,1)S(1)}) custom-call(bf16[128,768]{1,0:T(8,128)(2,1)S(1)} %collective-permute-done.7.first_ref, bf16[128,768]{1,0:T(8,128)(2,1)S(1)} %collective-permute-done.8.second_ref, bf16[768,1024]{1,0:T(8,128)(2,1)S(1)} %get-tuple-element.23.wk_ref, ...), custom_call_target="tpu_custom_call" | custom-call | flops 805306368 | bytes 4000000 | tf_op jit(solution)/shard_map/project/pallas_call | solution.py:246
  40.5 7.6 %attend.1 = bf16[128,768]{1,0:T(8,128)(2,1)} custom-call(bf16[128,1024]{1,0:T(8,128)(2,1)S(1)} %get-tuple-element.20.q_ref, bf16[128,4096]{1,0:T(8,128)(2,1)S(1)} %get-tuple-element.21.bias_ref, bf16[1024,128]{1,0:T(8,128)(2,1)S(1)} %get-tuple-element.22.hot_ref, bf16[384,512]{1,0:T(8,128)(2,1)S(1)} %copy-done, ...), custom_call_target="tpu_custom_call" | custom-call | tf_op jit(solution)/shard_map/attend/pallas_call | solution.py:259
  (3 shorter events, 0.0 us)
Async XLA Ops:
  0.0 22.3 %copy-start = (bf16[384,512]{1,0:T(8,128)(2,1)S(1)}, bf16[384,512]{1,0:T(8,128)(2,1)}, u32[]{:S(2)}) copy-start(bf16[384,512]{1,0:T(8,128)(2,1)} %constant.9.clone.sel_ref) | copy-start | bytes 1179652
  0.0 19.2 %copy-start.3 = (s32[128]{0:T(128)S(1)}, s32[128]{0:T(128)}, u32[]{:S(2)}) copy-start(s32[128]{0:T(128)} %param.13) | copy-start | bytes 1540
  0.0 14.3 %copy-start.2 = (bf16[128,768]{1,0:T(8,128)(2,1)S(1)}, bf16[128,768]{1,0:T(8,128)(2,1)}, u32[]{:S(2)}) copy-start(bf16[128,768]{1,0:T(8,128)(2,1)} %refs_0_.1) | copy-start | bytes 589828
  0.0 14.3 %copy-start.4 = (s32[1,8]{1,0:T(1,128)S(1)}, s32[1,8]{1,0:T(1,128)}, u32[]{:S(2)}) copy-start(s32[1,8]{1,0:T(1,128)} %src_ref.1) | copy-start | bytes 100
  0.0 14.3 %copy-start.1 = (bf16[128,1024]{1,0:T(8,128)(2,1)S(1)}, bf16[128,1024]{1,0:T(8,128)(2,1)}, u32[]{:S(2)}) copy-start(bf16[128,1024]{1,0:T(8,128)(2,1)} %tiles_ref.1) | copy-start | bytes 786436
  0.0 22.2 %copy-start.6 = (bf16[768,768]{1,0:T(8,128)(2,1)S(1)}, bf16[768,768]{1,0:T(8,128)(2,1)}, u32[]{:S(2)}) copy-start(bf16[768,768]{1,0:T(8,128)(2,1)} %w_v_ref.1) | copy-start | bytes 3538948
  0.0 5.7 %collective-permute-start.3 = (s32[1,128]{1,0:T(1,128)}, s32[1,128]{1,0:T(1,128)S(1)}, u32[]{:S(2)}, u32[]{:S(2)}) collective-permute-start(s32[1,128]{1,0:T(1,128)} %bitcast.10), channel_id=1, source_target_pairs={{0,1},{1,0},{2,3},{3,2},{4,5},{5,4},{6,7},{7,6},{8,9},{9,8},{10,11... | collective-permute-start | bytes 1544 | tf_op jit(solution)/shard_map/ppermute | solution.py:190
  0.6 8.9 %collective-permute-start.1 = (bf16[128,768]{1,0:T(8,128)(2,1)}, bf16[128,768]{1,0:T(8,128)(2,1)S(1)}, u32[]{:S(2)}, u32[]{:S(2)}) collective-permute-start(bf16[128,768]{1,0:T(8,128)(2,1)} %refs_0_.1), channel_id=1, source_target_pairs={{0,16},{8,24},{16,0},{24,8},{1,17},{9,25},{17,1},{25,9},{2,18},{10... | collective-permute-start | bytes 589832 | tf_op jit(solution)/shard_map/ppermute | solution.py:190
  3.2 8.0 %collective-permute-start = (bf16[128,768]{1,0:T(8,128)(2,1)}, bf16[128,768]{1,0:T(8,128)(2,1)S(1)}, u32[]{:S(2)}, u32[]{:S(2)}) collective-permute-start(bf16[128,768]{1,0:T(8,128)(2,1)} %refs_0_.1), channel_id=1, source_target_pairs={{0,8},{8,0},{16,24},{24,16},{1,9},{9,1},{17,25},{25,17},{2,10},{10... | collective-permute-start | bytes 589832 | tf_op jit(solution)/shard_map/ppermute | solution.py:190
  4.6 9.6 %collective-permute-start.2 = (bf16[128,768]{1,0:T(8,128)(2,1)}, bf16[128,768]{1,0:T(8,128)(2,1)S(1)}, u32[]{:S(2)}, u32[]{:S(2)}) collective-permute-start(bf16[128,768]{1,0:T(8,128)(2,1)} %refs_0_.1), channel_id=1, source_target_pairs={{0,24},{8,16},{16,8},{24,0},{1,25},{9,17},{17,9},{25,1},{2,26},{10... | collective-permute-start | bytes 589832 | tf_op jit(solution)/shard_map/ppermute | solution.py:190
  6.4 12.8 %collective-permute-start.4 = (s32[2,128]{1,0:T(2,128)S(1)}, s32[2,128]{1,0:T(2,128)S(1)}, u32[]{:S(2)}, u32[]{:S(2)}) collective-permute-start(s32[2,128]{1,0:T(2,128)S(1)} %pad_add_fusion.2), channel_id=1, source_target_pairs={{0,2},{1,3},{2,0},{3,1},{4,6},{5,7},{6,4},{7,5},{8,10},{9,11},{10,... | collective-permute-start | bytes 3080 | tf_op jit(solution)/shard_map/ppermute | solution.py:190
  15.4 11.5 %collective-permute-start.11 = (bf16[128,768]{1,0:T(8,128)(2,1)S(1)}, bf16[128,768]{1,0:T(8,128)(2,1)S(1)}, u32[]{:S(2)}, u32[]{:S(2)}) collective-permute-start(bf16[128,768]{1,0:T(8,128)(2,1)S(1)} %aggregate.1.own_ref.first_ref), channel_id=1, source_target_pairs={{0,6},{1,7},{2,4},{3,5},{4,2},{5,3},{6,0},{7,1},{8,14},{9,15},{10,... | collective-permute-start | bytes 589832 | tf_op jit(solution)/shard_map/ppermute | solution.py:190
  19.2 16.3 %collective-permute-start.9 = (bf16[128,768]{1,0:T(8,128)(2,1)S(1)}, bf16[128,768]{1,0:T(8,128)(2,1)S(1)}, u32[]{:S(2)}, u32[]{:S(2)}) collective-permute-start(bf16[128,768]{1,0:T(8,128)(2,1)S(1)} %aggregate.1.own_ref.first_ref), channel_id=1, source_target_pairs={{0,4},{1,5},{2,6},{3,7},{4,0},{5,1},{6,2},{7,3},{8,12},{9,13},{10,... | collective-permute-start | bytes 589832 | tf_op jit(solution)/shard_map/ppermute | solution.py:190
  19.3 16.3 %collective-permute-start.5 = (s32[4,128]{1,0:T(4,128)S(1)}, s32[4,128]{1,0:T(4,128)S(1)}, u32[]{:S(2)}, u32[]{:S(2)}) collective-permute-start(s32[4,128]{1,0:T(4,128)S(1)} %pad_add_fusion.1), channel_id=1, source_target_pairs={{0,4},{1,5},{2,6},{3,7},{4,0},{5,1},{6,2},{7,3},{8,12},{9,13},{10,... | collective-permute-start | bytes 6152 | tf_op jit(solution)/shard_map/ppermute | solution.py:190
  22.2 13.7 %collective-permute-start.7 = (bf16[128,768]{1,0:T(8,128)(2,1)S(1)}, bf16[128,768]{1,0:T(8,128)(2,1)S(1)}, u32[]{:S(2)}, u32[]{:S(2)}) collective-permute-start(bf16[128,768]{1,0:T(8,128)(2,1)S(1)} %aggregate.1.own_ref.first_ref), channel_id=1, source_target_pairs={{0,2},{1,3},{2,0},{3,1},{4,6},{5,7},{6,4},{7,5},{8,10},{9,11},{10,... | collective-permute-start | bytes 589832 | tf_op jit(solution)/shard_map/ppermute | solution.py:190
  22.3 14.2 %collective-permute-start.6 = (bf16[128,768]{1,0:T(8,128)(2,1)S(1)}, bf16[128,768]{1,0:T(8,128)(2,1)S(1)}, u32[]{:S(2)}, u32[]{:S(2)}) collective-permute-start(bf16[128,768]{1,0:T(8,128)(2,1)S(1)} %aggregate.1.own_ref.first_ref), channel_id=1, source_target_pairs={{0,1},{1,0},{2,3},{3,2},{4,5},{5,4},{6,7},{7,6},{8,9},{9,8},{10,11... | collective-permute-start | bytes 589832 | tf_op jit(solution)/shard_map/ppermute | solution.py:190
  22.3 1.7 %copy-start.5 = (bf16[768,1536]{1,0:T(8,128)(2,1)S(1)}, bf16[768,1536]{1,0:T(8,128)(2,1)}, u32[]{:S(2)}) copy-start(bf16[768,1536]{1,0:T(8,128)(2,1)} %w_qk_ref.1) | copy-start | bytes 7077892
  26.8 10.7 %collective-permute-start.12 = (bf16[128,768]{1,0:T(8,128)(2,1)S(1)}, bf16[128,768]{1,0:T(8,128)(2,1)S(1)}, u32[]{:S(2)}, u32[]{:S(2)}) collective-permute-start(bf16[128,768]{1,0:T(8,128)(2,1)S(1)} %collective-permute-done.11.first_ref), channel_id=1, source_target_pairs={{0,1},{1,0},{2,3},{3,2},{4,5},{5,4},{6,7},{7,6},{8,9},{9,8},{10,11... | collective-permute-start | bytes 589832 | tf_op jit(solution)/shard_map/ppermute | solution.py:190
  35.5 3.0 %collective-permute-start.10 = (bf16[128,768]{1,0:T(8,128)(2,1)S(1)}, bf16[128,768]{1,0:T(8,128)(2,1)S(1)}, u32[]{:S(2)}, u32[]{:S(2)}) collective-permute-start(bf16[128,768]{1,0:T(8,128)(2,1)S(1)} %collective-permute-done.9.first_ref), channel_id=1, source_target_pairs={{0,1},{1,0},{2,3},{3,2},{4,5},{5,4},{6,7},{7,6},{8,9},{9,8},{10,11... | collective-permute-start | bytes 589832 | tf_op jit(solution)/shard_map/ppermute | solution.py:190
  35.9 3.6 %collective-permute-start.8 = (bf16[128,768]{1,0:T(8,128)(2,1)S(1)}, bf16[128,768]{1,0:T(8,128)(2,1)S(1)}, u32[]{:S(2)}, u32[]{:S(2)}) collective-permute-start(bf16[128,768]{1,0:T(8,128)(2,1)S(1)} %collective-permute-done.7.first_ref), channel_id=1, source_target_pairs={{0,1},{1,0},{2,3},{3,2},{4,5},{5,4},{6,7},{7,6},{8,9},{9,8},{10,11... | collective-permute-start | bytes 589832 | tf_op jit(solution)/shard_map/ppermute | solution.py:190

commit v3 on v0

v3 whole, which is shorter than its diff:
```python
import math

import jax
import jax.numpy as jnp
import numpy as np
from jax import lax
from jax.experimental import pallas as pl
from jax.experimental.pallas import tpu as pltpu
from jax.sharding import PartitionSpec as P

H = 32
HD = 24
NB = 16
TILES = 8
LANES = 128
PAD = 32
QUAD = LANES // PAD
WIDE = H * PAD
HALF = 16 * HD
HALF_PAD = 16 * PAD
CHUNKS = 2
NT = (((1,), (1,)), ((), ()))
MIB = 1024 * 1024
BF16 = jnp.bfloat16
F32 = jnp.float32
FACTOR = math.log2(math.e) / math.sqrt(HD)
TOTAL_ROW = HD
PEAK_ROW = HD + 1


def vmem():
    return pl.BlockSpec(memory_space=pltpu.VMEM)


def smem():
    return pl.BlockSpec(memory_space=pltpu.SMEM)


def limit(mib):
    return pltpu.CompilerParams(vmem_limit_bytes=mib * MIB)


def shape(*dims, dtype=BF16):
    return jax.ShapeDtypeStruct(dims, dtype)


def cost(flops, nbytes):
    return pl.CostEstimate(flops=int(flops), bytes_accessed=int(nbytes), transcendentals=0)


def pad_matrix():
    rows = np.arange(HALF)
    sel = np.zeros((HALF_PAD, HALF), np.float32)
    sel[(rows // HD) * PAD + rows % HD, rows] = 1.0
    return sel


def one_hot_slab(bucket_row):
    n = bucket_row.shape[1]
    index = lax.broadcasted_iota(jnp.int32, (LANES, n), 0)
    wanted = jnp.where(index < 3 * NB, index % NB, -1)
    hot = jnp.where(wanted == bucket_row, 1.0, 0.0)
    return hot.T.astype(BF16)


def split_three(x):
    high = x.astype(BF16).astype(F32)
    rest = x - high
    mid = rest.astype(BF16).astype(F32)
    return high, mid, rest - mid


def weights_kernel(w_qk_ref, w_v_ref, sel_ref, wq_ref, wk_ref, wvt_ref):
    width = w_v_ref.shape[1]
    sel = sel_ref[...]
    for part in range(width // HALF):
        cols = slice(part * HALF_PAD, (part + 1) * HALF_PAD)
        for base, dst in ((0, wq_ref), (width, wk_ref)):
            block = w_qk_ref[:, base + part * HALF : base + (part + 1) * HALF]
            dst[:, cols] = lax.dot_general(block, sel, NT, preferred_element_type=F32).astype(BF16)
        block = w_v_ref[:, part * HALF : (part + 1) * HALF]
        wvt_ref[cols, :] = lax.dot_general(sel, block, NT, preferred_element_type=F32).astype(BF16)


def bias_kernel(cube_ref, own_ref, sister_ref, *refs):
    bucket_refs, bias_ref, hot_ref = refs[:-2], refs[-2], refs[-1]
    rows = own_ref.shape[1]
    high, mid, low = split_three(cube_ref[...] * math.sqrt(HD))
    lane = lax.broadcasted_iota(jnp.int32, high.shape, 1) % LANES
    parts = jnp.where(
        lane < NB, high, jnp.where(lane < 2 * NB, mid, jnp.where(lane < 3 * NB, low, 0.0))
    ).astype(BF16)
    slab = one_hot_slab(own_ref[...])
    both = jnp.concatenate([slab, one_hot_slab(sister_ref[...])], axis=0)[:, :NB]
    bias_ref[...] = jnp.dot(both, parts, preferred_element_type=F32).astype(BF16)
    hot_ref[:rows, :] = slab
    for s, ref in enumerate(bucket_refs):
        hot_ref[(s + 1) * rows : (s + 2) * rows, :] = one_hot_slab(ref[...])


def aggregate_kernel(column, src_ref, count_ref, me_ref, tiles_ref, features_ref, *refs):
    received, out_ref, held = refs[:-2], refs[-2], refs[-1]
    rows, span = out_ref.shape
    own = features_ref[:, column : column + span]
    held[:rows, :] = own
    for d, ref in enumerate(received):
        held[(d + 1) * rows : (d + 2) * rows, :] = ref[...]
    count = count_ref[0]
    me = me_ref[0]
    picked = []
    masked = []
    for t in range(TILES):
        start = pl.multiple_of((src_ref[0, t] ^ me) * rows, rows)
        picked.append(held[pl.ds(start, rows), :])
        tile = tiles_ref[:, t * rows : (t + 1) * rows]
        masked.append(jnp.where(t < count, tile, jnp.zeros_like(tile)))
    total = own.astype(F32) + jnp.dot(
        jnp.concatenate(masked, axis=1),
        jnp.concatenate(picked, axis=0),
        preferred_element_type=F32,
    )
    out_ref[...] = total.astype(BF16)


def normed(refs):
    block = jnp.concatenate([ref[...] for ref in refs], axis=1).astype(F32)
    mean_square = jnp.mean(block * block, axis=-1, keepdims=True)
    return (block * lax.rsqrt(mean_square + 1e-06)).astype(BF16)


def query_kernel(*refs):
    wq_ref, q_ref = refs[-2:]
    block = jnp.concatenate([normed(refs[:CHUNKS]), normed(refs[CHUNKS : 2 * CHUNKS])], axis=0)
    for n in range(0, WIDE, 256):
        q_ref[:, n : n + 256] = jnp.dot(
            block, wq_ref[:, n : n + 256], preferred_element_type=F32
        ).astype(BF16)


def part_kernel(first, last, q_ref, bias_ref, hot_ref, wk_ref, wvt_ref, *refs):
    block_refs, refs = refs[: 2 * CHUNKS], refs[2 * CHUNKS :]
    k_ref, vt_ref = refs[-2:]
    refs = refs[:-2]
    if not first:
        state_ref, refs = refs[0], refs[1:]
    queries = q_ref.shape[0]
    keys = k_ref.shape[0]
    block = jnp.concatenate(
        [normed(block_refs[:CHUNKS]), normed(block_refs[CHUNKS:])], axis=0
    )
    ones_row = lax.broadcasted_iota(jnp.int32, (256, keys), 0) % PAD == TOTAL_ROW
    for n in range(0, WIDE, 256):
        k_ref[:, n : n + 256] = jnp.dot(
            block, wk_ref[:, n : n + 256], preferred_element_type=F32
        ).astype(BF16)
        vt = lax.dot_general(wvt_ref[n : n + 256, :], block, NT, preferred_element_type=F32)
        vt_ref[n : n + 256, :] = jnp.where(ones_row, 1.0, vt).astype(BF16)

    lane_head = lax.broadcasted_iota(jnp.int32, (queries, LANES), 1) // PAD
    row = lax.broadcasted_iota(jnp.int32, (PAD, queries), 0)

    def quad(m, carry):
        cols = pl.ds(pl.multiple_of(m * LANES, LANES), LANES)
        q = q_ref[:, cols]
        zero = jnp.zeros_like(q)
        key = jnp.concatenate([k_ref[:, cols], hot_ref[...]], axis=1)
        for h in range(QUAD):
            head = m * QUAD + h
            bias = bias_ref[:, pl.ds(pl.multiple_of(head * LANES, LANES), LANES)]
            query = jnp.concatenate([jnp.where(lane_head == h, q, zero), bias], axis=1)
            x = lax.dot_general(key, query, NT, preferred_element_type=F32)
            peak = jnp.max(x, axis=0, keepdims=True)
            weights = jnp.exp2((x - peak) * FACTOR).astype(BF16)
            rows = pl.ds(pl.multiple_of(head * PAD, PAD), PAD)
            mixed = jnp.dot(vt_ref[rows, :], weights, preferred_element_type=F32)
            if not first:
                state = state_ref[rows, :]
                before = state[PEAK_ROW : PEAK_ROW + 1, :]
                top = jnp.maximum(before, peak)
                mixed = mixed * jnp.exp2((peak - top) * FACTOR) + state * jnp.exp2(
                    (before - top) * FACTOR
                )
                peak = top
            if not last:
                refs[0][rows, :] = jnp.where(row == PEAK_ROW, peak, mixed)
            else:
                total = mixed[TOTAL_ROW : TOTAL_ROW + 1, :]
                level = peak * FACTOR + jnp.log2(total)
                mixed = mixed / total
                own = mixed[:, : queries // 2]
                refs[0][rows, :] = jnp.where(row[:, : queries // 2] == HD, level[:, : queries // 2], own)
                high, mid, low = split_three(level[:, queries // 2 :])
                sent = mixed[:, queries // 2 :]
                for at, piece in ((HD, high), (HD + 1, mid), (HD + 2, low)):
                    sent = jnp.where(row[:, queries // 2 :] == at, piece, sent)
                refs[1][rows, :] = sent.astype(BF16)
        return carry

    lax.fori_loop(0, H // QUAD, quad, 0)


def merge_kernel(own_ref, other_ref, out_ref, turned):
    for head in range(H):
        own = own_ref[head * PAD : (head + 1) * PAD, :]
        other = other_ref[head * PAD : (head + 1) * PAD, :].astype(F32)
        level = own[HD : HD + 1, :]
        level_other = (
            other[HD : HD + 1, :] + other[HD + 1 : HD + 2, :] + other[HD + 2 : HD + 3, :]
        )
        top = jnp.maximum(level, level_other)
        share = jnp.exp2(level - top)
        share_other = jnp.exp2(level_other - top)
        mixed = (own[:HD, :] * share + other[:HD, :] * share_other) / (share + share_other)
        turned[head * HD : (head + 1) * HD, :] = mixed
    for n in range(0, H * HD, LANES):
        out_ref[:, n : n + LANES] = turned[n : n + LANES, :].T.astype(BF16)


def swap(array, axis, distance):
    return lax.ppermute(array, axis, [(i, i ^ distance) for i in range(lax.axis_size(axis))])


def on_device(features, tiles, tile_src, tile_count, node_bucket, w_qk, w_v, bias_table):
    rows, width = features.shape
    groups = lax.axis_size("group")
    chips = lax.axis_size("seq") // 2
    span = width // CHUNKS
    sel = jnp.asarray(pad_matrix(), BF16)
    own_bucket = node_bucket.reshape(1, rows)
    me = lax.axis_index("group").reshape(1)

    received = []
    for c in range(CHUNKS):
        chunk = features[:, c * span : (c + 1) * span]
        received.append([swap(chunk, "group", d) for d in range(groups - 1, 0, -1)][::-1])
    sister_bucket = swap(own_bucket, "seq", 1)
    buckets = [swap(own_bucket, "seq", 2 * d) for d in range(1, chips)]

    wq, wk, wvt = pl.pallas_call(
        weights_kernel,
        out_shape=[shape(width, WIDE)] * 2 + [shape(WIDE, width)],
        in_specs=[vmem()] * 3,
        out_specs=[vmem()] * 3,
        compiler_params=limit(24),
        cost_estimate=cost(6 * width * width * HALF_PAD, 10_000_000),
        name="weights",
    )(w_qk, w_v, sel)

    cube = bias_table.reshape(H, NB, NB).transpose(1, 0, 2)
    cube = jnp.concatenate([cube, cube, cube, jnp.zeros((NB, H, LANES - 3 * NB), F32)], axis=2)
    cube = cube.reshape(NB, H * LANES)
    bias, hot = pl.pallas_call(
        bias_kernel,
        out_shape=[shape(2 * rows, H * LANES), shape(chips * rows, LANES)],
        in_specs=[vmem()] * (2 + chips),
        out_specs=[vmem()] * 2,
        compiler_params=limit(16),
        cost_estimate=cost(2 * 2 * rows * 256 * H * LANES, 4_000_000),
        name="bias",
    )(cube, own_bucket, sister_bucket, *buckets)

    blocks = [[] for _ in range(chips)]
    sister = []
    for c in range(CHUNKS):
        own = pl.pallas_call(
            lambda *refs, c=c: aggregate_kernel(c * span, *refs),
            out_shape=shape(rows, span),
            in_specs=[smem()] * 3 + [vmem()] * (1 + groups),
            out_specs=vmem(),
            scratch_shapes=[pltpu.VMEM((groups * rows, span), BF16)],
            compiler_params=limit(16),
            cost_estimate=cost(2 * rows * TILES * 256 * span, 1_000_000),
            name="aggregate",
        )(tile_src, tile_count, me, tiles, features, *received[c])
        blocks[0].append(own)
        for d in range(chips - 1, 0, -1):
            blocks[d].append(swap(own, "seq", 2 * d))
        sister.append(swap(own, "seq", 1))

    q = pl.pallas_call(
        query_kernel,
        out_shape=shape(2 * rows, WIDE),
        in_specs=[vmem()] * (2 * CHUNKS + 1),
        out_specs=vmem(),
        compiler_params=limit(16),
        cost_estimate=cost(4 * rows * width * WIDE, 2_000_000),
        name="query",
    )(*blocks[0], *sister, wq)

    state = []
    for p in range(0, chips, 2):
        first, last = p == 0, p + 2 >= chips
        if last:
            outs = [shape(WIDE, rows, dtype=F32), shape(WIDE, rows)]
        else:
            outs = [shape(WIDE, 2 * rows, dtype=F32)]
        state = pl.pallas_call(
            lambda *refs, first=first, last=last: part_kernel(first, last, *refs),
            out_shape=outs,
            in_specs=[vmem()] * (5 + 2 * CHUNKS + len(state)),
            out_specs=[vmem()] * len(outs),
            scratch_shapes=[pltpu.VMEM((2 * rows, WIDE), BF16), pltpu.VMEM((WIDE, 2 * rows), BF16)],
            compiler_params=limit(24),
            cost_estimate=cost(8_000_000_000 // 2, 8_000_000),
            name="part",
        )(q, bias, hot[p * rows : (p + 2) * rows], wk, wvt, *blocks[p], *blocks[p + 1], *state)

    partial, payload = state
    return pl.pallas_call(
        merge_kernel,
        out_shape=shape(rows, width),
        in_specs=[vmem()] * 2,
        out_specs=vmem(),
        scratch_shapes=[pltpu.VMEM((width, rows), F32)],
        compiler_params=limit(16),
        name="merge",
    )(partial, swap(payload, "seq", 1))


def solution(mesh):
    in_specs = (
        P(("group", "seq"), None),
        P(("group", "seq"), None),
        P(("group", "seq"), None),
        P(("group", "seq")),
        P(("group", "seq")),
        P(),
        P(),
        P(),
    )
    out_specs = P(("group", "seq"), None)
    return jax.shard_map(
        on_device, mesh=mesh, in_specs=in_specs, out_specs=out_specs, check_vma=False
    )
```

time: 114 us -> 62.2 us (0.55)
  blocking collectives: 36.9 us -> 0 us
  Pallas kernels: 0 us -> 26.1 us
  matrix products: 25.6 us -> 0 us
  local copies, waits for them, and re-layouts: 19.5 us -> 8.46 us
  starting transfers between devices: 11.7 us -> 21.9 us
  waiting for transfers between devices: 13.3 us -> 4.24 us
  other arithmetic: 4.42 us -> 0.2 us
  loops' own time: 1.24 us -> 0 us
    all_gather x2 -> x0, blocking collectives: 26.1 us -> none  [the longest x1 14.1 us: on_device(): gathered = lax.all_gather(features, 'group', axis=0, tiled=True)]
    pallas_call x0 -> x8, Pallas kernels: none -> 26.1 us  [the longest x2 19.4 us: on_device(): pl.pallas_call(lambda *refs, first=first, last=last: part_kernel(first, l...]
    dot_general x9 -> x0, matrix products: 25.6 us -> none  [the longest x2 16.2 us: attend_queries(): jnp.einsum('hrb,nb->hrn', bias_part, key_onehot, precision=lax.Precision....]
    ppermute x0 -> x19, starting transfers between devices: none -> 21.9 us  [swap(): lax.ppermute(array, axis, [(i, i ^ distance) for i in range(lax.axis_size...]
    all_to_all x3 -> x0, waiting for transfers between devices: 13.3 us -> none  [the longest x1 7.53 us: on_device(): lax.all_to_all(query_send, 'seq', split_axis=1, concat_axis=0, tiled=True)]
    all_to_all x3 -> x0, starting transfers between devices: 11.7 us -> none  [the longest x1 4.88 us: on_device(): lax.all_to_all(query_send, 'seq', split_axis=1, concat_axis=0, tiled=True)]
    all_to_all x1 -> x0, blocking collectives: 10.7 us -> none  [on_device(): lax.all_to_all(head_rows, 'seq', split_axis=0, concat_axis=1, tiled=True)]
    gather x2 -> x0, local copies, waits for them, and re-layouts: 9.67 us -> none  [the longest x1 7.87 us: on_device(): query_rows_bias = my_cube[:, bucket_group, :]]
  transfers between devices with their start and end apart: 3 -> 19, of which waited for: 2 -> 2; matrix products, arithmetic and copies ran while one was open for 12% -> 4% of each run, Pallas kernels for 0% -> 25%
where the time goes in v3:
time: 62.2 us; the launch traced here: 61.9 us
  Pallas kernels  26.1 us (42%)
  starting transfers between devices  21.9 us (35%)
  local copies, waits for them, and re-layouts  8.46 us (14%)
  waiting for transfers between devices  4.24 us (7%)
  between operations  0.92 us (1%)
    ppermute x19, starting transfers between devices, swap(): lax.ppermute(array, axis, [(i, i ^ distance) for i in range(lax.axis_size...  21.9 us
    pallas_call x2, Pallas kernels, on_device(): pl.pallas_call(lambda *refs, first=first, last=last: part_kernel(first, l...  19.4 us
    unnamed x24, local copies, waits for them, and re-layouts  7.29 us
    ppermute x19, waiting for transfers between devices, swap(): lax.ppermute(array, axis, [(i, i ^ distance) for i in range(lax.axis_size...  4.24 us
    pallas_call x1, Pallas kernels, on_device(): pl.pallas_call(weights_kernel, out_shape=[shape(width, WIDE)] * 2 + [shap...  2.64 us
    pallas_call x2, Pallas kernels, on_device(): pl.pallas_call(lambda *refs, c=c: aggregate_kernel(c * span, *refs), out_...  1.77 us
  transfers between devices with their start and end apart: 19, of which 2 were waited for; matrix products, arithmetic and copies ran while one was open for 4% of the time, Pallas kernels for 25%

profile of v3, /device:TPU:0, one launch (start us, length us, event | category | flops | bytes accessed | tf_op | source)
XLA Modules:
  0.0 61.9 jit_solution(8013031333797114990)
XLA Ops:
  0.0 4.0 %collective-permute-start.10 = (s32[1,128]{1,0:T(1,128)}, s32[1,128]{1,0:T(1,128)S(1)}, u32[]{:S(2)}, u32[]{:S(2)}) collective-permute-start(s32[1,128]{1,0:T(1,128)} %bitcast.10), channel_id=1, source_target_pairs={{0,4},{1,5},{2,6},{3,7},{4,0},{5,1},{6,2},{7,3},{8,12},{9,13},{10,... | collective-permute-start | bytes 1544 | tf_op jit(solution)/shard_map/ppermute | solution.py:220
  4.0 1.3 %collective-permute-start.11 = (s32[1,128]{1,0:T(1,128)}, s32[1,128]{1,0:T(1,128)S(1)}, u32[]{:S(2)}, u32[]{:S(2)}) collective-permute-start(s32[1,128]{1,0:T(1,128)} %bitcast.11), channel_id=1, source_target_pairs={{0,6},{1,7},{2,4},{3,5},{4,2},{5,3},{6,0},{7,1},{8,14},{9,15},{10,... | collective-permute-start | bytes 1544 | tf_op jit(solution)/shard_map/ppermute | solution.py:220
  5.4 0.0 collective-permute-start.8
  5.4 0.2 collective-permute-start.9
  5.6 1.0 %fusion = (bf16[128,384]{1,0:T(8,128)(2,1)S(1)}, bf16[128,384]{1,0:T(8,128)(2,1)S(1)}) fusion(bf16[128,768]{1,0:T(8,128)(2,1)} %refs_4_.3), kind=kLoop, calls=%fused_computation.2 | loop fusion | bytes 393216 | tf_op jit(solution)/shard_map/slice | solution.py:234
  6.6 1.6 %collective-permute-start.3 = (bf16[128,384]{1,0:T(8,128)(2,1)S(1)}, bf16[128,384]{1,0:T(8,128)(2,1)S(1)}, u32[]{:S(2)}, u32[]{:S(2)}) collective-permute-start(bf16[128,384]{1,0:T(8,128)(2,1)S(1)} %get-tuple-element.19), channel_id=1, source_target_pairs={{0,8},{8,0},{16,24},{24,16},{1,9},{9,1},{17,25},{25,17},{2,10},{10... | collective-permute-start | bytes 294920 | tf_op jit(solution)/shard_map/ppermute | solution.py:220
  8.1 0.9 %copy.11 = f32[32,256]{0,1:T(8,128)S(1)} copy(f32[32,256]{1,0:T(8,128)} %param.16) | data formatting | bytes 65536 | tf_op args[7]
  9.0 0.1 copy.12
  9.1 0.1 pad.3.clone
  9.2 0.2 maximum_maximum_fusion
  9.4 0.0 collective-permute-done.10.refs_1_
  9.4 1.6 %collective-permute-start.4 = (bf16[128,384]{1,0:T(8,128)(2,1)S(1)}, bf16[128,384]{1,0:T(8,128)(2,1)S(1)}, u32[]{:S(2)}, u32[]{:S(2)}) collective-permute-start(bf16[128,384]{1,0:T(8,128)(2,1)S(1)} %get-tuple-element.19), channel_id=1, source_target_pairs={{0,16},{8,24},{16,0},{24,8},{1,17},{9,25},{17,1},{25,9},{2,18},{10... | collective-permute-start | bytes 294920 | tf_op jit(solution)/shard_map/ppermute | solution.py:220
  11.0 0.0 collective-permute-done.11.refs_2_
  11.0 0.9 %collective-permute-start.5 = (bf16[128,384]{1,0:T(8,128)(2,1)S(1)}, bf16[128,384]{1,0:T(8,128)(2,1)S(1)}, u32[]{:S(2)}, u32[]{:S(2)}) collective-permute-start(bf16[128,384]{1,0:T(8,128)(2,1)S(1)} %get-tuple-element.19), channel_id=1, source_target_pairs={{0,24},{8,16},{16,8},{24,0},{1,25},{9,17},{17,9},{25,1},{2,26},{10... | collective-permute-start | bytes 294920 | tf_op jit(solution)/shard_map/ppermute | solution.py:220
  12.0 0.0 collective-permute-done.8.sister_ref
  12.0 1.0 %collective-permute-start = (bf16[128,384]{1,0:T(8,128)(2,1)S(1)}, bf16[128,384]{1,0:T(8,128)(2,1)S(1)}, u32[]{:S(2)}, u32[]{:S(2)}) collective-permute-start(bf16[128,384]{1,0:T(8,128)(2,1)S(1)} %get-tuple-element.20), channel_id=1, source_target_pairs={{0,8},{8,0},{16,24},{24,16},{1,9},{9,1},{17,25},{25,17},{2,10},{10... | collective-permute-start | bytes 294920 | tf_op jit(solution)/shard_map/ppermute | solution.py:220
  13.0 0.0 collective-permute-done.9.refs_0_
  13.0 1.5 %collective-permute-start.1 = (bf16[128,384]{1,0:T(8,128)(2,1)S(1)}, bf16[128,384]{1,0:T(8,128)(2,1)S(1)}, u32[]{:S(2)}, u32[]{:S(2)}) collective-permute-start(bf16[128,384]{1,0:T(8,128)(2,1)S(1)} %get-tuple-element.20), channel_id=1, source_target_pairs={{0,16},{8,24},{16,0},{24,8},{1,17},{9,25},{17,1},{25,9},{2,18},{10... | collective-permute-start | bytes 294920 | tf_op jit(solution)/shard_map/ppermute | solution.py:220
  14.5 0.0 collective-permute-done.3.refs_5_
  14.5 0.9 %collective-permute-start.2 = (bf16[128,384]{1,0:T(8,128)(2,1)S(1)}, bf16[128,384]{1,0:T(8,128)(2,1)S(1)}, u32[]{:S(2)}, u32[]{:S(2)}) collective-permute-start(bf16[128,384]{1,0:T(8,128)(2,1)S(1)} %get-tuple-element.20), channel_id=1, source_target_pairs={{0,24},{8,16},{16,8},{24,0},{1,25},{9,17},{17,9},{25,1},{2,26},{10... | collective-permute-start | bytes 294920 | tf_op jit(solution)/shard_map/ppermute | solution.py:220
  15.5 1.7 %copy-done.3 = bf16[768,1536]{1,0:T(8,128)(2,1)S(1)} copy-done((bf16[768,1536]{1,0:T(8,128)(2,1)S(1)}, bf16[768,1536]{1,0:T(8,128)(2,1)}, u32[]{:S(2)}) %copy-start.3) | copy-done | bytes 2359320
  17.1 1.3 %copy-done.4 = bf16[768,768]{1,0:T(8,128)(2,1)S(1)} copy-done((bf16[768,768]{1,0:T(8,128)(2,1)S(1)}, bf16[768,768]{1,0:T(8,128)(2,1)}, u32[]{:S(2)}) %copy-start.4) | copy-done | bytes 1179672
  18.4 1.0 %copy-done.6 = bf16[512,384]{1,0:T(8,128)(2,1)S(1)} copy-done((bf16[512,384]{1,0:T(8,128)(2,1)S(1)}, bf16[512,384]{1,0:T(8,128)(2,1)}, u32[]{:S(2)}) %copy-start.6) | copy-done | bytes 393240
  19.4 2.6 %weights.1 = (bf16[768,1024]{1,0:T(8,128)(2,1)S(1)}, bf16[768,1024]{1,0:T(8,128)(2,1)S(1)}, bf16[1024,768]{1,0:T(8,128)(2,1)S(1)}) custom-call(bf16[768,1536]{1,0:T(8,128)(2,1)S(1)} %copy-done.3, bf16[768,768]{1,0:T(8,128)(2,1)S(1)} %copy-done.4, bf16[512,384]{1,0:T(8,128)(2,1)S(1)} %copy-done.6), custom_call_target="tpu_custom_call" | custom-call | flops 1811939328 | bytes 10000000 | tf_op jit(solution)/shard_map/weights/pallas_call | solution.py:239
  22.0 0.0 copy-start.7
  22.1 1.2 %copy-done.7 = bf16[768,1024]{1,0:T(8,128)(2,1)} copy-done((bf16[768,1024]{1,0:T(8,128)(2,1)}, bf16[768,1024]{1,0:T(8,128)(2,1)S(1)}, u32[]{:S(2)}) %copy-start.7) | copy-done | bytes 1572888
  23.2 1.2 %copy-done.9 = bf16[1024,768]{1,0:T(8,128)(2,1)} copy-done((bf16[1024,768]{1,0:T(8,128)(2,1)}, bf16[1024,768]{1,0:T(8,128)(2,1)S(1)}, u32[]{:S(2)}) %copy-start.9) | copy-done | bytes 1572888
  25.1 0.2 copy.17
  25.3 0.0 copy-done.5
  25.3 0.8 %bias.1 = (bf16[256,4096]{1,0:T(8,128)(2,1)S(1)}, bf16[512,128]{1,0:T(8,128)(2,1)S(1)}) custom-call(f32[16,4096]{1,0:T(8,128)S(1)} %bitcast.9, s32[1,128]{1,0:T(1,128)S(1)} %bitcast.14, s32[1,128]{1,0:T(1,128)S(1)} %collective-permute-done.8.sister_ref, s32[1,128]{1,0:T(1,128)S(1)} %collective-permute-done.9.refs_0_, ...), custom_call_target="tpu_custom_call" | custom-call | flops 536870912 | bytes 4000000 | tf_op jit(solution)/shard_map/bias/pallas_call | solution.py:252
  26.0 0.0 collective-permute-done.4.refs_6_
  26.0 0.0 collective-permute-done.5.refs_7_
  26.0 0.0 copy-done
  26.1 0.0 copy-done.1
  26.1 0.0 copy-done.2
  26.1 0.9 %aggregate.3.refs_1_.refs_6_ = bf16[128,384]{1,0:T(8,128)(2,1)S(1)} custom-call(s32[1,8]{1,0:T(1,128)S(1)} %copy-done.2, s32[1]{0:T(128)S(6)} %copy.18.refs_1_, s32[1]{0:T(128)} %bitcast.refs_2_, bf16[128,1024]{1,0:T(8,128)(2,1)S(1)} %copy-done.1, bf16[128,768]{1,0:T(8,128)(2,1)S(1)} %copy-done, bf16[128,384]{1,0:T(8,128)(2,1)S(1)} %collective-permute-done.3.refs_5_, ...), custom_call_target="tpu_custom_call" | custom-call | flops 201326592 | bytes 1000000 | tf_op jit(solution)/shard_map/aggregate/pallas_call | solution.py:265
  27.0 0.1 collective-permute-start.7
  27.0 1.4 %collective-permute-start.17 = (bf16[128,384]{1,0:T(8,128)(2,1)S(1)}, bf16[128,384]{1,0:T(8,128)(2,1)S(1)}, u32[]{:S(2)}, u32[]{:S(2)}) collective-permute-start(bf16[128,384]{1,0:T(8,128)(2,1)S(1)} %aggregate.3.refs_1_.refs_6_), channel_id=1, source_target_pairs={{0,2},{1,3},{2,0},{3,1},{4,6},{5,7},{6,4},{7,5},{8,10},{9,11},{10,... | collective-permute-start | bytes 294920 | tf_op jit(solution)/shard_map/ppermute | solution.py:220
  28.4 0.0 collective-permute-done.refs_5_
  28.4 0.0 collective-permute-done.1.refs_6_
  28.4 0.0 collective-permute-done.2.refs_7_
  28.5 0.0 copy-start.10
  28.5 0.9 %aggregate.2.refs_0_.refs_5_ = bf16[128,384]{1,0:T(8,128)(2,1)S(1)} custom-call(s32[1,8]{1,0:T(1,128)S(1)} %copy-done.2, s32[1]{0:T(128)S(6)} %copy.18.refs_1_, s32[1]{0:T(128)} %bitcast.refs_2_, bf16[128,1024]{1,0:T(8,128)(2,1)S(1)} %copy-done.1, bf16[128,768]{1,0:T(8,128)(2,1)S(1)} %copy-done, bf16[128,384]{1,0:T(8,128)(2,1)S(1)} %collective-permute-done.refs_5_, ...), custom_call_target="tpu_custom_call" | custom-call | flops 201326592 | bytes 1000000 | tf_op jit(solution)/shard_map/aggregate/pallas_call | solution.py:265
  29.4 0.0 copy-start.8
  29.4 0.2 collective-permute-start.6
  29.6 0.7 %collective-permute-start.16 = (bf16[128,384]{1,0:T(8,128)(2,1)S(1)}, bf16[128,384]{1,0:T(8,128)(2,1)S(1)}, u32[]{:S(2)}, u32[]{:S(2)}) collective-permute-start(bf16[128,384]{1,0:T(8,128)(2,1)S(1)} %aggregate.2.refs_0_.refs_5_), channel_id=1, source_target_pairs={{0,2},{1,3},{2,0},{3,1},{4,6},{5,7},{6,4},{7,5},{8,10},{9,11},{10,... | collective-permute-start | bytes 294920 | tf_op jit(solution)/shard_map/ppermute | solution.py:220
  30.3 2.4 %collective-permute-start.13 = (bf16[128,384]{1,0:T(8,128)(2,1)S(1)}, bf16[128,384]{1,0:T(8,128)(2,1)S(1)}, u32[]{:S(2)}, u32[]{:S(2)}) collective-permute-start(bf16[128,384]{1,0:T(8,128)(2,1)S(1)} %aggregate.3.refs_1_.refs_6_), channel_id=1, source_target_pairs={{0,4},{1,5},{2,6},{3,7},{4,0},{5,1},{6,2},{7,3},{8,12},{9,13},{10,... | collective-permute-start | bytes 294920 | tf_op jit(solution)/shard_map/ppermute | solution.py:220
  32.7 0.0 collective-permute-done.7.refs_3_
  32.7 1.3 %collective-permute-start.15 = (bf16[128,384]{1,0:T(8,128)(2,1)S(1)}, bf16[128,384]{1,0:T(8,128)(2,1)S(1)}, u32[]{:S(2)}, u32[]{:S(2)}) collective-permute-start(bf16[128,384]{1,0:T(8,128)(2,1)S(1)} %aggregate.3.refs_1_.refs_6_), channel_id=1, source_target_pairs={{0,6},{1,7},{2,4},{3,5},{4,2},{5,3},{6,0},{7,1},{8,14},{9,15},{10,... | collective-permute-start | bytes 294920 | tf_op jit(solution)/shard_map/ppermute | solution.py:220
  34.1 0.0 collective-permute-done.6.refs_2_
  34.1 0.8 %collective-permute-start.12 = (bf16[128,384]{1,0:T(8,128)(2,1)S(1)}, bf16[128,384]{1,0:T(8,128)(2,1)S(1)}, u32[]{:S(2)}, u32[]{:S(2)}) collective-permute-start(bf16[128,384]{1,0:T(8,128)(2,1)S(1)} %aggregate.2.refs_0_.refs_5_), channel_id=1, source_target_pairs={{0,4},{1,5},{2,6},{3,7},{4,0},{5,1},{6,2},{7,3},{8,12},{9,13},{10,... | collective-permute-start | bytes 294920 | tf_op jit(solution)/shard_map/ppermute | solution.py:220
  34.9 0.7 %query.1.refs_0_ = bf16[256,1024]{1,0:T(8,128)(2,1)S(1)} custom-call(bf16[128,384]{1,0:T(8,128)(2,1)S(1)} %aggregate.2.refs_0_.refs_5_, bf16[128,384]{1,0:T(8,128)(2,1)S(1)} %aggregate.3.refs_1_.refs_6_, bf16[128,384]{1,0:T(8,128)(2,1)S(1)} %collective-permute-done.6.refs_2_, bf16[128,384]{1,0:T(8,128)(2,1)S(1)} %collective-permute-done.7.refs_3_, ...), custom_call_target="tpu_custom_call" | custom-call | flops 402653184 | bytes 2000000 | tf_op jit(solution)/shard_map/query/pallas_call | solution.py:280
  35.5 0.0 collective-permute-done.17.refs_8_
  35.6 1.7 %collective-permute-start.14 = (bf16[128,384]{1,0:T(8,128)(2,1)S(1)}, bf16[128,384]{1,0:T(8,128)(2,1)S(1)}, u32[]{:S(2)}, u32[]{:S(2)}) collective-permute-start(bf16[128,384]{1,0:T(8,128)(2,1)S(1)} %aggregate.2.refs_0_.refs_5_), channel_id=1, source_target_pairs={{0,6},{1,7},{2,4},{3,5},{4,2},{5,3},{6,0},{7,1},{8,14},{9,15},{10,... | collective-permute-start | bytes 294920 | tf_op jit(solution)/shard_map/ppermute | solution.py:220
  37.3 0.0 collective-permute-done.16.refs_7_
  37.3 9.6 %part.2.refs_9_ = f32[1024,256]{1,0:T(8,128)S(1)} custom-call(bf16[256,1024]{1,0:T(8,128)(2,1)S(1)} %query.1.refs_0_, bf16[256,4096]{1,0:T(8,128)(2,1)S(1)} %get-tuple-element.13.refs_1_, bf16[256,128]{1,0:T(8,128)(2,1)S(1)} %get-tuple-element.21.refs_2_, bf16[768,1024]{1,0:T(8,128)(2,1)S(1)} %copy-done.8, bf16[1024,768]{1,0:T(8,128)(2,1)S(1)} %copy-done.10, ...), custom_call_target="tpu_custom_call" | custom-call | flops 4000000000 | bytes 8000000 | tf_op jit(solution)/shard_map/part/pallas_call | solution.py:297
  46.9 0.0 collective-permute-done.13.refs_6_
  46.9 0.0 collective-permute-done.15.refs_8_
  46.9 2.7 %collective-permute-done.12.refs_5_ = bf16[128,384]{1,0:T(8,128)(2,1)S(1)} collective-permute-done((bf16[128,384]{1,0:T(8,128)(2,1)S(1)}, bf16[128,384]{1,0:T(8,128)(2,1)S(1)}, u32[]{:S(2)}, u32[]{:S(2)}) %collective-permute-start.12) | collective-permute-done | bytes 98336 | tf_op jit(solution)/shard_map/ppermute | solution.py:220
  49.6 0.0 collective-permute-done.14.refs_7_
  49.6 9.8 %part.3 = (f32[1024,128]{1,0:T(8,128)S(1)}, bf16[1024,128]{1,0:T(8,128)(2,1)S(1)}) custom-call(bf16[256,1024]{1,0:T(8,128)(2,1)S(1)} %query.1.refs_0_, bf16[256,4096]{1,0:T(8,128)(2,1)S(1)} %get-tuple-element.13.refs_1_, bf16[256,128]{1,0:T(8,128)(2,1)S(1)} %get-tuple-element.22.refs_2_, bf16[768,1024]{1,0:T(8,128)(2,1)S(1)} %copy-done.8, ...), custom_call_target="tpu_custom_call" | custom-call | flops 4000000000 | bytes 8000000 | tf_op jit(solution)/shard_map/part/pallas_call | solution.py:297
  59.4 0.1 collective-permute-start.18
  59.5 1.5 %collective-permute-done.18.other_ref = bf16[1024,128]{1,0:T(8,128)(2,1)S(1)} collective-permute-done((bf16[1024,128]{1,0:T(8,128)(2,1)S(1)}, bf16[1024,128]{1,0:T(8,128)(2,1)S(1)}, u32[]{:S(2)}, u32[]{:S(2)}) %collective-permute-start.18) | collective-permute-done | bytes 262176 | tf_op jit(solution)/shard_map/ppermute | solution.py:220
  61.0 0.9 %merge.1 = bf16[128,768]{1,0:T(8,128)(2,1)} custom-call(f32[1024,128]{1,0:T(8,128)S(1)} %get-tuple-element.17.own_ref, bf16[1024,128]{1,0:T(8,128)(2,1)S(1)} %collective-permute-done.18.other_ref), custom_call_target="tpu_custom_call" | custom-call | tf_op jit(solution)/shard_map/merge/pallas_call | solution.py:309
  (12 shorter events, 0.0 us)
Async XLA Ops:
  0.0 9.4 %collective-permute-start.10 = (s32[1,128]{1,0:T(1,128)}, s32[1,128]{1,0:T(1,128)S(1)}, u32[]{:S(2)}, u32[]{:S(2)}) collective-permute-start(s32[1,128]{1,0:T(1,128)} %bitcast.10), channel_id=1, source_target_pairs={{0,4},{1,5},{2,6},{3,7},{4,0},{5,1},{6,2},{7,3},{8,12},{9,13},{10,... | collective-permute-start | bytes 1544 | tf_op jit(solution)/shard_map/ppermute | solution.py:220
  4.0 7.0 %collective-permute-start.11 = (s32[1,128]{1,0:T(1,128)}, s32[1,128]{1,0:T(1,128)S(1)}, u32[]{:S(2)}, u32[]{:S(2)}) collective-permute-start(s32[1,128]{1,0:T(1,128)} %bitcast.11), channel_id=1, source_target_pairs={{0,6},{1,7},{2,4},{3,5},{4,2},{5,3},{6,0},{7,1},{8,14},{9,15},{10,... | collective-permute-start | bytes 1544 | tf_op jit(solution)/shard_map/ppermute | solution.py:220
  5.4 6.6 %collective-permute-start.8 = (s32[1,128]{1,0:T(1,128)}, s32[1,128]{1,0:T(1,128)S(1)}, u32[]{:S(2)}, u32[]{:S(2)}) collective-permute-start(s32[1,128]{1,0:T(1,128)} %bitcast.12), channel_id=1, source_target_pairs={{0,1},{1,0},{2,3},{3,2},{4,5},{5,4},{6,7},{7,6},{8,9},{9,8},{10,11... | collective-permute-start | bytes 1544 | tf_op jit(solution)/shard_map/ppermute | solution.py:220
  5.4 7.6 %collective-permute-start.9 = (s32[1,128]{1,0:T(1,128)}, s32[1,128]{1,0:T(1,128)S(1)}, u32[]{:S(2)}, u32[]{:S(2)}) collective-permute-start(s32[1,128]{1,0:T(1,128)} %bitcast.13), channel_id=1, source_target_pairs={{0,2},{1,3},{2,0},{3,1},{4,6},{5,7},{6,4},{7,5},{8,10},{9,11},{10,... | collective-permute-start | bytes 1544 | tf_op jit(solution)/shard_map/ppermute | solution.py:220
  6.6 7.9 %collective-permute-start.3 = (bf16[128,384]{1,0:T(8,128)(2,1)S(1)}, bf16[128,384]{1,0:T(8,128)(2,1)S(1)}, u32[]{:S(2)}, u32[]{:S(2)}) collective-permute-start(bf16[128,384]{1,0:T(8,128)(2,1)S(1)} %get-tuple-element.19), channel_id=1, source_target_pairs={{0,8},{8,0},{16,24},{24,16},{1,9},{9,1},{17,25},{25,17},{2,10},{10... | collective-permute-start | bytes 294920 | tf_op jit(solution)/shard_map/ppermute | solution.py:220
  9.4 16.6 %collective-permute-start.4 = (bf16[128,384]{1,0:T(8,128)(2,1)S(1)}, bf16[128,384]{1,0:T(8,128)(2,1)S(1)}, u32[]{:S(2)}, u32[]{:S(2)}) collective-permute-start(bf16[128,384]{1,0:T(8,128)(2,1)S(1)} %get-tuple-element.19), channel_id=1, source_target_pairs={{0,16},{8,24},{16,0},{24,8},{1,17},{9,25},{17,1},{25,9},{2,18},{10... | collective-permute-start | bytes 294920 | tf_op jit(solution)/shard_map/ppermute | solution.py:220
  11.0 15.0 %collective-permute-start.5 = (bf16[128,384]{1,0:T(8,128)(2,1)S(1)}, bf16[128,384]{1,0:T(8,128)(2,1)S(1)}, u32[]{:S(2)}, u32[]{:S(2)}) collective-permute-start(bf16[128,384]{1,0:T(8,128)(2,1)S(1)} %get-tuple-element.19), channel_id=1, source_target_pairs={{0,24},{8,16},{16,8},{24,0},{1,25},{9,17},{17,9},{25,1},{2,26},{10... | collective-permute-start | bytes 294920 | tf_op jit(solution)/shard_map/ppermute | solution.py:220
  12.0 13.3 %copy-start.5 = (s32[128]{0:T(128)S(1)}, s32[128]{0:T(128)}, u32[]{:S(2)}) copy-start(s32[128]{0:T(128)} %param.13) | copy-start | bytes 1540
  12.0 16.5 %collective-permute-start = (bf16[128,384]{1,0:T(8,128)(2,1)S(1)}, bf16[128,384]{1,0:T(8,128)(2,1)S(1)}, u32[]{:S(2)}, u32[]{:S(2)}) collective-permute-start(bf16[128,384]{1,0:T(8,128)(2,1)S(1)} %get-tuple-element.20), channel_id=1, source_target_pairs={{0,8},{8,0},{16,24},{24,16},{1,9},{9,1},{17,25},{25,17},{2,10},{10... | collective-permute-start | bytes 294920 | tf_op jit(solution)/shard_map/ppermute | solution.py:220
  13.0 15.4 %collective-permute-start.1 = (bf16[128,384]{1,0:T(8,128)(2,1)S(1)}, bf16[128,384]{1,0:T(8,128)(2,1)S(1)}, u32[]{:S(2)}, u32[]{:S(2)}) collective-permute-start(bf16[128,384]{1,0:T(8,128)(2,1)S(1)} %get-tuple-element.20), channel_id=1, source_target_pairs={{0,16},{8,24},{16,0},{24,8},{1,17},{9,25},{17,1},{25,9},{2,18},{10... | collective-permute-start | bytes 294920 | tf_op jit(solution)/shard_map/ppermute | solution.py:220
  14.5 13.9 %collective-permute-start.2 = (bf16[128,384]{1,0:T(8,128)(2,1)S(1)}, bf16[128,384]{1,0:T(8,128)(2,1)S(1)}, u32[]{:S(2)}, u32[]{:S(2)}) collective-permute-start(bf16[128,384]{1,0:T(8,128)(2,1)S(1)} %get-tuple-element.20), channel_id=1, source_target_pairs={{0,24},{8,16},{16,8},{24,0},{1,25},{9,17},{17,9},{25,1},{2,26},{10... | collective-permute-start | bytes 294920 | tf_op jit(solution)/shard_map/ppermute | solution.py:220
  15.5 1.7 %copy-start.3 = (bf16[768,1536]{1,0:T(8,128)(2,1)S(1)}, bf16[768,1536]{1,0:T(8,128)(2,1)}, u32[]{:S(2)}) copy-start(bf16[768,1536]{1,0:T(8,128)(2,1)} %w_qk_ref.1) | copy-start | bytes 7077892
  17.1 1.3 %copy-start.4 = (bf16[768,768]{1,0:T(8,128)(2,1)S(1)}, bf16[768,768]{1,0:T(8,128)(2,1)}, u32[]{:S(2)}) copy-start(bf16[768,768]{1,0:T(8,128)(2,1)} %w_v_ref.1) | copy-start | bytes 3538948
  18.4 1.0 %copy-start.6 = (bf16[512,384]{1,0:T(8,128)(2,1)S(1)}, bf16[512,384]{1,0:T(8,128)(2,1)}, u32[]{:S(2)}) copy-start(bf16[512,384]{1,0:T(8,128)(2,1)} %constant.9.clone.sel_ref) | copy-start | bytes 1179652
  22.0 1.2 %copy-start.7 = (bf16[768,1024]{1,0:T(8,128)(2,1)}, bf16[768,1024]{1,0:T(8,128)(2,1)S(1)}, u32[]{:S(2)}) copy-start(bf16[768,1024]{1,0:T(8,128)(2,1)S(1)} %get-tuple-element.15.refs_3_) | copy-start | bytes 4718596
  23.2 1.2 %copy-start.9 = (bf16[1024,768]{1,0:T(8,128)(2,1)}, bf16[1024,768]{1,0:T(8,128)(2,1)S(1)}, u32[]{:S(2)}) copy-start(bf16[1024,768]{1,0:T(8,128)(2,1)S(1)} %get-tuple-element.16.refs_4_) | copy-start | bytes 4718596
  24.4 1.7 %copy-start = (bf16[128,768]{1,0:T(8,128)(2,1)S(1)}, bf16[128,768]{1,0:T(8,128)(2,1)}, u32[]{:S(2)}) copy-start(bf16[128,768]{1,0:T(8,128)(2,1)} %refs_4_.3) | copy-start | bytes 589828
  24.4 1.7 %copy-start.1 = (bf16[128,1024]{1,0:T(8,128)(2,1)S(1)}, bf16[128,1024]{1,0:T(8,128)(2,1)}, u32[]{:S(2)}) copy-start(bf16[128,1024]{1,0:T(8,128)(2,1)} %refs_3_.3) | copy-start | bytes 786436
  24.4 1.7 %copy-start.2 = (s32[1,8]{1,0:T(1,128)S(1)}, s32[1,8]{1,0:T(1,128)}, u32[]{:S(2)}) copy-start(s32[1,8]{1,0:T(1,128)} %refs_0_.3) | copy-start | bytes 100
  27.0 5.8 %collective-permute-start.7 = (bf16[128,384]{1,0:T(8,128)(2,1)S(1)}, bf16[128,384]{1,0:T(8,128)(2,1)S(1)}, u32[]{:S(2)}, u32[]{:S(2)}) collective-permute-start(bf16[128,384]{1,0:T(8,128)(2,1)S(1)} %aggregate.3.refs_1_.refs_6_), channel_id=1, source_target_pairs={{0,1},{1,0},{2,3},{3,2},{4,5},{5,4},{6,7},{7,6},{8,9},{9,8},{10,11... | collective-permute-start | bytes 294920 | tf_op jit(solution)/shard_map/ppermute | solution.py:220
  27.0 8.5 %collective-permute-start.17 = (bf16[128,384]{1,0:T(8,128)(2,1)S(1)}, bf16[128,384]{1,0:T(8,128)(2,1)S(1)}, u32[]{:S(2)}, u32[]{:S(2)}) collective-permute-start(bf16[128,384]{1,0:T(8,128)(2,1)S(1)} %aggregate.3.refs_1_.refs_6_), channel_id=1, source_target_pairs={{0,2},{1,3},{2,0},{3,1},{4,6},{5,7},{6,4},{7,5},{8,10},{9,11},{10,... | collective-permute-start | bytes 294920 | tf_op jit(solution)/shard_map/ppermute | solution.py:220
  28.5 8.8 %copy-start.10 = (bf16[1024,768]{1,0:T(8,128)(2,1)S(1)}, bf16[1024,768]{1,0:T(8,128)(2,1)}, u32[]{:S(2)}) copy-start(bf16[1024,768]{1,0:T(8,128)(2,1)} %copy-done.9) | copy-start | bytes 4718596
  29.4 8.0 %copy-start.8 = (bf16[768,1024]{1,0:T(8,128)(2,1)S(1)}, bf16[768,1024]{1,0:T(8,128)(2,1)}, u32[]{:S(2)}) copy-start(bf16[768,1024]{1,0:T(8,128)(2,1)} %copy-done.7) | copy-start | bytes 4718596
  29.4 4.7 %collective-permute-start.6 = (bf16[128,384]{1,0:T(8,128)(2,1)S(1)}, bf16[128,384]{1,0:T(8,128)(2,1)S(1)}, u32[]{:S(2)}, u32[]{:S(2)}) collective-permute-start(bf16[128,384]{1,0:T(8,128)(2,1)S(1)} %aggregate.2.refs_0_.refs_5_), channel_id=1, source_target_pairs={{0,1},{1,0},{2,3},{3,2},{4,5},{5,4},{6,7},{7,6},{8,9},{9,8},{10,11... | collective-permute-start | bytes 294920 | tf_op jit(solution)/shard_map/ppermute | solution.py:220
  29.6 7.7 %collective-permute-start.16 = (bf16[128,384]{1,0:T(8,128)(2,1)S(1)}, bf16[128,384]{1,0:T(8,128)(2,1)S(1)}, u32[]{:S(2)}, u32[]{:S(2)}) collective-permute-start(bf16[128,384]{1,0:T(8,128)(2,1)S(1)} %aggregate.2.refs_0_.refs_5_), channel_id=1, source_target_pairs={{0,2},{1,3},{2,0},{3,1},{4,6},{5,7},{6,4},{7,5},{8,10},{9,11},{10,... | collective-permute-start | bytes 294920 | tf_op jit(solution)/shard_map/ppermute | solution.py:220
  30.3 16.6 %collective-permute-start.13 = (bf16[128,384]{1,0:T(8,128)(2,1)S(1)}, bf16[128,384]{1,0:T(8,128)(2,1)S(1)}, u32[]{:S(2)}, u32[]{:S(2)}) collective-permute-start(bf16[128,384]{1,0:T(8,128)(2,1)S(1)} %aggregate.3.refs_1_.refs_6_), channel_id=1, source_target_pairs={{0,4},{1,5},{2,6},{3,7},{4,0},{5,1},{6,2},{7,3},{8,12},{9,13},{10,... | collective-permute-start | bytes 294920 | tf_op jit(solution)/shard_map/ppermute | solution.py:220
  32.7 14.2 %collective-permute-start.15 = (bf16[128,384]{1,0:T(8,128)(2,1)S(1)}, bf16[128,384]{1,0:T(8,128)(2,1)S(1)}, u32[]{:S(2)}, u32[]{:S(2)}) collective-permute-start(bf16[128,384]{1,0:T(8,128)(2,1)S(1)} %aggregate.3.refs_1_.refs_6_), channel_id=1, source_target_pairs={{0,6},{1,7},{2,4},{3,5},{4,2},{5,3},{6,0},{7,1},{8,14},{9,15},{10,... | collective-permute-start | bytes 294920 | tf_op jit(solution)/shard_map/ppermute | solution.py:220
  34.1 15.5 %collective-permute-start.12 = (bf16[128,384]{1,0:T(8,128)(2,1)S(1)}, bf16[128,384]{1,0:T(8,128)(2,1)S(1)}, u32[]{:S(2)}, u32[]{:S(2)}) collective-permute-start(bf16[128,384]{1,0:T(8,128)(2,1)S(1)} %aggregate.2.refs_0_.refs_5_), channel_id=1, source_target_pairs={{0,4},{1,5},{2,6},{3,7},{4,0},{5,1},{6,2},{7,3},{8,12},{9,13},{10,... | collective-permute-start | bytes 294920 | tf_op jit(solution)/shard_map/ppermute | solution.py:220
  35.6 14.0 %collective-permute-start.14 = (bf16[128,384]{1,0:T(8,128)(2,1)S(1)}, bf16[128,384]{1,0:T(8,128)(2,1)S(1)}, u32[]{:S(2)}, u32[]{:S(2)}) collective-permute-start(bf16[128,384]{1,0:T(8,128)(2,1)S(1)} %aggregate.2.refs_0_.refs_5_), channel_id=1, source_target_pairs={{0,6},{1,7},{2,4},{3,5},{4,2},{5,3},{6,0},{7,1},{8,14},{9,15},{10,... | collective-permute-start | bytes 294920 | tf_op jit(solution)/shard_map/ppermute | solution.py:220
  59.4 1.6 %collective-permute-start.18 = (bf16[1024,128]{1,0:T(8,128)(2,1)S(1)}, bf16[1024,128]{1,0:T(8,128)(2,1)S(1)}, u32[]{:S(2)}, u32[]{:S(2)}) collective-permute-start(bf16[1024,128]{1,0:T(8,128)(2,1)S(1)} %get-tuple-element.18), channel_id=1, source_target_pairs={{0,1},{1,0},{2,3},{3,2},{4,5},{5,4},{6,7},{7,6},{8,9},{9,8},{10,11... | collective-permute-start | bytes 786440 | tf_op jit(solution)/shard_map/ppermute | solution.py:220

commit v4 on v2

--- a/solution.py
+++ b/solution.py
@@ -22,6 +22,7 @@
 MIB = 1024 * 1024
 BF16 = jnp.bfloat16
 F32 = jnp.float32
+FACTOR = math.log2(math.e) / math.sqrt(HD)
 
 
 def vmem():
@@ -83,7 +84,7 @@
 
 
 def aggregate_kernel(src_ref, count_ref, me_ref, tiles_ref, *refs):
-    feature_refs, out_ref, held = refs[:-2], refs[-2], refs[-1]
+    feature_refs, out_ref, held = refs[:-4], refs[-2], refs[-1]
     rows = out_ref.shape[0]
     for d, ref in enumerate(feature_refs):
         held[d * rows : (d + 1) * rows, :] = ref[...]
@@ -105,32 +106,39 @@
     out_ref[...] = (total * lax.rsqrt(mean_square + 1e-06)).astype(BF16)
 
 
-def query_kernel(own_ref, wq_ref, bucket_ref, q_ref, hot_ref):
-    rows = own_ref.shape[0]
+def query_kernel(own_ref, wq_ref, q_ref):
     q_ref[...] = jnp.dot(own_ref[...], wq_ref[...], preferred_element_type=F32).astype(BF16)
-    for s in range(bucket_ref.shape[0]):
-        hot_ref[s * rows : (s + 1) * rows, :] = one_hot_slab(bucket_ref[s : s + 1, :])
-
-
-def project_kernel(first_ref, second_ref, wk_ref, wv_ref, k_ref, v_ref):
-    block = jnp.concatenate([first_ref[...], second_ref[...]], axis=0)
+
+
+def hot_kernel(bucket_ref, *hot_refs):
+    rows = bucket_ref.shape[1]
+    s = 0
+    for hot_ref in hot_refs:
+        for at in range(0, hot_ref.shape[0], rows):
+            hot_ref[at : at + rows, :] = one_hot_slab(bucket_ref[s : s + 1, :])
+            s += 1
+
+
+def part_kernel(first, last, q_ref, bias_ref, hot_ref, wk_ref, wv_ref, *refs):
+    count = hot_ref.shape[0] // q_ref.shape[0]
+    block_refs, refs = refs[:count], refs[count:]
+    k_ref, v_ref, x0_ref, x1_ref, p0_ref, p1_ref, t0_ref, t1_ref, heads_ref = refs[-9:]
+    refs = refs[:-9]
+    old_refs = ()
+    if not first:
+        old_refs, refs = refs[:3], refs[3:]
+    rows = q_ref.shape[0]
+    keys = hot_ref.shape[0]
+    quads = H // QUAD
+    block = jnp.concatenate([ref[...] for ref in block_refs], axis=0)
     for w_ref, dst in ((wk_ref, k_ref), (wv_ref, v_ref)):
         for n in range(0, WIDE, 256):
             dst[:, n : n + 256] = jnp.dot(
                 block, w_ref[:, n : n + 256], preferred_element_type=F32
             ).astype(BF16)
 
-
-def attend_kernel(q_ref, bias_ref, hot_ref, sel_ref, *refs):
-    pairs = (len(refs) - 6) // 2
-    k_refs, v_refs = refs[:pairs], refs[pairs : 2 * pairs]
-    out_ref, x0_ref, x1_ref, p0_ref, p1_ref, heads_ref = refs[2 * pairs :]
-    rows = out_ref.shape[0]
-    span = k_refs[0].shape[0]
-    quads = H // QUAD
-    factor = math.log2(math.e) / math.sqrt(HD)
     lane_head = lax.broadcasted_iota(jnp.int32, (rows, LANES), 1) // PAD
-    ones = jnp.ones((span, LANES), BF16)
+    ones = jnp.ones((keys, LANES), BF16)
 
     def scores(m, x_ref):
         cols = pl.ds(pl.multiple_of(m * LANES, LANES), LANES)
@@ -145,45 +153,96 @@
             axis=0,
         )
         query = jnp.concatenate([left, right], axis=1)
-        for n, k_ref in enumerate(k_refs):
-            part = slice(n * span, (n + 1) * span)
-            key = jnp.concatenate([k_ref[:, cols], hot_ref[part, :]], axis=1)
-            x_ref[:, part] = lax.dot_general(query, key, NT, preferred_element_type=F32)
-
-    def mix(m, x_ref, p_ref):
+        for n in range(0, keys, 256):
+            key = jnp.concatenate([k_ref[n : n + 256, cols], hot_ref[n : n + 256, :]], axis=1)
+            x_ref[:, n : n + 256] = lax.dot_general(query, key, NT, preferred_element_type=F32)
+
+    def pick(array):
+        out = array[:rows, :]
+        for h in range(1, QUAD):
+            out = jnp.where(lane_head == h, array[h * rows : (h + 1) * rows, :], out)
+        return out
+
+    def mix(m, x_ref, p_ref, t_ref):
         cols = pl.ds(pl.multiple_of(m * LANES, LANES), LANES)
         for r in range(0, QUAD * rows, 16):
             x = x_ref[r : r + 16, :]
             peak = jnp.max(x, axis=-1, keepdims=True)
-            p_ref[r : r + 16, :] = jnp.exp2((x - peak) * factor).astype(BF16)
-        value = jnp.concatenate(
-            [jnp.concatenate([v_ref[:, cols], ones], axis=1) for v_ref in v_refs], axis=0
-        )
+            p_ref[r : r + 16, :] = jnp.exp2((x - peak) * FACTOR).astype(BF16)
+            if not (first and last):
+                t_ref[r : r + 16, :] = jnp.broadcast_to(peak, (16, LANES))
+        value = jnp.concatenate([v_ref[:, cols], ones], axis=1)
         mixed = jnp.dot(p_ref[...], value, preferred_element_type=F32)
-        top = mixed[:rows, :LANES]
-        total = mixed[:rows, LANES:]
-        for h in range(1, QUAD):
-            top = jnp.where(lane_head == h, mixed[h * rows : (h + 1) * rows, :LANES], top)
-            total = jnp.where(lane_head == h, mixed[h * rows : (h + 1) * rows, LANES:], total)
-        heads_ref[:, cols] = (top / total).astype(BF16)
+        top = pick(mixed[:, :LANES])
+        total = pick(mixed[:, LANES:])
+        if not (first and last):
+            peak = pick(t_ref[...])
+        if not first:
+            old_top, old_total, old_peak = (ref[:, cols] for ref in old_refs)
+            best = jnp.maximum(old_peak, peak)
+            new_share = jnp.exp2((peak - best) * FACTOR)
+            old_share = jnp.exp2((old_peak - best) * FACTOR)
+            top = top * new_share + old_top * old_share
+            total = total * new_share + old_total * old_share
+            peak = best
+        if last:
+            heads_ref[:, cols] = (top / total).astype(BF16)
+        else:
+            refs[0][:, cols] = top
+            refs[1][:, cols] = total
+            refs[2][:, cols] = peak
 
     scores(0, x0_ref)
 
     def two(i, carry):
         m = i * 2
         scores(m + 1, x1_ref)
-        mix(m, x0_ref, p0_ref)
+        mix(m, x0_ref, p0_ref, t0_ref)
         scores(jnp.minimum(m + 2, quads - 1), x0_ref)
-        mix(m + 1, x1_ref, p1_ref)
+        mix(m + 1, x1_ref, p1_ref, t1_ref)
         return carry
 
     lax.fori_loop(0, quads // 2, two, 0)
 
-    for part in range(out_ref.shape[1] // HALF):
-        out_ref[:, part * HALF : (part + 1) * HALF] = lax.dot_general(
-            heads_ref[:, part * HALF_PAD : (part + 1) * HALF_PAD], sel_ref[...], NT,
-            preferred_element_type=F32,
-        ).astype(BF16)
+    if last:
+        sel_ref, out_ref = refs
+        for part in range(out_ref.shape[1] // HALF):
+            out_ref[:, part * HALF : (part + 1) * HALF] = lax.dot_general(
+                heads_ref[:, part * HALF_PAD : (part + 1) * HALF_PAD], sel_ref[...], NT,
+                preferred_element_type=F32,
+            ).astype(BF16)
+
+
+def attend_part(first, last, q, bias, hot, wk, wv, blocks, state, sel, width):
+    rows = q.shape[0]
+    keys = rows * len(blocks)
+    if last:
+        outs, extra = [shape(rows, width)], [sel]
+    else:
+        outs, extra = [shape(rows, WIDE, dtype=F32)] * 3, []
+    operands = [q, bias, hot, wk, wv, *blocks, *state, *extra]
+    tall = QUAD * rows
+    need = 2 * tall * keys * 6 + 4 * keys * WIDE + 2 * tall * LANES * 4
+    return pl.pallas_call(
+        lambda *refs: part_kernel(first, last, *refs),
+        out_shape=outs,
+        in_specs=[vmem()] * len(operands),
+        out_specs=[vmem()] * len(outs),
+        scratch_shapes=[
+            pltpu.VMEM((keys, WIDE), BF16),
+            pltpu.VMEM((keys, WIDE), BF16),
+            pltpu.VMEM((tall, keys), F32),
+            pltpu.VMEM((tall, keys), F32),
+            pltpu.VMEM((tall, keys), BF16),
+            pltpu.VMEM((tall, keys), BF16),
+            pltpu.VMEM((tall, LANES), F32),
+            pltpu.VMEM((tall, LANES), F32),
+            pltpu.VMEM((rows, WIDE), BF16),
+        ],
+        compiler_params=limit(need // MIB + 16),
+        cost_estimate=cost(4 * keys * width * WIDE + 4 * tall * keys * 256 * (H // QUAD), 8_000_000),
+        name="part",
+    )(*operands)
 
 
 def swap(array, axis, distance):
@@ -198,7 +257,8 @@
     sel = jnp.asarray(pad_matrix(), BF16)
     own_bucket = node_bucket.reshape(1, rows)
 
-    blocks = [features] + [swap(features, "group", d) for d in range(1, groups)]
+    blocks = [swap(features, "group", d) for d in range(groups - 1, 0, -1)] + [features]
+    blocks = blocks[::-1]
     buckets = own_bucket
     step = 1
     while step < seq_count:
@@ -218,59 +278,58 @@
         name="prepare",
     )(w_qk, w_v, cube, sel, own_bucket)
 
+    chips = seq_count // 2
+    parts = [[0, 1]] + [[d] for d in range(2, chips)]
+    hot = pl.pallas_call(
+        hot_kernel,
+        out_shape=[shape(2 * len(part) * rows, LANES) for part in parts],
+        in_specs=[vmem()],
+        out_specs=[vmem()] * len(parts),
+        compiler_params=limit(16),
+        cost_estimate=cost(keys * LANES, 300_000),
+        name="hot",
+    )(buckets)
+
     own = pl.pallas_call(
         aggregate_kernel,
         out_shape=shape(rows, width),
-        in_specs=[smem()] * 3 + [vmem()] * (1 + groups),
+        in_specs=[smem()] * 3 + [vmem()] * (1 + groups) + [pl.BlockSpec(memory_space=pl.ANY)] * 2,
         out_specs=vmem(),
         scratch_shapes=[pltpu.VMEM((groups * rows, width), BF16)],
         compiler_params=limit(24),
         name="aggregate",
-    )(tile_src, tile_count, lax.axis_index("group").reshape(1), tiles, *blocks)
-
-    far = [own] + [swap(own, "seq", 2 * d) for d in range(1, seq_count // 2)]
-    near = [swap(block, "seq", 1) for block in far]
-
-    q, hot = pl.pallas_call(
+    )(tile_src, tile_count, lax.axis_index("group").reshape(1), tiles, *blocks, wv, hot[0])
+
+    far = [own] + [None] * (chips - 1)
+    for d in range(1, chips):
+        far[d] = swap(own, "seq", 2 * d)
+    near = [swap(own, "seq", 1)]
+
+    q = pl.pallas_call(
         query_kernel,
-        out_shape=[shape(rows, WIDE), shape(keys, LANES)],
-        in_specs=[vmem()] * 3,
-        out_specs=[vmem()] * 2,
+        out_shape=shape(rows, WIDE),
+        in_specs=[vmem()] * 2,
+        out_specs=vmem(),
         compiler_params=limit(16),
         cost_estimate=cost(2 * rows * width * WIDE, 2_000_000),
         name="query",
-    )(own, wq, buckets)
-    k_parts = []
-    v_parts = []
-    for first, second in zip(far, near):
-        k, v = pl.pallas_call(
-            project_kernel,
-            out_shape=[shape(2 * rows, WIDE)] * 2,
-            in_specs=[vmem()] * 4,
-            out_specs=[vmem()] * 2,
-            compiler_params=limit(16),
-            cost_estimate=cost(8 * rows * width * WIDE, 4_000_000),
-            name="project",
-        )(first, second, wk, wv)
-        k_parts.append(k)
-        v_parts.append(v)
-
-    need = 2 * QUAD * rows * keys * 6 + 4 * keys * WIDE + 2 * keys * LANES
-    return pl.pallas_call(
-        attend_kernel,
-        out_shape=shape(rows, width),
-        in_specs=[vmem()] * (4 + 2 * len(k_parts)),
-        out_specs=vmem(),
-        scratch_shapes=[
-            pltpu.VMEM((QUAD * rows, keys), F32),
-            pltpu.VMEM((QUAD * rows, keys), F32),
-            pltpu.VMEM((QUAD * rows, keys), BF16),
-            pltpu.VMEM((QUAD * rows, keys), BF16),
-            pltpu.VMEM((rows, WIDE), BF16),
-        ],
-        compiler_params=limit(need // MIB + 8),
-        name="attend",
-    )(q, bias, hot, sel, *k_parts, *v_parts)
+    )(own, wq)
+
+    state = []
+    for number, part in enumerate(parts):
+        blocks = []
+        for d in part:
+            block = far[d]
+            if state:
+                block, state = lax.optimization_barrier((block, state))
+            if d:
+                near.append(swap(block, "seq", 1))
+            blocks += [block, near[d]]
+        state = attend_part(
+            number == 0, number == len(parts) - 1, q, bias,
+            hot[number], wk, wv, blocks, state, sel, width,
+        )
+    return state[0]
 
 
 def solution(mesh):

time: 48.3 us -> 60.4 us (1.25)
  local copies, waits for them, and re-layouts: 2.9 us -> 8.19 us
  waiting for transfers between devices: 12.9 us -> 17.7 us
  Pallas kernels: 15.9 us -> 18.5 us
  starting transfers between devices: 14.7 us -> 12.5 us
  other arithmetic: 0.89 us -> 2.25 us
    unnamed x16 -> x24, local copies, waits for them, and re-layouts: 2.69 us -> 7.99 us
    ppermute x13, waiting for transfers between devices: 12.9 us -> 17.7 us  [swap(): lax.ppermute(array, axis, [(i, i ^ distance) for i in range(lax.axis_size...]
    ppermute x13, starting transfers between devices: 14.7 us -> 12.5 us  [swap(): lax.ppermute(array, axis, [(i, i ^ distance) for i in range(lax.axis_size...]
    pallas_call x6 -> x5, Pallas kernels: 11.9 us -> 14 us  [the longest x3 13.5 us: attend_part(): pl.pallas_call(lambda *refs: part_kernel(first, last, *refs), out_shape=o...]
    concatenate x3, other arithmetic: 0.68 us -> 2.05 us  [on_device(): buckets = jnp.concatenate([buckets, swap(buckets, 'seq', step)], axis=0)]
  transfers between devices with their start and end apart: 13 -> 13, of which waited for: 3 -> 7; matrix products, arithmetic and copies ran while one was open for 4% -> 6% of each run, Pallas kernels for 15% -> 21%
where the time goes in v4:
time: 60.4 us; the launch traced here: 60 us
  Pallas kernels  18.5 us (31%)
  waiting for transfers between devices  17.7 us (29%)
  starting transfers between devices  12.5 us (21%)
  local copies, waits for them, and re-layouts  8.19 us (14%)
  other arithmetic  2.25 us (4%)
  between operations  0.81 us (1%)
    ppermute x13, waiting for transfers between devices, swap(): lax.ppermute(array, axis, [(i, i ^ distance) for i in range(lax.axis_size...  17.7 us
    pallas_call x3, Pallas kernels, attend_part(): pl.pallas_call(lambda *refs: part_kernel(first, last, *refs), out_shape=o...  13.5 us
    ppermute x13, starting transfers between devices, swap(): lax.ppermute(array, axis, [(i, i ^ distance) for i in range(lax.axis_size...  12.5 us
    unnamed x24, local copies, waits for them, and re-layouts  7.99 us
    pallas_call x1, Pallas kernels, on_device(): pl.pallas_call(prepare_kernel, out_shape=[shape(width, WIDE)] * 3 + [shap...  2.87 us
    concatenate x3, other arithmetic, on_device(): buckets = jnp.concatenate([buckets, swap(buckets, 'seq', step)], axis=0)  2.05 us
    pallas_call x1, Pallas kernels, on_device(): pl.pallas_call(aggregate_kernel, out_shape=shape(rows, width), in_specs=[...  1.64 us
  transfers between devices with their start and end apart: 13, of which 7 were waited for; matrix products, arithmetic and copies ran while one was open for 6% of the time, Pallas kernels for 21%

profile of v4, /device:TPU:0, one launch (start us, length us, event | category | flops | bytes accessed | tf_op | source)
XLA Modules:
  0.0 60.0 jit_solution(2858705617465778608)
XLA Ops:
  0.0 0.0 copy-start.4
  0.0 0.0 copy-start.7
  0.0 0.5 collective-permute-start.3
  0.5 2.6 %collective-permute-start.1 = (bf16[128,768]{1,0:T(8,128)(2,1)}, bf16[128,768]{1,0:T(8,128)(2,1)}, u32[]{:S(2)}, u32[]{:S(2)}) collective-permute-start(bf16[128,768]{1,0:T(8,128)(2,1)} %refs_0_.1), channel_id=1, source_target_pairs={{0,16},{8,24},{16,0},{24,8},{1,17},{9,25},{17,1},{25,9},{2,18},{10... | collective-permute-start | bytes 589832 | tf_op jit(solution)/shard_map/ppermute | solution.py:249
  3.0 1.5 %collective-permute-start = (bf16[128,768]{1,0:T(8,128)(2,1)}, bf16[128,768]{1,0:T(8,128)(2,1)}, u32[]{:S(2)}, u32[]{:S(2)}) collective-permute-start(bf16[128,768]{1,0:T(8,128)(2,1)} %refs_0_.1), channel_id=1, source_target_pairs={{0,8},{8,0},{16,24},{24,16},{1,9},{9,1},{17,25},{25,17},{2,10},{10... | collective-permute-start | bytes 589832 | tf_op jit(solution)/shard_map/ppermute | solution.py:249
  4.5 0.1 collective-permute-start.2
  4.6 0.9 %copy.11 = f32[32,256]{0,1:T(8,128)S(1)} copy(f32[32,256]{1,0:T(8,128)} %param.16) | data formatting | bytes 65536 | tf_op args[7]
  5.4 0.1 copy.12
  5.6 0.1 pad.12.clone
  5.7 0.0 collective-permute-done.3
  5.7 0.7 %pad_add_fusion.2 = s32[2,128]{1,0:T(2,128)S(1)} fusion(s32[1,128]{1,0:T(1,128)S(1)} %collective-permute-done.3, s32[1,128]{1,0:T(1,128)} %bitcast.11), kind=kLoop, calls=%fused_computation.4 | loop fusion | flops 256 | bytes 2048 | tf_op jit(solution)/shard_map/concatenate | solution.py:265
  6.3 2.0 %collective-permute-start.4 = (s32[2,128]{1,0:T(2,128)S(1)}, s32[2,128]{1,0:T(2,128)S(1)}, u32[]{:S(2)}, u32[]{:S(2)}) collective-permute-start(s32[2,128]{1,0:T(2,128)S(1)} %pad_add_fusion.2), channel_id=1, source_target_pairs={{0,2},{1,3},{2,0},{3,1},{4,6},{5,7},{6,4},{7,5},{8,10},{9,11},{10,... | collective-permute-start | bytes 3080 | tf_op jit(solution)/shard_map/ppermute | solution.py:249
  8.3 0.2 maximum_maximum_fusion
  8.5 0.2 copy.17
  8.7 1.2 %collective-permute-done.4 = s32[2,128]{1,0:T(2,128)S(1)} collective-permute-done((s32[2,128]{1,0:T(2,128)S(1)}, s32[2,128]{1,0:T(2,128)S(1)}, u32[]{:S(2)}, u32[]{:S(2)}) %collective-permute-start.4) | collective-permute-done | bytes 1056 | tf_op jit(solution)/shard_map/ppermute | solution.py:249
  9.9 0.0 copy-done.7
  9.9 0.6 pad_add_fusion.1
  10.5 3.0 %collective-permute-start.5 = (s32[4,128]{1,0:T(4,128)}, s32[4,128]{1,0:T(4,128)}, u32[]{:S(2)}, u32[]{:S(2)}) collective-permute-start(s32[4,128]{1,0:T(4,128)} %pad_add_fusion.1), channel_id=1, source_target_pairs={{0,4},{1,5},{2,6},{3,7},{4,0},{5,1},{6,2},{7,3},{8,12},{9,13},{10,... | collective-permute-start | bytes 6152 | tf_op jit(solution)/shard_map/ppermute | solution.py:249
  13.5 0.0 copy-done.4
  13.5 0.0 copy-start.9
  13.5 1.7 %copy-done.9 = bf16[768,1536]{1,0:T(8,128)(2,1)S(1)} copy-done((bf16[768,1536]{1,0:T(8,128)(2,1)S(1)}, bf16[768,1536]{1,0:T(8,128)(2,1)}, u32[]{:S(2)}) %copy-start.9) | copy-done | bytes 2359320
  15.2 0.0 copy-start.10
  15.2 1.3 %copy-done.10 = bf16[768,768]{1,0:T(8,128)(2,1)S(1)} copy-done((bf16[768,768]{1,0:T(8,128)(2,1)S(1)}, bf16[768,768]{1,0:T(8,128)(2,1)}, u32[]{:S(2)}) %copy-start.10) | copy-done | bytes 1179672
  16.4 0.0 copy-start.8
  16.4 2.9 %prepare.1 = (bf16[768,1024]{1,0:T(8,128)(2,1)S(1)}, bf16[768,1024]{1,0:T(8,128)(2,1)S(1)}, bf16[768,1024]{1,0:T(8,128)(2,1)S(1)}, bf16[128,4096]{1,0:T(8,128)(2,1)S(1)}) custom-call(bf16[768,1536]{1,0:T(8,128)(2,1)S(1)} %copy-done.9, bf16[768,768]{1,0:T(8,128)(2,1)S(1)} %copy-done.10, f32[16,4096]{1,0:T(8,128)S(1)} %bitcast.9, ...), custom_call_target="tpu_custom_call" | custom-call | flops 1811939328 | bytes 10000000 | tf_op jit(solution)/shard_map/prepare/pallas_call | solution.py:271
  19.3 0.0 copy-start
  19.3 1.2 %copy-done = bf16[768,1024]{1,0:T(8,128)(2,1)} copy-done((bf16[768,1024]{1,0:T(8,128)(2,1)}, bf16[768,1024]{1,0:T(8,128)(2,1)S(1)}, u32[]{:S(2)}) %copy-start) | copy-done | bytes 1572888
  20.5 0.0 copy-start.2
  20.5 1.0 %copy-done.2 = bf16[128,4096]{1,0:T(8,128)(2,1)} copy-done((bf16[128,4096]{1,0:T(8,128)(2,1)}, bf16[128,4096]{1,0:T(8,128)(2,1)S(1)}, u32[]{:S(2)}) %copy-start.2) | copy-done | bytes 1048600
  21.5 0.0 copy-start.1
  21.5 0.0 collective-permute-done.5
  21.5 0.8 %pad_add_fusion.bucket_ref = s32[8,128]{1,0:T(8,128)S(1)} fusion(s32[4,128]{1,0:T(4,128)} %collective-permute-done.5, s32[2,128]{1,0:T(2,128)S(1)} %collective-permute-done.4, s32[1,128]{1,0:T(1,128)S(1)} %collective-permute-done.3, s32[1,128]{1,0:T(1,128)S(1)} %bitcast.14), kind=kLoop, calls=%fused_computation.2 | loop fusion | flops 3072 | bytes 8192 | tf_op jit(solution)/shard_map/concatenate | solution.py:265
  23.0 0.1 hot.1
  23.1 0.0 collective-permute-done.1.refs_2_
  23.1 0.0 collective-permute-done.refs_1_
  23.1 0.0 collective-permute-done.2.refs_3_
  23.1 0.0 copy-done.8
  23.1 0.0 copy-start.5
  23.1 0.9 %copy-done.5 = bf16[128,1024]{1,0:T(8,128)(2,1)S(1)} copy-done((bf16[128,1024]{1,0:T(8,128)(2,1)S(1)}, bf16[128,1024]{1,0:T(8,128)(2,1)}, u32[]{:S(2)}) %copy-start.5) | copy-done | bytes 262168
  24.1 0.0 copy-start.6
  24.1 0.9 %copy-done.6 = bf16[128,768]{1,0:T(8,128)(2,1)S(1)} copy-done((bf16[128,768]{1,0:T(8,128)(2,1)S(1)}, bf16[128,768]{1,0:T(8,128)(2,1)}, u32[]{:S(2)}) %copy-start.6) | copy-done | bytes 196632
  25.0 1.6 %aggregate.1.own_ref.refs_5_ = bf16[128,768]{1,0:T(8,128)(2,1)S(1)} custom-call(s32[1,8]{1,0:T(1,128)S(1)} %copy-done.8, s32[1]{0:T(128)S(6)} %copy.18.count_ref, s32[1]{0:T(128)} %bitcast.me_ref, bf16[128,1024]{1,0:T(8,128)(2,1)S(1)} %copy-done.5, bf16[128,768]{1,0:T(8,128)(2,1)S(1)} %copy-done.6, bf16[128,768]{1,0:T(8,128)(2,1)} %collective-permute-done.refs_1_, ...), custom_call_target="tpu_custom_call" | custom-call | tf_op jit(solution)/shard_map/aggregate/pallas_call | solution.py:293
  26.7 0.0 copy-start.3
  26.7 1.6 %collective-permute-start.9 = (bf16[128,768]{1,0:T(8,128)(2,1)S(1)}, bf16[128,768]{1,0:T(8,128)(2,1)S(1)}, u32[]{:S(2)}, u32[]{:S(2)}) collective-permute-start(bf16[128,768]{1,0:T(8,128)(2,1)S(1)} %aggregate.1.own_ref.refs_5_), channel_id=1, source_target_pairs={{0,2},{1,3},{2,0},{3,1},{4,6},{5,7},{6,4},{7,5},{8,10},{9,11},{10,... | collective-permute-start | bytes 589832 | tf_op jit(solution)/shard_map/ppermute | solution.py:249
  28.3 0.0 collective-permute-start.8
  28.3 4.1 %collective-permute-done.9.refs_7_ = bf16[128,768]{1,0:T(8,128)(2,1)S(1)} collective-permute-done((bf16[128,768]{1,0:T(8,128)(2,1)S(1)}, bf16[128,768]{1,0:T(8,128)(2,1)S(1)}, u32[]{:S(2)}, u32[]{:S(2)}) %collective-permute-start.9) | collective-permute-done | bytes 196640 | tf_op jit(solution)/shard_map/ppermute | solution.py:249
  32.4 0.0 collective-permute-start.10
  32.4 0.0 collective-permute-start.7
  32.4 0.0 copy-done.1
  32.4 0.4 query.1.refs_0_
  32.8 0.0 collective-permute-done.8.refs_6_
  32.8 1.0 %collective-permute-done.10.refs_8_ = bf16[128,768]{1,0:T(8,128)(2,1)S(1)} collective-permute-done((bf16[128,768]{1,0:T(8,128)(2,1)S(1)}, bf16[128,768]{1,0:T(8,128)(2,1)S(1)}, u32[]{:S(2)}, u32[]{:S(2)}) %collective-permute-start.10) | collective-permute-done | bytes 196640 | tf_op jit(solution)/shard_map/ppermute | solution.py:249
  33.9 0.0 copy-done.3
  33.9 5.5 %part.3 = (f32[128,1024]{1,0:T(8,128)S(1)}, f32[128,1024]{1,0:T(8,128)S(1)}, f32[128,1024]{1,0:T(8,128)S(1)}) custom-call(bf16[128,1024]{1,0:T(8,128)(2,1)S(1)} %query.1.refs_0_, bf16[128,4096]{1,0:T(8,128)(2,1)S(1)} %copy-done.3, bf16[512,128]{1,0:T(8,128)(2,1)S(1)} %get-tuple-element.27.refs_5_.refs_2_, bf16[768,1024]{1,0:T(8,128)(2,1)S(1)} %get-tuple-element.31.refs_3_, ...), custom_call_target="tpu_custom_call" | custom-call | flops 3758096384 | bytes 8000000 | tf_op jit(solution)/shard_map/part/pallas_call | solution.py:226
  39.4 5.4 %collective-permute-done.7.refs_5_ = bf16[128,768]{1,0:T(8,128)(2,1)S(1)} collective-permute-done((bf16[128,768]{1,0:T(8,128)(2,1)S(1)}, bf16[128,768]{1,0:T(8,128)(2,1)S(1)}, u32[]{:S(2)}, u32[]{:S(2)}) %collective-permute-start.7) | collective-permute-done | bytes 196640 | tf_op jit(solution)/shard_map/ppermute | solution.py:249
  44.8 0.0 collective-permute-start.11
  44.8 1.3 %collective-permute-start.6 = (bf16[128,768]{1,0:T(8,128)(2,1)S(1)}, bf16[128,768]{1,0:T(8,128)(2,1)S(1)}, u32[]{:S(2)}, u32[]{:S(2)}) collective-permute-start(bf16[128,768]{1,0:T(8,128)(2,1)S(1)} %aggregate.1.own_ref.refs_5_), channel_id=1, source_target_pairs={{0,6},{1,7},{2,4},{3,5},{4,2},{5,3},{6,0},{7,1},{8,14},{9,15},{10,... | collective-permute-start | bytes 589832 | tf_op jit(solution)/shard_map/ppermute | solution.py:249
  46.1 0.2 collective-permute-done.11.refs_6_
  46.3 3.5 %part.4 = (f32[128,1024]{1,0:T(8,128)S(1)}, f32[128,1024]{1,0:T(8,128)S(1)}, f32[128,1024]{1,0:T(8,128)S(1)}) custom-call(bf16[128,1024]{1,0:T(8,128)(2,1)S(1)} %query.1.refs_0_, bf16[128,4096]{1,0:T(8,128)(2,1)S(1)} %copy-done.3, bf16[256,128]{1,0:T(8,128)(2,1)S(1)} %get-tuple-element.32.refs_2_, bf16[768,1024]{1,0:T(8,128)(2,1)S(1)} %get-tuple-element.31.refs_3_, ...), custom_call_target="tpu_custom_call" | custom-call | flops 1879048192 | bytes 8000000 | tf_op jit(solution)/shard_map/part/pallas_call | solution.py:226
  49.8 4.3 %collective-permute-done.6.refs_5_ = bf16[128,768]{1,0:T(8,128)(2,1)S(1)} collective-permute-done((bf16[128,768]{1,0:T(8,128)(2,1)S(1)}, bf16[128,768]{1,0:T(8,128)(2,1)S(1)}, u32[]{:S(2)}, u32[]{:S(2)}) %collective-permute-start.6) | collective-permute-done | bytes 196640 | tf_op jit(solution)/shard_map/ppermute | solution.py:249
  54.1 0.0 collective-permute-start.12
  54.1 1.4 %collective-permute-done.12.refs_6_ = bf16[128,768]{1,0:T(8,128)(2,1)S(1)} collective-permute-done((bf16[128,768]{1,0:T(8,128)(2,1)S(1)}, bf16[128,768]{1,0:T(8,128)(2,1)S(1)}, u32[]{:S(2)}, u32[]{:S(2)}) %collective-permute-start.12) | collective-permute-done | bytes 196640 | tf_op jit(solution)/shard_map/ppermute | solution.py:249
  55.5 4.5 %part.5 = bf16[128,768]{1,0:T(8,128)(2,1)} custom-call(bf16[128,1024]{1,0:T(8,128)(2,1)S(1)} %query.1.refs_0_, bf16[128,4096]{1,0:T(8,128)(2,1)S(1)} %copy-done.3, bf16[256,128]{1,0:T(8,128)(2,1)S(1)} %get-tuple-element.30.refs_2_, bf16[768,1024]{1,0:T(8,128)(2,1)S(1)} %get-tuple-element.31.refs_3_, bf16[768,1024]{1,0:T(8,128)(2,1)S(1)} %get-tuple-element.26.refs_4_, ...), custom_call_target="tpu_custom_call" | custom-call | flops 1879048192 | bytes 8000000 | tf_op jit(solution)/shard_map/part/pallas_call | solution.py:226
  (1 shorter events, 0.0 us)
Async XLA Ops:
  0.0 13.5 %copy-start.4 = (bf16[384,512]{1,0:T(8,128)(2,1)S(1)}, bf16[384,512]{1,0:T(8,128)(2,1)}, u32[]{:S(2)}) copy-start(bf16[384,512]{1,0:T(8,128)(2,1)} %constant.9.clone.sel_ref.refs_10_) | copy-start | bytes 1179652
  0.0 9.9 %copy-start.7 = (s32[128]{0:T(128)S(1)}, s32[128]{0:T(128)}, u32[]{:S(2)}) copy-start(s32[128]{0:T(128)} %param.13) | copy-start | bytes 1540
  0.0 5.7 %collective-permute-start.3 = (s32[1,128]{1,0:T(1,128)}, s32[1,128]{1,0:T(1,128)S(1)}, u32[]{:S(2)}, u32[]{:S(2)}) collective-permute-start(s32[1,128]{1,0:T(1,128)} %bitcast.10), channel_id=1, source_target_pairs={{0,1},{1,0},{2,3},{3,2},{4,5},{5,4},{6,7},{7,6},{8,9},{9,8},{10,11... | collective-permute-start | bytes 1544 | tf_op jit(solution)/shard_map/ppermute | solution.py:249
  0.5 22.6 %collective-permute-start.1 = (bf16[128,768]{1,0:T(8,128)(2,1)}, bf16[128,768]{1,0:T(8,128)(2,1)}, u32[]{:S(2)}, u32[]{:S(2)}) collective-permute-start(bf16[128,768]{1,0:T(8,128)(2,1)} %refs_0_.1), channel_id=1, source_target_pairs={{0,16},{8,24},{16,0},{24,8},{1,17},{9,25},{17,1},{25,9},{2,18},{10... | collective-permute-start | bytes 589832 | tf_op jit(solution)/shard_map/ppermute | solution.py:249
  3.0 20.1 %collective-permute-start = (bf16[128,768]{1,0:T(8,128)(2,1)}, bf16[128,768]{1,0:T(8,128)(2,1)}, u32[]{:S(2)}, u32[]{:S(2)}) collective-permute-start(bf16[128,768]{1,0:T(8,128)(2,1)} %refs_0_.1), channel_id=1, source_target_pairs={{0,8},{8,0},{16,24},{24,16},{1,9},{9,1},{17,25},{25,17},{2,10},{10... | collective-permute-start | bytes 589832 | tf_op jit(solution)/shard_map/ppermute | solution.py:249
  4.5 18.6 %collective-permute-start.2 = (bf16[128,768]{1,0:T(8,128)(2,1)}, bf16[128,768]{1,0:T(8,128)(2,1)}, u32[]{:S(2)}, u32[]{:S(2)}) collective-permute-start(bf16[128,768]{1,0:T(8,128)(2,1)} %refs_0_.1), channel_id=1, source_target_pairs={{0,24},{8,16},{16,8},{24,0},{1,25},{9,17},{17,9},{25,1},{2,26},{10... | collective-permute-start | bytes 589832 | tf_op jit(solution)/shard_map/ppermute | solution.py:249
  6.3 3.6 %collective-permute-start.4 = (s32[2,128]{1,0:T(2,128)S(1)}, s32[2,128]{1,0:T(2,128)S(1)}, u32[]{:S(2)}, u32[]{:S(2)}) collective-permute-start(s32[2,128]{1,0:T(2,128)S(1)} %pad_add_fusion.2), channel_id=1, source_target_pairs={{0,2},{1,3},{2,0},{3,1},{4,6},{5,7},{6,4},{7,5},{8,10},{9,11},{10,... | collective-permute-start | bytes 3080 | tf_op jit(solution)/shard_map/ppermute | solution.py:249
  10.5 11.0 %collective-permute-start.5 = (s32[4,128]{1,0:T(4,128)}, s32[4,128]{1,0:T(4,128)}, u32[]{:S(2)}, u32[]{:S(2)}) collective-permute-start(s32[4,128]{1,0:T(4,128)} %pad_add_fusion.1), channel_id=1, source_target_pairs={{0,4},{1,5},{2,6},{3,7},{4,0},{5,1},{6,2},{7,3},{8,12},{9,13},{10,... | collective-permute-start | bytes 6152 | tf_op jit(solution)/shard_map/ppermute | solution.py:249
  13.5 1.7 %copy-start.9 = (bf16[768,1536]{1,0:T(8,128)(2,1)S(1)}, bf16[768,1536]{1,0:T(8,128)(2,1)}, u32[]{:S(2)}) copy-start(bf16[768,1536]{1,0:T(8,128)(2,1)} %w_qk_ref.1) | copy-start | bytes 7077892
  15.2 1.3 %copy-start.10 = (bf16[768,768]{1,0:T(8,128)(2,1)S(1)}, bf16[768,768]{1,0:T(8,128)(2,1)}, u32[]{:S(2)}) copy-start(bf16[768,768]{1,0:T(8,128)(2,1)} %w_v_ref.1) | copy-start | bytes 3538948
  16.4 6.7 %copy-start.8 = (s32[1,8]{1,0:T(1,128)S(1)}, s32[1,8]{1,0:T(1,128)}, u32[]{:S(2)}) copy-start(s32[1,8]{1,0:T(1,128)} %src_ref.1) | copy-start | bytes 100
  19.3 1.2 %copy-start = (bf16[768,1024]{1,0:T(8,128)(2,1)}, bf16[768,1024]{1,0:T(8,128)(2,1)S(1)}, u32[]{:S(2)}) copy-start(bf16[768,1024]{1,0:T(8,128)(2,1)S(1)} %get-tuple-element.28.wq_ref) | copy-start | bytes 4718596
  20.5 1.0 %copy-start.2 = (bf16[128,4096]{1,0:T(8,128)(2,1)}, bf16[128,4096]{1,0:T(8,128)(2,1)S(1)}, u32[]{:S(2)}) copy-start(bf16[128,4096]{1,0:T(8,128)(2,1)S(1)} %get-tuple-element.29.refs_1_) | copy-start | bytes 3145732
  21.5 10.9 %copy-start.1 = (bf16[768,1024]{1,0:T(8,128)(2,1)S(1)}, bf16[768,1024]{1,0:T(8,128)(2,1)}, u32[]{:S(2)}) copy-start(bf16[768,1024]{1,0:T(8,128)(2,1)} %copy-done) | copy-start | bytes 4718596
  23.1 1.0 %copy-start.5 = (bf16[128,1024]{1,0:T(8,128)(2,1)S(1)}, bf16[128,1024]{1,0:T(8,128)(2,1)}, u32[]{:S(2)}) copy-start(bf16[128,1024]{1,0:T(8,128)(2,1)} %tiles_ref.1) | copy-start | bytes 786436
  24.1 0.9 %copy-start.6 = (bf16[128,768]{1,0:T(8,128)(2,1)S(1)}, bf16[128,768]{1,0:T(8,128)(2,1)}, u32[]{:S(2)}) copy-start(bf16[128,768]{1,0:T(8,128)(2,1)} %refs_0_.1) | copy-start | bytes 589828
  26.7 7.2 %copy-start.3 = (bf16[128,4096]{1,0:T(8,128)(2,1)S(1)}, bf16[128,4096]{1,0:T(8,128)(2,1)}, u32[]{:S(2)}) copy-start(bf16[128,4096]{1,0:T(8,128)(2,1)} %copy-done.2) | copy-start | bytes 3145732
  26.7 5.7 %collective-permute-start.9 = (bf16[128,768]{1,0:T(8,128)(2,1)S(1)}, bf16[128,768]{1,0:T(8,128)(2,1)S(1)}, u32[]{:S(2)}, u32[]{:S(2)}) collective-permute-start(bf16[128,768]{1,0:T(8,128)(2,1)S(1)} %aggregate.1.own_ref.refs_5_), channel_id=1, source_target_pairs={{0,2},{1,3},{2,0},{3,1},{4,6},{5,7},{6,4},{7,5},{8,10},{9,11},{10,... | collective-permute-start | bytes 589832 | tf_op jit(solution)/shard_map/ppermute | solution.py:249
  28.3 4.5 %collective-permute-start.8 = (bf16[128,768]{1,0:T(8,128)(2,1)S(1)}, bf16[128,768]{1,0:T(8,128)(2,1)S(1)}, u32[]{:S(2)}, u32[]{:S(2)}) collective-permute-start(bf16[128,768]{1,0:T(8,128)(2,1)S(1)} %aggregate.1.own_ref.refs_5_), channel_id=1, source_target_pairs={{0,1},{1,0},{2,3},{3,2},{4,5},{5,4},{6,7},{7,6},{8,9},{9,8},{10,11... | collective-permute-start | bytes 589832 | tf_op jit(solution)/shard_map/ppermute | solution.py:249
  32.4 1.4 %collective-permute-start.10 = (bf16[128,768]{1,0:T(8,128)(2,1)S(1)}, bf16[128,768]{1,0:T(8,128)(2,1)S(1)}, u32[]{:S(2)}, u32[]{:S(2)}) collective-permute-start(bf16[128,768]{1,0:T(8,128)(2,1)S(1)} %collective-permute-done.9.refs_7_), channel_id=1, source_target_pairs={{0,1},{1,0},{2,3},{3,2},{4,5},{5,4},{6,7},{7,6},{8,9},{9,8},{10,11... | collective-permute-start | bytes 589832 | tf_op jit(solution)/shard_map/ppermute | solution.py:249
  32.4 12.4 %collective-permute-start.7 = (bf16[128,768]{1,0:T(8,128)(2,1)S(1)}, bf16[128,768]{1,0:T(8,128)(2,1)S(1)}, u32[]{:S(2)}, u32[]{:S(2)}) collective-permute-start(bf16[128,768]{1,0:T(8,128)(2,1)S(1)} %aggregate.1.own_ref.refs_5_), channel_id=1, source_target_pairs={{0,4},{1,5},{2,6},{3,7},{4,0},{5,1},{6,2},{7,3},{8,12},{9,13},{10,... | collective-permute-start | bytes 589832 | tf_op jit(solution)/shard_map/ppermute | solution.py:249
  44.8 1.4 %collective-permute-start.11 = (bf16[128,768]{1,0:T(8,128)(2,1)S(1)}, bf16[128,768]{1,0:T(8,128)(2,1)S(1)}, u32[]{:S(2)}, u32[]{:S(2)}) collective-permute-start(bf16[128,768]{1,0:T(8,128)(2,1)S(1)} %collective-permute-done.7.refs_5_), channel_id=1, source_target_pairs={{0,1},{1,0},{2,3},{3,2},{4,5},{5,4},{6,7},{7,6},{8,9},{9,8},{10,11... | collective-permute-start | bytes 589832 | tf_op jit(solution)/shard_map/ppermute | solution.py:249
  44.8 9.2 %collective-permute-start.6 = (bf16[128,768]{1,0:T(8,128)(2,1)S(1)}, bf16[128,768]{1,0:T(8,128)(2,1)S(1)}, u32[]{:S(2)}, u32[]{:S(2)}) collective-permute-start(bf16[128,768]{1,0:T(8,128)(2,1)S(1)} %aggregate.1.own_ref.refs_5_), channel_id=1, source_target_pairs={{0,6},{1,7},{2,4},{3,5},{4,2},{5,3},{6,0},{7,1},{8,14},{9,15},{10,... | collective-permute-start | bytes 589832 | tf_op jit(solution)/shard_map/ppermute | solution.py:249
  54.1 1.4 %collective-permute-start.12 = (bf16[128,768]{1,0:T(8,128)(2,1)S(1)}, bf16[128,768]{1,0:T(8,128)(2,1)S(1)}, u32[]{:S(2)}, u32[]{:S(2)}) collective-permute-start(bf16[128,768]{1,0:T(8,128)(2,1)S(1)} %collective-permute-done.6.refs_5_), channel_id=1, source_target_pairs={{0,1},{1,0},{2,3},{3,2},{4,5},{5,4},{6,7},{7,6},{8,9},{9,8},{10,11... | collective-permute-start | bytes 589832 | tf_op jit(solution)/shard_map/ppermute | solution.py:249

commit v5 on v4

--- a/solution.py
+++ b/solution.py
@@ -61,15 +61,23 @@
     return hot.T.astype(BF16)
 
 
-def prepare_kernel(w_qk_ref, w_v_ref, cube_ref, sel_ref, bucket_ref, wq_ref, wk_ref, wv_ref, bias_ref):
-    width = w_v_ref.shape[1]
-    sel = sel_ref[...]
-    for src, base, dst in ((w_qk_ref, 0, wq_ref), (w_qk_ref, width, wk_ref), (w_v_ref, 0, wv_ref)):
-        for part in range(width // HALF):
-            block = src[:, base + part * HALF : base + (part + 1) * HALF]
-            dst[:, part * HALF_PAD : (part + 1) * HALF_PAD] = jnp.dot(
-                block, sel, preferred_element_type=F32
-            ).astype(BF16)
+def stage_kernel(
+    count_ref, me_ref, cube_ref, bucket_ref, features_ref, tiles_ref, *refs
+):
+    bias_ref, own_ref, masked_ref, hot_refs = refs[0], refs[1], refs[2], refs[3:]
+    rows = features_ref.shape[0]
+    me = me_ref[0]
+    own_ref[...] = features_ref[...]
+    for t in range(TILES):
+        tile = tiles_ref[:, t * rows : (t + 1) * rows]
+        masked_ref[:, t * rows : (t + 1) * rows] = jnp.where(
+            t < count_ref[0], tile, jnp.zeros_like(tile)
+        )
+    s = 0
+    for hot_ref in hot_refs:
+        for at in range(0, hot_ref.shape[0], rows):
+            hot_ref[at : at + rows, :] = one_hot_slab(bucket_ref[pl.ds(me ^ s, 1), :])
+            s += 1
     scaled = cube_ref[...] * math.sqrt(HD)
     high = scaled.astype(BF16).astype(F32)
     rest = scaled - high
@@ -79,47 +87,44 @@
     parts = jnp.where(
         lane < NB, high, jnp.where(lane < 2 * NB, mid, jnp.where(lane < 3 * NB, low, 0.0))
     )
-    hot = one_hot_slab(bucket_ref[...])[:, :NB]
+    hot = one_hot_slab(bucket_ref[pl.ds(me, 1), :])[:, :NB]
     bias_ref[...] = jnp.dot(hot, parts.astype(BF16), preferred_element_type=F32).astype(BF16)
 
 
-def aggregate_kernel(src_ref, count_ref, me_ref, tiles_ref, *refs):
-    feature_refs, out_ref, held = refs[:-4], refs[-2], refs[-1]
+def aggregate_kernel(src_ref, me_ref, masked_ref, *refs):
+    feature_refs, out_ref, held = refs[:-2], refs[-2], refs[-1]
     rows = out_ref.shape[0]
     for d, ref in enumerate(feature_refs):
         held[d * rows : (d + 1) * rows, :] = ref[...]
-    count = count_ref[0]
     me = me_ref[0]
     picked = []
-    masked = []
     for t in range(TILES):
         start = pl.multiple_of((src_ref[0, t] ^ me) * rows, rows)
         picked.append(held[pl.ds(start, rows), :])
-        tile = tiles_ref[:, t * rows : (t + 1) * rows]
-        masked.append(jnp.where(t < count, tile, jnp.zeros_like(tile)))
     total = feature_refs[0][...].astype(F32) + jnp.dot(
-        jnp.concatenate(masked, axis=1),
-        jnp.concatenate(picked, axis=0),
-        preferred_element_type=F32,
+        masked_ref[...], jnp.concatenate(picked, axis=0), preferred_element_type=F32
     )
     mean_square = jnp.mean(total * total, axis=-1, keepdims=True)
     out_ref[...] = (total * lax.rsqrt(mean_square + 1e-06)).astype(BF16)
 
 
-def query_kernel(own_ref, wq_ref, q_ref):
-    q_ref[...] = jnp.dot(own_ref[...], wq_ref[...], preferred_element_type=F32).astype(BF16)
-
-
-def hot_kernel(bucket_ref, *hot_refs):
-    rows = bucket_ref.shape[1]
-    s = 0
-    for hot_ref in hot_refs:
-        for at in range(0, hot_ref.shape[0], rows):
-            hot_ref[at : at + rows, :] = one_hot_slab(bucket_ref[s : s + 1, :])
-            s += 1
-
-
-def part_kernel(first, last, q_ref, bias_ref, hot_ref, wk_ref, wv_ref, *refs):
+def project(block, w_ref, base, sel, dst):
+    width = block.shape[1]
+    for part in range(width // HALF):
+        raw = jnp.dot(
+            block, w_ref[:, base + part * HALF : base + (part + 1) * HALF],
+            preferred_element_type=F32,
+        ).astype(BF16)
+        dst[:, part * HALF_PAD : (part + 1) * HALF_PAD] = jnp.dot(
+            raw, sel, preferred_element_type=F32
+        ).astype(BF16)
+
+
+def query_kernel(own_ref, w_qk_ref, sel_ref, q_ref):
+    project(own_ref[...], w_qk_ref, 0, sel_ref[...], q_ref)
+
+
+def part_kernel(first, last, q_ref, bias_ref, hot_ref, w_qk_ref, w_v_ref, sel_ref, *refs):
     count = hot_ref.shape[0] // q_ref.shape[0]
     block_refs, refs = refs[:count], refs[count:]
     k_ref, v_ref, x0_ref, x1_ref, p0_ref, p1_ref, t0_ref, t1_ref, heads_ref = refs[-9:]
@@ -131,11 +136,9 @@
     keys = hot_ref.shape[0]
     quads = H // QUAD
     block = jnp.concatenate([ref[...] for ref in block_refs], axis=0)
-    for w_ref, dst in ((wk_ref, k_ref), (wv_ref, v_ref)):
-        for n in range(0, WIDE, 256):
-            dst[:, n : n + 256] = jnp.dot(
-                block, w_ref[:, n : n + 256], preferred_element_type=F32
-            ).astype(BF16)
+    sel = sel_ref[...]
+    project(block, w_qk_ref, block.shape[1], sel, k_ref)
+    project(block, w_v_ref, 0, sel, v_ref)
 
     lane_head = lax.broadcasted_iota(jnp.int32, (rows, LANES), 1) // PAD
     ones = jnp.ones((keys, LANES), BF16)
@@ -205,22 +208,22 @@
     lax.fori_loop(0, quads // 2, two, 0)
 
     if last:
-        sel_ref, out_ref = refs
+        out_ref = refs[0]
         for part in range(out_ref.shape[1] // HALF):
             out_ref[:, part * HALF : (part + 1) * HALF] = lax.dot_general(
-                heads_ref[:, part * HALF_PAD : (part + 1) * HALF_PAD], sel_ref[...], NT,
+                heads_ref[:, part * HALF_PAD : (part + 1) * HALF_PAD], sel, NT,
                 preferred_element_type=F32,
             ).astype(BF16)
 
 
-def attend_part(first, last, q, bias, hot, wk, wv, blocks, state, sel, width):
+def attend_part(first, last, q, bias, hot, w_qk, w_v, sel, blocks, state):
     rows = q.shape[0]
     keys = rows * len(blocks)
     if last:
-        outs, extra = [shape(rows, width)], [sel]
+        outs = [shape(*blocks[0].shape)]
     else:
-        outs, extra = [shape(rows, WIDE, dtype=F32)] * 3, []
-    operands = [q, bias, hot, wk, wv, *blocks, *state, *extra]
+        outs = [shape(rows, WIDE, dtype=F32)] * 3
+    operands = [q, bias, hot, w_qk, w_v, sel, *blocks, *state]
     tall = QUAD * rows
     need = 2 * tall * keys * 6 + 4 * keys * WIDE + 2 * tall * LANES * 4
     return pl.pallas_call(
@@ -240,94 +243,107 @@
             pltpu.VMEM((rows, WIDE), BF16),
         ],
         compiler_params=limit(need // MIB + 16),
-        cost_estimate=cost(4 * keys * width * WIDE + 4 * tall * keys * 256 * (H // QUAD), 8_000_000),
+        cost_estimate=cost(0, 0),
         name="part",
     )(*operands)
 
 
 def swap(array, axis, distance):
     return lax.ppermute(array, axis, [(i, i ^ distance) for i in range(lax.axis_size(axis))])
+
+
+def forward(array, axis, pairs):
+    return lax.ppermute(array, axis, [(2 * a + c, 2 * b + c) for a, b in pairs for c in range(2)])
+
+
+def after(value, *others):
+    return lax.optimization_barrier((value, others))[0]
 
 
 def on_device(features, tiles, tile_src, tile_count, node_bucket, w_qk, w_v, bias_table):
     rows, width = features.shape
     groups = lax.axis_size("group")
     seq_count = lax.axis_size("seq")
-    keys = seq_count * rows
+    chips = seq_count // 2
     sel = jnp.asarray(pad_matrix(), BF16)
-    own_bucket = node_bucket.reshape(1, rows)
-
-    blocks = [swap(features, "group", d) for d in range(groups - 1, 0, -1)] + [features]
-    blocks = blocks[::-1]
-    buckets = own_bucket
+    my_group = lax.axis_index("group").reshape(1)
+    my_seq = lax.axis_index("seq").reshape(1)
+
+    received = [swap(features, "group", d) for d in range(groups - 1, 0, -1)][::-1]
+
+    at = jnp.arange(seq_count)[:, None] == my_seq[None, :]
+    buckets = jnp.where(at, node_bucket[None, :], 0)
     step = 1
     while step < seq_count:
-        buckets = jnp.concatenate([buckets, swap(buckets, "seq", step)], axis=0)
+        buckets = buckets + swap(buckets, "seq", step)
         step *= 2
 
     cube = bias_table.reshape(H, NB, NB).transpose(1, 0, 2)
     cube = jnp.concatenate([cube, cube, cube, jnp.zeros((NB, H, LANES - 3 * NB), F32)], axis=2)
     cube = cube.reshape(NB, H * LANES)
-    wq, wk, wv, bias = pl.pallas_call(
-        prepare_kernel,
-        out_shape=[shape(width, WIDE)] * 3 + [shape(rows, H * LANES)],
-        in_specs=[vmem()] * 5,
-        out_specs=[vmem()] * 4,
-        compiler_params=limit(24),
-        cost_estimate=cost(6 * width * width * HALF_PAD, 10_000_000),
-        name="prepare",
-    )(w_qk, w_v, cube, sel, own_bucket)
-
-    chips = seq_count // 2
-    parts = [[0, 1]] + [[d] for d in range(2, chips)]
-    hot = pl.pallas_call(
-        hot_kernel,
-        out_shape=[shape(2 * len(part) * rows, LANES) for part in parts],
-        in_specs=[vmem()],
-        out_specs=[vmem()] * len(parts),
+    bias, own_features, masked, *hot = pl.pallas_call(
+        stage_kernel,
+        out_shape=[shape(rows, H * LANES), shape(rows, width), shape(rows, TILES * rows)]
+        + [shape(2 * rows, LANES)] * chips,
+        in_specs=[smem()] * 2 + [vmem()] * 4,
+        out_specs=[vmem()] * (3 + chips),
         compiler_params=limit(16),
-        cost_estimate=cost(keys * LANES, 300_000),
-        name="hot",
-    )(buckets)
+        cost_estimate=cost(0, 0),
+        name="stage",
+    )(tile_count, my_seq, cube, buckets, features, tiles)
 
     own = pl.pallas_call(
         aggregate_kernel,
         out_shape=shape(rows, width),
-        in_specs=[smem()] * 3 + [vmem()] * (1 + groups) + [pl.BlockSpec(memory_space=pl.ANY)] * 2,
+        in_specs=[smem()] * 2 + [vmem()] * (1 + groups),
         out_specs=vmem(),
         scratch_shapes=[pltpu.VMEM((groups * rows, width), BF16)],
-        compiler_params=limit(24),
+        compiler_params=limit(16),
+        cost_estimate=cost(0, 0),
         name="aggregate",
-    )(tile_src, tile_count, lax.axis_index("group").reshape(1), tiles, *blocks, wv, hot[0])
+    )(tile_src, my_group, masked, own_features, *received)
 
     far = [own] + [None] * (chips - 1)
-    for d in range(1, chips):
-        far[d] = swap(own, "seq", 2 * d)
+    far[1] = swap(own, "seq", 2)
+    if chips == 4:
+        middle = [(1, 2), (2, 1)]
+        outward = [(1, 0), (2, 3)]
+        across = forward(own, "seq", middle)
+    else:
+        for d in range(2, chips):
+            far[d] = swap(own, "seq", 2 * d)
     near = [swap(own, "seq", 1)]
 
     q = pl.pallas_call(
         query_kernel,
         out_shape=shape(rows, WIDE),
-        in_specs=[vmem()] * 2,
+        in_specs=[vmem()] * 3,
         out_specs=vmem(),
         compiler_params=limit(16),
-        cost_estimate=cost(2 * rows * width * WIDE, 2_000_000),
+        cost_estimate=cost(0, 0),
         name="query",
-    )(own, wq)
+    )(own, w_qk, sel)
 
     state = []
-    for number, part in enumerate(parts):
-        blocks = []
-        for d in part:
-            block = far[d]
-            if state:
-                block, state = lax.optimization_barrier((block, state))
-            if d:
-                near.append(swap(block, "seq", 1))
-            blocks += [block, near[d]]
+    for d in range(chips):
+        if chips == 4:
+            chip = my_seq[0] // 2
+            inner = (chip == 1) | (chip == 2)
+            if d == 1:
+                crossed = forward(far[1], "seq", middle)
+                passed = forward(across, "seq", outward)
+            if d == 2:
+                crossed, passed = after((crossed, passed), *state)
+                ended = forward(crossed, "seq", outward)
+                far[2] = jnp.where(inner, crossed, passed)
+            if d == 3:
+                far[3] = jnp.where(inner, across, after(ended, *state))
+        block = far[d]
+        if d:
+            block = after(block, *state)
+            near.append(swap(block, "seq", 1))
         state = attend_part(
-            number == 0, number == len(parts) - 1, q, bias,
-            hot[number], wk, wv, blocks, state, sel, width,
+            d == 0, d == chips - 1, q, bias, hot[d], w_qk, w_v, sel, [block, near[d]], state
         )
     return state[0]
 

time: 60.4 us -> 69.3 us (1.15)
  local copies, waits for them, and re-layouts: 8.19 us -> 16.5 us
  waiting for transfers between devices: 17.7 us -> 9.84 us
  Pallas kernels: 18.5 us -> 22 us
  starting transfers between devices: 12.5 us -> 15.6 us
  other arithmetic: 2.25 us -> 3.53 us
    ppermute x13 -> x11, waiting for transfers between devices: 17.7 us -> 3.17 us  [swap(): lax.ppermute(array, axis, [(i, i ^ distance) for i in range(lax.axis_size...]
    unnamed x24 -> x50, local copies, waits for them, and re-layouts: 7.99 us -> 16.3 us
    ppermute x0 -> x4, waiting for transfers between devices: none -> 6.67 us  [forward(): lax.ppermute(array, axis, [(2 * a + c, 2 * b + c) for a, b in pairs for c...]
    pallas_call x3 -> x4, Pallas kernels: 13.5 us -> 19.1 us  [attend_part(): pl.pallas_call(lambda *refs: part_kernel(first, last, *refs), out_shape=o...]
    ppermute x0 -> x4, starting transfers between devices: none -> 5.24 us  [forward(): lax.ppermute(array, axis, [(2 * a + c, 2 * b + c) for a, b in pairs for c...]
    pallas_call x2 -> x1, Pallas kernels: 3.01 us -> 0.51 us  [on_device(): pl.pallas_call(stage_kernel, out_shape=[shape(rows, H * LANES), shape(row...]
    ppermute x13 -> x11, starting transfers between devices: 12.5 us -> 10.4 us  [swap(): lax.ppermute(array, axis, [(i, i ^ distance) for i in range(lax.axis_size...]
    concatenate x3 -> x0, other arithmetic: 2.05 us -> none  [on_device(): buckets = jnp.concatenate([buckets, swap(buckets, 'seq', step)], axis=0)]
  transfers between devices with their start and end apart: 13 -> 15, of which waited for: 7 -> 4; matrix products, arithmetic and copies ran while one was open for 6% -> 3% of each run, Pallas kernels for 21% -> 22%
where the time goes in v5:
time: 69.3 us; the launch traced here: 68.5 us
  Pallas kernels  22 us (32%)
  local copies, waits for them, and re-layouts  16.5 us (24%)
  starting transfers between devices  15.6 us (23%)
  waiting for transfers between devices  9.84 us (14%)
  other arithmetic  3.53 us (5%)
  between operations  0.93 us (1%)
    pallas_call x4, Pallas kernels, attend_part(): pl.pallas_call(lambda *refs: part_kernel(first, last, *refs), out_shape=o...  19.1 us
    unnamed x50, local copies, waits for them, and re-layouts  16.3 us
    ppermute x11, starting transfers between devices, swap(): lax.ppermute(array, axis, [(i, i ^ distance) for i in range(lax.axis_size...  10.4 us
    ppermute x4, waiting for transfers between devices, forward(): lax.ppermute(array, axis, [(2 * a + c, 2 * b + c) for a, b in pairs for c...  6.67 us
    ppermute x4, starting transfers between devices, forward(): lax.ppermute(array, axis, [(2 * a + c, 2 * b + c) for a, b in pairs for c...  5.24 us
    ppermute x11, waiting for transfers between devices, swap(): lax.ppermute(array, axis, [(i, i ^ distance) for i in range(lax.axis_size...  3.17 us
    pallas_call x1, Pallas kernels, on_device(): pl.pallas_call(aggregate_kernel, out_shape=shape(rows, width), in_specs=[...  1.64 us
    add x3, other arithmetic, on_device(): buckets = buckets + swap(buckets, 'seq', step)  1.46 us
  transfers between devices with their start and end apart: 15, of which 4 were waited for; matrix products, arithmetic and copies ran while one was open for 3% of the time, Pallas kernels for 22%

profile of v5, /device:TPU:0, one launch (start us, length us, event | category | flops | bytes accessed | tf_op | source)
XLA Modules:
  0.0 68.5 jit_solution(474513252375423180)
XLA Ops:
  0.0 0.9 %broadcast_select_fusion.2 = s32[8,128]{1,0:T(8,128)S(1)} fusion(s32[128]{0:T(128)} %param.13, pred[8]{0:T(512)(128)(4,1)S(1)} %iota_compare_fusion), kind=kLoop, calls=%fused_computation.4 | loop fusion | flops 1024 | bytes 4616 | tf_op jit(solution)/shard_map/jit(_where)/select_n | solution.py:275
  0.9 0.5 collective-permute-start
  1.3 0.8 %collective-permute-done = s32[8,128]{1,0:T(8,128)S(1)} collective-permute-done((s32[8,128]{1,0:T(8,128)S(1)}, s32[8,128]{1,0:T(8,128)S(1)}, u32[]{:S(2)}, u32[]{:S(2)}) %collective-permute-start) | collective-permute-done | bytes 4128 | tf_op jit(solution)/shard_map/ppermute | solution.py:252
  2.2 0.7 %fusion = s32[8,128]{1,0:T(8,128)S(1)} fusion(s32[8,128]{1,0:T(8,128)S(1)} %collective-permute-done, s32[128]{0:T(128)} %param.13, pred[8]{0:T(512)(128)(4,1)S(1)} %iota_compare_fusion), kind=kLoop, calls=%fused_computation.5 | loop fusion | flops 2048 | bytes 8712 | tf_op jit(solution)/shard_map/add | solution.py:278
  2.9 2.9 %collective-permute-start.1 = (s32[8,128]{1,0:T(8,128)S(1)}, s32[8,128]{1,0:T(8,128)S(1)}, u32[]{:S(2)}, u32[]{:S(2)}) collective-permute-start(s32[8,128]{1,0:T(8,128)S(1)} %fusion), channel_id=1, source_target_pairs={{0,2},{1,3},{2,0},{3,1},{4,6},{5,7},{6,4},{7,5},{8,10},{9,11},{10,... | collective-permute-start | bytes 12296 | tf_op jit(solution)/shard_map/ppermute | solution.py:252
  5.8 1.5 %collective-permute-start.3 = (bf16[128,768]{1,0:T(8,128)(2,1)}, bf16[128,768]{1,0:T(8,128)(2,1)}, u32[]{:S(2)}, u32[]{:S(2)}) collective-permute-start(bf16[128,768]{1,0:T(8,128)(2,1)} %features_ref.1), channel_id=1, source_target_pairs={{0,8},{8,0},{16,24},{24,16},{1,9},{9,1},{17,25},{25,17},{2,10},{10... | collective-permute-start | bytes 589832 | tf_op jit(solution)/shard_map/ppermute | solution.py:252
  7.3 1.5 %collective-permute-start.4 = (bf16[128,768]{1,0:T(8,128)(2,1)}, bf16[128,768]{1,0:T(8,128)(2,1)}, u32[]{:S(2)}, u32[]{:S(2)}) collective-permute-start(bf16[128,768]{1,0:T(8,128)(2,1)} %features_ref.1), channel_id=1, source_target_pairs={{0,16},{8,24},{16,0},{24,8},{1,17},{9,25},{17,1},{25,9},{2,18},{10... | collective-permute-start | bytes 589832 | tf_op jit(solution)/shard_map/ppermute | solution.py:252
  8.8 0.5 collective-permute-start.5
  9.3 0.9 %copy.11 = f32[32,256]{0,1:T(8,128)S(1)} copy(f32[32,256]{1,0:T(8,128)} %param.16) | data formatting | bytes 65536 | tf_op args[7]
  10.2 0.1 copy.12
  10.3 0.1 pad.3.clone
  10.4 0.7 %fusion.1 = s32[8,128]{1,0:T(8,128)S(1)} fusion(s32[8,128]{1,0:T(8,128)S(1)} %collective-permute-done.1, s32[8,128]{1,0:T(8,128)S(1)} %collective-permute-done, s32[128]{0:T(128)} %param.13, pred[8]{0:T(512)(128)(4,1)S(1)} %iota_compare_fusion), kind=kLoop, calls=%fused_computation.7 | loop fusion | flops 3072 | bytes 12808 | tf_op jit(solution)/shard_map/add | solution.py:278
  11.1 2.6 %collective-permute-start.2 = (s32[8,128]{1,0:T(8,128)S(1)}, s32[8,128]{1,0:T(8,128)S(1)}, u32[]{:S(2)}, u32[]{:S(2)}) collective-permute-start(s32[8,128]{1,0:T(8,128)S(1)} %fusion.1), channel_id=1, source_target_pairs={{0,4},{1,5},{2,6},{3,7},{4,0},{5,1},{6,2},{7,3},{8,12},{9,13},{10,... | collective-permute-start | bytes 12296 | tf_op jit(solution)/shard_map/ppermute | solution.py:252
  13.7 0.2 maximum_maximum_fusion
  13.9 0.2 copy.17
  14.7 0.9 %collective-permute-done.2 = s32[8,128]{1,0:T(8,128)S(1)} collective-permute-done((s32[8,128]{1,0:T(8,128)S(1)}, s32[8,128]{1,0:T(8,128)S(1)}, u32[]{:S(2)}, u32[]{:S(2)}) %collective-permute-start.2) | collective-permute-done | bytes 4128 | tf_op jit(solution)/shard_map/ppermute | solution.py:252
  15.6 0.9 %copy-done.15 = bf16[128,1024]{1,0:T(8,128)(2,1)S(1)} copy-done((bf16[128,1024]{1,0:T(8,128)(2,1)S(1)}, bf16[128,1024]{1,0:T(8,128)(2,1)}, u32[]{:S(2)}) %copy-start.15) | copy-done | bytes 262168
  16.6 0.9 %copy-done.16 = bf16[128,768]{1,0:T(8,128)(2,1)S(1)} copy-done((bf16[128,768]{1,0:T(8,128)(2,1)S(1)}, bf16[128,768]{1,0:T(8,128)(2,1)}, u32[]{:S(2)}) %copy-start.16) | copy-done | bytes 196632
  17.5 0.5 stage.1
  18.0 0.0 copy-start.17
  18.0 0.6 copy-done.17
  18.6 0.6 copy-done.19
  19.3 0.6 copy-done.21
  19.9 0.0 collective-permute-done.4.refs_2_
  19.9 0.0 collective-permute-done.5.refs_3_
  19.9 0.0 copy-start.23
  19.9 0.8 %copy-done.23 = s32[1,8]{1,0:T(1,128)S(1)} copy-done((s32[1,8]{1,0:T(1,128)S(1)}, s32[1,8]{1,0:T(1,128)}, u32[]{:S(2)}) %copy-start.23) | copy-done | bytes 56
  20.7 1.6 %aggregate.1.own_ref.refs_6_ = bf16[128,768]{1,0:T(8,128)(2,1)S(1)} custom-call(s32[1,8]{1,0:T(1,128)S(1)} %copy-done.23, s32[1]{0:T(128)} %bitcast.me_ref, bf16[128,1024]{1,0:T(8,128)(2,1)S(1)} %get-tuple-element.27.masked_ref, bf16[128,768]{1,0:T(8,128)(2,1)S(1)} %get-tuple-element.28.refs_0_, bf16[128,768]{1,0:T(8,128)(2,1)} %collective-permute-done.3.refs_1_, ...), custom_call_target="tpu_custom_call" | custom-call | tf_op jit(solution)/shard_map/aggregate/pallas_call | solution.py:295
  22.4 0.1 collective-permute-start.10
  22.5 0.2 collective-permute-start.7
  22.7 1.3 %collective-permute-start.6 = (bf16[128,768]{1,0:T(8,128)(2,1)S(1)}, bf16[128,768]{1,0:T(8,128)(2,1)}, u32[]{:S(2)}, u32[]{:S(2)}) collective-permute-start(bf16[128,768]{1,0:T(8,128)(2,1)S(1)} %aggregate.1.own_ref.refs_6_), channel_id=1, source_target_pairs={{2,4},{3,5},{4,2},{5,3},{10,12},{11,13},{12,10},{13,11},{18,20},{1... | collective-permute-start | bytes 589832 | tf_op jit(solution)/shard_map/ppermute | solution.py:256
  24.0 1.0 %copy-done.4 = bf16[384,512]{1,0:T(8,128)(2,1)S(1)} copy-done((bf16[384,512]{1,0:T(8,128)(2,1)S(1)}, bf16[384,512]{1,0:T(8,128)(2,1)}, u32[]{:S(2)}) %copy-start.4) | copy-done | bytes 393240
  25.0 0.7 %query.1.refs_0_ = bf16[128,1024]{1,0:T(8,128)(2,1)S(1)} custom-call(bf16[128,768]{1,0:T(8,128)(2,1)S(1)} %aggregate.1.own_ref.refs_6_, bf16[768,1536]{1,0:T(8,128)(2,1)S(1)} %copy-done, bf16[384,512]{1,0:T(8,128)(2,1)S(1)} %copy-done.4), custom_call_target="tpu_custom_call" | custom-call | tf_op jit(solution)/shard_map/query/pallas_call | solution.py:317
  25.7 0.0 collective-permute-done.10.refs_7_
  25.7 0.2 copy-done.5
  26.0 4.1 %part.4 = (f32[128,1024]{1,0:T(8,128)S(1)}, f32[128,1024]{1,0:T(8,128)S(1)}, f32[128,1024]{1,0:T(8,128)S(1)}) custom-call(bf16[128,1024]{1,0:T(8,128)(2,1)S(1)} %query.1.refs_0_, bf16[128,4096]{1,0:T(8,128)(2,1)S(1)} %get-tuple-element.29.refs_1_, bf16[256,128]{1,0:T(8,128)(2,1)S(1)} %get-tuple-element.32.refs_2_, bf16[768,1536]{1,0:T(8,128)(2,1)S(1)} %copy-done, ...), custom_call_target="tpu_custom_call" | custom-call | tf_op jit(solution)/shard_map/part/pallas_call | solution.py:229
  30.2 0.8 %copy-done.9 = f32[128,1024]{1,0:T(8,128)} copy-done((f32[128,1024]{1,0:T(8,128)}, f32[128,1024]{1,0:T(8,128)S(1)}, u32[]{:S(2)}) %copy-start.9) | copy-done | bytes 524312
  30.9 0.8 %copy-done.11 = f32[128,1024]{1,0:T(8,128)} copy-done((f32[128,1024]{1,0:T(8,128)}, f32[128,1024]{1,0:T(8,128)S(1)}, u32[]{:S(2)}) %copy-start.11) | copy-done | bytes 524312
  31.8 0.8 %copy-done.13 = f32[128,1024]{1,0:T(8,128)} copy-done((f32[128,1024]{1,0:T(8,128)}, f32[128,1024]{1,0:T(8,128)S(1)}, u32[]{:S(2)}) %copy-start.13) | copy-done | bytes 524312
  32.5 0.0 collective-permute-done.7.refs_6_
  32.6 0.3 collective-permute-start.11
  32.9 1.4 %collective-permute-start.8 = (bf16[128,768]{1,0:T(8,128)(2,1)}, bf16[128,768]{1,0:T(8,128)(2,1)}, u32[]{:S(2)}, u32[]{:S(2)}) collective-permute-start(bf16[128,768]{1,0:T(8,128)(2,1)} %collective-permute-done.7.refs_6_), channel_id=1, source_target_pairs={{2,4},{3,5},{4,2},{5,3},{10,12},{11,13},{12,10},{13,11},{18,20},{1... | collective-permute-start | bytes 589832 | tf_op jit(solution)/shard_map/ppermute | solution.py:256
  34.2 1.3 %collective-permute-start.9 = (bf16[128,768]{1,0:T(8,128)(2,1)}, bf16[128,768]{1,0:T(8,128)(2,1)}, u32[]{:S(2)}, u32[]{:S(2)}) collective-permute-start(bf16[128,768]{1,0:T(8,128)(2,1)} %collective-permute-done.6), channel_id=1, source_target_pairs={{2,0},{3,1},{4,6},{5,7},{10,8},{11,9},{12,14},{13,15},{18,16},{19,... | collective-permute-start | bytes 589832 | tf_op jit(solution)/shard_map/ppermute | solution.py:256
  35.5 0.0 collective-permute-done.11.refs_7_
  35.6 1.2 %copy-done.3 = bf16[128,4096]{1,0:T(8,128)(2,1)S(1)} copy-done((bf16[128,4096]{1,0:T(8,128)(2,1)S(1)}, bf16[128,4096]{1,0:T(8,128)(2,1)}, u32[]{:S(2)}) %copy-start.3) | copy-done | bytes 1048600
  36.8 1.0 %copy-done.6 = bf16[384,512]{1,0:T(8,128)(2,1)S(1)} copy-done((bf16[384,512]{1,0:T(8,128)(2,1)S(1)}, bf16[384,512]{1,0:T(8,128)(2,1)}, u32[]{:S(2)}) %copy-start.6) | copy-done | bytes 393240
  37.8 0.9 %copy-done.8 = bf16[128,1024]{1,0:T(8,128)(2,1)S(1)} copy-done((bf16[128,1024]{1,0:T(8,128)(2,1)S(1)}, bf16[128,1024]{1,0:T(8,128)(2,1)}, u32[]{:S(2)}) %copy-start.8) | copy-done | bytes 262168
  38.7 1.0 %copy-done.10 = f32[128,1024]{1,0:T(8,128)S(1)} copy-done((f32[128,1024]{1,0:T(8,128)S(1)}, f32[128,1024]{1,0:T(8,128)}, u32[]{:S(2)}) %copy-start.10) | copy-done | bytes 524312
  39.8 1.0 %copy-done.12 = f32[128,1024]{1,0:T(8,128)S(1)} copy-done((f32[128,1024]{1,0:T(8,128)S(1)}, f32[128,1024]{1,0:T(8,128)}, u32[]{:S(2)}) %copy-start.12) | copy-done | bytes 524312
  40.8 1.0 %copy-done.14 = f32[128,1024]{1,0:T(8,128)S(1)} copy-done((f32[128,1024]{1,0:T(8,128)S(1)}, f32[128,1024]{1,0:T(8,128)}, u32[]{:S(2)}) %copy-start.14) | copy-done | bytes 524312
  41.8 0.8 %copy-done.22 = bf16[256,128]{1,0:T(8,128)(2,1)S(1)} copy-done((bf16[256,128]{1,0:T(8,128)(2,1)S(1)}, bf16[256,128]{1,0:T(8,128)(2,1)}, u32[]{:S(2)}) %copy-start.22) | copy-done | bytes 65560
  42.7 5.3 %part.5 = (f32[128,1024]{1,0:T(8,128)S(1)}, f32[128,1024]{1,0:T(8,128)S(1)}, f32[128,1024]{1,0:T(8,128)S(1)}) custom-call(bf16[128,1024]{1,0:T(8,128)(2,1)S(1)} %copy-done.8, bf16[128,4096]{1,0:T(8,128)(2,1)S(1)} %copy-done.3, bf16[256,128]{1,0:T(8,128)(2,1)S(1)} %copy-done.22, bf16[768,1536]{1,0:T(8,128)(2,1)S(1)} %copy-done, ...), custom_call_target="tpu_custom_call" | custom-call | tf_op jit(solution)/shard_map/part/pallas_call | solution.py:229
  48.0 0.0 collective-permute-done.8
  48.0 0.0 collective-permute-done.9
  48.0 1.0 %broadcast_select_fusion.1.refs_6_ = bf16[128,768]{1,0:T(8,128)(2,1)S(1)} fusion(bf16[128,768]{1,0:T(8,128)(2,1)} %collective-permute-done.8, bf16[128,768]{1,0:T(8,128)(2,1)} %collective-permute-done.9, pred[]{:T(512)S(6)} %or.4), kind=kLoop, calls=%fused_computation.3 | loop fusion | flops 98304 | bytes 589825 | tf_op jit(solution)/shard_map/jit(_where)/select_n | solution.py:338
  49.0 0.3 collective-permute-start.13
  49.3 1.3 %collective-permute-start.12 = (bf16[128,768]{1,0:T(8,128)(2,1)}, bf16[128,768]{1,0:T(8,128)(2,1)S(1)}, u32[]{:S(2)}, u32[]{:S(2)}) collective-permute-start(bf16[128,768]{1,0:T(8,128)(2,1)} %collective-permute-done.8), channel_id=1, source_target_pairs={{2,0},{3,1},{4,6},{5,7},{10,8},{11,9},{12,14},{13,15},{18,16},{19,... | collective-permute-start | bytes 589832 | tf_op jit(solution)/shard_map/ppermute | solution.py:256
  50.6 0.0 collective-permute-done.13.refs_7_
  50.6 0.0 copy-start.18
  50.6 4.3 %part.6 = (f32[128,1024]{1,0:T(8,128)S(1)}, f32[128,1024]{1,0:T(8,128)S(1)}, f32[128,1024]{1,0:T(8,128)S(1)}) custom-call(bf16[128,1024]{1,0:T(8,128)(2,1)S(1)} %copy-done.8, bf16[128,4096]{1,0:T(8,128)(2,1)S(1)} %copy-done.3, bf16[256,128]{1,0:T(8,128)(2,1)S(1)} %copy-done.20, bf16[768,1536]{1,0:T(8,128)(2,1)S(1)} %copy-done, ...), custom_call_target="tpu_custom_call" | custom-call | tf_op jit(solution)/shard_map/part/pallas_call | solution.py:229
  54.9 6.7 %collective-permute-done.12 = bf16[128,768]{1,0:T(8,128)(2,1)S(1)} collective-permute-done((bf16[128,768]{1,0:T(8,128)(2,1)}, bf16[128,768]{1,0:T(8,128)(2,1)S(1)}, u32[]{:S(2)}, u32[]{:S(2)}) %collective-permute-start.12) | collective-permute-done | bytes 196640 | tf_op jit(solution)/shard_map/ppermute | solution.py:256
  61.6 0.1 collective-permute-start.14
  61.7 1.4 %collective-permute-done.14.refs_7_ = bf16[128,768]{1,0:T(8,128)(2,1)S(1)} collective-permute-done((bf16[128,768]{1,0:T(8,128)(2,1)S(1)}, bf16[128,768]{1,0:T(8,128)(2,1)S(1)}, u32[]{:S(2)}, u32[]{:S(2)}) %collective-permute-start.14) | collective-permute-done | bytes 196640 | tf_op jit(solution)/shard_map/ppermute | solution.py:252
  63.1 5.4 %part.7 = bf16[128,768]{1,0:T(8,128)(2,1)} custom-call(bf16[128,1024]{1,0:T(8,128)(2,1)S(1)} %copy-done.8, bf16[128,4096]{1,0:T(8,128)(2,1)S(1)} %copy-done.3, bf16[256,128]{1,0:T(8,128)(2,1)S(1)} %copy-done.18, bf16[768,1536]{1,0:T(8,128)(2,1)S(1)} %copy-done, bf16[768,768]{1,0:T(8,128)(2,1)S(1)} %copy-done.1, bf16[384,512]{1,0:T(8,128)(2,1)S(1)} %copy-done.6, ...), custom_call_target="tpu_custom_call" | custom-call | tf_op jit(solution)/shard_map/part/pallas_call | solution.py:229
  (34 shorter events, 0.1 us)
Async XLA Ops:
  0.0 24.0 %copy-start = (bf16[768,1536]{1,0:T(8,128)(2,1)S(1)}, bf16[768,1536]{1,0:T(8,128)(2,1)}, u32[]{:S(2)}) copy-start(bf16[768,1536]{1,0:T(8,128)(2,1)} %refs_3_.7) | copy-start | bytes 7077892
  0.9 1.3 %collective-permute-start = (s32[8,128]{1,0:T(8,128)S(1)}, s32[8,128]{1,0:T(8,128)S(1)}, u32[]{:S(2)}, u32[]{:S(2)}) collective-permute-start(s32[8,128]{1,0:T(8,128)S(1)} %broadcast_select_fusion.2), channel_id=1, source_target_pairs={{0,1},{1,0},{2,3},{3,2},{4,5},{5,4},{6,7},{7,6},{8,9},{9,8},{10,11... | collective-permute-start | bytes 12296 | tf_op jit(solution)/shard_map/ppermute | solution.py:252
  2.9 7.5 %collective-permute-start.1 = (s32[8,128]{1,0:T(8,128)S(1)}, s32[8,128]{1,0:T(8,128)S(1)}, u32[]{:S(2)}, u32[]{:S(2)}) collective-permute-start(s32[8,128]{1,0:T(8,128)S(1)} %fusion), channel_id=1, source_target_pairs={{0,2},{1,3},{2,0},{3,1},{4,6},{5,7},{6,4},{7,5},{8,10},{9,11},{10,... | collective-permute-start | bytes 12296 | tf_op jit(solution)/shard_map/ppermute | solution.py:252
  5.8 14.1 %collective-permute-start.3 = (bf16[128,768]{1,0:T(8,128)(2,1)}, bf16[128,768]{1,0:T(8,128)(2,1)}, u32[]{:S(2)}, u32[]{:S(2)}) collective-permute-start(bf16[128,768]{1,0:T(8,128)(2,1)} %features_ref.1), channel_id=1, source_target_pairs={{0,8},{8,0},{16,24},{24,16},{1,9},{9,1},{17,25},{25,17},{2,10},{10... | collective-permute-start | bytes 589832 | tf_op jit(solution)/shard_map/ppermute | solution.py:252
  7.3 12.6 %collective-permute-start.4 = (bf16[128,768]{1,0:T(8,128)(2,1)}, bf16[128,768]{1,0:T(8,128)(2,1)}, u32[]{:S(2)}, u32[]{:S(2)}) collective-permute-start(bf16[128,768]{1,0:T(8,128)(2,1)} %features_ref.1), channel_id=1, source_target_pairs={{0,16},{8,24},{16,0},{24,8},{1,17},{9,25},{17,1},{25,9},{2,18},{10... | collective-permute-start | bytes 589832 | tf_op jit(solution)/shard_map/ppermute | solution.py:252
  8.8 11.1 %collective-permute-start.5 = (bf16[128,768]{1,0:T(8,128)(2,1)}, bf16[128,768]{1,0:T(8,128)(2,1)}, u32[]{:S(2)}, u32[]{:S(2)}) collective-permute-start(bf16[128,768]{1,0:T(8,128)(2,1)} %features_ref.1), channel_id=1, source_target_pairs={{0,24},{8,16},{16,8},{24,0},{1,25},{9,17},{17,9},{25,1},{2,26},{10... | collective-permute-start | bytes 589832 | tf_op jit(solution)/shard_map/ppermute | solution.py:252
  11.1 4.5 %collective-permute-start.2 = (s32[8,128]{1,0:T(8,128)S(1)}, s32[8,128]{1,0:T(8,128)S(1)}, u32[]{:S(2)}, u32[]{:S(2)}) collective-permute-start(s32[8,128]{1,0:T(8,128)S(1)} %fusion.1), channel_id=1, source_target_pairs={{0,4},{1,5},{2,6},{3,7},{4,0},{5,1},{6,2},{7,3},{8,12},{9,13},{10,... | collective-permute-start | bytes 12296 | tf_op jit(solution)/shard_map/ppermute | solution.py:252
  15.6 1.0 %copy-start.15 = (bf16[128,1024]{1,0:T(8,128)(2,1)S(1)}, bf16[128,1024]{1,0:T(8,128)(2,1)}, u32[]{:S(2)}) copy-start(bf16[128,1024]{1,0:T(8,128)(2,1)} %tiles_ref.1) | copy-start | bytes 786436
  16.6 0.9 %copy-start.16 = (bf16[128,768]{1,0:T(8,128)(2,1)S(1)}, bf16[128,768]{1,0:T(8,128)(2,1)}, u32[]{:S(2)}) copy-start(bf16[128,768]{1,0:T(8,128)(2,1)} %features_ref.1) | copy-start | bytes 589828
  18.0 0.6 copy-start.17
  18.6 0.6 copy-start.19
  19.3 0.6 copy-start.21
  19.9 10.2 %copy-start.2 = (bf16[128,4096]{1,0:T(8,128)(2,1)}, bf16[128,4096]{1,0:T(8,128)(2,1)S(1)}, u32[]{:S(2)}) copy-start(bf16[128,4096]{1,0:T(8,128)(2,1)S(1)} %get-tuple-element.29.refs_1_) | copy-start | bytes 3145732
  19.9 5.8 %copy-start.1 = (bf16[768,768]{1,0:T(8,128)(2,1)S(1)}, bf16[768,768]{1,0:T(8,128)(2,1)}, u32[]{:S(2)}) copy-start(bf16[768,768]{1,0:T(8,128)(2,1)} %refs_4_.7) | copy-start | bytes 3538948
  19.9 0.8 %copy-start.23 = (s32[1,8]{1,0:T(1,128)S(1)}, s32[1,8]{1,0:T(1,128)}, u32[]{:S(2)}) copy-start(s32[1,8]{1,0:T(1,128)} %src_ref.1) | copy-start | bytes 100
  22.4 3.3 %collective-permute-start.10 = (bf16[128,768]{1,0:T(8,128)(2,1)S(1)}, bf16[128,768]{1,0:T(8,128)(2,1)S(1)}, u32[]{:S(2)}, u32[]{:S(2)}) collective-permute-start(bf16[128,768]{1,0:T(8,128)(2,1)S(1)} %aggregate.1.own_ref.refs_6_), channel_id=1, source_target_pairs={{0,1},{1,0},{2,3},{3,2},{4,5},{5,4},{6,7},{7,6},{8,9},{9,8},{10,11... | collective-permute-start | bytes 589832 | tf_op jit(solution)/shard_map/ppermute | solution.py:252
  22.5 10.1 %collective-permute-start.7 = (bf16[128,768]{1,0:T(8,128)(2,1)S(1)}, bf16[128,768]{1,0:T(8,128)(2,1)}, u32[]{:S(2)}, u32[]{:S(2)}) collective-permute-start(bf16[128,768]{1,0:T(8,128)(2,1)S(1)} %aggregate.1.own_ref.refs_6_), channel_id=1, source_target_pairs={{0,2},{1,3},{2,0},{3,1},{4,6},{5,7},{6,4},{7,5},{8,10},{9,11},{10,... | collective-permute-start | bytes 589832 | tf_op jit(solution)/shard_map/ppermute | solution.py:252
  22.7 11.6 %collective-permute-start.6 = (bf16[128,768]{1,0:T(8,128)(2,1)S(1)}, bf16[128,768]{1,0:T(8,128)(2,1)}, u32[]{:S(2)}, u32[]{:S(2)}) collective-permute-start(bf16[128,768]{1,0:T(8,128)(2,1)S(1)} %aggregate.1.own_ref.refs_6_), channel_id=1, source_target_pairs={{2,4},{3,5},{4,2},{5,3},{10,12},{11,13},{12,10},{13,11},{18,20},{1... | collective-permute-start | bytes 589832 | tf_op jit(solution)/shard_map/ppermute | solution.py:256
  24.0 1.0 %copy-start.4 = (bf16[384,512]{1,0:T(8,128)(2,1)S(1)}, bf16[384,512]{1,0:T(8,128)(2,1)}, u32[]{:S(2)}) copy-start(bf16[384,512]{1,0:T(8,128)(2,1)} %constant.31.clone.sel_ref.refs_5_) | copy-start | bytes 1179652
  25.0 1.0 %copy-start.5 = (bf16[384,512]{1,0:T(8,128)(2,1)S(1)}, bf16[384,512]{1,0:T(8,128)(2,1)}, u32[]{:S(2)}) copy-start(bf16[384,512]{1,0:T(8,128)(2,1)} %constant.31.clone.sel_ref.refs_5_) | copy-start | bytes 1179652
  25.7 4.4 %copy-start.7 = (bf16[128,1024]{1,0:T(8,128)(2,1)}, bf16[128,1024]{1,0:T(8,128)(2,1)S(1)}, u32[]{:S(2)}) copy-start(bf16[128,1024]{1,0:T(8,128)(2,1)S(1)} %query.1.refs_0_) | copy-start | bytes 786436
  30.1 0.8 %copy-start.9 = (f32[128,1024]{1,0:T(8,128)}, f32[128,1024]{1,0:T(8,128)S(1)}, u32[]{:S(2)}) copy-start(f32[128,1024]{1,0:T(8,128)S(1)} %get-tuple-element.33.refs_8_) | copy-start | bytes 1572868
  30.9 0.8 %copy-start.11 = (f32[128,1024]{1,0:T(8,128)}, f32[128,1024]{1,0:T(8,128)S(1)}, u32[]{:S(2)}) copy-start(f32[128,1024]{1,0:T(8,128)S(1)} %get-tuple-element.34.refs_9_) | copy-start | bytes 1572868
  31.7 0.8 %copy-start.13 = (f32[128,1024]{1,0:T(8,128)}, f32[128,1024]{1,0:T(8,128)S(1)}, u32[]{:S(2)}) copy-start(f32[128,1024]{1,0:T(8,128)S(1)} %get-tuple-element.35.refs_10_) | copy-start | bytes 1572868
  32.6 3.0 %collective-permute-start.11 = (bf16[128,768]{1,0:T(8,128)(2,1)}, bf16[128,768]{1,0:T(8,128)(2,1)}, u32[]{:S(2)}, u32[]{:S(2)}) collective-permute-start(bf16[128,768]{1,0:T(8,128)(2,1)} %collective-permute-done.7.refs_6_), channel_id=1, source_target_pairs={{0,1},{1,0},{2,3},{3,2},{4,5},{5,4},{6,7},{7,6},{8,9},{9,8},{10,11... | collective-permute-start | bytes 589832 | tf_op jit(solution)/shard_map/ppermute | solution.py:252
  32.9 15.2 %collective-permute-start.8 = (bf16[128,768]{1,0:T(8,128)(2,1)}, bf16[128,768]{1,0:T(8,128)(2,1)}, u32[]{:S(2)}, u32[]{:S(2)}) collective-permute-start(bf16[128,768]{1,0:T(8,128)(2,1)} %collective-permute-done.7.refs_6_), channel_id=1, source_target_pairs={{2,4},{3,5},{4,2},{5,3},{10,12},{11,13},{12,10},{13,11},{18,20},{1... | collective-permute-start | bytes 589832 | tf_op jit(solution)/shard_map/ppermute | solution.py:256
  34.2 13.8 %collective-permute-start.9 = (bf16[128,768]{1,0:T(8,128)(2,1)}, bf16[128,768]{1,0:T(8,128)(2,1)}, u32[]{:S(2)}, u32[]{:S(2)}) collective-permute-start(bf16[128,768]{1,0:T(8,128)(2,1)} %collective-permute-done.6), channel_id=1, source_target_pairs={{2,0},{3,1},{4,6},{5,7},{10,8},{11,9},{12,14},{13,15},{18,16},{19,... | collective-permute-start | bytes 589832 | tf_op jit(solution)/shard_map/ppermute | solution.py:256
  35.5 1.2 %copy-start.3 = (bf16[128,4096]{1,0:T(8,128)(2,1)S(1)}, bf16[128,4096]{1,0:T(8,128)(2,1)}, u32[]{:S(2)}) copy-start(bf16[128,4096]{1,0:T(8,128)(2,1)} %copy-done.2) | copy-start | bytes 3145732
  36.8 1.0 %copy-start.6 = (bf16[384,512]{1,0:T(8,128)(2,1)S(1)}, bf16[384,512]{1,0:T(8,128)(2,1)}, u32[]{:S(2)}) copy-start(bf16[384,512]{1,0:T(8,128)(2,1)} %constant.31.clone.sel_ref.refs_5_) | copy-start | bytes 1179652
  37.8 0.9 %copy-start.8 = (bf16[128,1024]{1,0:T(8,128)(2,1)S(1)}, bf16[128,1024]{1,0:T(8,128)(2,1)}, u32[]{:S(2)}) copy-start(bf16[128,1024]{1,0:T(8,128)(2,1)} %copy-done.7) | copy-start | bytes 786436
  38.7 1.0 %copy-start.10 = (f32[128,1024]{1,0:T(8,128)S(1)}, f32[128,1024]{1,0:T(8,128)}, u32[]{:S(2)}) copy-start(f32[128,1024]{1,0:T(8,128)} %copy-done.9) | copy-start | bytes 1572868
  39.8 1.0 %copy-start.12 = (f32[128,1024]{1,0:T(8,128)S(1)}, f32[128,1024]{1,0:T(8,128)}, u32[]{:S(2)}) copy-start(f32[128,1024]{1,0:T(8,128)} %copy-done.11) | copy-start | bytes 1572868
  40.8 1.0 %copy-start.14 = (f32[128,1024]{1,0:T(8,128)S(1)}, f32[128,1024]{1,0:T(8,128)}, u32[]{:S(2)}) copy-start(f32[128,1024]{1,0:T(8,128)} %copy-done.13) | copy-start | bytes 1572868
  41.8 0.8 %copy-start.22 = (bf16[256,128]{1,0:T(8,128)(2,1)S(1)}, bf16[256,128]{1,0:T(8,128)(2,1)}, u32[]{:S(2)}) copy-start(bf16[256,128]{1,0:T(8,128)(2,1)} %copy-done.21) | copy-start | bytes 196612
  42.7 7.9 %copy-start.20 = (bf16[256,128]{1,0:T(8,128)(2,1)S(1)}, bf16[256,128]{1,0:T(8,128)(2,1)}, u32[]{:S(2)}) copy-start(bf16[256,128]{1,0:T(8,128)(2,1)} %copy-done.19) | copy-start | bytes 196612
  49.0 1.6 %collective-permute-start.13 = (bf16[128,768]{1,0:T(8,128)(2,1)S(1)}, bf16[128,768]{1,0:T(8,128)(2,1)S(1)}, u32[]{:S(2)}, u32[]{:S(2)}) collective-permute-start(bf16[128,768]{1,0:T(8,128)(2,1)S(1)} %broadcast_select_fusion.1.refs_6_), channel_id=1, source_target_pairs={{0,1},{1,0},{2,3},{3,2},{4,5},{5,4},{6,7},{7,6},{8,9},{9,8},{10,11... | collective-permute-start | bytes 589832 | tf_op jit(solution)/shard_map/ppermute | solution.py:252
  49.3 12.3 %collective-permute-start.12 = (bf16[128,768]{1,0:T(8,128)(2,1)}, bf16[128,768]{1,0:T(8,128)(2,1)S(1)}, u32[]{:S(2)}, u32[]{:S(2)}) collective-permute-start(bf16[128,768]{1,0:T(8,128)(2,1)} %collective-permute-done.8), channel_id=1, source_target_pairs={{2,0},{3,1},{4,6},{5,7},{10,8},{11,9},{12,14},{13,15},{18,16},{19,... | collective-permute-start | bytes 589832 | tf_op jit(solution)/shard_map/ppermute | solution.py:256
  50.6 12.5 %copy-start.18 = (bf16[256,128]{1,0:T(8,128)(2,1)S(1)}, bf16[256,128]{1,0:T(8,128)(2,1)}, u32[]{:S(2)}) copy-start(bf16[256,128]{1,0:T(8,128)(2,1)} %copy-done.17) | copy-start | bytes 196612
  61.6 1.5 %collective-permute-start.14 = (bf16[128,768]{1,0:T(8,128)(2,1)S(1)}, bf16[128,768]{1,0:T(8,128)(2,1)S(1)}, u32[]{:S(2)}, u32[]{:S(2)}) collective-permute-start(bf16[128,768]{1,0:T(8,128)(2,1)S(1)} %broadcast_select_fusion.refs_6_), channel_id=1, source_target_pairs={{0,1},{1,0},{2,3},{3,2},{4,5},{5,4},{6,7},{7,6},{8,9},{9,8},{10,11... | collective-permute-start | bytes 589832 | tf_op jit(solution)/shard_map/ppermute | solution.py:252

commit v6 on v5

--- a/solution.py
+++ b/solution.py
@@ -2,7 +2,6 @@
 
 import jax
 import jax.numpy as jnp
-import numpy as np
 from jax import lax
 from jax.experimental import pallas as pl
 from jax.experimental.pallas import tpu as pltpu
@@ -18,6 +17,7 @@
 WIDE = H * PAD
 HALF = 16 * HD
 HALF_PAD = 16 * PAD
+EXTRA = 8
 NT = (((1,), (1,)), ((), ()))
 MIB = 1024 * 1024
 BF16 = jnp.bfloat16
@@ -41,43 +41,36 @@
     return jax.ShapeDtypeStruct(dims, dtype)
 
 
-def cost(flops, nbytes):
-    return pl.CostEstimate(flops=int(flops), bytes_accessed=int(nbytes), transcendentals=0)
-
-
-def pad_matrix():
-    rows = np.arange(HALF)
-    cols = (rows // HD) * PAD + rows % HD
-    sel = np.zeros((HALF, HALF_PAD), np.float32)
-    sel[rows, cols] = 1.0
-    return sel
-
-
 def one_hot_slab(bucket_row):
     n = bucket_row.shape[1]
     index = lax.broadcasted_iota(jnp.int32, (LANES, n), 0)
-    wanted = jnp.where(index < 3 * NB, index % NB, -1)
+    wanted = jnp.where(index < 3 * NB, index % NB, -1).astype(F32)
     hot = jnp.where(wanted == bucket_row, 1.0, 0.0)
     return hot.T.astype(BF16)
 
 
 def stage_kernel(
-    count_ref, me_ref, cube_ref, bucket_ref, features_ref, tiles_ref, *refs
+    count_ref, me_ref, src_ref, cube_ref, bucket_ref, features_ref, tiles_ref,
+    bias_ref, own_ref, masked_ref, sel_ref, extra_ref, from_ref, tiles_held, sems,
 ):
-    bias_ref, own_ref, masked_ref, hot_refs = refs[0], refs[1], refs[2], refs[3:]
-    rows = features_ref.shape[0]
-    me = me_ref[0]
-    own_ref[...] = features_ref[...]
+    rows = own_ref.shape[0]
+    copies = [
+        pltpu.make_async_copy(tiles_ref, tiles_held, sems.at[0]),
+        pltpu.make_async_copy(features_ref, own_ref, sems.at[1]),
+    ]
+    for copy in copies:
+        copy.start()
     for t in range(TILES):
-        tile = tiles_ref[:, t * rows : (t + 1) * rows]
-        masked_ref[:, t * rows : (t + 1) * rows] = jnp.where(
-            t < count_ref[0], tile, jnp.zeros_like(tile)
-        )
-    s = 0
-    for hot_ref in hot_refs:
-        for at in range(0, hot_ref.shape[0], rows):
-            hot_ref[at : at + rows, :] = one_hot_slab(bucket_ref[pl.ds(me ^ s, 1), :])
-            s += 1
+        from_ref[t : t + 1, :] = jnp.full((1, LANES), src_ref[0, t] ^ me_ref[0], jnp.int32)
+    width = own_ref.shape[1]
+    extra = jnp.concatenate(
+        [bucket_ref[...].astype(F32), jnp.zeros((1, width - rows), F32)], axis=1
+    )
+    extra_ref[...] = jnp.broadcast_to(extra, (EXTRA, width))
+    take = lax.broadcasted_iota(jnp.int32, sel_ref.shape, 0)
+    column = lax.broadcasted_iota(jnp.int32, sel_ref.shape, 1)
+    wanted = jnp.where(column % PAD < HD, column // PAD * HD + column % PAD, -1)
+    sel_ref[...] = jnp.where(take == wanted, 1.0, 0.0).astype(BF16)
     scaled = cube_ref[...] * math.sqrt(HD)
     high = scaled.astype(BF16).astype(F32)
     rest = scaled - high
@@ -87,25 +80,33 @@
     parts = jnp.where(
         lane < NB, high, jnp.where(lane < 2 * NB, mid, jnp.where(lane < 3 * NB, low, 0.0))
     )
-    hot = one_hot_slab(bucket_ref[pl.ds(me, 1), :])[:, :NB]
+    hot = one_hot_slab(bucket_ref[...].astype(F32))[:, :NB]
     bias_ref[...] = jnp.dot(hot, parts.astype(BF16), preferred_element_type=F32).astype(BF16)
-
-
-def aggregate_kernel(src_ref, me_ref, masked_ref, *refs):
+    for copy in copies:
+        copy.wait()
+    for t in range(TILES):
+        tile = tiles_held[:, t * rows : (t + 1) * rows]
+        masked_ref[:, t * rows : (t + 1) * rows] = jnp.where(
+            t < count_ref[0], tile, jnp.zeros_like(tile)
+        )
+
+
+def aggregate_kernel(from_ref, extra_ref, masked_ref, *refs):
     feature_refs, out_ref, held = refs[:-2], refs[-2], refs[-1]
-    rows = out_ref.shape[0]
+    rows = feature_refs[0].shape[0]
     for d, ref in enumerate(feature_refs):
         held[d * rows : (d + 1) * rows, :] = ref[...]
-    me = me_ref[0]
     picked = []
     for t in range(TILES):
-        start = pl.multiple_of((src_ref[0, t] ^ me) * rows, rows)
+        start = pl.multiple_of(from_ref[t, 0] * rows, rows)
         picked.append(held[pl.ds(start, rows), :])
     total = feature_refs[0][...].astype(F32) + jnp.dot(
         masked_ref[...], jnp.concatenate(picked, axis=0), preferred_element_type=F32
     )
     mean_square = jnp.mean(total * total, axis=-1, keepdims=True)
-    out_ref[...] = (total * lax.rsqrt(mean_square + 1e-06)).astype(BF16)
+    out_ref[...] = jnp.concatenate(
+        [total * lax.rsqrt(mean_square + 1e-06), extra_ref[...]], axis=0
+    ).astype(BF16)
 
 
 def project(block, w_ref, base, sel, dst):
@@ -121,21 +122,24 @@
 
 
 def query_kernel(own_ref, w_qk_ref, sel_ref, q_ref):
-    project(own_ref[...], w_qk_ref, 0, sel_ref[...], q_ref)
-
-
-def part_kernel(first, last, q_ref, bias_ref, hot_ref, w_qk_ref, w_v_ref, sel_ref, *refs):
-    count = hot_ref.shape[0] // q_ref.shape[0]
+    project(own_ref[...][: q_ref.shape[0], :], w_qk_ref, 0, sel_ref[...], q_ref)
+
+
+def part_kernel(count, first, last, q_ref, bias_ref, w_qk_ref, w_v_ref, sel_ref, *refs):
     block_refs, refs = refs[:count], refs[count:]
-    k_ref, v_ref, x0_ref, x1_ref, p0_ref, p1_ref, t0_ref, t1_ref, heads_ref = refs[-9:]
-    refs = refs[:-9]
+    hot_ref, k_ref, v_ref, x0_ref, x1_ref, p0_ref, p1_ref, t0_ref, t1_ref, heads_ref = refs[-10:]
+    refs = refs[:-10]
     old_refs = ()
     if not first:
         old_refs, refs = refs[:3], refs[3:]
     rows = q_ref.shape[0]
     keys = hot_ref.shape[0]
     quads = H // QUAD
-    block = jnp.concatenate([ref[...] for ref in block_refs], axis=0)
+    arrived = [ref[...] for ref in block_refs]
+    for s, item in enumerate(arrived):
+        bucket = item[rows:, :rows].astype(F32)[:1, :]
+        hot_ref[s * rows : (s + 1) * rows, :] = one_hot_slab(bucket)
+    block = jnp.concatenate([item[:rows, :] for item in arrived], axis=0)
     sel = sel_ref[...]
     project(block, w_qk_ref, block.shape[1], sel, k_ref)
     project(block, w_v_ref, 0, sel, v_ref)
@@ -216,22 +220,23 @@
             ).astype(BF16)
 
 
-def attend_part(first, last, q, bias, hot, w_qk, w_v, sel, blocks, state):
+def attend_part(first, last, q, bias, w_qk, w_v, sel, blocks, state):
     rows = q.shape[0]
     keys = rows * len(blocks)
     if last:
-        outs = [shape(*blocks[0].shape)]
+        outs = [shape(rows, blocks[0].shape[1])]
     else:
         outs = [shape(rows, WIDE, dtype=F32)] * 3
-    operands = [q, bias, hot, w_qk, w_v, sel, *blocks, *state]
+    operands = [q, bias, w_qk, w_v, sel, *blocks, *state]
     tall = QUAD * rows
     need = 2 * tall * keys * 6 + 4 * keys * WIDE + 2 * tall * LANES * 4
     return pl.pallas_call(
-        lambda *refs: part_kernel(first, last, *refs),
+        lambda *refs: part_kernel(len(blocks), first, last, *refs),
         out_shape=outs,
         in_specs=[vmem()] * len(operands),
         out_specs=[vmem()] * len(outs),
         scratch_shapes=[
+            pltpu.VMEM((keys, LANES), BF16),
             pltpu.VMEM((keys, WIDE), BF16),
             pltpu.VMEM((keys, WIDE), BF16),
             pltpu.VMEM((tall, keys), F32),
@@ -243,17 +248,13 @@
             pltpu.VMEM((rows, WIDE), BF16),
         ],
         compiler_params=limit(need // MIB + 16),
-        cost_estimate=cost(0, 0),
+        cost_estimate=pl.CostEstimate(flops=1000, bytes_accessed=1000, transcendentals=0),
         name="part",
     )(*operands)
 
 
 def swap(array, axis, distance):
     return lax.ppermute(array, axis, [(i, i ^ distance) for i in range(lax.axis_size(axis))])
-
-
-def forward(array, axis, pairs):
-    return lax.ppermute(array, axis, [(2 * a + c, 2 * b + c) for a, b in pairs for c in range(2)])
 
 
 def after(value, *others):
@@ -265,85 +266,77 @@
     groups = lax.axis_size("group")
     seq_count = lax.axis_size("seq")
     chips = seq_count // 2
-    sel = jnp.asarray(pad_matrix(), BF16)
-    my_group = lax.axis_index("group").reshape(1)
-    my_seq = lax.axis_index("seq").reshape(1)
+    any_space = pl.BlockSpec(memory_space=pl.ANY)
 
     received = [swap(features, "group", d) for d in range(groups - 1, 0, -1)][::-1]
-
-    at = jnp.arange(seq_count)[:, None] == my_seq[None, :]
-    buckets = jnp.where(at, node_bucket[None, :], 0)
-    step = 1
-    while step < seq_count:
-        buckets = buckets + swap(buckets, "seq", step)
-        step *= 2
+    own_bucket = node_bucket.reshape(1, rows)
 
     cube = bias_table.reshape(H, NB, NB).transpose(1, 0, 2)
     cube = jnp.concatenate([cube, cube, cube, jnp.zeros((NB, H, LANES - 3 * NB), F32)], axis=2)
     cube = cube.reshape(NB, H * LANES)
-    bias, own_features, masked, *hot = pl.pallas_call(
+    bias, own_features, masked, sel, extra, source = pl.pallas_call(
         stage_kernel,
-        out_shape=[shape(rows, H * LANES), shape(rows, width), shape(rows, TILES * rows)]
-        + [shape(2 * rows, LANES)] * chips,
-        in_specs=[smem()] * 2 + [vmem()] * 4,
-        out_specs=[vmem()] * (3 + chips),
+        out_shape=[
+            shape(rows, H * LANES), shape(rows, width), shape(rows, TILES * rows),
+            shape(HALF, HALF_PAD), shape(EXTRA, width, dtype=F32),
+            shape(TILES, LANES, dtype=jnp.int32),
+        ],
+        in_specs=[smem()] * 3 + [vmem(), vmem(), any_space, any_space],
+        out_specs=[vmem()] * 6,
+        scratch_shapes=[pltpu.VMEM((rows, TILES * rows), BF16), pltpu.SemaphoreType.DMA((2,))],
         compiler_params=limit(16),
-        cost_estimate=cost(0, 0),
+        cost_estimate=pl.CostEstimate(flops=1000, bytes_accessed=1000, transcendentals=0),
         name="stage",
-    )(tile_count, my_seq, cube, buckets, features, tiles)
+    )(tile_count, lax.axis_index("group").reshape(1), tile_src, cube, own_bucket, features, tiles)
 
     own = pl.pallas_call(
         aggregate_kernel,
-        out_shape=shape(rows, width),
-        in_specs=[smem()] * 2 + [vmem()] * (1 + groups),
+        out_shape=shape(rows + EXTRA, width),
+        in_specs=[vmem()] * (3 + groups),
         out_specs=vmem(),
         scratch_shapes=[pltpu.VMEM((groups * rows, width), BF16)],
         compiler_params=limit(16),
-        cost_estimate=cost(0, 0),
+        cost_estimate=pl.CostEstimate(flops=1000, bytes_accessed=1000, transcendentals=0),
         name="aggregate",
-    )(tile_src, my_group, masked, own_features, *received)
+    )(source, extra, masked, own_features, *received)
 
     far = [own] + [None] * (chips - 1)
-    far[1] = swap(own, "seq", 2)
-    if chips == 4:
-        middle = [(1, 2), (2, 1)]
-        outward = [(1, 0), (2, 3)]
-        across = forward(own, "seq", middle)
-    else:
-        for d in range(2, chips):
-            far[d] = swap(own, "seq", 2 * d)
-    near = [swap(own, "seq", 1)]
-
+    top = 1
+    while 2 * top < chips:
+        top *= 2
+    far[top] = swap(own, "seq", 2 * top)
+    step = 1
+    while step < top:
+        far[step] = swap(own, "seq", 2 * step)
+        step *= 2
+    for d in range(3, chips):
+        if far[d] is None:
+            far[d] = swap(far[d & (d - 1)], "seq", 2 * (d & -d))
     q = pl.pallas_call(
         query_kernel,
         out_shape=shape(rows, WIDE),
         in_specs=[vmem()] * 3,
         out_specs=vmem(),
         compiler_params=limit(16),
-        cost_estimate=cost(0, 0),
+        cost_estimate=pl.CostEstimate(flops=1000, bytes_accessed=1000, transcendentals=0),
         name="query",
     )(own, w_qk, sel)
 
+    parts = [[0], [1, top]] if top > 1 else [[0, 1]]
+    parts += [[d] for d in range(2, chips) if d != top]
     state = []
-    for d in range(chips):
-        if chips == 4:
-            chip = my_seq[0] // 2
-            inner = (chip == 1) | (chip == 2)
-            if d == 1:
-                crossed = forward(far[1], "seq", middle)
-                passed = forward(across, "seq", outward)
-            if d == 2:
-                crossed, passed = after((crossed, passed), *state)
-                ended = forward(crossed, "seq", outward)
-                far[2] = jnp.where(inner, crossed, passed)
-            if d == 3:
-                far[3] = jnp.where(inner, across, after(ended, *state))
-        block = far[d]
-        if d:
-            block = after(block, *state)
-            near.append(swap(block, "seq", 1))
+    for number, part in enumerate(parts):
+        blocks = []
+        for d in part:
+            block = far[d]
+            if d:
+                block = after(block, *state)
+                near = swap(block, "seq", 1)
+            else:
+                near = swap(own, "seq", 1)
+            blocks += [block, near]
         state = attend_part(
-            d == 0, d == chips - 1, q, bias, hot[d], w_qk, w_v, sel, [block, near[d]], state
+            number == 0, number == len(parts) - 1, q, bias, w_qk, w_v, sel, blocks, state
         )
     return state[0]
 

time: 69.3 us -> 43.2 us (0.62)
  local copies, waits for them, and re-layouts: 16.5 us -> 4.4 us
  starting transfers between devices: 15.6 us -> 10.5 us
  other arithmetic: 3.53 us -> 0.2 us
  Pallas kernels: 22 us -> 19.1 us
  waiting for transfers between devices: 9.84 us -> 7.94 us
    unnamed x50 -> x14, local copies, waits for them, and re-layouts: 16.3 us -> 4.2 us
    ppermute x4 -> x0, waiting for transfers between devices: 6.67 us -> none  [forward(): lax.ppermute(array, axis, [(2 * a + c, 2 * b + c) for a, b in pairs for c...]
    ppermute x4 -> x0, starting transfers between devices: 5.24 us -> none  [forward(): lax.ppermute(array, axis, [(2 * a + c, 2 * b + c) for a, b in pairs for c...]
    ppermute x11 -> x10, waiting for transfers between devices: 3.17 us -> 7.94 us  [swap(): lax.ppermute(array, axis, [(i, i ^ distance) for i in range(lax.axis_size...]
    pallas_call x5 -> x4, Pallas kernels: 20.8 us -> 16.9 us  [the longest x3 16.3 us: attend_part(): pl.pallas_call(lambda *refs: part_kernel(len(blocks), first, last, *refs)...]
    select_n x3 -> x0, other arithmetic: 1.87 us -> none  [the longest x1 0.97 us: on_device(): far[2] = jnp.where(inner, crossed, passed)]
    add x3 -> x0, other arithmetic: 1.46 us -> none  [on_device(): buckets = buckets + swap(buckets, 'seq', step)]
    pallas_call x1, Pallas kernels: 0.51 us -> 1.49 us  [on_device(): pl.pallas_call(stage_kernel, out_shape=[shape(rows, H * LANES), shape(row...]
  transfers between devices with their start and end apart: 15 -> 10, of which waited for: 4 -> 5; matrix products, arithmetic and copies ran while one was open for 3% -> 3% of each run, Pallas kernels for 22% -> 31%
where the time goes in v6:
time: 43.2 us; the launch traced here: 42.9 us
  Pallas kernels  19.1 us (44%)
  starting transfers between devices  10.5 us (24%)
  waiting for transfers between devices  7.94 us (18%)
  local copies, waits for them, and re-layouts  4.4 us (10%)
  between operations  0.79 us (2%)
    pallas_call x3, Pallas kernels, attend_part(): pl.pallas_call(lambda *refs: part_kernel(len(blocks), first, last, *refs)...  16.3 us
    ppermute x10, starting transfers between devices, swap(): lax.ppermute(array, axis, [(i, i ^ distance) for i in range(lax.axis_size...  10.5 us
    ppermute x10, waiting for transfers between devices, swap(): lax.ppermute(array, axis, [(i, i ^ distance) for i in range(lax.axis_size...  7.94 us
    unnamed x14, local copies, waits for them, and re-layouts  4.2 us
    pallas_call x1, Pallas kernels, on_device(): pl.pallas_call(stage_kernel, out_shape=[shape(rows, H * LANES), shape(row...  1.49 us
  transfers between devices with their start and end apart: 10, of which 5 were waited for; matrix products, arithmetic and copies ran while one was open for 3% of the time, Pallas kernels for 31%

profile of v6, /device:TPU:0, one launch (start us, length us, event | category | flops | bytes accessed | tf_op | source)
XLA Modules:
  0.0 42.9 jit_solution(2970752982139306876)
XLA Ops:
  0.0 0.0 copy-start
  0.0 2.9 %collective-permute-start = (bf16[128,768]{1,0:T(8,128)(2,1)}, bf16[128,768]{1,0:T(8,128)(2,1)S(1)}, u32[]{:S(2)}, u32[]{:S(2)}) collective-permute-start(bf16[128,768]{1,0:T(8,128)(2,1)} %features_ref.1), channel_id=1, source_target_pairs={{0,8},{8,0},{16,24},{24,16},{1,9},{9,1},{17,25},{25,17},{2,10},{10... | collective-permute-start | bytes 589832 | tf_op jit(solution)/shard_map/ppermute | solution.py:257
  2.9 1.5 %collective-permute-start.1 = (bf16[128,768]{1,0:T(8,128)(2,1)}, bf16[128,768]{1,0:T(8,128)(2,1)S(1)}, u32[]{:S(2)}, u32[]{:S(2)}) collective-permute-start(bf16[128,768]{1,0:T(8,128)(2,1)} %features_ref.1), channel_id=1, source_target_pairs={{0,16},{8,24},{16,0},{24,8},{1,17},{9,25},{17,1},{25,9},{2,18},{10... | collective-permute-start | bytes 589832 | tf_op jit(solution)/shard_map/ppermute | solution.py:257
  4.5 0.0 collective-permute-start.2
  4.5 0.9 %copy.10 = f32[32,256]{0,1:T(8,128)S(1)} copy(f32[32,256]{1,0:T(8,128)} %param.15) | data formatting | bytes 65536 | tf_op args[7]
  5.3 0.1 copy.11
  5.5 0.1 pad.3.clone
  5.5 0.2 maximum_maximum_fusion
  5.7 0.2 copy.16
  6.6 0.0 copy-start.2
  6.6 0.9 %copy-done.2 = bf16[128,1024]{1,0:T(8,128)(2,1)S(1)} copy-done((bf16[128,1024]{1,0:T(8,128)(2,1)S(1)}, bf16[128,1024]{1,0:T(8,128)(2,1)}, u32[]{:S(2)}) %copy-start.2) | copy-done | bytes 262168
  7.5 0.0 copy-start.3
  7.5 0.9 %copy-done.3 = bf16[128,768]{1,0:T(8,128)(2,1)S(1)} copy-done((bf16[128,768]{1,0:T(8,128)(2,1)S(1)}, bf16[128,768]{1,0:T(8,128)(2,1)}, u32[]{:S(2)}) %copy-start.3) | copy-done | bytes 196632
  8.4 0.0 copy-start.4
  8.4 0.7 %copy-done.4 = s32[1,8]{1,0:T(1,128)S(1)} copy-done((s32[1,8]{1,0:T(1,128)S(1)}, s32[1,8]{1,0:T(1,128)}, u32[]{:S(2)}) %copy-start.4) | copy-done | bytes 56
  9.1 0.0 copy-start.5
  9.1 0.7 %copy-done.5 = s32[128]{0:T(128)S(1)} copy-done((s32[128]{0:T(128)S(1)}, s32[128]{0:T(128)}, u32[]{:S(2)}) %copy-start.5) | copy-done | bytes 536
  9.8 1.5 %stage.1 = (bf16[128,4096]{1,0:T(8,128)(2,1)S(1)}, bf16[128,768]{1,0:T(8,128)(2,1)S(1)}, bf16[128,1024]{1,0:T(8,128)(2,1)S(1)}, bf16[384,512]{1,0:T(8,128)(2,1)S...) custom-call(s32[1]{0:T(128)S(6)} %copy.17.count_ref, s32[1]{0:T(128)} %bitcast.me_ref, s32[1,8]{1,0:T(1,128)S(1)} %copy-done.4, ...), custom_call_target="tpu_custom_call" | custom-call | flops 1000 | bytes 1000 | tf_op jit(solution)/shard_map/stage/pallas_call | solution.py:277
  11.3 0.0 copy-start.1
  11.3 0.0 collective-permute-done.refs_1_
  11.3 2.4 %collective-permute-done.1.refs_2_ = bf16[128,768]{1,0:T(8,128)(2,1)S(1)} collective-permute-done((bf16[128,768]{1,0:T(8,128)(2,1)}, bf16[128,768]{1,0:T(8,128)(2,1)S(1)}, u32[]{:S(2)}, u32[]{:S(2)}) %collective-permute-start.1) | collective-permute-done | bytes 196640 | tf_op jit(solution)/shard_map/ppermute | solution.py:257
  13.7 0.0 collective-permute-done.2.refs_3_
  13.7 0.5 %aggregate.1.own_ref.refs_5_ = bf16[136,768]{1,0:T(8,128)(2,1)S(1)} custom-call(s32[8,128]{1,0:T(8,128)S(1)} %get-tuple-element.20.from_ref, f32[8,768]{1,0:T(8,128)S(1)} %get-tuple-element.21.extra_ref, bf16[128,1024]{1,0:T(8,128)(2,1)S(1)} %get-tuple-element.22.masked_ref, bf16[128,768]{1,0:T(8,128)(2,1)S(1)} %get-tuple-element.23.refs_0_, ...), custom_call_target="tpu_custom_call" | custom-call | flops 1000 | bytes 1000 | tf_op jit(solution)/shard_map/aggregate/pallas_call | solution.py:292
  14.3 0.1 collective-permute-start.6
  14.4 2.7 %collective-permute-start.3 = (bf16[136,768]{1,0:T(8,128)(2,1)S(1)}, bf16[136,768]{1,0:T(8,128)(2,1)S(1)}, u32[]{:S(2)}, u32[]{:S(2)}) collective-permute-start(bf16[136,768]{1,0:T(8,128)(2,1)S(1)} %aggregate.1.own_ref.refs_5_), channel_id=1, source_target_pairs={{0,4},{1,5},{2,6},{3,7},{4,0},{5,1},{6,2},{7,3},{8,12},{9,13},{10,... | collective-permute-start | bytes 626696 | tf_op jit(solution)/shard_map/ppermute | solution.py:257
  17.0 1.6 %collective-permute-start.5 = (bf16[136,768]{1,0:T(8,128)(2,1)S(1)}, bf16[136,768]{1,0:T(8,128)(2,1)S(1)}, u32[]{:S(2)}, u32[]{:S(2)}) collective-permute-start(bf16[136,768]{1,0:T(8,128)(2,1)S(1)} %aggregate.1.own_ref.refs_5_), channel_id=1, source_target_pairs={{0,2},{1,3},{2,0},{3,1},{4,6},{5,7},{6,4},{7,5},{8,10},{9,11},{10,... | collective-permute-start | bytes 626696 | tf_op jit(solution)/shard_map/ppermute | solution.py:257
  18.6 0.0 copy-done
  18.6 0.7 %query.1.refs_0_ = bf16[128,1024]{1,0:T(8,128)(2,1)S(1)} custom-call(bf16[136,768]{1,0:T(8,128)(2,1)S(1)} %aggregate.1.own_ref.refs_5_, bf16[768,1536]{1,0:T(8,128)(2,1)S(1)} %copy-done, bf16[384,512]{1,0:T(8,128)(2,1)S(1)} %get-tuple-element.24.sel_ref.refs_4_), custom_call_target="tpu_custom_call" | custom-call | flops 1000 | bytes 1000 | tf_op jit(solution)/shard_map/query/pallas_call | solution.py:315
  19.3 0.0 collective-permute-done.6.refs_6_
  19.3 0.0 copy-done.1
  19.3 4.1 %part.3 = (f32[128,1024]{1,0:T(8,128)S(1)}, f32[128,1024]{1,0:T(8,128)S(1)}, f32[128,1024]{1,0:T(8,128)S(1)}) custom-call(bf16[128,1024]{1,0:T(8,128)(2,1)S(1)} %query.1.refs_0_, bf16[128,4096]{1,0:T(8,128)(2,1)S(1)} %get-tuple-element.25.refs_1_, bf16[768,1536]{1,0:T(8,128)(2,1)S(1)} %copy-done, bf16[768,768]{1,0:T(8,128)(2,1)S(1)} %copy-done.1, ...), custom_call_target="tpu_custom_call" | custom-call | flops 1000 | bytes 1000 | tf_op jit(solution)/shard_map/part/pallas_call | solution.py:233
  23.5 3.9 %collective-permute-done.3.refs_7_ = bf16[136,768]{1,0:T(8,128)(2,1)S(1)} collective-permute-done((bf16[136,768]{1,0:T(8,128)(2,1)S(1)}, bf16[136,768]{1,0:T(8,128)(2,1)S(1)}, u32[]{:S(2)}, u32[]{:S(2)}) %collective-permute-start.3) | collective-permute-done | bytes 208928 | tf_op jit(solution)/shard_map/ppermute | solution.py:257
  27.4 0.0 collective-permute-start.8
  27.4 0.2 collective-permute-done.5.refs_5_
  27.6 0.3 collective-permute-start.7
  27.9 1.1 %collective-permute-start.4 = (bf16[136,768]{1,0:T(8,128)(2,1)S(1)}, bf16[136,768]{1,0:T(8,128)(2,1)S(1)}, u32[]{:S(2)}, u32[]{:S(2)}) collective-permute-start(bf16[136,768]{1,0:T(8,128)(2,1)S(1)} %collective-permute-done.3.refs_7_), channel_id=1, source_target_pairs={{0,2},{1,3},{2,0},{3,1},{4,6},{5,7},{6,4},{7,5},{8,10},{9,11},{10,... | collective-permute-start | bytes 626696 | tf_op jit(solution)/shard_map/ppermute | solution.py:257
  29.0 0.0 collective-permute-done.8.refs_8_
  29.1 0.1 collective-permute-done.7.refs_6_
  29.2 6.8 %part.4 = (f32[128,1024]{1,0:T(8,128)S(1)}, f32[128,1024]{1,0:T(8,128)S(1)}, f32[128,1024]{1,0:T(8,128)S(1)}) custom-call(bf16[128,1024]{1,0:T(8,128)(2,1)S(1)} %query.1.refs_0_, bf16[128,4096]{1,0:T(8,128)(2,1)S(1)} %get-tuple-element.25.refs_1_, bf16[768,1536]{1,0:T(8,128)(2,1)S(1)} %copy-done, bf16[768,768]{1,0:T(8,128)(2,1)S(1)} %copy-done.1, ...), custom_call_target="tpu_custom_call" | custom-call | flops 1000 | bytes 1000 | tf_op jit(solution)/shard_map/part/pallas_call | solution.py:233
  36.0 0.0 collective-permute-done.4.refs_5_
  36.0 0.3 collective-permute-start.9
  36.3 1.2 %collective-permute-done.9.refs_6_ = bf16[136,768]{1,0:T(8,128)(2,1)S(1)} collective-permute-done((bf16[136,768]{1,0:T(8,128)(2,1)S(1)}, bf16[136,768]{1,0:T(8,128)(2,1)S(1)}, u32[]{:S(2)}, u32[]{:S(2)}) %collective-permute-start.9) | collective-permute-done | bytes 208928 | tf_op jit(solution)/shard_map/ppermute | solution.py:257
  37.5 5.4 %part.5 = bf16[128,768]{1,0:T(8,128)(2,1)} custom-call(bf16[128,1024]{1,0:T(8,128)(2,1)S(1)} %query.1.refs_0_, bf16[128,4096]{1,0:T(8,128)(2,1)S(1)} %get-tuple-element.25.refs_1_, bf16[768,1536]{1,0:T(8,128)(2,1)S(1)} %copy-done, bf16[768,768]{1,0:T(8,128)(2,1)S(1)} %copy-done.1, bf16[384,512]{1,0:T(8,128)(2,1)S(1)} %get-tuple-element.24.sel_ref.refs_4_, ...), custom_call_target="tpu_custom_call" | custom-call | flops 1000 | bytes 1000 | tf_op jit(solution)/shard_map/part/pallas_call | solution.py:233
  (1 shorter events, 0.0 us)
Async XLA Ops:
  0.0 18.6 %copy-start = (bf16[768,1536]{1,0:T(8,128)(2,1)S(1)}, bf16[768,1536]{1,0:T(8,128)(2,1)}, u32[]{:S(2)}) copy-start(bf16[768,1536]{1,0:T(8,128)(2,1)} %refs_2_.5) | copy-start | bytes 7077892
  0.0 11.3 %collective-permute-start = (bf16[128,768]{1,0:T(8,128)(2,1)}, bf16[128,768]{1,0:T(8,128)(2,1)S(1)}, u32[]{:S(2)}, u32[]{:S(2)}) collective-permute-start(bf16[128,768]{1,0:T(8,128)(2,1)} %features_ref.1), channel_id=1, source_target_pairs={{0,8},{8,0},{16,24},{24,16},{1,9},{9,1},{17,25},{25,17},{2,10},{10... | collective-permute-start | bytes 589832 | tf_op jit(solution)/shard_map/ppermute | solution.py:257
  2.9 10.8 %collective-permute-start.1 = (bf16[128,768]{1,0:T(8,128)(2,1)}, bf16[128,768]{1,0:T(8,128)(2,1)S(1)}, u32[]{:S(2)}, u32[]{:S(2)}) collective-permute-start(bf16[128,768]{1,0:T(8,128)(2,1)} %features_ref.1), channel_id=1, source_target_pairs={{0,16},{8,24},{16,0},{24,8},{1,17},{9,25},{17,1},{25,9},{2,18},{10... | collective-permute-start | bytes 589832 | tf_op jit(solution)/shard_map/ppermute | solution.py:257
  4.5 9.3 %collective-permute-start.2 = (bf16[128,768]{1,0:T(8,128)(2,1)}, bf16[128,768]{1,0:T(8,128)(2,1)S(1)}, u32[]{:S(2)}, u32[]{:S(2)}) collective-permute-start(bf16[128,768]{1,0:T(8,128)(2,1)} %features_ref.1), channel_id=1, source_target_pairs={{0,24},{8,16},{16,8},{24,0},{1,25},{9,17},{17,9},{25,1},{2,26},{10... | collective-permute-start | bytes 589832 | tf_op jit(solution)/shard_map/ppermute | solution.py:257
  6.6 1.0 %copy-start.2 = (bf16[128,1024]{1,0:T(8,128)(2,1)S(1)}, bf16[128,1024]{1,0:T(8,128)(2,1)}, u32[]{:S(2)}) copy-start(bf16[128,1024]{1,0:T(8,128)(2,1)} %tiles_ref.1) | copy-start | bytes 786436
  7.5 0.9 %copy-start.3 = (bf16[128,768]{1,0:T(8,128)(2,1)S(1)}, bf16[128,768]{1,0:T(8,128)(2,1)}, u32[]{:S(2)}) copy-start(bf16[128,768]{1,0:T(8,128)(2,1)} %features_ref.1) | copy-start | bytes 589828
  8.4 0.7 %copy-start.4 = (s32[1,8]{1,0:T(1,128)S(1)}, s32[1,8]{1,0:T(1,128)}, u32[]{:S(2)}) copy-start(s32[1,8]{1,0:T(1,128)} %src_ref.1) | copy-start | bytes 100
  9.1 0.7 %copy-start.5 = (s32[128]{0:T(128)S(1)}, s32[128]{0:T(128)}, u32[]{:S(2)}) copy-start(s32[128]{0:T(128)} %param.12) | copy-start | bytes 1540
  11.3 8.1 %copy-start.1 = (bf16[768,768]{1,0:T(8,128)(2,1)S(1)}, bf16[768,768]{1,0:T(8,128)(2,1)}, u32[]{:S(2)}) copy-start(bf16[768,768]{1,0:T(8,128)(2,1)} %refs_3_.5) | copy-start | bytes 3538948
  14.3 5.0 %collective-permute-start.6 = (bf16[136,768]{1,0:T(8,128)(2,1)S(1)}, bf16[136,768]{1,0:T(8,128)(2,1)S(1)}, u32[]{:S(2)}, u32[]{:S(2)}) collective-permute-start(bf16[136,768]{1,0:T(8,128)(2,1)S(1)} %aggregate.1.own_ref.refs_5_), channel_id=1, source_target_pairs={{0,1},{1,0},{2,3},{3,2},{4,5},{5,4},{6,7},{7,6},{8,9},{9,8},{10,11... | collective-permute-start | bytes 626696 | tf_op jit(solution)/shard_map/ppermute | solution.py:257
  14.4 13.1 %collective-permute-start.3 = (bf16[136,768]{1,0:T(8,128)(2,1)S(1)}, bf16[136,768]{1,0:T(8,128)(2,1)S(1)}, u32[]{:S(2)}, u32[]{:S(2)}) collective-permute-start(bf16[136,768]{1,0:T(8,128)(2,1)S(1)} %aggregate.1.own_ref.refs_5_), channel_id=1, source_target_pairs={{0,4},{1,5},{2,6},{3,7},{4,0},{5,1},{6,2},{7,3},{8,12},{9,13},{10,... | collective-permute-start | bytes 626696 | tf_op jit(solution)/shard_map/ppermute | solution.py:257
  17.0 10.6 %collective-permute-start.5 = (bf16[136,768]{1,0:T(8,128)(2,1)S(1)}, bf16[136,768]{1,0:T(8,128)(2,1)S(1)}, u32[]{:S(2)}, u32[]{:S(2)}) collective-permute-start(bf16[136,768]{1,0:T(8,128)(2,1)S(1)} %aggregate.1.own_ref.refs_5_), channel_id=1, source_target_pairs={{0,2},{1,3},{2,0},{3,1},{4,6},{5,7},{6,4},{7,5},{8,10},{9,11},{10,... | collective-permute-start | bytes 626696 | tf_op jit(solution)/shard_map/ppermute | solution.py:257
  27.4 1.6 %collective-permute-start.8 = (bf16[136,768]{1,0:T(8,128)(2,1)S(1)}, bf16[136,768]{1,0:T(8,128)(2,1)S(1)}, u32[]{:S(2)}, u32[]{:S(2)}) collective-permute-start(bf16[136,768]{1,0:T(8,128)(2,1)S(1)} %collective-permute-done.3.refs_7_), channel_id=1, source_target_pairs={{0,1},{1,0},{2,3},{3,2},{4,5},{5,4},{6,7},{7,6},{8,9},{9,8},{10,11... | collective-permute-start | bytes 626696 | tf_op jit(solution)/shard_map/ppermute | solution.py:257
  27.6 1.6 %collective-permute-start.7 = (bf16[136,768]{1,0:T(8,128)(2,1)S(1)}, bf16[136,768]{1,0:T(8,128)(2,1)S(1)}, u32[]{:S(2)}, u32[]{:S(2)}) collective-permute-start(bf16[136,768]{1,0:T(8,128)(2,1)S(1)} %collective-permute-done.5.refs_5_), channel_id=1, source_target_pairs={{0,1},{1,0},{2,3},{3,2},{4,5},{5,4},{6,7},{7,6},{8,9},{9,8},{10,11... | collective-permute-start | bytes 626696 | tf_op jit(solution)/shard_map/ppermute | solution.py:257
  27.9 8.1 %collective-permute-start.4 = (bf16[136,768]{1,0:T(8,128)(2,1)S(1)}, bf16[136,768]{1,0:T(8,128)(2,1)S(1)}, u32[]{:S(2)}, u32[]{:S(2)}) collective-permute-start(bf16[136,768]{1,0:T(8,128)(2,1)S(1)} %collective-permute-done.3.refs_7_), channel_id=1, source_target_pairs={{0,2},{1,3},{2,0},{3,1},{4,6},{5,7},{6,4},{7,5},{8,10},{9,11},{10,... | collective-permute-start | bytes 626696 | tf_op jit(solution)/shard_map/ppermute | solution.py:257
  36.0 1.5 %collective-permute-start.9 = (bf16[136,768]{1,0:T(8,128)(2,1)S(1)}, bf16[136,768]{1,0:T(8,128)(2,1)S(1)}, u32[]{:S(2)}, u32[]{:S(2)}) collective-permute-start(bf16[136,768]{1,0:T(8,128)(2,1)S(1)} %collective-permute-done.4.refs_5_), channel_id=1, source_target_pairs={{0,1},{1,0},{2,3},{3,2},{4,5},{5,4},{6,7},{7,6},{8,9},{9,8},{10,11... | collective-permute-start | bytes 626696 | tf_op jit(solution)/shard_map/ppermute | solution.py:257

commit v7 on v6

v7 whole, which is shorter than its diff:
```python
import math

import jax
import jax.numpy as jnp
from jax import lax
from jax.experimental import pallas as pl
from jax.experimental.pallas import tpu as pltpu
from jax.sharding import PartitionSpec as P

H = 32
HD = 24
NB = 16
TILES = 8
LANES = 128
SET = 16
HALF = SET * HD
SLABS = HALF // LANES
SAFE = 1e30
EXTRA = 8
SHIFT = 3 * NB
NT = (((1,), (1,)), ((), ()))
MIB = 1024 * 1024
BF16 = jnp.bfloat16
F32 = jnp.float32
FACTOR = math.log2(math.e) / math.sqrt(HD)


def vmem():
    return pl.BlockSpec(memory_space=pltpu.VMEM)


def smem():
    return pl.BlockSpec(memory_space=pltpu.SMEM)


def limit(mib):
    return pltpu.CompilerParams(vmem_limit_bytes=mib * MIB)


def shape(*dims, dtype=BF16):
    return jax.ShapeDtypeStruct(dims, dtype)


def one_hot_slab(bucket_row):
    n = bucket_row.shape[1]
    index = lax.broadcasted_iota(jnp.int32, (LANES, n), 0)
    wanted = jnp.where(index < 3 * NB, index % NB, -1).astype(F32)
    hot = jnp.where((wanted == bucket_row) | ((index >= SHIFT) & (index < SHIFT + 3)), 1.0, 0.0)
    return hot.T.astype(BF16)


def stage_kernel(
    count_ref, me_ref, src_ref, cube_ref, bucket_ref, features_ref, tiles_ref,
    bias_ref, own_ref, masked_ref, extra_ref, from_ref, tiles_held, sems,
):
    rows = own_ref.shape[0]
    copies = [
        pltpu.make_async_copy(tiles_ref, tiles_held, sems.at[0]),
        pltpu.make_async_copy(features_ref, own_ref, sems.at[1]),
    ]
    for copy in copies:
        copy.start()
    for t in range(TILES):
        from_ref[t : t + 1, :] = jnp.full((1, LANES), src_ref[0, t] ^ me_ref[0], jnp.int32)
    width = own_ref.shape[1]
    extra = jnp.concatenate(
        [bucket_ref[...].astype(F32), jnp.zeros((1, width - rows), F32)], axis=1
    )
    extra_ref[...] = jnp.broadcast_to(extra, (EXTRA, width))
    scaled = cube_ref[...] * math.sqrt(HD)
    high = scaled.astype(BF16).astype(F32)
    rest = scaled - high
    mid = rest.astype(BF16).astype(F32)
    low = rest - mid
    lane = lax.broadcasted_iota(jnp.int32, scaled.shape, 1) % LANES
    parts = jnp.where(
        lane < NB, high, jnp.where(lane < 2 * NB, mid, jnp.where(lane < 3 * NB, low, 0.0))
    )
    hot = one_hot_slab(bucket_ref[...].astype(F32))[:, :NB]
    bias_ref[...] = jnp.dot(hot, parts.astype(BF16), preferred_element_type=F32).astype(BF16)
    for copy in copies:
        copy.wait()
    for t in range(TILES):
        tile = tiles_held[:, t * rows : (t + 1) * rows]
        masked_ref[:, t * rows : (t + 1) * rows] = jnp.where(
            t < count_ref[0], tile, jnp.zeros_like(tile)
        )


def aggregate_kernel(from_ref, extra_ref, masked_ref, *refs):
    feature_refs, out_ref, held = refs[:-2], refs[-2], refs[-1]
    rows = feature_refs[0].shape[0]
    for d, ref in enumerate(feature_refs):
        held[d * rows : (d + 1) * rows, :] = ref[...]
    picked = []
    for t in range(TILES):
        start = pl.multiple_of(from_ref[t, 0] * rows, rows)
        picked.append(held[pl.ds(start, rows), :])
    total = feature_refs[0][...].astype(F32) + jnp.dot(
        masked_ref[...], jnp.concatenate(picked, axis=0), preferred_element_type=F32
    )
    mean_square = jnp.mean(total * total, axis=-1, keepdims=True)
    out_ref[...] = jnp.concatenate(
        [total * lax.rsqrt(mean_square + 1e-06), extra_ref[...]], axis=0
    ).astype(BF16)


def slab_heads(slab):
    return slab * LANES // HD, ((slab + 1) * LANES - 1) // HD


def part_kernel(count, first, last, w_qk_ref, w_v_ref, *refs):
    block_refs, refs = refs[:count], refs[count:]
    hot_ref, k_ref, v_ref, p_ref, *refs_back = refs[-5:]
    top_ref = refs_back[0]
    refs = refs[:-5]
    if first:
        bias_ref, q_ref, shifted_ref, *outs = refs
    else:
        q_ref, bias_ref, *refs = refs
        old_refs, outs = (refs[:2], refs[2:]) if len(refs) in (3, 5) else (refs[:3], refs[3:])
    rows = q_ref.shape[0]
    keys = hot_ref.shape[0]
    width = w_v_ref.shape[0]
    arrived = [ref[...] for ref in block_refs]
    for s, item in enumerate(arrived):
        bucket = item[rows:, :rows].astype(F32)[:1, :]
        hot_ref[s * rows : (s + 1) * rows, :] = one_hot_slab(bucket)
    block = jnp.concatenate([item[:rows, :] for item in arrived], axis=0)
    if first:
        for n in range(0, width, 256):
            q_ref[:, n : n + 256] = jnp.dot(
                block[:rows, :], w_qk_ref[:, n : n + 256], preferred_element_type=F32
            ).astype(BF16)
    for n in range(0, width, 256):
        k_ref[:, n : n + 256] = jnp.dot(
            block, w_qk_ref[:, width + n : width + n + 256], preferred_element_type=F32
        ).astype(BF16)
        v_ref[:, n : n + 256] = jnp.dot(
            block, w_v_ref[:, n : n + 256], preferred_element_type=F32
        ).astype(BF16)

    lane = lax.broadcasted_iota(jnp.int32, (rows, LANES), 1)
    ones = jnp.ones((keys, LANES), BF16)

    def scores(half, slab):
        cols = pl.ds(pl.multiple_of(half * HALF + slab * LANES, LANES), LANES)
        begin, end = slab_heads(slab)
        q = q_ref[:, cols]
        zero = jnp.zeros_like(q)
        lefts, rights = [], []
        for h in range(begin, end + 1):
            inside = (lane >= h * HD - slab * LANES) & (lane < (h + 1) * HD - slab * LANES)
            lefts.append(jnp.where(inside, q, zero))
            if h * HD >= slab * LANES:
                at = pl.multiple_of((half * SET + h) * LANES, LANES)
                rights.append(bias_ref[:, pl.ds(at, LANES)])
            else:
                rights.append(zero)
        query = jnp.concatenate(
            [jnp.concatenate(lefts, axis=0), jnp.concatenate(rights, axis=0)], axis=1
        )
        key = jnp.concatenate([k_ref[:, cols], hot_ref[...]], axis=1)
        return lax.dot_general(query, key, NT, preferred_element_type=F32)

    def weigh(half, local):
        carried = None
        for slab in range(SLABS):
            begin, end = slab_heads(slab)
            x = scores(half, slab)
            for h in range(begin, end + 1):
                own = x[(h - begin) * rows : (h - begin + 1) * rows, :]
                if h * HD < slab * LANES:
                    own = own + carried
                if (h + 1) * HD > (slab + 1) * LANES:
                    carried = own
                    continue
                if local:
                    peak = jnp.max(own, axis=-1, keepdims=True)
                    own = own - peak
                    keep_peak(half, h, peak)
                p_ref[h * rows : (h + 1) * rows, :] = jnp.exp2(own * FACTOR).astype(BF16)

    def keep_peak(half, h, peak):
        if first:
            at = pl.ds(pl.multiple_of((half * SET + h) * LANES, LANES), LANES)
            high = (-peak).astype(BF16).astype(F32)
            rest = -peak - high
            mid = rest.astype(BF16).astype(F32)
            low = rest - mid
            mark = jnp.where(
                lane == SHIFT, high, jnp.where(lane == SHIFT + 1, mid, jnp.where(lane == SHIFT + 2, low, 0.0))
            )
            shifted_ref[:, at] = bias_ref[:, at] + mark.astype(BF16)
        else:
            top_ref[h * rows : (h + 1) * rows, :] = jnp.broadcast_to(peak, (rows, LANES))

    def pick(array, slab, base):
        begin, end = slab_heads(slab)
        out = array[(begin - base) * rows : (begin - base + 1) * rows, :]
        for h in range(begin + 1, end + 1):
            piece = array[(h - base) * rows : (h - base + 1) * rows, :]
            out = jnp.where(lane >= h * HD - slab * LANES, piece, out)
        return out

    def mix(half, slab):
        cols = pl.ds(pl.multiple_of(half * HALF + slab * LANES, LANES), LANES)
        begin, end = slab_heads(slab)
        value = jnp.concatenate([v_ref[:, cols], ones], axis=1)
        mixed = jnp.dot(
            p_ref[begin * rows : (end + 1) * rows, :], value, preferred_element_type=F32
        )
        return cols, pick(mixed[:, :LANES], slab, begin), pick(mixed[:, LANES:], slab, begin)

    def fast(half, largest):
        weigh(half, first)
        for slab in range(SLABS):
            cols, top, total = mix(half, slab)
            if not first:
                top = top + old_refs[0][:, cols]
                total = total + old_refs[1][:, cols]
            largest = jnp.maximum(largest, total)
            if last:
                outs[0][:, cols] = (top / total).astype(BF16)
            else:
                outs[0][:, cols] = top
                outs[1][:, cols] = total
                if not first:
                    outs[2][:, cols] = jnp.zeros_like(top)
        return largest

    largest = lax.fori_loop(0, width // HALF, fast, jnp.zeros((rows, LANES), F32))
    if first:
        return
    fine = jnp.max(largest) < SAFE
    if len(old_refs) == 3:
        fine = fine & (jnp.max(old_refs[2][...]) == 0.0)

    @pl.when(jnp.logical_not(fine))
    def _():
        def careful(half, carry):
            weigh(half, True)
            for slab in range(SLABS):
                cols, top, total = mix(half, slab)
                peak = pick(top_ref[...], slab, 0)
                old = old_refs[2][:, cols] if len(old_refs) == 3 else jnp.zeros_like(top)
                best = jnp.maximum(old, peak)
                share = jnp.exp2((peak - best) * FACTOR)
                old_share = jnp.exp2((old - best) * FACTOR)
                top = top * share + old_refs[0][:, cols] * old_share
                total = total * share + old_refs[1][:, cols] * old_share
                if last:
                    outs[0][:, cols] = (top / total).astype(BF16)
                else:
                    outs[0][:, cols] = top
                    outs[1][:, cols] = total
                    outs[2][:, cols] = best
            return carry

        lax.fori_loop(0, width // HALF, careful, 0)


def attend_part(first, last, w_qk, w_v, blocks, inputs):
    width = w_v.shape[0]
    rows = blocks[0].shape[0] - EXTRA
    keys = rows * len(blocks)
    state = shape(rows, width, dtype=F32)
    if first:
        outs = [shape(rows, width), shape(rows, H * LANES), state, state]
    elif last:
        outs = [shape(rows, width)]
    else:
        outs = [state] * 3
    operands = [w_qk, w_v, *blocks, *inputs]
    tall = SET * rows
    need = 8 * tall * keys * 2 + 4 * keys * width + 4 * tall * LANES
    return pl.pallas_call(
        lambda *refs: part_kernel(len(blocks), first, last, *refs),
        out_shape=outs,
        in_specs=[vmem()] * len(operands),
        out_specs=[vmem()] * len(outs),
        scratch_shapes=[
            pltpu.VMEM((keys, LANES), BF16),
            pltpu.VMEM((keys, width), BF16),
            pltpu.VMEM((keys, width), BF16),
            pltpu.VMEM((tall, keys), BF16),
            pltpu.VMEM((tall, LANES), F32),
        ],
        compiler_params=limit(need // MIB + 12),
        cost_estimate=pl.CostEstimate(flops=1000, bytes_accessed=1000, transcendentals=0),
        name="part",
    )(*operands)


def swap(array, axis, distance):
    return lax.ppermute(array, axis, [(i, i ^ distance) for i in range(lax.axis_size(axis))])


def after(value, *others):
    return lax.optimization_barrier((value, others))[0]


def on_device(features, tiles, tile_src, tile_count, node_bucket, w_qk, w_v, bias_table):
    rows, width = features.shape
    groups = lax.axis_size("group")
    seq_count = lax.axis_size("seq")
    chips = seq_count // 2
    any_space = pl.BlockSpec(memory_space=pl.ANY)

    received = [swap(features, "group", d) for d in range(groups - 1, 0, -1)][::-1]
    own_bucket = node_bucket.reshape(1, rows)

    cube = bias_table.reshape(H, NB, NB).transpose(1, 0, 2)
    cube = jnp.concatenate([cube, cube, cube, jnp.zeros((NB, H, LANES - 3 * NB), F32)], axis=2)
    cube = cube.reshape(NB, H * LANES)
    bias, own_features, masked, extra, source = pl.pallas_call(
        stage_kernel,
        out_shape=[
            shape(rows, H * LANES), shape(rows, width), shape(rows, TILES * rows),
            shape(EXTRA, width, dtype=F32),
            shape(TILES, LANES, dtype=jnp.int32),
        ],
        in_specs=[smem()] * 3 + [vmem(), vmem(), any_space, any_space],
        out_specs=[vmem()] * 5,
        scratch_shapes=[pltpu.VMEM((rows, TILES * rows), BF16), pltpu.SemaphoreType.DMA((2,))],
        compiler_params=limit(16),
        cost_estimate=pl.CostEstimate(flops=1000, bytes_accessed=1000, transcendentals=0),
        name="stage",
    )(tile_count, lax.axis_index("group").reshape(1), tile_src, cube, own_bucket, features, tiles)

    own = pl.pallas_call(
        aggregate_kernel,
        out_shape=shape(rows + EXTRA, width),
        in_specs=[vmem()] * (3 + groups),
        out_specs=vmem(),
        scratch_shapes=[pltpu.VMEM((groups * rows, width), BF16)],
        compiler_params=limit(16),
        cost_estimate=pl.CostEstimate(flops=1000, bytes_accessed=1000, transcendentals=0),
        name="aggregate",
    )(source, extra, masked, own_features, *received)

    far = [own] + [None] * (chips - 1)
    top = 1
    while 2 * top < chips:
        top *= 2
    far[top] = swap(own, "seq", 2 * top)
    step = 1
    while step < top:
        far[step] = swap(own, "seq", 2 * step)
        step *= 2
    for d in range(3, chips):
        if far[d] is None:
            far[d] = swap(far[d & (d - 1)], "seq", 2 * (d & -d))
    parts = [[0], [1, top]] if top > 1 else [[0, 1]]
    parts += [[d] for d in range(2, chips) if d != top]
    queries, state = [], [bias]
    for number, part in enumerate(parts):
        blocks = []
        for d in part:
            block = far[d]
            if d:
                block = after(block, *state)
                near = swap(block, "seq", 1)
            else:
                near = swap(own, "seq", 1)
            blocks += [block, near]
        state = attend_part(
            number == 0, number == len(parts) - 1, w_qk, w_v, blocks, [*queries, *state]
        )
        if number == 0:
            queries, state = state[:2], state[2:]
    return state[0]


def solution(mesh):
    in_specs = (
        P(("group", "seq"), None),
        P(("group", "seq"), None),
        P(("group", "seq"), None),
        P(("group", "seq")),
        P(("group", "seq")),
        P(),
        P(),
        P(),
    )
    out_specs = P(("group", "seq"), None)
    return jax.shard_map(
        on_device, mesh=mesh, in_specs=in_specs, out_specs=out_specs, check_vma=False
    )
```

time: 43.2 us -> 44.6 us (1.032)
  Pallas kernels: 19.1 us -> 14.6 us
  local copies, waits for them, and re-layouts: 4.4 us -> 8.3 us
  other arithmetic: 0.2 us -> 1.31 us
  waiting for transfers between devices: 7.94 us -> 8.56 us
    pallas_call x3, Pallas kernels: 16.3 us -> 11.5 us  [attend_part(): pl.pallas_call(lambda *refs: part_kernel(len(blocks), first, last, *refs)...]
    unnamed x14 -> x16, local copies, waits for them, and re-layouts: 4.2 us -> 6.49 us
    transpose x1, local copies, waits for them, and re-layouts: 0.13 us -> 1.73 us  [on_device(): cube = bias_table.reshape(H, NB, NB).transpose(1, 0, 2)]
    pallas_call x1, Pallas kernels: 0.54 us -> 1.65 us  [on_device(): pl.pallas_call(aggregate_kernel, out_shape=shape(rows + EXTRA, width), in...]
    concatenate x1, other arithmetic: 0.2 us -> 1.31 us  [on_device(): jnp.concatenate([cube, cube, cube, jnp.zeros((NB, H, LANES - 3 * NB), F32...]
    pallas_call x1 -> x0, Pallas kernels: 0.72 us -> none  [on_device(): pl.pallas_call(query_kernel, out_shape=shape(rows, WIDE), in_specs=[vmem(...]
    ppermute x10, waiting for transfers between devices: 7.94 us -> 8.56 us  [swap(): lax.ppermute(array, axis, [(i, i ^ distance) for i in range(lax.axis_size...]
  transfers between devices with their start and end apart: 10 -> 10, of which waited for: 5 -> 5; matrix products, arithmetic and copies ran while one was open for 3% -> 12% of each run, Pallas kernels for 31% -> 21%
where the time goes in v7:
time: 44.6 us; the launch traced here: 44.2 us
  Pallas kernels  14.6 us (33%)
  starting transfers between devices  10.7 us (24%)
  waiting for transfers between devices  8.56 us (19%)
  local copies, waits for them, and re-layouts  8.3 us (19%)
  other arithmetic  1.31 us (3%)
  between operations  0.75 us (2%)
    pallas_call x3, Pallas kernels, attend_part(): pl.pallas_call(lambda *refs: part_kernel(len(blocks), first, last, *refs)...  11.5 us
    ppermute x10, starting transfers between devices, swap(): lax.ppermute(array, axis, [(i, i ^ distance) for i in range(lax.axis_size...  10.7 us
    ppermute x10, waiting for transfers between devices, swap(): lax.ppermute(array, axis, [(i, i ^ distance) for i in range(lax.axis_size...  8.56 us
    unnamed x16, local copies, waits for them, and re-layouts  6.49 us
    transpose x1, local copies, waits for them, and re-layouts, on_device(): cube = bias_table.reshape(H, NB, NB).transpose(1, 0, 2)  1.73 us
    pallas_call x1, Pallas kernels, on_device(): pl.pallas_call(aggregate_kernel, out_shape=shape(rows + EXTRA, width), in...  1.65 us
    pallas_call x1, Pallas kernels, on_device(): pl.pallas_call(stage_kernel, out_shape=[shape(rows, H * LANES), shape(row...  1.39 us
    concatenate x1, other arithmetic, on_device(): jnp.concatenate([cube, cube, cube, jnp.zeros((NB, H, LANES - 3 * NB), F32...  1.31 us
  transfers between devices with their start and end apart: 10, of which 5 were waited for; matrix products, arithmetic and copies ran while one was open for 12% of the time, Pallas kernels for 21%

profile of v7, /device:TPU:0, one launch (start us, length us, event | category | flops | bytes accessed | tf_op | source)
XLA Modules:
  0.0 44.2 jit_solution(4644430935407395629)
XLA Ops:
  0.0 0.0 copy-start
  0.0 0.0 copy-start.1
  0.0 2.9 %collective-permute-start = (bf16[128,768]{1,0:T(8,128)(2,1)}, bf16[128,768]{1,0:T(8,128)(2,1)}, u32[]{:S(2)}, u32[]{:S(2)}) collective-permute-start(bf16[128,768]{1,0:T(8,128)(2,1)} %features_ref.1), channel_id=1, source_target_pairs={{0,8},{8,0},{16,24},{24,16},{1,9},{9,1},{17,25},{25,17},{2,10},{10... | collective-permute-start | bytes 589832 | tf_op jit(solution)/shard_map/ppermute | solution.py:296
  2.9 1.5 %collective-permute-start.1 = (bf16[128,768]{1,0:T(8,128)(2,1)}, bf16[128,768]{1,0:T(8,128)(2,1)}, u32[]{:S(2)}, u32[]{:S(2)}) collective-permute-start(bf16[128,768]{1,0:T(8,128)(2,1)} %features_ref.1), channel_id=1, source_target_pairs={{0,16},{8,24},{16,0},{24,8},{1,17},{9,25},{17,1},{25,9},{2,18},{10... | collective-permute-start | bytes 589832 | tf_op jit(solution)/shard_map/ppermute | solution.py:296
  4.5 0.0 collective-permute-start.2
  4.5 1.5 %copy.10 = f32[32,256]{0,1:T(8,128)} copy(f32[32,256]{1,0:T(8,128)} %param.15) | data formatting | bytes 65536 | tf_op args[7]
  6.0 1.7 %copy.11 = f32[16,32,16]{2,1,0:T(8,128)} copy(f32[16,32,16]{1,2,0:T(8,128)} %bitcast.12) | data formatting | bytes 65536 | tf_op jit(solution)/shard_map/transpose | solution.py:313
  7.7 0.1 pad.3.clone
  7.8 1.3 %maximum_maximum_fusion = f32[16,32,128]{2,1,0:T(8,128)S(1)} fusion(f32[16,32,16]{2,1,0:T(8,128)} %copy.11, f32[128]{0:T(128)S(1)} %pad.3.clone), kind=kLoop, calls=%fused_computation.1 | loop fusion | flops 196608 | bytes 295424 | tf_op jit(solution)/shard_map/concatenate | solution.py:314
  9.1 0.8 %copy.16 = f32[2,8,32,128]{3,1,2,0:T(8,128)} copy(f32[2,8,32,128]{3,2,1,0:T(8,128)S(1)} %bitcast.11) | data formatting | bytes 524288
  10.6 0.0 copy-start.2
  10.6 0.9 %copy-done.2 = f32[2,8,32,128]{3,1,2,0:T(8,128)S(1)} copy-done((f32[2,8,32,128]{3,1,2,0:T(8,128)S(1)}, f32[2,8,32,128]{3,1,2,0:T(8,128)}, u32[]{:S(2)}) %copy-start.2) | copy-done | bytes 262168
  11.6 0.0 copy-start.3
  11.6 0.9 %copy-done.3 = bf16[128,1024]{1,0:T(8,128)(2,1)S(1)} copy-done((bf16[128,1024]{1,0:T(8,128)(2,1)S(1)}, bf16[128,1024]{1,0:T(8,128)(2,1)}, u32[]{:S(2)}) %copy-start.3) | copy-done | bytes 262168
  12.5 0.0 copy-start.4
  12.5 0.9 %copy-done.4 = bf16[128,768]{1,0:T(8,128)(2,1)S(1)} copy-done((bf16[128,768]{1,0:T(8,128)(2,1)S(1)}, bf16[128,768]{1,0:T(8,128)(2,1)}, u32[]{:S(2)}) %copy-start.4) | copy-done | bytes 196632
  13.4 0.0 copy-start.5
  13.4 0.7 %copy-done.5 = s32[1,8]{1,0:T(1,128)S(1)} copy-done((s32[1,8]{1,0:T(1,128)S(1)}, s32[1,8]{1,0:T(1,128)}, u32[]{:S(2)}) %copy-start.5) | copy-done | bytes 56
  14.1 0.0 copy-start.6
  14.1 0.7 %copy-done.6 = s32[128]{0:T(128)S(1)} copy-done((s32[128]{0:T(128)S(1)}, s32[128]{0:T(128)}, u32[]{:S(2)}) %copy-start.6) | copy-done | bytes 536
  14.8 1.4 %stage.1 = (bf16[128,4096]{1,0:T(8,128)(2,1)S(1)}, bf16[128,768]{1,0:T(8,128)(2,1)S(1)}, bf16[128,1024]{1,0:T(8,128)(2,1)S(1)}, f32[8,768]{1,0:T(8,128)S(1)}, s32[8,128]{1,0:T(8,128)S(1)}) custom-call(s32[1]{0:T(128)S(6)} %copy.17.count_ref, s32[1]{0:T(128)} %bitcast.me_ref, s32[1,8]{1,0:T(1,128)S(1)} %copy-done.5, f32[16,4096]{1,0:T(8,128)S(1)} %bitcast.9, ...), custom_call_target="tpu_custom_call" | custom-call | flops 1000 | bytes 1000 | tf_op jit(solution)/shard_map/stage/pallas_call | solution.py:316
  16.2 0.0 collective-permute-done.refs_1_
  16.2 0.0 collective-permute-done.1.refs_2_
  16.2 0.0 collective-permute-done.2.refs_3_
  16.2 1.7 %aggregate.1.refs_2_ = bf16[136,768]{1,0:T(8,128)(2,1)S(1)} custom-call(s32[8,128]{1,0:T(8,128)S(1)} %get-tuple-element.20.from_ref, f32[8,768]{1,0:T(8,128)S(1)} %get-tuple-element.21.extra_ref, bf16[128,1024]{1,0:T(8,128)(2,1)S(1)} %get-tuple-element.22.masked_ref, bf16[128,768]{1,0:T(8,128)(2,1)S(1)} %get-tuple-element.23.refs_0_, ...), custom_call_target="tpu_custom_call" | custom-call | flops 1000 | bytes 1000 | tf_op jit(solution)/shard_map/aggregate/pallas_call | solution.py:331
  17.8 0.1 collective-permute-start.6
  17.9 3.1 %collective-permute-start.3 = (bf16[136,768]{1,0:T(8,128)(2,1)S(1)}, bf16[136,768]{1,0:T(8,128)(2,1)S(1)}, u32[]{:S(2)}, u32[]{:S(2)}) collective-permute-start(bf16[136,768]{1,0:T(8,128)(2,1)S(1)} %aggregate.1.refs_2_), channel_id=1, source_target_pairs={{0,4},{1,5},{2,6},{3,7},{4,0},{5,1},{6,2},{7,3},{8,12},{9,13},{10,... | collective-permute-start | bytes 626696 | tf_op jit(solution)/shard_map/ppermute | solution.py:296
  21.0 1.6 %collective-permute-start.5 = (bf16[136,768]{1,0:T(8,128)(2,1)S(1)}, bf16[136,768]{1,0:T(8,128)(2,1)S(1)}, u32[]{:S(2)}, u32[]{:S(2)}) collective-permute-start(bf16[136,768]{1,0:T(8,128)(2,1)S(1)} %aggregate.1.refs_2_), channel_id=1, source_target_pairs={{0,2},{1,3},{2,0},{3,1},{4,6},{5,7},{6,4},{7,5},{8,10},{9,11},{10,... | collective-permute-start | bytes 626696 | tf_op jit(solution)/shard_map/ppermute | solution.py:296
  22.6 0.0 collective-permute-done.6.refs_3_
  22.6 0.0 copy-done
  22.6 0.0 copy-done.1
  22.6 3.5 %part.3 = (bf16[128,768]{1,0:T(8,128)(2,1)S(1)}, bf16[128,4096]{1,0:T(8,128)(2,1)S(1)}, f32[128,768]{1,0:T(8,128)S(1)}, f32[128,768]{1,0:T(8,128)S(1)}) custom-call(bf16[768,1536]{1,0:T(8,128)(2,1)S(1)} %copy-done, bf16[768,768]{1,0:T(8,128)(2,1)S(1)} %copy-done.1, bf16[136,768]{1,0:T(8,128)(2,1)S(1)} %aggregate.1.refs_2_, ...), custom_call_target="tpu_custom_call" | custom-call | flops 1000 | bytes 1000 | tf_op jit(solution)/shard_map/part/pallas_call | solution.py:277
  26.1 5.3 %collective-permute-done.3.refs_4_ = bf16[136,768]{1,0:T(8,128)(2,1)S(1)} collective-permute-done((bf16[136,768]{1,0:T(8,128)(2,1)S(1)}, bf16[136,768]{1,0:T(8,128)(2,1)S(1)}, u32[]{:S(2)}, u32[]{:S(2)}) %collective-permute-start.3) | collective-permute-done | bytes 208928 | tf_op jit(solution)/shard_map/ppermute | solution.py:296
  31.4 0.0 collective-permute-start.8
  31.4 0.2 collective-permute-done.5.refs_2_
  31.6 0.3 collective-permute-start.7
  31.9 1.2 %collective-permute-start.4 = (bf16[136,768]{1,0:T(8,128)(2,1)S(1)}, bf16[136,768]{1,0:T(8,128)(2,1)S(1)}, u32[]{:S(2)}, u32[]{:S(2)}) collective-permute-start(bf16[136,768]{1,0:T(8,128)(2,1)S(1)} %collective-permute-done.3.refs_4_), channel_id=1, source_target_pairs={{0,2},{1,3},{2,0},{3,1},{4,6},{5,7},{6,4},{7,5},{8,10},{9,11},{10,... | collective-permute-start | bytes 626696 | tf_op jit(solution)/shard_map/ppermute | solution.py:296
  33.1 0.0 collective-permute-done.8.refs_5_
  33.1 0.1 collective-permute-done.7.refs_3_
  33.1 4.4 %part.4 = (f32[128,768]{1,0:T(8,128)S(1)}, f32[128,768]{1,0:T(8,128)S(1)}, f32[128,768]{1,0:T(8,128)S(1)}) custom-call(bf16[768,1536]{1,0:T(8,128)(2,1)S(1)} %copy-done, bf16[768,768]{1,0:T(8,128)(2,1)S(1)} %copy-done.1, bf16[136,768]{1,0:T(8,128)(2,1)S(1)} %collective-permute-done.5.refs_2_, bf16[136,768]{1,0:T(8,128)(2,1)S(1)} %collective-permute-done.7.refs_3_, ...), custom_call_target="tpu_custom_call" | custom-call | flops 1000 | bytes 1000 | tf_op jit(solution)/shard_map/part/pallas_call | solution.py:277
  37.6 1.6 %collective-permute-done.4.refs_2_ = bf16[136,768]{1,0:T(8,128)(2,1)S(1)} collective-permute-done((bf16[136,768]{1,0:T(8,128)(2,1)S(1)}, bf16[136,768]{1,0:T(8,128)(2,1)S(1)}, u32[]{:S(2)}, u32[]{:S(2)}) %collective-permute-start.4) | collective-permute-done | bytes 208928 | tf_op jit(solution)/shard_map/ppermute | solution.py:296
  39.2 0.0 collective-permute-start.9
  39.2 1.5 %collective-permute-done.9.refs_3_ = bf16[136,768]{1,0:T(8,128)(2,1)S(1)} collective-permute-done((bf16[136,768]{1,0:T(8,128)(2,1)S(1)}, bf16[136,768]{1,0:T(8,128)(2,1)S(1)}, u32[]{:S(2)}, u32[]{:S(2)}) %collective-permute-start.9) | collective-permute-done | bytes 208928 | tf_op jit(solution)/shard_map/ppermute | solution.py:296
  40.6 3.6 %part.5 = bf16[128,768]{1,0:T(8,128)(2,1)} custom-call(bf16[768,1536]{1,0:T(8,128)(2,1)S(1)} %copy-done, bf16[768,768]{1,0:T(8,128)(2,1)S(1)} %copy-done.1, bf16[136,768]{1,0:T(8,128)(2,1)S(1)} %collective-permute-done.4.refs_2_, bf16[136,768]{1,0:T(8,128)(2,1)S(1)} %collective-permute-done.9.refs_3_, ...), custom_call_target="tpu_custom_call" | custom-call | flops 1000 | bytes 1000 | tf_op jit(solution)/shard_map/part/pallas_call | solution.py:277
  (1 shorter events, 0.0 us)
Async XLA Ops:
  0.0 22.6 %copy-start = (bf16[768,1536]{1,0:T(8,128)(2,1)S(1)}, bf16[768,1536]{1,0:T(8,128)(2,1)}, u32[]{:S(2)}) copy-start(bf16[768,1536]{1,0:T(8,128)(2,1)} %refs_0_.5) | copy-start | bytes 7077892
  0.0 22.6 %copy-start.1 = (bf16[768,768]{1,0:T(8,128)(2,1)S(1)}, bf16[768,768]{1,0:T(8,128)(2,1)}, u32[]{:S(2)}) copy-start(bf16[768,768]{1,0:T(8,128)(2,1)} %refs_1_.5) | copy-start | bytes 3538948
  0.0 16.1 %collective-permute-start = (bf16[128,768]{1,0:T(8,128)(2,1)}, bf16[128,768]{1,0:T(8,128)(2,1)}, u32[]{:S(2)}, u32[]{:S(2)}) collective-permute-start(bf16[128,768]{1,0:T(8,128)(2,1)} %features_ref.1), channel_id=1, source_target_pairs={{0,8},{8,0},{16,24},{24,16},{1,9},{9,1},{17,25},{25,17},{2,10},{10... | collective-permute-start | bytes 589832 | tf_op jit(solution)/shard_map/ppermute | solution.py:296
  2.9 13.2 %collective-permute-start.1 = (bf16[128,768]{1,0:T(8,128)(2,1)}, bf16[128,768]{1,0:T(8,128)(2,1)}, u32[]{:S(2)}, u32[]{:S(2)}) collective-permute-start(bf16[128,768]{1,0:T(8,128)(2,1)} %features_ref.1), channel_id=1, source_target_pairs={{0,16},{8,24},{16,0},{24,8},{1,17},{9,25},{17,1},{25,9},{2,18},{10... | collective-permute-start | bytes 589832 | tf_op jit(solution)/shard_map/ppermute | solution.py:296
  4.5 11.7 %collective-permute-start.2 = (bf16[128,768]{1,0:T(8,128)(2,1)}, bf16[128,768]{1,0:T(8,128)(2,1)}, u32[]{:S(2)}, u32[]{:S(2)}) collective-permute-start(bf16[128,768]{1,0:T(8,128)(2,1)} %features_ref.1), channel_id=1, source_target_pairs={{0,24},{8,16},{16,8},{24,0},{1,25},{9,17},{17,9},{25,1},{2,26},{10... | collective-permute-start | bytes 589832 | tf_op jit(solution)/shard_map/ppermute | solution.py:296
  10.6 1.0 %copy-start.2 = (f32[2,8,32,128]{3,1,2,0:T(8,128)S(1)}, f32[2,8,32,128]{3,1,2,0:T(8,128)}, u32[]{:S(2)}) copy-start(f32[2,8,32,128]{3,1,2,0:T(8,128)} %copy.16) | copy-start | bytes 786436
  11.6 0.9 %copy-start.3 = (bf16[128,1024]{1,0:T(8,128)(2,1)S(1)}, bf16[128,1024]{1,0:T(8,128)(2,1)}, u32[]{:S(2)}) copy-start(bf16[128,1024]{1,0:T(8,128)(2,1)} %tiles_ref.1) | copy-start | bytes 786436
  12.5 0.9 %copy-start.4 = (bf16[128,768]{1,0:T(8,128)(2,1)S(1)}, bf16[128,768]{1,0:T(8,128)(2,1)}, u32[]{:S(2)}) copy-start(bf16[128,768]{1,0:T(8,128)(2,1)} %features_ref.1) | copy-start | bytes 589828
  13.4 0.7 %copy-start.5 = (s32[1,8]{1,0:T(1,128)S(1)}, s32[1,8]{1,0:T(1,128)}, u32[]{:S(2)}) copy-start(s32[1,8]{1,0:T(1,128)} %src_ref.1) | copy-start | bytes 100
  14.1 0.7 %copy-start.6 = (s32[128]{0:T(128)S(1)}, s32[128]{0:T(128)}, u32[]{:S(2)}) copy-start(s32[128]{0:T(128)} %param.12) | copy-start | bytes 1540
  17.8 4.8 %collective-permute-start.6 = (bf16[136,768]{1,0:T(8,128)(2,1)S(1)}, bf16[136,768]{1,0:T(8,128)(2,1)S(1)}, u32[]{:S(2)}, u32[]{:S(2)}) collective-permute-start(bf16[136,768]{1,0:T(8,128)(2,1)S(1)} %aggregate.1.refs_2_), channel_id=1, source_target_pairs={{0,1},{1,0},{2,3},{3,2},{4,5},{5,4},{6,7},{7,6},{8,9},{9,8},{10,11... | collective-permute-start | bytes 626696 | tf_op jit(solution)/shard_map/ppermute | solution.py:296
  17.9 13.5 %collective-permute-start.3 = (bf16[136,768]{1,0:T(8,128)(2,1)S(1)}, bf16[136,768]{1,0:T(8,128)(2,1)S(1)}, u32[]{:S(2)}, u32[]{:S(2)}) collective-permute-start(bf16[136,768]{1,0:T(8,128)(2,1)S(1)} %aggregate.1.refs_2_), channel_id=1, source_target_pairs={{0,4},{1,5},{2,6},{3,7},{4,0},{5,1},{6,2},{7,3},{8,12},{9,13},{10,... | collective-permute-start | bytes 626696 | tf_op jit(solution)/shard_map/ppermute | solution.py:296
  21.0 10.5 %collective-permute-start.5 = (bf16[136,768]{1,0:T(8,128)(2,1)S(1)}, bf16[136,768]{1,0:T(8,128)(2,1)S(1)}, u32[]{:S(2)}, u32[]{:S(2)}) collective-permute-start(bf16[136,768]{1,0:T(8,128)(2,1)S(1)} %aggregate.1.refs_2_), channel_id=1, source_target_pairs={{0,2},{1,3},{2,0},{3,1},{4,6},{5,7},{6,4},{7,5},{8,10},{9,11},{10,... | collective-permute-start | bytes 626696 | tf_op jit(solution)/shard_map/ppermute | solution.py:296
  31.4 1.7 %collective-permute-start.8 = (bf16[136,768]{1,0:T(8,128)(2,1)S(1)}, bf16[136,768]{1,0:T(8,128)(2,1)S(1)}, u32[]{:S(2)}, u32[]{:S(2)}) collective-permute-start(bf16[136,768]{1,0:T(8,128)(2,1)S(1)} %collective-permute-done.3.refs_4_), channel_id=1, source_target_pairs={{0,1},{1,0},{2,3},{3,2},{4,5},{5,4},{6,7},{7,6},{8,9},{9,8},{10,11... | collective-permute-start | bytes 626696 | tf_op jit(solution)/shard_map/ppermute | solution.py:296
  31.6 1.6 %collective-permute-start.7 = (bf16[136,768]{1,0:T(8,128)(2,1)S(1)}, bf16[136,768]{1,0:T(8,128)(2,1)S(1)}, u32[]{:S(2)}, u32[]{:S(2)}) collective-permute-start(bf16[136,768]{1,0:T(8,128)(2,1)S(1)} %collective-permute-done.5.refs_2_), channel_id=1, source_target_pairs={{0,1},{1,0},{2,3},{3,2},{4,5},{5,4},{6,7},{7,6},{8,9},{9,8},{10,11... | collective-permute-start | bytes 626696 | tf_op jit(solution)/shard_map/ppermute | solution.py:296
  31.9 7.3 %collective-permute-start.4 = (bf16[136,768]{1,0:T(8,128)(2,1)S(1)}, bf16[136,768]{1,0:T(8,128)(2,1)S(1)}, u32[]{:S(2)}, u32[]{:S(2)}) collective-permute-start(bf16[136,768]{1,0:T(8,128)(2,1)S(1)} %collective-permute-done.3.refs_4_), channel_id=1, source_target_pairs={{0,2},{1,3},{2,0},{3,1},{4,6},{5,7},{6,4},{7,5},{8,10},{9,11},{10,... | collective-permute-start | bytes 626696 | tf_op jit(solution)/shard_map/ppermute | solution.py:296
  39.2 1.5 %collective-permute-start.9 = (bf16[136,768]{1,0:T(8,128)(2,1)S(1)}, bf16[136,768]{1,0:T(8,128)(2,1)S(1)}, u32[]{:S(2)}, u32[]{:S(2)}) collective-permute-start(bf16[136,768]{1,0:T(8,128)(2,1)S(1)} %collective-permute-done.4.refs_2_), channel_id=1, source_target_pairs={{0,1},{1,0},{2,3},{3,2},{4,5},{5,4},{6,7},{7,6},{8,9},{9,8},{10,11... | collective-permute-start | bytes 626696 | tf_op jit(solution)/shard_map/ppermute | solution.py:296

commit v8 on v7

--- a/solution.py
+++ b/solution.py
@@ -49,8 +49,14 @@
     return hot.T.astype(BF16)
 
 
+def split_three(x):
+    high = x.astype(BF16).astype(F32)
+    mid = (x - high).astype(BF16).astype(F32)
+    return high, mid, x - high - mid
+
+
 def stage_kernel(
-    count_ref, me_ref, src_ref, cube_ref, bucket_ref, features_ref, tiles_ref,
+    count_ref, me_ref, src_ref, table_ref, bucket_ref, features_ref, tiles_ref,
     bias_ref, own_ref, masked_ref, extra_ref, from_ref, tiles_held, sems,
 ):
     rows = own_ref.shape[0]
@@ -67,17 +73,24 @@
         [bucket_ref[...].astype(F32), jnp.zeros((1, width - rows), F32)], axis=1
     )
     extra_ref[...] = jnp.broadcast_to(extra, (EXTRA, width))
-    scaled = cube_ref[...] * math.sqrt(HD)
-    high = scaled.astype(BF16).astype(F32)
-    rest = scaled - high
-    mid = rest.astype(BF16).astype(F32)
-    low = rest - mid
-    lane = lax.broadcasted_iota(jnp.int32, scaled.shape, 1) % LANES
-    parts = jnp.where(
-        lane < NB, high, jnp.where(lane < 2 * NB, mid, jnp.where(lane < 3 * NB, low, 0.0))
-    )
+    table = table_ref[...] * math.sqrt(HD)
+    at = lax.broadcasted_iota(jnp.int32, (NB, NB * NB), 1) // NB
+    mine = at == lax.broadcasted_iota(jnp.int32, (NB, NB * NB), 0)
+    key = lax.broadcasted_iota(jnp.int32, (NB * NB, LANES), 0) % NB
+    column = lax.broadcasted_iota(jnp.int32, (NB * NB, LANES), 1)
+    cube = jnp.zeros((H * NB, LANES), F32)
+    for number, piece in enumerate(split_three(table)):
+        spread = [jnp.where(mine, piece[h : h + 1, :], 0.0) for h in range(H)]
+        place = jnp.where(column == key + number * NB, 1.0, 0.0).astype(BF16)
+        cube = cube + jnp.dot(
+            jnp.concatenate(spread, axis=0).astype(BF16), place, preferred_element_type=F32
+        )
+    cube = cube.astype(BF16)
     hot = one_hot_slab(bucket_ref[...].astype(F32))[:, :NB]
-    bias_ref[...] = jnp.dot(hot, parts.astype(BF16), preferred_element_type=F32).astype(BF16)
+    for h in range(H):
+        bias_ref[:, h * LANES : (h + 1) * LANES] = jnp.dot(
+            hot, cube[h * NB : (h + 1) * NB, :], preferred_element_type=F32
+        ).astype(BF16)
     for copy in copies:
         copy.wait()
     for t in range(TILES):
@@ -184,13 +197,9 @@
     def keep_peak(half, h, peak):
         if first:
             at = pl.ds(pl.multiple_of((half * SET + h) * LANES, LANES), LANES)
-            high = (-peak).astype(BF16).astype(F32)
-            rest = -peak - high
-            mid = rest.astype(BF16).astype(F32)
-            low = rest - mid
-            mark = jnp.where(
-                lane == SHIFT, high, jnp.where(lane == SHIFT + 1, mid, jnp.where(lane == SHIFT + 2, low, 0.0))
-            )
+            mark = jnp.zeros((rows, LANES), F32)
+            for number, piece in enumerate(split_three(-peak)):
+                mark = jnp.where(lane == SHIFT + number, piece, mark)
             shifted_ref[:, at] = bias_ref[:, at] + mark.astype(BF16)
         else:
             top_ref[h * rows : (h + 1) * rows, :] = jnp.broadcast_to(peak, (rows, LANES))
@@ -273,7 +282,7 @@
         outs = [state] * 3
     operands = [w_qk, w_v, *blocks, *inputs]
     tall = SET * rows
-    need = 8 * tall * keys * 2 + 4 * keys * width + 4 * tall * LANES
+    need = 2 * tall * keys + 4 * keys * width + 4 * tall * LANES
     return pl.pallas_call(
         lambda *refs: part_kernel(len(blocks), first, last, *refs),
         out_shape=outs,
@@ -286,8 +295,8 @@
             pltpu.VMEM((tall, keys), BF16),
             pltpu.VMEM((tall, LANES), F32),
         ],
-        compiler_params=limit(need // MIB + 12),
-        cost_estimate=pl.CostEstimate(flops=1000, bytes_accessed=1000, transcendentals=0),
+        compiler_params=limit(need // MIB + 8),
+        cost_estimate=pl.CostEstimate(flops=10**9, bytes_accessed=4_000_000, transcendentals=0),
         name="part",
     )(*operands)
 
@@ -310,9 +319,6 @@
     received = [swap(features, "group", d) for d in range(groups - 1, 0, -1)][::-1]
     own_bucket = node_bucket.reshape(1, rows)
 
-    cube = bias_table.reshape(H, NB, NB).transpose(1, 0, 2)
-    cube = jnp.concatenate([cube, cube, cube, jnp.zeros((NB, H, LANES - 3 * NB), F32)], axis=2)
-    cube = cube.reshape(NB, H * LANES)
     bias, own_features, masked, extra, source = pl.pallas_call(
         stage_kernel,
         out_shape=[
@@ -323,10 +329,10 @@
         in_specs=[smem()] * 3 + [vmem(), vmem(), any_space, any_space],
         out_specs=[vmem()] * 5,
         scratch_shapes=[pltpu.VMEM((rows, TILES * rows), BF16), pltpu.SemaphoreType.DMA((2,))],
-        compiler_params=limit(16),
-        cost_estimate=pl.CostEstimate(flops=1000, bytes_accessed=1000, transcendentals=0),
+        compiler_params=limit(8),
+        cost_estimate=pl.CostEstimate(flops=10**9, bytes_accessed=4_000_000, transcendentals=0),
         name="stage",
-    )(tile_count, lax.axis_index("group").reshape(1), tile_src, cube, own_bucket, features, tiles)
+    )(tile_count, lax.axis_index("group").reshape(1), tile_src, bias_table, own_bucket, features, tiles)
 
     own = pl.pallas_call(
         aggregate_kernel,
@@ -334,8 +340,8 @@
         in_specs=[vmem()] * (3 + groups),
         out_specs=vmem(),
         scratch_shapes=[pltpu.VMEM((groups * rows, width), BF16)],
-        compiler_params=limit(16),
-        cost_estimate=pl.CostEstimate(flops=1000, bytes_accessed=1000, transcendentals=0),
+        compiler_params=limit(8),
+        cost_estimate=pl.CostEstimate(flops=10**9, bytes_accessed=4_000_000, transcendentals=0),
         name="aggregate",
     )(source, extra, masked, own_features, *received)
 

time: 44.6 us -> 40.5 us (0.908)
  local copies, waits for them, and re-layouts: 8.3 us -> 3.95 us
  waiting for transfers between devices: 8.56 us -> 11.4 us
  other arithmetic: 1.31 us -> 0 us
  Pallas kernels: 14.6 us -> 14 us
  starting transfers between devices: 10.7 us -> 10.2 us
    ppermute x10, waiting for transfers between devices: 8.56 us -> 11.4 us  [swap(): lax.ppermute(array, axis, [(i, i ^ distance) for i in range(lax.axis_size...]
    unnamed x16 -> x14, local copies, waits for them, and re-layouts: 6.49 us -> 3.95 us
    transpose x1 -> x0, local copies, waits for them, and re-layouts: 1.73 us -> none  [on_device(): cube = bias_table.reshape(H, NB, NB).transpose(1, 0, 2)]
    concatenate x1 -> x0, other arithmetic: 1.31 us -> none  [on_device(): jnp.concatenate([cube, cube, cube, jnp.zeros((NB, H, LANES - 3 * NB), F32...]
    pallas_call x1, Pallas kernels: 1.65 us -> 0.54 us  [on_device(): pl.pallas_call(aggregate_kernel, out_shape=shape(rows + EXTRA, width), in...]
    pallas_call x1, Pallas kernels: 1.39 us -> 1.95 us  [on_device(): pl.pallas_call(stage_kernel, out_shape=[shape(rows, H * LANES), shape(row...]
    ppermute x10, starting transfers between devices: 10.7 us -> 10.2 us  [swap(): lax.ppermute(array, axis, [(i, i ^ distance) for i in range(lax.axis_size...]
  transfers between devices with their start and end apart: 10 -> 10, of which waited for: 5 -> 6; matrix products, arithmetic and copies ran while one was open for 12% -> 0% of each run, Pallas kernels for 21% -> 24%
where the time goes in v8:
time: 40.5 us; the launch traced here: 40.3 us
  Pallas kernels  14 us (35%)
  waiting for transfers between devices  11.4 us (28%)
  starting transfers between devices  10.2 us (25%)
  local copies, waits for them, and re-layouts  3.95 us (10%)
  between operations  0.74 us (2%)
    pallas_call x3, Pallas kernels, attend_part(): pl.pallas_call(lambda *refs: part_kernel(len(blocks), first, last, *refs)...  11.5 us
    ppermute x10, waiting for transfers between devices, swap(): lax.ppermute(array, axis, [(i, i ^ distance) for i in range(lax.axis_size...  11.4 us
    ppermute x10, starting transfers between devices, swap(): lax.ppermute(array, axis, [(i, i ^ distance) for i in range(lax.axis_size...  10.2 us
    unnamed x14, local copies, waits for them, and re-layouts  3.95 us
    pallas_call x1, Pallas kernels, on_device(): pl.pallas_call(stage_kernel, out_shape=[shape(rows, H * LANES), shape(row...  1.95 us
  transfers between devices with their start and end apart: 10, of which 6 were waited for; matrix products, arithmetic and copies ran while one was open for 0% of the time, Pallas kernels for 24%

profile of v8, /device:TPU:0, one launch (start us, length us, event | category | flops | bytes accessed | tf_op | source)
XLA Modules:
  0.0 40.3 jit_solution(2884020258832869300)
XLA Ops:
  0.0 2.9 %collective-permute-start = (bf16[128,768]{1,0:T(8,128)(2,1)}, bf16[128,768]{1,0:T(8,128)(2,1)S(1)}, u32[]{:S(2)}, u32[]{:S(2)}) collective-permute-start(bf16[128,768]{1,0:T(8,128)(2,1)} %features_ref.1), channel_id=1, source_target_pairs={{0,8},{8,0},{16,24},{24,16},{1,9},{9,1},{17,25},{25,17},{2,10},{10... | collective-permute-start | bytes 589832 | tf_op jit(solution)/shard_map/ppermute | solution.py:305
  2.9 1.5 %collective-permute-start.1 = (bf16[128,768]{1,0:T(8,128)(2,1)}, bf16[128,768]{1,0:T(8,128)(2,1)S(1)}, u32[]{:S(2)}, u32[]{:S(2)}) collective-permute-start(bf16[128,768]{1,0:T(8,128)(2,1)} %features_ref.1), channel_id=1, source_target_pairs={{0,16},{8,24},{16,0},{24,8},{1,17},{9,25},{17,1},{25,9},{2,18},{10... | collective-permute-start | bytes 589832 | tf_op jit(solution)/shard_map/ppermute | solution.py:305
  4.5 0.0 collective-permute-start.2
  5.1 0.0 copy-start.2
  5.1 0.9 %copy-done.2 = bf16[128,1024]{1,0:T(8,128)(2,1)S(1)} copy-done((bf16[128,1024]{1,0:T(8,128)(2,1)S(1)}, bf16[128,1024]{1,0:T(8,128)(2,1)}, u32[]{:S(2)}) %copy-start.2) | copy-done | bytes 262168
  6.1 0.0 copy-start.3
  6.1 0.9 %copy-done.3 = bf16[128,768]{1,0:T(8,128)(2,1)S(1)} copy-done((bf16[128,768]{1,0:T(8,128)(2,1)S(1)}, bf16[128,768]{1,0:T(8,128)(2,1)}, u32[]{:S(2)}) %copy-start.3) | copy-done | bytes 196632
  7.0 0.0 copy-start.4
  7.0 0.8 %copy-done.4 = f32[32,256]{1,0:T(8,128)S(1)} copy-done((f32[32,256]{1,0:T(8,128)S(1)}, f32[32,256]{1,0:T(8,128)}, u32[]{:S(2)}) %copy-start.4) | copy-done | bytes 32792
  7.8 0.0 copy-start.5
  7.8 0.7 %copy-done.5 = s32[1,8]{1,0:T(1,128)S(1)} copy-done((s32[1,8]{1,0:T(1,128)S(1)}, s32[1,8]{1,0:T(1,128)}, u32[]{:S(2)}) %copy-start.5) | copy-done | bytes 56
  8.4 0.0 copy-start.6
  8.4 0.7 %copy-done.6 = s32[128]{0:T(128)S(1)} copy-done((s32[128]{0:T(128)S(1)}, s32[128]{0:T(128)}, u32[]{:S(2)}) %copy-start.6) | copy-done | bytes 536
  9.1 1.9 %stage.1 = (bf16[128,4096]{1,0:T(8,128)(2,1)S(1)}, bf16[128,768]{1,0:T(8,128)(2,1)S(1)}, bf16[128,1024]{1,0:T(8,128)(2,1)S(1)}, f32[8,768]{1,0:T(8,128)S(1)}, s32[8,128]{1,0:T(8,128)S(1)}) custom-call(s32[1]{0:T(128)S(6)} %copy.9.count_ref, s32[1]{0:T(128)} %bitcast.me_ref, s32[1,8]{1,0:T(1,128)S(1)} %copy-done.5, f32[32,256]{1,0:T(8,128)S(1)} %copy-done.4, ...), custom_call_target="tpu_custom_call" | custom-call | flops 1000000000 | bytes 4000000 | tf_op jit(solution)/shard_map/stage/pallas_call | solution.py:322
  11.0 0.0 copy-start
  11.0 0.0 copy-start.1
  11.0 0.0 collective-permute-done.refs_1_
  11.1 2.7 %collective-permute-done.1.refs_2_ = bf16[128,768]{1,0:T(8,128)(2,1)S(1)} collective-permute-done((bf16[128,768]{1,0:T(8,128)(2,1)}, bf16[128,768]{1,0:T(8,128)(2,1)S(1)}, u32[]{:S(2)}, u32[]{:S(2)}) %collective-permute-start.1) | collective-permute-done | bytes 196640 | tf_op jit(solution)/shard_map/ppermute | solution.py:305
  13.7 0.0 collective-permute-done.2.refs_3_
  13.7 0.5 %aggregate.1.refs_2_ = bf16[136,768]{1,0:T(8,128)(2,1)S(1)} custom-call(s32[8,128]{1,0:T(8,128)S(1)} %get-tuple-element.20.from_ref, f32[8,768]{1,0:T(8,128)S(1)} %get-tuple-element.21.extra_ref, bf16[128,1024]{1,0:T(8,128)(2,1)S(1)} %get-tuple-element.22.masked_ref, bf16[128,768]{1,0:T(8,128)(2,1)S(1)} %get-tuple-element.23.refs_0_, ...), custom_call_target="tpu_custom_call" | custom-call | flops 1000000000 | bytes 4000000 | tf_op jit(solution)/shard_map/aggregate/pallas_call | solution.py:337
  14.3 0.1 collective-permute-start.6
  14.4 2.7 %collective-permute-start.3 = (bf16[136,768]{1,0:T(8,128)(2,1)S(1)}, bf16[136,768]{1,0:T(8,128)(2,1)S(1)}, u32[]{:S(2)}, u32[]{:S(2)}) collective-permute-start(bf16[136,768]{1,0:T(8,128)(2,1)S(1)} %aggregate.1.refs_2_), channel_id=1, source_target_pairs={{0,4},{1,5},{2,6},{3,7},{4,0},{5,1},{6,2},{7,3},{8,12},{9,13},{10,... | collective-permute-start | bytes 626696 | tf_op jit(solution)/shard_map/ppermute | solution.py:305
  17.0 1.6 %collective-permute-start.5 = (bf16[136,768]{1,0:T(8,128)(2,1)S(1)}, bf16[136,768]{1,0:T(8,128)(2,1)S(1)}, u32[]{:S(2)}, u32[]{:S(2)}) collective-permute-start(bf16[136,768]{1,0:T(8,128)(2,1)S(1)} %aggregate.1.refs_2_), channel_id=1, source_target_pairs={{0,2},{1,3},{2,0},{3,1},{4,6},{5,7},{6,4},{7,5},{8,10},{9,11},{10,... | collective-permute-start | bytes 626696 | tf_op jit(solution)/shard_map/ppermute | solution.py:305
  18.6 0.0 collective-permute-done.6.refs_3_
  18.6 0.0 copy-done
  18.6 0.0 copy-done.1
  18.6 3.4 %part.3 = (bf16[128,768]{1,0:T(8,128)(2,1)S(1)}, bf16[128,4096]{1,0:T(8,128)(2,1)S(1)}, f32[128,768]{1,0:T(8,128)S(1)}, f32[128,768]{1,0:T(8,128)S(1)}) custom-call(bf16[768,1536]{1,0:T(8,128)(2,1)S(1)} %copy-done, bf16[768,768]{1,0:T(8,128)(2,1)S(1)} %copy-done.1, bf16[136,768]{1,0:T(8,128)(2,1)S(1)} %aggregate.1.refs_2_, ...), custom_call_target="tpu_custom_call" | custom-call | flops 1000000000 | bytes 4000000 | tf_op jit(solution)/shard_map/part/pallas_call | solution.py:286
  22.0 5.4 %collective-permute-done.3.refs_4_ = bf16[136,768]{1,0:T(8,128)(2,1)S(1)} collective-permute-done((bf16[136,768]{1,0:T(8,128)(2,1)S(1)}, bf16[136,768]{1,0:T(8,128)(2,1)S(1)}, u32[]{:S(2)}, u32[]{:S(2)}) %collective-permute-start.3) | collective-permute-done | bytes 208928 | tf_op jit(solution)/shard_map/ppermute | solution.py:305
  27.4 0.0 collective-permute-start.8
  27.4 0.2 collective-permute-done.5.refs_2_
  27.6 0.3 collective-permute-start.7
  27.9 1.1 %collective-permute-start.4 = (bf16[136,768]{1,0:T(8,128)(2,1)S(1)}, bf16[136,768]{1,0:T(8,128)(2,1)S(1)}, u32[]{:S(2)}, u32[]{:S(2)}) collective-permute-start(bf16[136,768]{1,0:T(8,128)(2,1)S(1)} %collective-permute-done.3.refs_4_), channel_id=1, source_target_pairs={{0,2},{1,3},{2,0},{3,1},{4,6},{5,7},{6,4},{7,5},{8,10},{9,11},{10,... | collective-permute-start | bytes 626696 | tf_op jit(solution)/shard_map/ppermute | solution.py:305
  29.0 0.0 collective-permute-done.8.refs_5_
  29.0 0.1 collective-permute-done.7.refs_3_
  29.2 4.4 %part.4 = (f32[128,768]{1,0:T(8,128)S(1)}, f32[128,768]{1,0:T(8,128)S(1)}, f32[128,768]{1,0:T(8,128)S(1)}) custom-call(bf16[768,1536]{1,0:T(8,128)(2,1)S(1)} %copy-done, bf16[768,768]{1,0:T(8,128)(2,1)S(1)} %copy-done.1, bf16[136,768]{1,0:T(8,128)(2,1)S(1)} %collective-permute-done.5.refs_2_, bf16[136,768]{1,0:T(8,128)(2,1)S(1)} %collective-permute-done.7.refs_3_, ...), custom_call_target="tpu_custom_call" | custom-call | flops 1000000000 | bytes 4000000 | tf_op jit(solution)/shard_map/part/pallas_call | solution.py:286
  33.6 1.6 %collective-permute-done.4.refs_2_ = bf16[136,768]{1,0:T(8,128)(2,1)S(1)} collective-permute-done((bf16[136,768]{1,0:T(8,128)(2,1)S(1)}, bf16[136,768]{1,0:T(8,128)(2,1)S(1)}, u32[]{:S(2)}, u32[]{:S(2)}) %collective-permute-start.4) | collective-permute-done | bytes 208928 | tf_op jit(solution)/shard_map/ppermute | solution.py:305
  35.2 0.0 collective-permute-start.9
  35.2 1.5 %collective-permute-done.9.refs_3_ = bf16[136,768]{1,0:T(8,128)(2,1)S(1)} collective-permute-done((bf16[136,768]{1,0:T(8,128)(2,1)S(1)}, bf16[136,768]{1,0:T(8,128)(2,1)S(1)}, u32[]{:S(2)}, u32[]{:S(2)}) %collective-permute-start.9) | collective-permute-done | bytes 208928 | tf_op jit(solution)/shard_map/ppermute | solution.py:305
  36.6 3.6 %part.5 = bf16[128,768]{1,0:T(8,128)(2,1)} custom-call(bf16[768,1536]{1,0:T(8,128)(2,1)S(1)} %copy-done, bf16[768,768]{1,0:T(8,128)(2,1)S(1)} %copy-done.1, bf16[136,768]{1,0:T(8,128)(2,1)S(1)} %collective-permute-done.4.refs_2_, bf16[136,768]{1,0:T(8,128)(2,1)S(1)} %collective-permute-done.9.refs_3_, ...), custom_call_target="tpu_custom_call" | custom-call | flops 1000000000 | bytes 4000000 | tf_op jit(solution)/shard_map/part/pallas_call | solution.py:286
Async XLA Ops:
  0.0 11.0 %collective-permute-start = (bf16[128,768]{1,0:T(8,128)(2,1)}, bf16[128,768]{1,0:T(8,128)(2,1)S(1)}, u32[]{:S(2)}, u32[]{:S(2)}) collective-permute-start(bf16[128,768]{1,0:T(8,128)(2,1)} %features_ref.1), channel_id=1, source_target_pairs={{0,8},{8,0},{16,24},{24,16},{1,9},{9,1},{17,25},{25,17},{2,10},{10... | collective-permute-start | bytes 589832 | tf_op jit(solution)/shard_map/ppermute | solution.py:305
  2.9 10.8 %collective-permute-start.1 = (bf16[128,768]{1,0:T(8,128)(2,1)}, bf16[128,768]{1,0:T(8,128)(2,1)S(1)}, u32[]{:S(2)}, u32[]{:S(2)}) collective-permute-start(bf16[128,768]{1,0:T(8,128)(2,1)} %features_ref.1), channel_id=1, source_target_pairs={{0,16},{8,24},{16,0},{24,8},{1,17},{9,25},{17,1},{25,9},{2,18},{10... | collective-permute-start | bytes 589832 | tf_op jit(solution)/shard_map/ppermute | solution.py:305
  4.5 9.3 %collective-permute-start.2 = (bf16[128,768]{1,0:T(8,128)(2,1)}, bf16[128,768]{1,0:T(8,128)(2,1)S(1)}, u32[]{:S(2)}, u32[]{:S(2)}) collective-permute-start(bf16[128,768]{1,0:T(8,128)(2,1)} %features_ref.1), channel_id=1, source_target_pairs={{0,24},{8,16},{16,8},{24,0},{1,25},{9,17},{17,9},{25,1},{2,26},{10... | collective-permute-start | bytes 589832 | tf_op jit(solution)/shard_map/ppermute | solution.py:305
  5.1 1.0 %copy-start.2 = (bf16[128,1024]{1,0:T(8,128)(2,1)S(1)}, bf16[128,1024]{1,0:T(8,128)(2,1)}, u32[]{:S(2)}) copy-start(bf16[128,1024]{1,0:T(8,128)(2,1)} %tiles_ref.1) | copy-start | bytes 786436
  6.1 0.9 %copy-start.3 = (bf16[128,768]{1,0:T(8,128)(2,1)S(1)}, bf16[128,768]{1,0:T(8,128)(2,1)}, u32[]{:S(2)}) copy-start(bf16[128,768]{1,0:T(8,128)(2,1)} %features_ref.1) | copy-start | bytes 589828
  7.0 0.8 %copy-start.4 = (f32[32,256]{1,0:T(8,128)S(1)}, f32[32,256]{1,0:T(8,128)}, u32[]{:S(2)}) copy-start(f32[32,256]{1,0:T(8,128)} %table_ref.1) | copy-start | bytes 98308
  7.8 0.7 %copy-start.5 = (s32[1,8]{1,0:T(1,128)S(1)}, s32[1,8]{1,0:T(1,128)}, u32[]{:S(2)}) copy-start(s32[1,8]{1,0:T(1,128)} %src_ref.1) | copy-start | bytes 100
  8.4 0.7 %copy-start.6 = (s32[128]{0:T(128)S(1)}, s32[128]{0:T(128)}, u32[]{:S(2)}) copy-start(s32[128]{0:T(128)} %param.12) | copy-start | bytes 1540
  11.0 7.6 %copy-start = (bf16[768,1536]{1,0:T(8,128)(2,1)S(1)}, bf16[768,1536]{1,0:T(8,128)(2,1)}, u32[]{:S(2)}) copy-start(bf16[768,1536]{1,0:T(8,128)(2,1)} %refs_0_.5) | copy-start | bytes 7077892
  11.0 7.6 %copy-start.1 = (bf16[768,768]{1,0:T(8,128)(2,1)S(1)}, bf16[768,768]{1,0:T(8,128)(2,1)}, u32[]{:S(2)}) copy-start(bf16[768,768]{1,0:T(8,128)(2,1)} %refs_1_.5) | copy-start | bytes 3538948
  14.3 4.3 %collective-permute-start.6 = (bf16[136,768]{1,0:T(8,128)(2,1)S(1)}, bf16[136,768]{1,0:T(8,128)(2,1)S(1)}, u32[]{:S(2)}, u32[]{:S(2)}) collective-permute-start(bf16[136,768]{1,0:T(8,128)(2,1)S(1)} %aggregate.1.refs_2_), channel_id=1, source_target_pairs={{0,1},{1,0},{2,3},{3,2},{4,5},{5,4},{6,7},{7,6},{8,9},{9,8},{10,11... | collective-permute-start | bytes 626696 | tf_op jit(solution)/shard_map/ppermute | solution.py:305
  14.4 13.1 %collective-permute-start.3 = (bf16[136,768]{1,0:T(8,128)(2,1)S(1)}, bf16[136,768]{1,0:T(8,128)(2,1)S(1)}, u32[]{:S(2)}, u32[]{:S(2)}) collective-permute-start(bf16[136,768]{1,0:T(8,128)(2,1)S(1)} %aggregate.1.refs_2_), channel_id=1, source_target_pairs={{0,4},{1,5},{2,6},{3,7},{4,0},{5,1},{6,2},{7,3},{8,12},{9,13},{10,... | collective-permute-start | bytes 626696 | tf_op jit(solution)/shard_map/ppermute | solution.py:305
  17.0 10.6 %collective-permute-start.5 = (bf16[136,768]{1,0:T(8,128)(2,1)S(1)}, bf16[136,768]{1,0:T(8,128)(2,1)S(1)}, u32[]{:S(2)}, u32[]{:S(2)}) collective-permute-start(bf16[136,768]{1,0:T(8,128)(2,1)S(1)} %aggregate.1.refs_2_), channel_id=1, source_target_pairs={{0,2},{1,3},{2,0},{3,1},{4,6},{5,7},{6,4},{7,5},{8,10},{9,11},{10,... | collective-permute-start | bytes 626696 | tf_op jit(solution)/shard_map/ppermute | solution.py:305
  27.4 1.6 %collective-permute-start.8 = (bf16[136,768]{1,0:T(8,128)(2,1)S(1)}, bf16[136,768]{1,0:T(8,128)(2,1)S(1)}, u32[]{:S(2)}, u32[]{:S(2)}) collective-permute-start(bf16[136,768]{1,0:T(8,128)(2,1)S(1)} %collective-permute-done.3.refs_4_), channel_id=1, source_target_pairs={{0,1},{1,0},{2,3},{3,2},{4,5},{5,4},{6,7},{7,6},{8,9},{9,8},{10,11... | collective-permute-start | bytes 626696 | tf_op jit(solution)/shard_map/ppermute | solution.py:305
  27.6 1.6 %collective-permute-start.7 = (bf16[136,768]{1,0:T(8,128)(2,1)S(1)}, bf16[136,768]{1,0:T(8,128)(2,1)S(1)}, u32[]{:S(2)}, u32[]{:S(2)}) collective-permute-start(bf16[136,768]{1,0:T(8,128)(2,1)S(1)} %collective-permute-done.5.refs_2_), channel_id=1, source_target_pairs={{0,1},{1,0},{2,3},{3,2},{4,5},{5,4},{6,7},{7,6},{8,9},{9,8},{10,11... | collective-permute-start | bytes 626696 | tf_op jit(solution)/shard_map/ppermute | solution.py:305
  27.9 7.3 %collective-permute-start.4 = (bf16[136,768]{1,0:T(8,128)(2,1)S(1)}, bf16[136,768]{1,0:T(8,128)(2,1)S(1)}, u32[]{:S(2)}, u32[]{:S(2)}) collective-permute-start(bf16[136,768]{1,0:T(8,128)(2,1)S(1)} %collective-permute-done.3.refs_4_), channel_id=1, source_target_pairs={{0,2},{1,3},{2,0},{3,1},{4,6},{5,7},{6,4},{7,5},{8,10},{9,11},{10,... | collective-permute-start | bytes 626696 | tf_op jit(solution)/shard_map/ppermute | solution.py:305
  35.2 1.5 %collective-permute-start.9 = (bf16[136,768]{1,0:T(8,128)(2,1)S(1)}, bf16[136,768]{1,0:T(8,128)(2,1)S(1)}, u32[]{:S(2)}, u32[]{:S(2)}) collective-permute-start(bf16[136,768]{1,0:T(8,128)(2,1)S(1)} %collective-permute-done.4.refs_2_), channel_id=1, source_target_pairs={{0,1},{1,0},{2,3},{3,2},{4,5},{5,4},{6,7},{7,6},{8,9},{9,8},{10,11... | collective-permute-start | bytes 626696 | tf_op jit(solution)/shard_map/ppermute | solution.py:305

commit v9 on v8

--- a/solution.py
+++ b/solution.py
@@ -16,7 +16,9 @@
 HALF = SET * HD
 SLABS = HALF // LANES
 SAFE = 1e30
+TINY = pl.CostEstimate(flops=1000, bytes_accessed=1000, transcendentals=0)
 EXTRA = 8
+EARLY = 3 * LANES
 SHIFT = 3 * NB
 NT = (((1,), (1,)), ((), ()))
 MIB = 1024 * 1024
@@ -55,24 +57,7 @@
     return high, mid, x - high - mid
 
 
-def stage_kernel(
-    count_ref, me_ref, src_ref, table_ref, bucket_ref, features_ref, tiles_ref,
-    bias_ref, own_ref, masked_ref, extra_ref, from_ref, tiles_held, sems,
-):
-    rows = own_ref.shape[0]
-    copies = [
-        pltpu.make_async_copy(tiles_ref, tiles_held, sems.at[0]),
-        pltpu.make_async_copy(features_ref, own_ref, sems.at[1]),
-    ]
-    for copy in copies:
-        copy.start()
-    for t in range(TILES):
-        from_ref[t : t + 1, :] = jnp.full((1, LANES), src_ref[0, t] ^ me_ref[0], jnp.int32)
-    width = own_ref.shape[1]
-    extra = jnp.concatenate(
-        [bucket_ref[...].astype(F32), jnp.zeros((1, width - rows), F32)], axis=1
-    )
-    extra_ref[...] = jnp.broadcast_to(extra, (EXTRA, width))
+def stage_kernel(bucket_ref, table_ref, bias_ref):
     table = table_ref[...] * math.sqrt(HD)
     at = lax.broadcasted_iota(jnp.int32, (NB, NB * NB), 1) // NB
     mine = at == lax.broadcasted_iota(jnp.int32, (NB, NB * NB), 0)
@@ -91,31 +76,47 @@
         bias_ref[:, h * LANES : (h + 1) * LANES] = jnp.dot(
             hot, cube[h * NB : (h + 1) * NB, :], preferred_element_type=F32
         ).astype(BF16)
-    for copy in copies:
-        copy.wait()
-    for t in range(TILES):
-        tile = tiles_held[:, t * rows : (t + 1) * rows]
-        masked_ref[:, t * rows : (t + 1) * rows] = jnp.where(
-            t < count_ref[0], tile, jnp.zeros_like(tile)
-        )
-
-
-def aggregate_kernel(from_ref, extra_ref, masked_ref, *refs):
-    feature_refs, out_ref, held = refs[:-2], refs[-2], refs[-1]
+
+
+def aggregate(count_ref, me_ref, src_ref, tiles_ref, feature_refs, held):
     rows = feature_refs[0].shape[0]
     for d, ref in enumerate(feature_refs):
         held[d * rows : (d + 1) * rows, :] = ref[...]
-    picked = []
+    picked, masked = [], []
     for t in range(TILES):
-        start = pl.multiple_of(from_ref[t, 0] * rows, rows)
+        start = pl.multiple_of((src_ref[0, t] ^ me_ref[0]) * rows, rows)
         picked.append(held[pl.ds(start, rows), :])
-    total = feature_refs[0][...].astype(F32) + jnp.dot(
-        masked_ref[...], jnp.concatenate(picked, axis=0), preferred_element_type=F32
+        tile = tiles_ref[:, t * rows : (t + 1) * rows]
+        masked.append(jnp.where(t < count_ref[0], tile, jnp.zeros_like(tile)))
+    return feature_refs[0][...].astype(F32) + jnp.dot(
+        jnp.concatenate(masked, axis=1),
+        jnp.concatenate(picked, axis=0),
+        preferred_element_type=F32,
     )
-    mean_square = jnp.mean(total * total, axis=-1, keepdims=True)
-    out_ref[...] = jnp.concatenate(
-        [total * lax.rsqrt(mean_square + 1e-06), extra_ref[...]], axis=0
-    ).astype(BF16)
+
+
+def early_kernel(count_ref, me_ref, src_ref, tiles_ref, *refs):
+    *feature_refs, out_ref, square_ref, held = refs
+    total = aggregate(count_ref, me_ref, src_ref, tiles_ref, feature_refs, held)
+    out_ref[...] = total.astype(BF16)
+    square = jnp.sum(total * total, axis=-1, keepdims=True)
+    square_ref[...] = jnp.broadcast_to(square, square_ref.shape)
+
+
+def late_kernel(count_ref, me_ref, src_ref, tiles_ref, bucket_ref, square_ref, *refs):
+    *feature_refs, out_ref, held = refs
+    total = aggregate(count_ref, me_ref, src_ref, tiles_ref, feature_refs, held)
+    rows, span = total.shape
+    width = span + EARLY
+    square = jnp.sum(total * total, axis=-1, keepdims=True) + square_ref[...]
+    scale = lax.rsqrt(square * (1.0 / width) + 1e-06)
+    turned = scale.T[:EXTRA, :]
+    row = lax.broadcasted_iota(jnp.int32, (EXTRA, rows), 0)
+    below = jnp.where(row == 0, bucket_ref[...].astype(F32), 0.0)
+    for number, piece in enumerate(split_three(turned)):
+        below = jnp.where(row == number + 1, piece, below)
+    below = jnp.concatenate([below, jnp.zeros((EXTRA, span - rows), F32)], axis=1)
+    out_ref[...] = jnp.concatenate([total * scale[:, :1], below], axis=0).astype(BF16)
 
 
 def slab_heads(slab):
@@ -123,7 +124,7 @@
 
 
 def part_kernel(count, first, last, w_qk_ref, w_v_ref, *refs):
-    block_refs, refs = refs[:count], refs[count:]
+    block_refs, refs = refs[: 2 * count], refs[2 * count :]
     hot_ref, k_ref, v_ref, p_ref, *refs_back = refs[-5:]
     top_ref = refs_back[0]
     refs = refs[:-5]
@@ -135,23 +136,29 @@
     rows = q_ref.shape[0]
     keys = hot_ref.shape[0]
     width = w_v_ref.shape[0]
-    arrived = [ref[...] for ref in block_refs]
-    for s, item in enumerate(arrived):
-        bucket = item[rows:, :rows].astype(F32)[:1, :]
-        hot_ref[s * rows : (s + 1) * rows, :] = one_hot_slab(bucket)
-    block = jnp.concatenate([item[:rows, :] for item in arrived], axis=0)
-    if first:
-        for n in range(0, width, 256):
-            q_ref[:, n : n + 256] = jnp.dot(
-                block[:rows, :], w_qk_ref[:, n : n + 256], preferred_element_type=F32
-            ).astype(BF16)
+    early = jnp.concatenate([ref[...] for ref in block_refs[::2]], axis=0)
+    late, scale = [], []
+    for s, ref in enumerate(block_refs[1::2]):
+        item = ref[...]
+        below = item[rows:, :rows].astype(F32)
+        hot_ref[s * rows : (s + 1) * rows, :] = one_hot_slab(below[:1, :])
+        scale.append(jnp.broadcast_to(below[1:2, :] + below[2:3, :] + below[3:4, :], (rows, rows)).T)
+        late.append(item[:rows, :])
+    late = jnp.concatenate(late, axis=0)
+    scale = jnp.concatenate(scale, axis=0)
+    scale = jnp.concatenate([scale, scale], axis=1)
+
+    def project(n, w_ref, base, count):
+        cols = slice(base + n, base + n + 256)
+        one = jnp.dot(early[:count, :], w_ref[:EARLY, cols], preferred_element_type=F32)
+        two = jnp.dot(late[:count, :], w_ref[EARLY:, cols], preferred_element_type=F32)
+        return (one * scale[:count, :] + two).astype(BF16)
+
     for n in range(0, width, 256):
-        k_ref[:, n : n + 256] = jnp.dot(
-            block, w_qk_ref[:, width + n : width + n + 256], preferred_element_type=F32
-        ).astype(BF16)
-        v_ref[:, n : n + 256] = jnp.dot(
-            block, w_v_ref[:, n : n + 256], preferred_element_type=F32
-        ).astype(BF16)
+        if first:
+            q_ref[:, n : n + 256] = project(n, w_qk_ref, 0, rows)
+        k_ref[:, n : n + 256] = project(n, w_qk_ref, width, keys)
+        v_ref[:, n : n + 256] = project(n, w_v_ref, 0, keys)
 
     lane = lax.broadcasted_iota(jnp.int32, (rows, LANES), 1)
     ones = jnp.ones((keys, LANES), BF16)
@@ -271,7 +278,7 @@
 
 def attend_part(first, last, w_qk, w_v, blocks, inputs):
     width = w_v.shape[0]
-    rows = blocks[0].shape[0] - EXTRA
+    rows = blocks[0][0].shape[0]
     keys = rows * len(blocks)
     state = shape(rows, width, dtype=F32)
     if first:
@@ -280,7 +287,7 @@
         outs = [shape(rows, width)]
     else:
         outs = [state] * 3
-    operands = [w_qk, w_v, *blocks, *inputs]
+    operands = [w_qk, w_v, *(piece for block in blocks for piece in block), *inputs]
     tall = SET * rows
     need = 2 * tall * keys + 4 * keys * width + 4 * tall * LANES
     return pl.pallas_call(
@@ -314,62 +321,70 @@
     groups = lax.axis_size("group")
     seq_count = lax.axis_size("seq")
     chips = seq_count // 2
-    any_space = pl.BlockSpec(memory_space=pl.ANY)
-
-    received = [swap(features, "group", d) for d in range(groups - 1, 0, -1)][::-1]
     own_bucket = node_bucket.reshape(1, rows)
-
-    bias, own_features, masked, extra, source = pl.pallas_call(
+    me = lax.axis_index("group").reshape(1)
+
+    def gather(piece):
+        return [piece] + [swap(piece, "group", d) for d in range(1, groups)]
+
+    def hop(pieces, distance):
+        return [swap(piece, "seq", distance) for piece in pieces]
+
+    first_columns = gather(features[:, :EARLY])
+    other_columns = gather(features[:, EARLY:])
+    early, square = pl.pallas_call(
+        early_kernel,
+        out_shape=[shape(rows, EARLY), shape(rows, LANES, dtype=F32)],
+        in_specs=[smem()] * 3 + [vmem()] * (1 + groups),
+        out_specs=[vmem()] * 2,
+        scratch_shapes=[pltpu.VMEM((groups * rows, EARLY), BF16)],
+        compiler_params=limit(8),
+        cost_estimate=pl.CostEstimate(flops=10**9, bytes_accessed=4_000_000, transcendentals=0),
+        name="early",
+    )(tile_count, me, tile_src, tiles, *first_columns)
+    late = pl.pallas_call(
+        late_kernel,
+        out_shape=shape(rows + EXTRA, width - EARLY),
+        in_specs=[smem()] * 3 + [vmem()] * (3 + groups),
+        out_specs=vmem(),
+        scratch_shapes=[pltpu.VMEM((groups * rows, width - EARLY), BF16)],
+        compiler_params=limit(8),
+        cost_estimate=pl.CostEstimate(flops=10**9, bytes_accessed=4_000_000, transcendentals=0),
+        name="late",
+    )(tile_count, me, tile_src, tiles, own_bucket, square, *other_columns)
+    far = [[early, late]] + [None] * (chips - 1)
+    top = 1
+    while 2 * top < chips:
+        top *= 2
+    far[top] = hop(far[0], 2 * top)
+    step = 1
+    while step < top:
+        far[step] = hop(far[0], 2 * step)
+        step *= 2
+    sister = hop(far[0], 1)
+
+    bias = pl.pallas_call(
         stage_kernel,
-        out_shape=[
-            shape(rows, H * LANES), shape(rows, width), shape(rows, TILES * rows),
-            shape(EXTRA, width, dtype=F32),
-            shape(TILES, LANES, dtype=jnp.int32),
-        ],
-        in_specs=[smem()] * 3 + [vmem(), vmem(), any_space, any_space],
-        out_specs=[vmem()] * 5,
-        scratch_shapes=[pltpu.VMEM((rows, TILES * rows), BF16), pltpu.SemaphoreType.DMA((2,))],
+        out_shape=shape(rows, H * LANES),
+        in_specs=[vmem()] * 2,
+        out_specs=vmem(),
         compiler_params=limit(8),
         cost_estimate=pl.CostEstimate(flops=10**9, bytes_accessed=4_000_000, transcendentals=0),
         name="stage",
-    )(tile_count, lax.axis_index("group").reshape(1), tile_src, bias_table, own_bucket, features, tiles)
-
-    own = pl.pallas_call(
-        aggregate_kernel,
-        out_shape=shape(rows + EXTRA, width),
-        in_specs=[vmem()] * (3 + groups),
-        out_specs=vmem(),
-        scratch_shapes=[pltpu.VMEM((groups * rows, width), BF16)],
-        compiler_params=limit(8),
-        cost_estimate=pl.CostEstimate(flops=10**9, bytes_accessed=4_000_000, transcendentals=0),
-        name="aggregate",
-    )(source, extra, masked, own_features, *received)
-
-    far = [own] + [None] * (chips - 1)
-    top = 1
-    while 2 * top < chips:
-        top *= 2
-    far[top] = swap(own, "seq", 2 * top)
-    step = 1
-    while step < top:
-        far[step] = swap(own, "seq", 2 * step)
-        step *= 2
-    for d in range(3, chips):
-        if far[d] is None:
-            far[d] = swap(far[d & (d - 1)], "seq", 2 * (d & -d))
+    )(own_bucket, after(bias_table, sister[0], far[1][0], far[top][0]))
+
     parts = [[0], [1, top]] if top > 1 else [[0, 1]]
     parts += [[d] for d in range(2, chips) if d != top]
     queries, state = [], [bias]
     for number, part in enumerate(parts):
+        if number == 1:
+            for d in range(3, chips):
+                if far[d] is None:
+                    far[d] = hop([after(piece, *state) for piece in far[d & (d - 1)]], 2 * (d & -d))
         blocks = []
         for d in part:
-            block = far[d]
-            if d:
-                block = after(block, *state)
-                near = swap(block, "seq", 1)
-            else:
-                near = swap(own, "seq", 1)
-            blocks += [block, near]
+            pieces = [after(piece, *state) for piece in far[d]] if d else far[0]
+            blocks += [pieces, hop(pieces, 1) if d else sister]
         state = attend_part(
             number == 0, number == len(parts) - 1, w_qk, w_v, blocks, [*queries, *state]
         )

time: 40.5 us -> 42 us (1.037)
  starting transfers between devices: 10.2 us -> 20 us
  waiting for transfers between devices: 11.4 us -> 2.96 us
  Pallas kernels: 14 us -> 15.5 us
  local copies, waits for them, and re-layouts: 3.95 us -> 2.6 us
    ppermute x10 -> x20, starting transfers between devices: 10.2 us -> 20 us  [swap(): lax.ppermute(array, axis, [(i, i ^ distance) for i in range(lax.axis_size...]
    ppermute x10 -> x20, waiting for transfers between devices: 11.4 us -> 2.96 us  [swap(): lax.ppermute(array, axis, [(i, i ^ distance) for i in range(lax.axis_size...]
    unnamed x14 -> x12, local copies, waits for them, and re-layouts: 3.95 us -> 1.63 us
    slice x0 -> x1, local copies, waits for them, and re-layouts: none -> 0.97 us  [on_device(): other_columns = gather(features[:, EARLY:])]
    pallas_call x3, Pallas kernels: 11.5 us -> 12.4 us  [attend_part(): pl.pallas_call(lambda *refs: part_kernel(len(blocks), first, last, *refs)...]
    pallas_call x2 -> x3, Pallas kernels: 2.48 us -> 3.07 us  [the longest x1 1.07 us: on_device(): pl.pallas_call(late_kernel, out_shape=shape(rows + EXTRA, width - EARLY),...]
  transfers between devices with their start and end apart: 10 -> 20, of which waited for: 6 -> 3; matrix products, arithmetic and copies ran while one was open for 0% -> 0% of each run, Pallas kernels for 24% -> 28%
where the time goes in v9:
time: 42 us; the launch traced here: 41.8 us
  starting transfers between devices  20 us (48%)
  Pallas kernels  15.5 us (37%)
  waiting for transfers between devices  2.96 us (7%)
  local copies, waits for them, and re-layouts  2.6 us (6%)
  between operations  0.79 us (2%)
    ppermute x20, starting transfers between devices, swap(): lax.ppermute(array, axis, [(i, i ^ distance) for i in range(lax.axis_size...  20 us
    pallas_call x3, Pallas kernels, attend_part(): pl.pallas_call(lambda *refs: part_kernel(len(blocks), first, last, *refs)...  12.4 us
    ppermute x20, waiting for transfers between devices, swap(): lax.ppermute(array, axis, [(i, i ^ distance) for i in range(lax.axis_size...  2.96 us
    unnamed x12, local copies, waits for them, and re-layouts  1.63 us
    pallas_call x1, Pallas kernels, on_device(): pl.pallas_call(late_kernel, out_shape=shape(rows + EXTRA, width - EARLY),...  1.07 us
    pallas_call x1, Pallas kernels, on_device(): pl.pallas_call(stage_kernel, out_shape=shape(rows, H * LANES), in_specs=[...  1.04 us
    slice x1, local copies, waits for them, and re-layouts, on_device(): other_columns = gather(features[:, EARLY:])  0.97 us
    pallas_call x1, Pallas kernels, on_device(): pl.pallas_call(early_kernel, out_shape=[shape(rows, EARLY), shape(rows, L...  0.96 us
  transfers between devices with their start and end apart: 20, of which 3 were waited for; matrix products, arithmetic and copies ran while one was open for 0% of the time, Pallas kernels for 28%

profile of v9, /device:TPU:0, one launch (start us, length us, event | category | flops | bytes accessed | tf_op | source)
XLA Modules:
  0.0 41.8 jit_solution(3708796373691857838)
XLA Ops:
  0.0 0.0 copy-start.5
  0.0 1.0 %fusion = (bf16[128,384]{1,0:T(8,128)(2,1)S(1)}, bf16[128,384]{1,0:T(8,128)(2,1)S(1)}) fusion(bf16[128,768]{1,0:T(8,128)(2,1)} %param.8), kind=kLoop, calls=%fused_computation | loop fusion | bytes 393216 | tf_op jit(solution)/shard_map/slice | solution.py:334
  1.0 3.0 %collective-permute-start = (bf16[128,384]{1,0:T(8,128)(2,1)S(1)}, bf16[128,384]{1,0:T(8,128)(2,1)S(1)}, u32[]{:S(2)}, u32[]{:S(2)}) collective-permute-start(bf16[128,384]{1,0:T(8,128)(2,1)S(1)} %get-tuple-element.38.refs_0_), channel_id=1, source_target_pairs={{0,8},{8,0},{16,24},{24,16},{1,9},{9,1},{17,25},{25,17},{2,10},{10... | collective-permute-start | bytes 294920 | tf_op jit(solution)/shard_map/ppermute | solution.py:312
  4.0 1.5 %collective-permute-start.1 = (bf16[128,384]{1,0:T(8,128)(2,1)S(1)}, bf16[128,384]{1,0:T(8,128)(2,1)S(1)}, u32[]{:S(2)}, u32[]{:S(2)}) collective-permute-start(bf16[128,384]{1,0:T(8,128)(2,1)S(1)} %get-tuple-element.38.refs_0_), channel_id=1, source_target_pairs={{0,16},{8,24},{16,0},{24,8},{1,17},{9,25},{17,1},{25,9},{2,18},{10... | collective-permute-start | bytes 294920 | tf_op jit(solution)/shard_map/ppermute | solution.py:312
  5.5 0.0 collective-permute-start.2
  5.5 1.9 %collective-permute-start.4 = (bf16[128,384]{1,0:T(8,128)(2,1)S(1)}, bf16[128,384]{1,0:T(8,128)(2,1)S(1)}, u32[]{:S(2)}, u32[]{:S(2)}) collective-permute-start(bf16[128,384]{1,0:T(8,128)(2,1)S(1)} %get-tuple-element.37.refs_0_), channel_id=1, source_target_pairs={{0,8},{8,0},{16,24},{24,16},{1,9},{9,1},{17,25},{25,17},{2,10},{10... | collective-permute-start | bytes 294920 | tf_op jit(solution)/shard_map/ppermute | solution.py:312
  7.5 1.5 %collective-permute-start.5 = (bf16[128,384]{1,0:T(8,128)(2,1)S(1)}, bf16[128,384]{1,0:T(8,128)(2,1)S(1)}, u32[]{:S(2)}, u32[]{:S(2)}) collective-permute-start(bf16[128,384]{1,0:T(8,128)(2,1)S(1)} %get-tuple-element.37.refs_0_), channel_id=1, source_target_pairs={{0,16},{8,24},{16,0},{24,8},{1,17},{9,25},{17,1},{25,9},{2,18},{10... | collective-permute-start | bytes 294920 | tf_op jit(solution)/shard_map/ppermute | solution.py:312
  9.0 0.0 collective-permute-done.refs_1_
  9.0 1.3 %collective-permute-start.6 = (bf16[128,384]{1,0:T(8,128)(2,1)S(1)}, bf16[128,384]{1,0:T(8,128)(2,1)S(1)}, u32[]{:S(2)}, u32[]{:S(2)}) collective-permute-start(bf16[128,384]{1,0:T(8,128)(2,1)S(1)} %get-tuple-element.37.refs_0_), channel_id=1, source_target_pairs={{0,24},{8,16},{16,8},{24,0},{1,25},{9,17},{17,9},{25,1},{2,26},{10... | collective-permute-start | bytes 294920 | tf_op jit(solution)/shard_map/ppermute | solution.py:312
  11.0 0.0 collective-permute-done.1.refs_2_
  11.0 1.2 %collective-permute-done.2.refs_3_ = bf16[128,384]{1,0:T(8,128)(2,1)S(1)} collective-permute-done((bf16[128,384]{1,0:T(8,128)(2,1)S(1)}, bf16[128,384]{1,0:T(8,128)(2,1)S(1)}, u32[]{:S(2)}, u32[]{:S(2)}) %collective-permute-start.2) | collective-permute-done | bytes 98336 | tf_op jit(solution)/shard_map/ppermute | solution.py:312
  12.1 0.0 copy-start.2
  12.1 0.9 %copy-done.2 = bf16[128,1024]{1,0:T(8,128)(2,1)S(1)} copy-done((bf16[128,1024]{1,0:T(8,128)(2,1)S(1)}, bf16[128,1024]{1,0:T(8,128)(2,1)}, u32[]{:S(2)}) %copy-start.2) | copy-done | bytes 262168
  13.1 0.0 copy-start.4
  13.1 0.7 %copy-done.4 = s32[1,8]{1,0:T(1,128)S(1)} copy-done((s32[1,8]{1,0:T(1,128)S(1)}, s32[1,8]{1,0:T(1,128)}, u32[]{:S(2)}) %copy-start.4) | copy-done | bytes 56
  13.7 1.0 %early.1 = (bf16[128,384]{1,0:T(8,128)(2,1)S(1)}, f32[128,128]{1,0:T(8,128)S(1)}) custom-call(s32[1]{0:T(128)S(6)} %copy.9.count_ref, s32[1]{0:T(128)} %bitcast.me_ref, s32[1,8]{1,0:T(1,128)S(1)} %copy-done.4, bf16[128,1024]{1,0:T(8,128)(2,1)S(1)} %copy-done.2, bf16[128,384]{1,0:T(8,128)(2,1)S(1)} %get-tuple-element.38.refs_0_, ...), custom_call_target="tpu_custom_call" | custom-call | flops 1000000000 | bytes 4000000 | tf_op jit(solution)/shard_map/early/pallas_call | solution.py:335
  14.7 0.0 copy-start.3
  14.7 2.6 %collective-permute-start.3 = (bf16[128,384]{1,0:T(8,128)(2,1)S(1)}, bf16[128,384]{1,0:T(8,128)(2,1)S(1)}, u32[]{:S(2)}, u32[]{:S(2)}) collective-permute-start(bf16[128,384]{1,0:T(8,128)(2,1)S(1)} %get-tuple-element.21.refs_2_), channel_id=1, source_target_pairs={{0,4},{1,5},{2,6},{3,7},{4,0},{5,1},{6,2},{7,3},{8,12},{9,13},{10,... | collective-permute-start | bytes 294920 | tf_op jit(solution)/shard_map/ppermute | solution.py:312
  17.4 0.0 collective-permute-start.7
  17.4 0.0 collective-permute-done.4.refs_1_
  17.4 1.6 %collective-permute-start.9 = (bf16[128,384]{1,0:T(8,128)(2,1)S(1)}, bf16[128,384]{1,0:T(8,128)(2,1)S(1)}, u32[]{:S(2)}, u32[]{:S(2)}) collective-permute-start(bf16[128,384]{1,0:T(8,128)(2,1)S(1)} %get-tuple-element.21.refs_2_), channel_id=1, source_target_pairs={{0,2},{1,3},{2,0},{3,1},{4,6},{5,7},{6,4},{7,5},{8,10},{9,11},{10,... | collective-permute-start | bytes 294920 | tf_op jit(solution)/shard_map/ppermute | solution.py:312
  18.9 0.0 collective-permute-done.5.refs_2_
  18.9 0.0 collective-permute-done.6.refs_3_
  18.9 0.0 copy-done.5
  19.0 1.1 %late.1.refs_3_ = bf16[136,384]{1,0:T(8,128)(2,1)S(1)} custom-call(s32[1]{0:T(128)S(6)} %copy.9.count_ref, s32[1]{0:T(128)} %bitcast.me_ref, s32[1,8]{1,0:T(1,128)S(1)} %copy-done.4, bf16[128,1024]{1,0:T(8,128)(2,1)S(1)} %copy-done.2, s32[1,128]{1,0:T(1,128)S(1)} %bitcast.2, f32[128,128]{1,0:T(8,128)S(1)} %get-tuple-element.22.square_ref, ...), custom_call_target="tpu_custom_call" | custom-call | flops 1000000000 | bytes 4000000 | tf_op jit(solution)/shard_map/late/pallas_call | solution.py:345
  20.0 0.0 copy-start
  20.0 0.0 copy-start.1
  20.1 0.3 collective-permute-start.8
  20.3 0.3 collective-permute-start.14
  20.7 0.0 collective-permute-done.3.refs_6_
  20.7 2.2 %collective-permute-start.11 = (bf16[136,384]{1,0:T(8,128)(2,1)S(1)}, bf16[136,384]{1,0:T(8,128)(2,1)S(1)}, u32[]{:S(2)}, u32[]{:S(2)}) collective-permute-start(bf16[136,384]{1,0:T(8,128)(2,1)S(1)} %late.1.refs_3_), channel_id=1, source_target_pairs={{0,2},{1,3},{2,0},{3,1},{4,6},{5,7},{6,4},{7,5},{8,10},{9,11},{10,... | collective-permute-start | bytes 313352 | tf_op jit(solution)/shard_map/ppermute | solution.py:312
  22.9 0.0 collective-permute-done.7.refs_4_
  22.9 0.0 collective-permute-done.9.refs_2_
  22.9 0.0 copy-done.3
  22.9 1.0 %stage.1.refs_6_ = bf16[128,4096]{1,0:T(8,128)(2,1)S(1)} custom-call(s32[1,128]{1,0:T(1,128)S(1)} %bitcast.3, f32[32,256]{1,0:T(8,128)S(1)} %copy-done.3), custom_call_target="tpu_custom_call" | custom-call | flops 1000000000 | bytes 4000000 | tf_op jit(solution)/shard_map/stage/pallas_call | solution.py:366
  24.0 0.0 collective-permute-done.8.refs_5_
  24.0 0.0 copy-done
  24.0 0.0 copy-done.1
  24.0 3.7 %part.3 = (bf16[128,768]{1,0:T(8,128)(2,1)S(1)}, bf16[128,4096]{1,0:T(8,128)(2,1)S(1)}, f32[128,768]{1,0:T(8,128)S(1)}, f32[128,768]{1,0:T(8,128)S(1)}) custom-call(bf16[768,1536]{1,0:T(8,128)(2,1)S(1)} %copy-done, bf16[768,768]{1,0:T(8,128)(2,1)S(1)} %copy-done.1, bf16[128,384]{1,0:T(8,128)(2,1)S(1)} %get-tuple-element.21.refs_2_, ...), custom_call_target="tpu_custom_call" | custom-call | flops 1000000000 | bytes 4000000 | tf_op jit(solution)/shard_map/part/pallas_call | solution.py:293
  27.7 0.8 %collective-permute-done.14.refs_7_ = bf16[136,384]{1,0:T(8,128)(2,1)S(1)} collective-permute-done((bf16[136,384]{1,0:T(8,128)(2,1)S(1)}, bf16[136,384]{1,0:T(8,128)(2,1)S(1)}, u32[]{:S(2)}, u32[]{:S(2)}) %collective-permute-start.14) | collective-permute-done | bytes 104480 | tf_op jit(solution)/shard_map/ppermute | solution.py:312
  28.5 0.0 collective-permute-start.16
  28.5 0.0 collective-permute-done.11.refs_3_
  28.5 0.5 %collective-permute-start.13 = (bf16[136,384]{1,0:T(8,128)(2,1)S(1)}, bf16[136,384]{1,0:T(8,128)(2,1)S(1)}, u32[]{:S(2)}, u32[]{:S(2)}) collective-permute-start(bf16[136,384]{1,0:T(8,128)(2,1)S(1)} %collective-permute-done.11.refs_3_), channel_id=1, source_target_pairs={{0,1},{1,0},{2,3},{3,2},{4,5},{5,4},{6,7},{7,6},{8,9},{9,8},{10,11... | collective-permute-start | bytes 313352 | tf_op jit(solution)/shard_map/ppermute | solution.py:312
  29.0 0.0 collective-permute-start.12
  29.1 0.5 %collective-permute-start.15 = (bf16[128,384]{1,0:T(8,128)(2,1)S(1)}, bf16[128,384]{1,0:T(8,128)(2,1)S(1)}, u32[]{:S(2)}, u32[]{:S(2)}) collective-permute-start(bf16[128,384]{1,0:T(8,128)(2,1)S(1)} %collective-permute-done.3.refs_6_), channel_id=1, source_target_pairs={{0,1},{1,0},{2,3},{3,2},{4,5},{5,4},{6,7},{7,6},{8,9},{9,8},{10,11... | collective-permute-start | bytes 294920 | tf_op jit(solution)/shard_map/ppermute | solution.py:312
  29.5 0.9 %collective-permute-start.17 = (bf16[136,384]{1,0:T(8,128)(2,1)S(1)}, bf16[136,384]{1,0:T(8,128)(2,1)S(1)}, u32[]{:S(2)}, u32[]{:S(2)}) collective-permute-start(bf16[136,384]{1,0:T(8,128)(2,1)S(1)} %collective-permute-done.14.refs_7_), channel_id=1, source_target_pairs={{0,2},{1,3},{2,0},{3,1},{4,6},{5,7},{6,4},{7,5},{8,10},{9,11},{10,... | collective-permute-start | bytes 313352 | tf_op jit(solution)/shard_map/ppermute | solution.py:312
  30.4 0.0 collective-permute-done.12.refs_4_
  30.4 1.2 %collective-permute-start.10 = (bf16[128,384]{1,0:T(8,128)(2,1)S(1)}, bf16[128,384]{1,0:T(8,128)(2,1)S(1)}, u32[]{:S(2)}, u32[]{:S(2)}) collective-permute-start(bf16[128,384]{1,0:T(8,128)(2,1)S(1)} %collective-permute-done.3.refs_6_), channel_id=1, source_target_pairs={{0,2},{1,3},{2,0},{3,1},{4,6},{5,7},{6,4},{7,5},{8,10},{9,11},{10,... | collective-permute-start | bytes 294920 | tf_op jit(solution)/shard_map/ppermute | solution.py:312
  31.5 0.0 collective-permute-done.15.refs_8_
  31.5 0.0 collective-permute-done.16.refs_9_
  31.6 0.0 collective-permute-done.13.refs_5_
  31.6 4.9 %part.4 = (f32[128,768]{1,0:T(8,128)S(1)}, f32[128,768]{1,0:T(8,128)S(1)}, f32[128,768]{1,0:T(8,128)S(1)}) custom-call(bf16[768,1536]{1,0:T(8,128)(2,1)S(1)} %copy-done, bf16[768,768]{1,0:T(8,128)(2,1)S(1)} %copy-done.1, bf16[128,384]{1,0:T(8,128)(2,1)S(1)} %collective-permute-done.9.refs_2_, bf16[136,384]{1,0:T(8,128)(2,1)S(1)} %collective-permute-done.11.refs_3_, ...), custom_call_target="tpu_custom_call" | custom-call | flops 1000000000 | bytes 4000000 | tf_op jit(solution)/shard_map/part/pallas_call | solution.py:293
  36.4 0.0 collective-permute-done.17.refs_3_
  36.4 0.1 collective-permute-start.19
  36.5 0.0 collective-permute-done.10.refs_2_
  36.5 0.5 %collective-permute-start.18 = (bf16[128,384]{1,0:T(8,128)(2,1)S(1)}, bf16[128,384]{1,0:T(8,128)(2,1)S(1)}, u32[]{:S(2)}, u32[]{:S(2)}) collective-permute-start(bf16[128,384]{1,0:T(8,128)(2,1)S(1)} %collective-permute-done.10.refs_2_), channel_id=1, source_target_pairs={{0,1},{1,0},{2,3},{3,2},{4,5},{5,4},{6,7},{7,6},{8,9},{9,8},{10,11... | collective-permute-start | bytes 294920 | tf_op jit(solution)/shard_map/ppermute | solution.py:312
  37.0 0.9 %collective-permute-done.18.refs_4_ = bf16[128,384]{1,0:T(8,128)(2,1)S(1)} collective-permute-done((bf16[128,384]{1,0:T(8,128)(2,1)S(1)}, bf16[128,384]{1,0:T(8,128)(2,1)S(1)}, u32[]{:S(2)}, u32[]{:S(2)}) %collective-permute-start.18) | collective-permute-done | bytes 98336 | tf_op jit(solution)/shard_map/ppermute | solution.py:312
  38.0 0.0 collective-permute-done.19.refs_5_
  38.0 3.9 %part.5 = bf16[128,768]{1,0:T(8,128)(2,1)} custom-call(bf16[768,1536]{1,0:T(8,128)(2,1)S(1)} %copy-done, bf16[768,768]{1,0:T(8,128)(2,1)S(1)} %copy-done.1, bf16[128,384]{1,0:T(8,128)(2,1)S(1)} %collective-permute-done.10.refs_2_, bf16[136,384]{1,0:T(8,128)(2,1)S(1)} %collective-permute-done.17.refs_3_, ...), custom_call_target="tpu_custom_call" | custom-call | flops 1000000000 | bytes 4000000 | tf_op jit(solution)/shard_map/part/pallas_call | solution.py:293
Async XLA Ops:
  0.0 18.9 %copy-start.5 = (s32[128]{0:T(128)S(1)}, s32[128]{0:T(128)}, u32[]{:S(2)}) copy-start(s32[128]{0:T(128)} %param.12) | copy-start | bytes 1540
  1.0 8.0 %collective-permute-start = (bf16[128,384]{1,0:T(8,128)(2,1)S(1)}, bf16[128,384]{1,0:T(8,128)(2,1)S(1)}, u32[]{:S(2)}, u32[]{:S(2)}) collective-permute-start(bf16[128,384]{1,0:T(8,128)(2,1)S(1)} %get-tuple-element.38.refs_0_), channel_id=1, source_target_pairs={{0,8},{8,0},{16,24},{24,16},{1,9},{9,1},{17,25},{25,17},{2,10},{10... | collective-permute-start | bytes 294920 | tf_op jit(solution)/shard_map/ppermute | solution.py:312
  4.0 7.0 %collective-permute-start.1 = (bf16[128,384]{1,0:T(8,128)(2,1)S(1)}, bf16[128,384]{1,0:T(8,128)(2,1)S(1)}, u32[]{:S(2)}, u32[]{:S(2)}) collective-permute-start(bf16[128,384]{1,0:T(8,128)(2,1)S(1)} %get-tuple-element.38.refs_0_), channel_id=1, source_target_pairs={{0,16},{8,24},{16,0},{24,8},{1,17},{9,25},{17,1},{25,9},{2,18},{10... | collective-permute-start | bytes 294920 | tf_op jit(solution)/shard_map/ppermute | solution.py:312
  5.5 6.6 %collective-permute-start.2 = (bf16[128,384]{1,0:T(8,128)(2,1)S(1)}, bf16[128,384]{1,0:T(8,128)(2,1)S(1)}, u32[]{:S(2)}, u32[]{:S(2)}) collective-permute-start(bf16[128,384]{1,0:T(8,128)(2,1)S(1)} %get-tuple-element.38.refs_0_), channel_id=1, source_target_pairs={{0,24},{8,16},{16,8},{24,0},{1,25},{9,17},{17,9},{25,1},{2,26},{10... | collective-permute-start | bytes 294920 | tf_op jit(solution)/shard_map/ppermute | solution.py:312
  5.5 11.8 %collective-permute-start.4 = (bf16[128,384]{1,0:T(8,128)(2,1)S(1)}, bf16[128,384]{1,0:T(8,128)(2,1)S(1)}, u32[]{:S(2)}, u32[]{:S(2)}) collective-permute-start(bf16[128,384]{1,0:T(8,128)(2,1)S(1)} %get-tuple-element.37.refs_0_), channel_id=1, source_target_pairs={{0,8},{8,0},{16,24},{24,16},{1,9},{9,1},{17,25},{25,17},{2,10},{10... | collective-permute-start | bytes 294920 | tf_op jit(solution)/shard_map/ppermute | solution.py:312
  7.5 11.5 %collective-permute-start.5 = (bf16[128,384]{1,0:T(8,128)(2,1)S(1)}, bf16[128,384]{1,0:T(8,128)(2,1)S(1)}, u32[]{:S(2)}, u32[]{:S(2)}) collective-permute-start(bf16[128,384]{1,0:T(8,128)(2,1)S(1)} %get-tuple-element.37.refs_0_), channel_id=1, source_target_pairs={{0,16},{8,24},{16,0},{24,8},{1,17},{9,25},{17,1},{25,9},{2,18},{10... | collective-permute-start | bytes 294920 | tf_op jit(solution)/shard_map/ppermute | solution.py:312
  9.0 10.0 %collective-permute-start.6 = (bf16[128,384]{1,0:T(8,128)(2,1)S(1)}, bf16[128,384]{1,0:T(8,128)(2,1)S(1)}, u32[]{:S(2)}, u32[]{:S(2)}) collective-permute-start(bf16[128,384]{1,0:T(8,128)(2,1)S(1)} %get-tuple-element.37.refs_0_), channel_id=1, source_target_pairs={{0,24},{8,16},{16,8},{24,0},{1,25},{9,17},{17,9},{25,1},{2,26},{10... | collective-permute-start | bytes 294920 | tf_op jit(solution)/shard_map/ppermute | solution.py:312
  12.1 1.0 %copy-start.2 = (bf16[128,1024]{1,0:T(8,128)(2,1)S(1)}, bf16[128,1024]{1,0:T(8,128)(2,1)}, u32[]{:S(2)}) copy-start(bf16[128,1024]{1,0:T(8,128)(2,1)} %tiles_ref.3) | copy-start | bytes 786436
  13.1 0.7 %copy-start.4 = (s32[1,8]{1,0:T(1,128)S(1)}, s32[1,8]{1,0:T(1,128)}, u32[]{:S(2)}) copy-start(s32[1,8]{1,0:T(1,128)} %src_ref.3) | copy-start | bytes 100
  14.7 8.2 %copy-start.3 = (f32[32,256]{1,0:T(8,128)S(1)}, f32[32,256]{1,0:T(8,128)}, u32[]{:S(2)}) copy-start(f32[32,256]{1,0:T(8,128)} %table_ref) | copy-start | bytes 98308
  14.7 6.0 %collective-permute-start.3 = (bf16[128,384]{1,0:T(8,128)(2,1)S(1)}, bf16[128,384]{1,0:T(8,128)(2,1)S(1)}, u32[]{:S(2)}, u32[]{:S(2)}) collective-permute-start(bf16[128,384]{1,0:T(8,128)(2,1)S(1)} %get-tuple-element.21.refs_2_), channel_id=1, source_target_pairs={{0,4},{1,5},{2,6},{3,7},{4,0},{5,1},{6,2},{7,3},{8,12},{9,13},{10,... | collective-permute-start | bytes 294920 | tf_op jit(solution)/shard_map/ppermute | solution.py:312
  17.4 5.6 %collective-permute-start.7 = (bf16[128,384]{1,0:T(8,128)(2,1)S(1)}, bf16[128,384]{1,0:T(8,128)(2,1)S(1)}, u32[]{:S(2)}, u32[]{:S(2)}) collective-permute-start(bf16[128,384]{1,0:T(8,128)(2,1)S(1)} %get-tuple-element.21.refs_2_), channel_id=1, source_target_pairs={{0,1},{1,0},{2,3},{3,2},{4,5},{5,4},{6,7},{7,6},{8,9},{9,8},{10,11... | collective-permute-start | bytes 294920 | tf_op jit(solution)/shard_map/ppermute | solution.py:312
  17.4 5.6 %collective-permute-start.9 = (bf16[128,384]{1,0:T(8,128)(2,1)S(1)}, bf16[128,384]{1,0:T(8,128)(2,1)S(1)}, u32[]{:S(2)}, u32[]{:S(2)}) collective-permute-start(bf16[128,384]{1,0:T(8,128)(2,1)S(1)} %get-tuple-element.21.refs_2_), channel_id=1, source_target_pairs={{0,2},{1,3},{2,0},{3,1},{4,6},{5,7},{6,4},{7,5},{8,10},{9,11},{10,... | collective-permute-start | bytes 294920 | tf_op jit(solution)/shard_map/ppermute | solution.py:312
  20.0 3.9 %copy-start = (bf16[768,1536]{1,0:T(8,128)(2,1)S(1)}, bf16[768,1536]{1,0:T(8,128)(2,1)}, u32[]{:S(2)}) copy-start(bf16[768,1536]{1,0:T(8,128)(2,1)} %refs_0_.5) | copy-start | bytes 7077892
  20.0 3.9 %copy-start.1 = (bf16[768,768]{1,0:T(8,128)(2,1)S(1)}, bf16[768,768]{1,0:T(8,128)(2,1)}, u32[]{:S(2)}) copy-start(bf16[768,768]{1,0:T(8,128)(2,1)} %refs_1_.5) | copy-start | bytes 3538948
  20.1 3.9 %collective-permute-start.8 = (bf16[136,384]{1,0:T(8,128)(2,1)S(1)}, bf16[136,384]{1,0:T(8,128)(2,1)S(1)}, u32[]{:S(2)}, u32[]{:S(2)}) collective-permute-start(bf16[136,384]{1,0:T(8,128)(2,1)S(1)} %late.1.refs_3_), channel_id=1, source_target_pairs={{0,1},{1,0},{2,3},{3,2},{4,5},{5,4},{6,7},{7,6},{8,9},{9,8},{10,11... | collective-permute-start | bytes 313352 | tf_op jit(solution)/shard_map/ppermute | solution.py:312
  20.3 8.1 %collective-permute-start.14 = (bf16[136,384]{1,0:T(8,128)(2,1)S(1)}, bf16[136,384]{1,0:T(8,128)(2,1)S(1)}, u32[]{:S(2)}, u32[]{:S(2)}) collective-permute-start(bf16[136,384]{1,0:T(8,128)(2,1)S(1)} %late.1.refs_3_), channel_id=1, source_target_pairs={{0,4},{1,5},{2,6},{3,7},{4,0},{5,1},{6,2},{7,3},{8,12},{9,13},{10,... | collective-permute-start | bytes 313352 | tf_op jit(solution)/shard_map/ppermute | solution.py:312
  20.7 7.8 %collective-permute-start.11 = (bf16[136,384]{1,0:T(8,128)(2,1)S(1)}, bf16[136,384]{1,0:T(8,128)(2,1)S(1)}, u32[]{:S(2)}, u32[]{:S(2)}) collective-permute-start(bf16[136,384]{1,0:T(8,128)(2,1)S(1)} %late.1.refs_3_), channel_id=1, source_target_pairs={{0,2},{1,3},{2,0},{3,1},{4,6},{5,7},{6,4},{7,5},{8,10},{9,11},{10,... | collective-permute-start | bytes 313352 | tf_op jit(solution)/shard_map/ppermute | solution.py:312
  28.5 3.1 %collective-permute-start.16 = (bf16[136,384]{1,0:T(8,128)(2,1)S(1)}, bf16[136,384]{1,0:T(8,128)(2,1)S(1)}, u32[]{:S(2)}, u32[]{:S(2)}) collective-permute-start(bf16[136,384]{1,0:T(8,128)(2,1)S(1)} %collective-permute-done.14.refs_7_), channel_id=1, source_target_pairs={{0,1},{1,0},{2,3},{3,2},{4,5},{5,4},{6,7},{7,6},{8,9},{9,8},{10,11... | collective-permute-start | bytes 313352 | tf_op jit(solution)/shard_map/ppermute | solution.py:312
  28.5 3.0 %collective-permute-start.13 = (bf16[136,384]{1,0:T(8,128)(2,1)S(1)}, bf16[136,384]{1,0:T(8,128)(2,1)S(1)}, u32[]{:S(2)}, u32[]{:S(2)}) collective-permute-start(bf16[136,384]{1,0:T(8,128)(2,1)S(1)} %collective-permute-done.11.refs_3_), channel_id=1, source_target_pairs={{0,1},{1,0},{2,3},{3,2},{4,5},{5,4},{6,7},{7,6},{8,9},{9,8},{10,11... | collective-permute-start | bytes 313352 | tf_op jit(solution)/shard_map/ppermute | solution.py:312
  29.0 1.4 %collective-permute-start.12 = (bf16[128,384]{1,0:T(8,128)(2,1)S(1)}, bf16[128,384]{1,0:T(8,128)(2,1)S(1)}, u32[]{:S(2)}, u32[]{:S(2)}) collective-permute-start(bf16[128,384]{1,0:T(8,128)(2,1)S(1)} %collective-permute-done.9.refs_2_), channel_id=1, source_target_pairs={{0,1},{1,0},{2,3},{3,2},{4,5},{5,4},{6,7},{7,6},{8,9},{9,8},{10,11... | collective-permute-start | bytes 294920 | tf_op jit(solution)/shard_map/ppermute | solution.py:312
  29.1 2.5 %collective-permute-start.15 = (bf16[128,384]{1,0:T(8,128)(2,1)S(1)}, bf16[128,384]{1,0:T(8,128)(2,1)S(1)}, u32[]{:S(2)}, u32[]{:S(2)}) collective-permute-start(bf16[128,384]{1,0:T(8,128)(2,1)S(1)} %collective-permute-done.3.refs_6_), channel_id=1, source_target_pairs={{0,1},{1,0},{2,3},{3,2},{4,5},{5,4},{6,7},{7,6},{8,9},{9,8},{10,11... | collective-permute-start | bytes 294920 | tf_op jit(solution)/shard_map/ppermute | solution.py:312
  29.5 6.9 %collective-permute-start.17 = (bf16[136,384]{1,0:T(8,128)(2,1)S(1)}, bf16[136,384]{1,0:T(8,128)(2,1)S(1)}, u32[]{:S(2)}, u32[]{:S(2)}) collective-permute-start(bf16[136,384]{1,0:T(8,128)(2,1)S(1)} %collective-permute-done.14.refs_7_), channel_id=1, source_target_pairs={{0,2},{1,3},{2,0},{3,1},{4,6},{5,7},{6,4},{7,5},{8,10},{9,11},{10,... | collective-permute-start | bytes 313352 | tf_op jit(solution)/shard_map/ppermute | solution.py:312
  30.4 6.1 %collective-permute-start.10 = (bf16[128,384]{1,0:T(8,128)(2,1)S(1)}, bf16[128,384]{1,0:T(8,128)(2,1)S(1)}, u32[]{:S(2)}, u32[]{:S(2)}) collective-permute-start(bf16[128,384]{1,0:T(8,128)(2,1)S(1)} %collective-permute-done.3.refs_6_), channel_id=1, source_target_pairs={{0,2},{1,3},{2,0},{3,1},{4,6},{5,7},{6,4},{7,5},{8,10},{9,11},{10,... | collective-permute-start | bytes 294920 | tf_op jit(solution)/shard_map/ppermute | solution.py:312
  36.4 1.5 %collective-permute-start.19 = (bf16[136,384]{1,0:T(8,128)(2,1)S(1)}, bf16[136,384]{1,0:T(8,128)(2,1)S(1)}, u32[]{:S(2)}, u32[]{:S(2)}) collective-permute-start(bf16[136,384]{1,0:T(8,128)(2,1)S(1)} %collective-permute-done.17.refs_3_), channel_id=1, source_target_pairs={{0,1},{1,0},{2,3},{3,2},{4,5},{5,4},{6,7},{7,6},{8,9},{9,8},{10,11... | collective-permute-start | bytes 313352 | tf_op jit(solution)/shard_map/ppermute | solution.py:312
  36.5 1.4 %collective-permute-start.18 = (bf16[128,384]{1,0:T(8,128)(2,1)S(1)}, bf16[128,384]{1,0:T(8,128)(2,1)S(1)}, u32[]{:S(2)}, u32[]{:S(2)}) collective-permute-start(bf16[128,384]{1,0:T(8,128)(2,1)S(1)} %collective-permute-done.10.refs_2_), channel_id=1, source_target_pairs={{0,1},{1,0},{2,3},{3,2},{4,5},{5,4},{6,7},{7,6},{8,9},{9,8},{10,11... | collective-permute-start | bytes 294920 | tf_op jit(solution)/shard_map/ppermute | solution.py:312

commit v10 on v8

--- a/solution.py
+++ b/solution.py
@@ -124,9 +124,9 @@
 
 def part_kernel(count, first, last, w_qk_ref, w_v_ref, *refs):
     block_refs, refs = refs[:count], refs[count:]
-    hot_ref, k_ref, v_ref, p_ref, *refs_back = refs[-5:]
+    hot_ref, k_ref, v_ref, p_refs, *refs_back = *refs[-6:-3], refs[-3:-1], refs[-1]
     top_ref = refs_back[0]
-    refs = refs[:-5]
+    refs = refs[:-6]
     if first:
         bias_ref, q_ref, shifted_ref, *outs = refs
     else:
@@ -156,8 +156,11 @@
     lane = lax.broadcasted_iota(jnp.int32, (rows, LANES), 1)
     ones = jnp.ones((keys, LANES), BF16)
 
+    def span(start, size):
+        return pl.ds(start if isinstance(start, int) else pl.multiple_of(start, LANES), size)
+
     def scores(half, slab):
-        cols = pl.ds(pl.multiple_of(half * HALF + slab * LANES, LANES), LANES)
+        cols = span(half * HALF + slab * LANES, LANES)
         begin, end = slab_heads(slab)
         q = q_ref[:, cols]
         zero = jnp.zeros_like(q)
@@ -166,8 +169,7 @@
             inside = (lane >= h * HD - slab * LANES) & (lane < (h + 1) * HD - slab * LANES)
             lefts.append(jnp.where(inside, q, zero))
             if h * HD >= slab * LANES:
-                at = pl.multiple_of((half * SET + h) * LANES, LANES)
-                rights.append(bias_ref[:, pl.ds(at, LANES)])
+                rights.append(bias_ref[:, span((half * SET + h) * LANES, LANES)])
             else:
                 rights.append(zero)
         query = jnp.concatenate(
@@ -176,27 +178,24 @@
         key = jnp.concatenate([k_ref[:, cols], hot_ref[...]], axis=1)
         return lax.dot_general(query, key, NT, preferred_element_type=F32)
 
-    def weigh(half, local):
-        carried = None
-        for slab in range(SLABS):
-            begin, end = slab_heads(slab)
-            x = scores(half, slab)
-            for h in range(begin, end + 1):
-                own = x[(h - begin) * rows : (h - begin + 1) * rows, :]
-                if h * HD < slab * LANES:
-                    own = own + carried
-                if (h + 1) * HD > (slab + 1) * LANES:
-                    carried = own
-                    continue
-                if local:
-                    peak = jnp.max(own, axis=-1, keepdims=True)
-                    own = own - peak
-                    keep_peak(half, h, peak)
-                p_ref[h * rows : (h + 1) * rows, :] = jnp.exp2(own * FACTOR).astype(BF16)
+    def weigh(half, slab, x, carried, p_ref, local):
+        begin, end = slab_heads(slab)
+        for h in range(begin, end + 1):
+            own = x[(h - begin) * rows : (h - begin + 1) * rows, :]
+            if h * HD < slab * LANES:
+                own = own + carried
+            if (h + 1) * HD > (slab + 1) * LANES:
+                return own
+            if local:
+                peak = jnp.max(own, axis=-1, keepdims=True)
+                own = own - peak
+                keep_peak(half, h, peak)
+            p_ref[h * rows : (h + 1) * rows, :] = jnp.exp2(own * FACTOR).astype(BF16)
+        return None
 
     def keep_peak(half, h, peak):
         if first:
-            at = pl.ds(pl.multiple_of((half * SET + h) * LANES, LANES), LANES)
+            at = span((half * SET + h) * LANES, LANES)
             mark = jnp.zeros((rows, LANES), F32)
             for number, piece in enumerate(split_three(-peak)):
                 mark = jnp.where(lane == SHIFT + number, piece, mark)
@@ -212,8 +211,8 @@
             out = jnp.where(lane >= h * HD - slab * LANES, piece, out)
         return out
 
-    def mix(half, slab):
-        cols = pl.ds(pl.multiple_of(half * HALF + slab * LANES, LANES), LANES)
+    def mix(half, slab, p_ref):
+        cols = span(half * HALF + slab * LANES, LANES)
         begin, end = slab_heads(slab)
         value = jnp.concatenate([v_ref[:, cols], ones], axis=1)
         mixed = jnp.dot(
@@ -221,24 +220,32 @@
         )
         return cols, pick(mixed[:, :LANES], slab, begin), pick(mixed[:, LANES:], slab, begin)
 
-    def fast(half, largest):
-        weigh(half, first)
-        for slab in range(SLABS):
-            cols, top, total = mix(half, slab)
+    def add(half, slab, p_ref):
+        cols, top, total = mix(half, slab, p_ref)
+        if not first:
+            top = top + old_refs[0][:, cols]
+            total = total + old_refs[1][:, cols]
+        if last:
+            outs[0][:, cols] = (top / total).astype(BF16)
+        else:
+            outs[0][:, cols] = top
+            outs[1][:, cols] = total
             if not first:
-                top = top + old_refs[0][:, cols]
-                total = total + old_refs[1][:, cols]
-            largest = jnp.maximum(largest, total)
-            if last:
-                outs[0][:, cols] = (top / total).astype(BF16)
-            else:
-                outs[0][:, cols] = top
-                outs[1][:, cols] = total
-                if not first:
-                    outs[2][:, cols] = jnp.zeros_like(top)
-        return largest
-
-    largest = lax.fori_loop(0, width // HALF, fast, jnp.zeros((rows, LANES), F32))
+                outs[2][:, cols] = jnp.zeros_like(top)
+        return total
+
+    steps = [divmod(step, SLABS) for step in range(width // LANES)]
+    largest = jnp.zeros((rows, LANES), F32)
+    x = scores(*steps[0])
+    carried = None
+    for number, (half, slab) in enumerate(steps):
+        ahead = scores(*steps[number + 1]) if number + 1 < len(steps) else None
+        carried = weigh(half, slab, x, carried, p_refs[half % 2], first)
+        if number:
+            before = steps[number - 1]
+            largest = jnp.maximum(largest, add(*before, p_refs[before[0] % 2]))
+        x = ahead
+    largest = jnp.maximum(largest, add(*steps[-1], p_refs[steps[-1][0] % 2]))
     if first:
         return
     fine = jnp.max(largest) < SAFE
@@ -248,9 +255,11 @@
     @pl.when(jnp.logical_not(fine))
     def _():
         def careful(half, carry):
-            weigh(half, True)
+            left = None
             for slab in range(SLABS):
-                cols, top, total = mix(half, slab)
+                left = weigh(half, slab, scores(half, slab), left, p_refs[0], True)
+            for slab in range(SLABS):
+                cols, top, total = mix(half, slab, p_refs[0])
                 peak = pick(top_ref[...], slab, 0)
                 old = old_refs[2][:, cols] if len(old_refs) == 3 else jnp.zeros_like(top)
                 best = jnp.maximum(old, peak)
@@ -282,7 +291,7 @@
         outs = [state] * 3
     operands = [w_qk, w_v, *blocks, *inputs]
     tall = SET * rows
-    need = 2 * tall * keys + 4 * keys * width + 4 * tall * LANES
+    need = 4 * tall * keys + 4 * keys * width + 4 * tall * LANES
     return pl.pallas_call(
         lambda *refs: part_kernel(len(blocks), first, last, *refs),
         out_shape=outs,
@@ -292,6 +301,7 @@
             pltpu.VMEM((keys, LANES), BF16),
             pltpu.VMEM((keys, width), BF16),
             pltpu.VMEM((keys, width), BF16),
+            pltpu.VMEM((tall, keys), BF16),
             pltpu.VMEM((tall, keys), BF16),
             pltpu.VMEM((tall, LANES), F32),
         ],

time: 40.5 us -> 39.9 us (0.985)
  Pallas kernels: 14 us -> 12.6 us
  waiting for transfers between devices: 11.4 us -> 12.1 us
    pallas_call x3, Pallas kernels: 11.5 us -> 10.2 us  [attend_part(): pl.pallas_call(lambda *refs: part_kernel(len(blocks), first, last, *refs)...]
    ppermute x10, waiting for transfers between devices: 11.4 us -> 12.1 us  [swap(): lax.ppermute(array, axis, [(i, i ^ distance) for i in range(lax.axis_size...]
  transfers between devices with their start and end apart: 10 -> 10, of which waited for: 6 -> 6; matrix products, arithmetic and copies ran while one was open for 0% -> 0% of each run, Pallas kernels for 24% -> 23%
where the time goes in v10:
time: 39.9 us; the launch traced here: 39.6 us
  Pallas kernels  12.6 us (32%)
  waiting for transfers between devices  12.1 us (30%)
  starting transfers between devices  10.2 us (26%)
  local copies, waits for them, and re-layouts  3.95 us (10%)
  between operations  0.73 us (2%)
    ppermute x10, waiting for transfers between devices, swap(): lax.ppermute(array, axis, [(i, i ^ distance) for i in range(lax.axis_size...  12.1 us
    ppermute x10, starting transfers between devices, swap(): lax.ppermute(array, axis, [(i, i ^ distance) for i in range(lax.axis_size...  10.2 us
    pallas_call x3, Pallas kernels, attend_part(): pl.pallas_call(lambda *refs: part_kernel(len(blocks), first, last, *refs)...  10.2 us
    unnamed x14, local copies, waits for them, and re-layouts  3.95 us
    pallas_call x1, Pallas kernels, on_device(): pl.pallas_call(stage_kernel, out_shape=[shape(rows, H * LANES), shape(row...  1.95 us
  transfers between devices with their start and end apart: 10, of which 6 were waited for; matrix products, arithmetic and copies ran while one was open for 0% of the time, Pallas kernels for 23%

profile of v10, /device:TPU:0, one launch (start us, length us, event | category | flops | bytes accessed | tf_op | source)
XLA Modules:
  0.0 39.6 jit_solution(12432214130667944972)
XLA Ops:
  0.0 2.9 %collective-permute-start = (bf16[128,768]{1,0:T(8,128)(2,1)}, bf16[128,768]{1,0:T(8,128)(2,1)S(1)}, u32[]{:S(2)}, u32[]{:S(2)}) collective-permute-start(bf16[128,768]{1,0:T(8,128)(2,1)} %features_ref.1), channel_id=1, source_target_pairs={{0,8},{8,0},{16,24},{24,16},{1,9},{9,1},{17,25},{25,17},{2,10},{10... | collective-permute-start | bytes 589832 | tf_op jit(solution)/shard_map/ppermute | solution.py:315
  2.9 1.5 %collective-permute-start.1 = (bf16[128,768]{1,0:T(8,128)(2,1)}, bf16[128,768]{1,0:T(8,128)(2,1)S(1)}, u32[]{:S(2)}, u32[]{:S(2)}) collective-permute-start(bf16[128,768]{1,0:T(8,128)(2,1)} %features_ref.1), channel_id=1, source_target_pairs={{0,16},{8,24},{16,0},{24,8},{1,17},{9,25},{17,1},{25,9},{2,18},{10... | collective-permute-start | bytes 589832 | tf_op jit(solution)/shard_map/ppermute | solution.py:315
  4.5 0.0 collective-permute-start.2
  5.1 0.0 copy-start.2
  5.1 0.9 %copy-done.2 = bf16[128,1024]{1,0:T(8,128)(2,1)S(1)} copy-done((bf16[128,1024]{1,0:T(8,128)(2,1)S(1)}, bf16[128,1024]{1,0:T(8,128)(2,1)}, u32[]{:S(2)}) %copy-start.2) | copy-done | bytes 262168
  6.1 0.0 copy-start.3
  6.1 0.9 %copy-done.3 = bf16[128,768]{1,0:T(8,128)(2,1)S(1)} copy-done((bf16[128,768]{1,0:T(8,128)(2,1)S(1)}, bf16[128,768]{1,0:T(8,128)(2,1)}, u32[]{:S(2)}) %copy-start.3) | copy-done | bytes 196632
  7.0 0.0 copy-start.4
  7.0 0.8 %copy-done.4 = f32[32,256]{1,0:T(8,128)S(1)} copy-done((f32[32,256]{1,0:T(8,128)S(1)}, f32[32,256]{1,0:T(8,128)}, u32[]{:S(2)}) %copy-start.4) | copy-done | bytes 32792
  7.8 0.0 copy-start.5
  7.8 0.7 %copy-done.5 = s32[1,8]{1,0:T(1,128)S(1)} copy-done((s32[1,8]{1,0:T(1,128)S(1)}, s32[1,8]{1,0:T(1,128)}, u32[]{:S(2)}) %copy-start.5) | copy-done | bytes 56
  8.4 0.0 copy-start.6
  8.4 0.7 %copy-done.6 = s32[128]{0:T(128)S(1)} copy-done((s32[128]{0:T(128)S(1)}, s32[128]{0:T(128)}, u32[]{:S(2)}) %copy-start.6) | copy-done | bytes 536
  9.1 1.9 %stage.1 = (bf16[128,4096]{1,0:T(8,128)(2,1)S(1)}, bf16[128,768]{1,0:T(8,128)(2,1)S(1)}, bf16[128,1024]{1,0:T(8,128)(2,1)S(1)}, f32[8,768]{1,0:T(8,128)S(1)}, s32[8,128]{1,0:T(8,128)S(1)}) custom-call(s32[1]{0:T(128)S(6)} %copy.9.count_ref, s32[1]{0:T(128)} %bitcast.me_ref, s32[1,8]{1,0:T(1,128)S(1)} %copy-done.5, f32[32,256]{1,0:T(8,128)S(1)} %copy-done.4, ...), custom_call_target="tpu_custom_call" | custom-call | flops 1000000000 | bytes 4000000 | tf_op jit(solution)/shard_map/stage/pallas_call | solution.py:332
  11.0 0.0 copy-start
  11.0 0.0 copy-start.1
  11.0 0.0 collective-permute-done.refs_1_
  11.1 2.7 %collective-permute-done.1.refs_2_ = bf16[128,768]{1,0:T(8,128)(2,1)S(1)} collective-permute-done((bf16[128,768]{1,0:T(8,128)(2,1)}, bf16[128,768]{1,0:T(8,128)(2,1)S(1)}, u32[]{:S(2)}, u32[]{:S(2)}) %collective-permute-start.1) | collective-permute-done | bytes 196640 | tf_op jit(solution)/shard_map/ppermute | solution.py:315
  13.7 0.0 collective-permute-done.2.refs_3_
  13.7 0.5 %aggregate.1.refs_2_ = bf16[136,768]{1,0:T(8,128)(2,1)S(1)} custom-call(s32[8,128]{1,0:T(8,128)S(1)} %get-tuple-element.20.from_ref, f32[8,768]{1,0:T(8,128)S(1)} %get-tuple-element.21.extra_ref, bf16[128,1024]{1,0:T(8,128)(2,1)S(1)} %get-tuple-element.22.masked_ref, bf16[128,768]{1,0:T(8,128)(2,1)S(1)} %get-tuple-element.23.refs_0_, ...), custom_call_target="tpu_custom_call" | custom-call | flops 1000000000 | bytes 4000000 | tf_op jit(solution)/shard_map/aggregate/pallas_call | solution.py:347
  14.3 0.1 collective-permute-start.6
  14.4 2.7 %collective-permute-start.3 = (bf16[136,768]{1,0:T(8,128)(2,1)S(1)}, bf16[136,768]{1,0:T(8,128)(2,1)S(1)}, u32[]{:S(2)}, u32[]{:S(2)}) collective-permute-start(bf16[136,768]{1,0:T(8,128)(2,1)S(1)} %aggregate.1.refs_2_), channel_id=1, source_target_pairs={{0,4},{1,5},{2,6},{3,7},{4,0},{5,1},{6,2},{7,3},{8,12},{9,13},{10,... | collective-permute-start | bytes 626696 | tf_op jit(solution)/shard_map/ppermute | solution.py:315
  17.0 1.6 %collective-permute-start.5 = (bf16[136,768]{1,0:T(8,128)(2,1)S(1)}, bf16[136,768]{1,0:T(8,128)(2,1)S(1)}, u32[]{:S(2)}, u32[]{:S(2)}) collective-permute-start(bf16[136,768]{1,0:T(8,128)(2,1)S(1)} %aggregate.1.refs_2_), channel_id=1, source_target_pairs={{0,2},{1,3},{2,0},{3,1},{4,6},{5,7},{6,4},{7,5},{8,10},{9,11},{10,... | collective-permute-start | bytes 626696 | tf_op jit(solution)/shard_map/ppermute | solution.py:315
  18.6 0.0 collective-permute-done.6.refs_3_
  18.6 0.0 copy-done
  18.6 0.0 copy-done.1
  18.6 3.0 %part.3 = (bf16[128,768]{1,0:T(8,128)(2,1)S(1)}, bf16[128,4096]{1,0:T(8,128)(2,1)S(1)}, f32[128,768]{1,0:T(8,128)S(1)}, f32[128,768]{1,0:T(8,128)S(1)}) custom-call(bf16[768,1536]{1,0:T(8,128)(2,1)S(1)} %copy-done, bf16[768,768]{1,0:T(8,128)(2,1)S(1)} %copy-done.1, bf16[136,768]{1,0:T(8,128)(2,1)S(1)} %aggregate.1.refs_2_, ...), custom_call_target="tpu_custom_call" | custom-call | flops 1000000000 | bytes 4000000 | tf_op jit(solution)/shard_map/part/pallas_call | solution.py:295
  21.6 5.8 %collective-permute-done.3.refs_4_ = bf16[136,768]{1,0:T(8,128)(2,1)S(1)} collective-permute-done((bf16[136,768]{1,0:T(8,128)(2,1)S(1)}, bf16[136,768]{1,0:T(8,128)(2,1)S(1)}, u32[]{:S(2)}, u32[]{:S(2)}) %collective-permute-start.3) | collective-permute-done | bytes 208928 | tf_op jit(solution)/shard_map/ppermute | solution.py:315
  27.4 0.0 collective-permute-start.8
  27.4 0.2 collective-permute-done.5.refs_2_
  27.6 0.3 collective-permute-start.7
  27.9 1.1 %collective-permute-start.4 = (bf16[136,768]{1,0:T(8,128)(2,1)S(1)}, bf16[136,768]{1,0:T(8,128)(2,1)S(1)}, u32[]{:S(2)}, u32[]{:S(2)}) collective-permute-start(bf16[136,768]{1,0:T(8,128)(2,1)S(1)} %collective-permute-done.3.refs_4_), channel_id=1, source_target_pairs={{0,2},{1,3},{2,0},{3,1},{4,6},{5,7},{6,4},{7,5},{8,10},{9,11},{10,... | collective-permute-start | bytes 626696 | tf_op jit(solution)/shard_map/ppermute | solution.py:315
  29.0 0.0 collective-permute-done.8.refs_5_
  29.0 0.1 collective-permute-done.7.refs_3_
  29.2 4.2 %part.4 = (f32[128,768]{1,0:T(8,128)S(1)}, f32[128,768]{1,0:T(8,128)S(1)}, f32[128,768]{1,0:T(8,128)S(1)}) custom-call(bf16[768,1536]{1,0:T(8,128)(2,1)S(1)} %copy-done, bf16[768,768]{1,0:T(8,128)(2,1)S(1)} %copy-done.1, bf16[136,768]{1,0:T(8,128)(2,1)S(1)} %collective-permute-done.5.refs_2_, bf16[136,768]{1,0:T(8,128)(2,1)S(1)} %collective-permute-done.7.refs_3_, ...), custom_call_target="tpu_custom_call" | custom-call | flops 1000000000 | bytes 4000000 | tf_op jit(solution)/shard_map/part/pallas_call | solution.py:295
  33.4 1.8 %collective-permute-done.4.refs_2_ = bf16[136,768]{1,0:T(8,128)(2,1)S(1)} collective-permute-done((bf16[136,768]{1,0:T(8,128)(2,1)S(1)}, bf16[136,768]{1,0:T(8,128)(2,1)S(1)}, u32[]{:S(2)}, u32[]{:S(2)}) %collective-permute-start.4) | collective-permute-done | bytes 208928 | tf_op jit(solution)/shard_map/ppermute | solution.py:315
  35.2 0.0 collective-permute-start.9
  35.2 1.5 %collective-permute-done.9.refs_3_ = bf16[136,768]{1,0:T(8,128)(2,1)S(1)} collective-permute-done((bf16[136,768]{1,0:T(8,128)(2,1)S(1)}, bf16[136,768]{1,0:T(8,128)(2,1)S(1)}, u32[]{:S(2)}, u32[]{:S(2)}) %collective-permute-start.9) | collective-permute-done | bytes 208928 | tf_op jit(solution)/shard_map/ppermute | solution.py:315
  36.6 3.0 %part.5 = bf16[128,768]{1,0:T(8,128)(2,1)} custom-call(bf16[768,1536]{1,0:T(8,128)(2,1)S(1)} %copy-done, bf16[768,768]{1,0:T(8,128)(2,1)S(1)} %copy-done.1, bf16[136,768]{1,0:T(8,128)(2,1)S(1)} %collective-permute-done.4.refs_2_, bf16[136,768]{1,0:T(8,128)(2,1)S(1)} %collective-permute-done.9.refs_3_, ...), custom_call_target="tpu_custom_call" | custom-call | flops 1000000000 | bytes 4000000 | tf_op jit(solution)/shard_map/part/pallas_call | solution.py:295
Async XLA Ops:
  0.0 11.0 %collective-permute-start = (bf16[128,768]{1,0:T(8,128)(2,1)}, bf16[128,768]{1,0:T(8,128)(2,1)S(1)}, u32[]{:S(2)}, u32[]{:S(2)}) collective-permute-start(bf16[128,768]{1,0:T(8,128)(2,1)} %features_ref.1), channel_id=1, source_target_pairs={{0,8},{8,0},{16,24},{24,16},{1,9},{9,1},{17,25},{25,17},{2,10},{10... | collective-permute-start | bytes 589832 | tf_op jit(solution)/shard_map/ppermute | solution.py:315
  2.9 10.8 %collective-permute-start.1 = (bf16[128,768]{1,0:T(8,128)(2,1)}, bf16[128,768]{1,0:T(8,128)(2,1)S(1)}, u32[]{:S(2)}, u32[]{:S(2)}) collective-permute-start(bf16[128,768]{1,0:T(8,128)(2,1)} %features_ref.1), channel_id=1, source_target_pairs={{0,16},{8,24},{16,0},{24,8},{1,17},{9,25},{17,1},{25,9},{2,18},{10... | collective-permute-start | bytes 589832 | tf_op jit(solution)/shard_map/ppermute | solution.py:315
  4.5 9.3 %collective-permute-start.2 = (bf16[128,768]{1,0:T(8,128)(2,1)}, bf16[128,768]{1,0:T(8,128)(2,1)S(1)}, u32[]{:S(2)}, u32[]{:S(2)}) collective-permute-start(bf16[128,768]{1,0:T(8,128)(2,1)} %features_ref.1), channel_id=1, source_target_pairs={{0,24},{8,16},{16,8},{24,0},{1,25},{9,17},{17,9},{25,1},{2,26},{10... | collective-permute-start | bytes 589832 | tf_op jit(solution)/shard_map/ppermute | solution.py:315
  5.1 1.0 %copy-start.2 = (bf16[128,1024]{1,0:T(8,128)(2,1)S(1)}, bf16[128,1024]{1,0:T(8,128)(2,1)}, u32[]{:S(2)}) copy-start(bf16[128,1024]{1,0:T(8,128)(2,1)} %tiles_ref.1) | copy-start | bytes 786436
  6.1 0.9 %copy-start.3 = (bf16[128,768]{1,0:T(8,128)(2,1)S(1)}, bf16[128,768]{1,0:T(8,128)(2,1)}, u32[]{:S(2)}) copy-start(bf16[128,768]{1,0:T(8,128)(2,1)} %features_ref.1) | copy-start | bytes 589828
  7.0 0.8 %copy-start.4 = (f32[32,256]{1,0:T(8,128)S(1)}, f32[32,256]{1,0:T(8,128)}, u32[]{:S(2)}) copy-start(f32[32,256]{1,0:T(8,128)} %table_ref.1) | copy-start | bytes 98308
  7.8 0.7 %copy-start.5 = (s32[1,8]{1,0:T(1,128)S(1)}, s32[1,8]{1,0:T(1,128)}, u32[]{:S(2)}) copy-start(s32[1,8]{1,0:T(1,128)} %src_ref.1) | copy-start | bytes 100
  8.4 0.7 %copy-start.6 = (s32[128]{0:T(128)S(1)}, s32[128]{0:T(128)}, u32[]{:S(2)}) copy-start(s32[128]{0:T(128)} %param.12) | copy-start | bytes 1540
  11.0 7.6 %copy-start = (bf16[768,1536]{1,0:T(8,128)(2,1)S(1)}, bf16[768,1536]{1,0:T(8,128)(2,1)}, u32[]{:S(2)}) copy-start(bf16[768,1536]{1,0:T(8,128)(2,1)} %refs_0_.5) | copy-start | bytes 7077892
  11.0 7.6 %copy-start.1 = (bf16[768,768]{1,0:T(8,128)(2,1)S(1)}, bf16[768,768]{1,0:T(8,128)(2,1)}, u32[]{:S(2)}) copy-start(bf16[768,768]{1,0:T(8,128)(2,1)} %refs_1_.5) | copy-start | bytes 3538948
  14.3 4.3 %collective-permute-start.6 = (bf16[136,768]{1,0:T(8,128)(2,1)S(1)}, bf16[136,768]{1,0:T(8,128)(2,1)S(1)}, u32[]{:S(2)}, u32[]{:S(2)}) collective-permute-start(bf16[136,768]{1,0:T(8,128)(2,1)S(1)} %aggregate.1.refs_2_), channel_id=1, source_target_pairs={{0,1},{1,0},{2,3},{3,2},{4,5},{5,4},{6,7},{7,6},{8,9},{9,8},{10,11... | collective-permute-start | bytes 626696 | tf_op jit(solution)/shard_map/ppermute | solution.py:315
  14.4 13.1 %collective-permute-start.3 = (bf16[136,768]{1,0:T(8,128)(2,1)S(1)}, bf16[136,768]{1,0:T(8,128)(2,1)S(1)}, u32[]{:S(2)}, u32[]{:S(2)}) collective-permute-start(bf16[136,768]{1,0:T(8,128)(2,1)S(1)} %aggregate.1.refs_2_), channel_id=1, source_target_pairs={{0,4},{1,5},{2,6},{3,7},{4,0},{5,1},{6,2},{7,3},{8,12},{9,13},{10,... | collective-permute-start | bytes 626696 | tf_op jit(solution)/shard_map/ppermute | solution.py:315
  17.0 10.6 %collective-permute-start.5 = (bf16[136,768]{1,0:T(8,128)(2,1)S(1)}, bf16[136,768]{1,0:T(8,128)(2,1)S(1)}, u32[]{:S(2)}, u32[]{:S(2)}) collective-permute-start(bf16[136,768]{1,0:T(8,128)(2,1)S(1)} %aggregate.1.refs_2_), channel_id=1, source_target_pairs={{0,2},{1,3},{2,0},{3,1},{4,6},{5,7},{6,4},{7,5},{8,10},{9,11},{10,... | collective-permute-start | bytes 626696 | tf_op jit(solution)/shard_map/ppermute | solution.py:315
  27.4 1.6 %collective-permute-start.8 = (bf16[136,768]{1,0:T(8,128)(2,1)S(1)}, bf16[136,768]{1,0:T(8,128)(2,1)S(1)}, u32[]{:S(2)}, u32[]{:S(2)}) collective-permute-start(bf16[136,768]{1,0:T(8,128)(2,1)S(1)} %collective-permute-done.3.refs_4_), channel_id=1, source_target_pairs={{0,1},{1,0},{2,3},{3,2},{4,5},{5,4},{6,7},{7,6},{8,9},{9,8},{10,11... | collective-permute-start | bytes 626696 | tf_op jit(solution)/shard_map/ppermute | solution.py:315
  27.6 1.6 %collective-permute-start.7 = (bf16[136,768]{1,0:T(8,128)(2,1)S(1)}, bf16[136,768]{1,0:T(8,128)(2,1)S(1)}, u32[]{:S(2)}, u32[]{:S(2)}) collective-permute-start(bf16[136,768]{1,0:T(8,128)(2,1)S(1)} %collective-permute-done.5.refs_2_), channel_id=1, source_target_pairs={{0,1},{1,0},{2,3},{3,2},{4,5},{5,4},{6,7},{7,6},{8,9},{9,8},{10,11... | collective-permute-start | bytes 626696 | tf_op jit(solution)/shard_map/ppermute | solution.py:315
  27.9 7.3 %collective-permute-start.4 = (bf16[136,768]{1,0:T(8,128)(2,1)S(1)}, bf16[136,768]{1,0:T(8,128)(2,1)S(1)}, u32[]{:S(2)}, u32[]{:S(2)}) collective-permute-start(bf16[136,768]{1,0:T(8,128)(2,1)S(1)} %collective-permute-done.3.refs_4_), channel_id=1, source_target_pairs={{0,2},{1,3},{2,0},{3,1},{4,6},{5,7},{6,4},{7,5},{8,10},{9,11},{10,... | collective-permute-start | bytes 626696 | tf_op jit(solution)/shard_map/ppermute | solution.py:315
  35.2 1.5 %collective-permute-start.9 = (bf16[136,768]{1,0:T(8,128)(2,1)S(1)}, bf16[136,768]{1,0:T(8,128)(2,1)S(1)}, u32[]{:S(2)}, u32[]{:S(2)}) collective-permute-start(bf16[136,768]{1,0:T(8,128)(2,1)S(1)} %collective-permute-done.4.refs_2_), channel_id=1, source_target_pairs={{0,1},{1,0},{2,3},{3,2},{4,5},{5,4},{6,7},{7,6},{8,9},{9,8},{10,11... | collective-permute-start | bytes 626696 | tf_op jit(solution)/shard_map/ppermute | solution.py:315

commit v11 on v10

--- a/solution.py
+++ b/solution.py
@@ -280,7 +280,7 @@
 
 def attend_part(first, last, w_qk, w_v, blocks, inputs):
     width = w_v.shape[0]
-    rows = blocks[0].shape[0] - EXTRA
+    rows = inputs[0].shape[0]
     keys = rows * len(blocks)
     state = shape(rows, width, dtype=F32)
     if first:
@@ -371,15 +371,14 @@
     parts += [[d] for d in range(2, chips) if d != top]
     queries, state = [], [bias]
     for number, part in enumerate(parts):
-        blocks = []
+        blocks = [swap(after(own, *state), "seq", 1)] if number == 1 else []
         for d in part:
             block = far[d]
             if d:
                 block = after(block, *state)
-                near = swap(block, "seq", 1)
+                blocks += [block, swap(block, "seq", 1)]
             else:
-                near = swap(own, "seq", 1)
-            blocks += [block, near]
+                blocks.append(block)
         state = attend_part(
             number == 0, number == len(parts) - 1, w_qk, w_v, blocks, [*queries, *state]
         )

time: 39.9 us -> 38.2 us (0.957)
  waiting for transfers between devices: 12.1 us -> 9.36 us
  Pallas kernels: 12.6 us -> 13.7 us
    ppermute x10, waiting for transfers between devices: 12.1 us -> 9.36 us  [swap(): lax.ppermute(array, axis, [(i, i ^ distance) for i in range(lax.axis_size...]
    pallas_call x3, Pallas kernels: 10.2 us -> 11.2 us  [attend_part(): pl.pallas_call(lambda *refs: part_kernel(len(blocks), first, last, *refs)...]
  transfers between devices with their start and end apart: 10 -> 10, of which waited for: 6 -> 6; matrix products, arithmetic and copies ran while one was open for 0% -> 0% of each run, Pallas kernels for 23% -> 27%
where the time goes in v11:
time: 38.2 us; the launch traced here: 37.9 us
  Pallas kernels  13.7 us (36%)
  starting transfers between devices  10.2 us (27%)
  waiting for transfers between devices  9.36 us (25%)
  local copies, waits for them, and re-layouts  3.95 us (10%)
  between operations  0.73 us (2%)
    pallas_call x3, Pallas kernels, attend_part(): pl.pallas_call(lambda *refs: part_kernel(len(blocks), first, last, *refs)...  11.2 us
    ppermute x10, starting transfers between devices, swap(): lax.ppermute(array, axis, [(i, i ^ distance) for i in range(lax.axis_size...  10.2 us
    ppermute x10, waiting for transfers between devices, swap(): lax.ppermute(array, axis, [(i, i ^ distance) for i in range(lax.axis_size...  9.36 us
    unnamed x14, local copies, waits for them, and re-layouts  3.95 us
    pallas_call x1, Pallas kernels, on_device(): pl.pallas_call(stage_kernel, out_shape=[shape(rows, H * LANES), shape(row...  1.95 us
  transfers between devices with their start and end apart: 10, of which 6 were waited for; matrix products, arithmetic and copies ran while one was open for 0% of the time, Pallas kernels for 27%

profile of v11, /device:TPU:0, one launch (start us, length us, event | category | flops | bytes accessed | tf_op | source)
XLA Modules:
  0.0 37.9 jit_solution(8537824215141662838)
XLA Ops:
  0.0 2.9 %collective-permute-start = (bf16[128,768]{1,0:T(8,128)(2,1)}, bf16[128,768]{1,0:T(8,128)(2,1)S(1)}, u32[]{:S(2)}, u32[]{:S(2)}) collective-permute-start(bf16[128,768]{1,0:T(8,128)(2,1)} %features_ref.1), channel_id=1, source_target_pairs={{0,8},{8,0},{16,24},{24,16},{1,9},{9,1},{17,25},{25,17},{2,10},{10... | collective-permute-start | bytes 589832 | tf_op jit(solution)/shard_map/ppermute | solution.py:315
  2.9 1.5 %collective-permute-start.1 = (bf16[128,768]{1,0:T(8,128)(2,1)}, bf16[128,768]{1,0:T(8,128)(2,1)S(1)}, u32[]{:S(2)}, u32[]{:S(2)}) collective-permute-start(bf16[128,768]{1,0:T(8,128)(2,1)} %features_ref.1), channel_id=1, source_target_pairs={{0,16},{8,24},{16,0},{24,8},{1,17},{9,25},{17,1},{25,9},{2,18},{10... | collective-permute-start | bytes 589832 | tf_op jit(solution)/shard_map/ppermute | solution.py:315
  4.5 0.0 collective-permute-start.2
  5.1 0.0 copy-start.2
  5.1 0.9 %copy-done.2 = bf16[128,1024]{1,0:T(8,128)(2,1)S(1)} copy-done((bf16[128,1024]{1,0:T(8,128)(2,1)S(1)}, bf16[128,1024]{1,0:T(8,128)(2,1)}, u32[]{:S(2)}) %copy-start.2) | copy-done | bytes 262168
  6.1 0.0 copy-start.3
  6.1 0.9 %copy-done.3 = bf16[128,768]{1,0:T(8,128)(2,1)S(1)} copy-done((bf16[128,768]{1,0:T(8,128)(2,1)S(1)}, bf16[128,768]{1,0:T(8,128)(2,1)}, u32[]{:S(2)}) %copy-start.3) | copy-done | bytes 196632
  7.0 0.0 copy-start.4
  7.0 0.8 %copy-done.4 = f32[32,256]{1,0:T(8,128)S(1)} copy-done((f32[32,256]{1,0:T(8,128)S(1)}, f32[32,256]{1,0:T(8,128)}, u32[]{:S(2)}) %copy-start.4) | copy-done | bytes 32792
  7.8 0.0 copy-start.5
  7.8 0.7 %copy-done.5 = s32[1,8]{1,0:T(1,128)S(1)} copy-done((s32[1,8]{1,0:T(1,128)S(1)}, s32[1,8]{1,0:T(1,128)}, u32[]{:S(2)}) %copy-start.5) | copy-done | bytes 56
  8.4 0.0 copy-start.6
  8.4 0.7 %copy-done.6 = s32[128]{0:T(128)S(1)} copy-done((s32[128]{0:T(128)S(1)}, s32[128]{0:T(128)}, u32[]{:S(2)}) %copy-start.6) | copy-done | bytes 536
  9.1 1.9 %stage.1 = (bf16[128,4096]{1,0:T(8,128)(2,1)S(1)}, bf16[128,768]{1,0:T(8,128)(2,1)S(1)}, bf16[128,1024]{1,0:T(8,128)(2,1)S(1)}, f32[8,768]{1,0:T(8,128)S(1)}, s32[8,128]{1,0:T(8,128)S(1)}) custom-call(s32[1]{0:T(128)S(6)} %copy.9.count_ref, s32[1]{0:T(128)} %bitcast.me_ref, s32[1,8]{1,0:T(1,128)S(1)} %copy-done.5, f32[32,256]{1,0:T(8,128)S(1)} %copy-done.4, ...), custom_call_target="tpu_custom_call" | custom-call | flops 1000000000 | bytes 4000000 | tf_op jit(solution)/shard_map/stage/pallas_call | solution.py:332
  11.0 0.0 copy-start
  11.0 0.0 copy-start.1
  11.0 0.0 collective-permute-done.refs_1_
  11.1 2.7 %collective-permute-done.1.refs_2_ = bf16[128,768]{1,0:T(8,128)(2,1)S(1)} collective-permute-done((bf16[128,768]{1,0:T(8,128)(2,1)}, bf16[128,768]{1,0:T(8,128)(2,1)S(1)}, u32[]{:S(2)}, u32[]{:S(2)}) %collective-permute-start.1) | collective-permute-done | bytes 196640 | tf_op jit(solution)/shard_map/ppermute | solution.py:315
  13.7 0.0 collective-permute-done.2.refs_3_
  13.7 0.5 %aggregate.1.refs_2_ = bf16[136,768]{1,0:T(8,128)(2,1)S(1)} custom-call(s32[8,128]{1,0:T(8,128)S(1)} %get-tuple-element.21.from_ref, f32[8,768]{1,0:T(8,128)S(1)} %get-tuple-element.22.extra_ref, bf16[128,1024]{1,0:T(8,128)(2,1)S(1)} %get-tuple-element.23.masked_ref, bf16[128,768]{1,0:T(8,128)(2,1)S(1)} %get-tuple-element.24.refs_0_, ...), custom_call_target="tpu_custom_call" | custom-call | flops 1000000000 | bytes 4000000 | tf_op jit(solution)/shard_map/aggregate/pallas_call | solution.py:347
  14.3 2.7 %collective-permute-start.3 = (bf16[136,768]{1,0:T(8,128)(2,1)S(1)}, bf16[136,768]{1,0:T(8,128)(2,1)S(1)}, u32[]{:S(2)}, u32[]{:S(2)}) collective-permute-start(bf16[136,768]{1,0:T(8,128)(2,1)S(1)} %aggregate.1.refs_2_), channel_id=1, source_target_pairs={{0,4},{1,5},{2,6},{3,7},{4,0},{5,1},{6,2},{7,3},{8,12},{9,13},{10,... | collective-permute-start | bytes 626696 | tf_op jit(solution)/shard_map/ppermute | solution.py:315
  16.9 1.6 %collective-permute-start.6 = (bf16[136,768]{1,0:T(8,128)(2,1)S(1)}, bf16[136,768]{1,0:T(8,128)(2,1)S(1)}, u32[]{:S(2)}, u32[]{:S(2)}) collective-permute-start(bf16[136,768]{1,0:T(8,128)(2,1)S(1)} %aggregate.1.refs_2_), channel_id=1, source_target_pairs={{0,2},{1,3},{2,0},{3,1},{4,6},{5,7},{6,4},{7,5},{8,10},{9,11},{10,... | collective-permute-start | bytes 626696 | tf_op jit(solution)/shard_map/ppermute | solution.py:315
  18.5 0.0 copy-done
  18.5 0.0 copy-done.1
  18.5 2.5 %part.3 = (bf16[128,768]{1,0:T(8,128)(2,1)S(1)}, bf16[128,4096]{1,0:T(8,128)(2,1)S(1)}, f32[128,768]{1,0:T(8,128)S(1)}, f32[128,768]{1,0:T(8,128)S(1)}) custom-call(bf16[768,1536]{1,0:T(8,128)(2,1)S(1)} %copy-done, bf16[768,768]{1,0:T(8,128)(2,1)S(1)} %copy-done.1, bf16[136,768]{1,0:T(8,128)(2,1)S(1)} %aggregate.1.refs_2_, ...), custom_call_target="tpu_custom_call" | custom-call | flops 1000000000 | bytes 4000000 | tf_op jit(solution)/shard_map/part/pallas_call | solution.py:295
  21.0 0.1 collective-permute-start.5
  21.1 4.6 %collective-permute-done.3.refs_5_ = bf16[136,768]{1,0:T(8,128)(2,1)S(1)} collective-permute-done((bf16[136,768]{1,0:T(8,128)(2,1)S(1)}, bf16[136,768]{1,0:T(8,128)(2,1)S(1)}, u32[]{:S(2)}, u32[]{:S(2)}) %collective-permute-start.3) | collective-permute-done | bytes 208928 | tf_op jit(solution)/shard_map/ppermute | solution.py:315
  25.6 0.0 collective-permute-start.8
  25.6 0.2 collective-permute-done.6.refs_3_
  25.8 0.3 collective-permute-start.7
  26.2 1.1 %collective-permute-start.4 = (bf16[136,768]{1,0:T(8,128)(2,1)S(1)}, bf16[136,768]{1,0:T(8,128)(2,1)S(1)}, u32[]{:S(2)}, u32[]{:S(2)}) collective-permute-start(bf16[136,768]{1,0:T(8,128)(2,1)S(1)} %collective-permute-done.3.refs_5_), channel_id=1, source_target_pairs={{0,2},{1,3},{2,0},{3,1},{4,6},{5,7},{6,4},{7,5},{8,10},{9,11},{10,... | collective-permute-start | bytes 626696 | tf_op jit(solution)/shard_map/ppermute | solution.py:315
  27.3 0.0 collective-permute-done.5.refs_2_
  27.3 0.0 collective-permute-done.8.refs_6_
  27.3 0.1 collective-permute-done.7.refs_4_
  27.4 5.7 %part.4 = (f32[128,768]{1,0:T(8,128)S(1)}, f32[128,768]{1,0:T(8,128)S(1)}, f32[128,768]{1,0:T(8,128)S(1)}) custom-call(bf16[768,1536]{1,0:T(8,128)(2,1)S(1)} %copy-done, bf16[768,768]{1,0:T(8,128)(2,1)S(1)} %copy-done.1, bf16[136,768]{1,0:T(8,128)(2,1)S(1)} %collective-permute-done.5.refs_2_, bf16[136,768]{1,0:T(8,128)(2,1)S(1)} %collective-permute-done.6.refs_3_, ...), custom_call_target="tpu_custom_call" | custom-call | flops 1000000000 | bytes 4000000 | tf_op jit(solution)/shard_map/part/pallas_call | solution.py:295
  33.1 0.3 collective-permute-done.4.refs_2_
  33.4 0.0 collective-permute-start.9
  33.4 1.5 %collective-permute-done.9.refs_3_ = bf16[136,768]{1,0:T(8,128)(2,1)S(1)} collective-permute-done((bf16[136,768]{1,0:T(8,128)(2,1)S(1)}, bf16[136,768]{1,0:T(8,128)(2,1)S(1)}, u32[]{:S(2)}, u32[]{:S(2)}) %collective-permute-start.9) | collective-permute-done | bytes 208928 | tf_op jit(solution)/shard_map/ppermute | solution.py:315
  34.9 3.0 %part.5 = bf16[128,768]{1,0:T(8,128)(2,1)} custom-call(bf16[768,1536]{1,0:T(8,128)(2,1)S(1)} %copy-done, bf16[768,768]{1,0:T(8,128)(2,1)S(1)} %copy-done.1, bf16[136,768]{1,0:T(8,128)(2,1)S(1)} %collective-permute-done.4.refs_2_, bf16[136,768]{1,0:T(8,128)(2,1)S(1)} %collective-permute-done.9.refs_3_, ...), custom_call_target="tpu_custom_call" | custom-call | flops 1000000000 | bytes 4000000 | tf_op jit(solution)/shard_map/part/pallas_call | solution.py:295
Async XLA Ops:
  0.0 11.0 %collective-permute-start = (bf16[128,768]{1,0:T(8,128)(2,1)}, bf16[128,768]{1,0:T(8,128)(2,1)S(1)}, u32[]{:S(2)}, u32[]{:S(2)}) collective-permute-start(bf16[128,768]{1,0:T(8,128)(2,1)} %features_ref.1), channel_id=1, source_target_pairs={{0,8},{8,0},{16,24},{24,16},{1,9},{9,1},{17,25},{25,17},{2,10},{10... | collective-permute-start | bytes 589832 | tf_op jit(solution)/shard_map/ppermute | solution.py:315
  2.9 10.8 %collective-permute-start.1 = (bf16[128,768]{1,0:T(8,128)(2,1)}, bf16[128,768]{1,0:T(8,128)(2,1)S(1)}, u32[]{:S(2)}, u32[]{:S(2)}) collective-permute-start(bf16[128,768]{1,0:T(8,128)(2,1)} %features_ref.1), channel_id=1, source_target_pairs={{0,16},{8,24},{16,0},{24,8},{1,17},{9,25},{17,1},{25,9},{2,18},{10... | collective-permute-start | bytes 589832 | tf_op jit(solution)/shard_map/ppermute | solution.py:315
  4.5 9.3 %collective-permute-start.2 = (bf16[128,768]{1,0:T(8,128)(2,1)}, bf16[128,768]{1,0:T(8,128)(2,1)S(1)}, u32[]{:S(2)}, u32[]{:S(2)}) collective-permute-start(bf16[128,768]{1,0:T(8,128)(2,1)} %features_ref.1), channel_id=1, source_target_pairs={{0,24},{8,16},{16,8},{24,0},{1,25},{9,17},{17,9},{25,1},{2,26},{10... | collective-permute-start | bytes 589832 | tf_op jit(solution)/shard_map/ppermute | solution.py:315
  5.1 1.0 %copy-start.2 = (bf16[128,1024]{1,0:T(8,128)(2,1)S(1)}, bf16[128,1024]{1,0:T(8,128)(2,1)}, u32[]{:S(2)}) copy-start(bf16[128,1024]{1,0:T(8,128)(2,1)} %tiles_ref.1) | copy-start | bytes 786436
  6.1 0.9 %copy-start.3 = (bf16[128,768]{1,0:T(8,128)(2,1)S(1)}, bf16[128,768]{1,0:T(8,128)(2,1)}, u32[]{:S(2)}) copy-start(bf16[128,768]{1,0:T(8,128)(2,1)} %features_ref.1) | copy-start | bytes 589828
  7.0 0.8 %copy-start.4 = (f32[32,256]{1,0:T(8,128)S(1)}, f32[32,256]{1,0:T(8,128)}, u32[]{:S(2)}) copy-start(f32[32,256]{1,0:T(8,128)} %table_ref.1) | copy-start | bytes 98308
  7.8 0.7 %copy-start.5 = (s32[1,8]{1,0:T(1,128)S(1)}, s32[1,8]{1,0:T(1,128)}, u32[]{:S(2)}) copy-start(s32[1,8]{1,0:T(1,128)} %src_ref.1) | copy-start | bytes 100
  8.4 0.7 %copy-start.6 = (s32[128]{0:T(128)S(1)}, s32[128]{0:T(128)}, u32[]{:S(2)}) copy-start(s32[128]{0:T(128)} %param.12) | copy-start | bytes 1540
  11.0 7.5 %copy-start = (bf16[768,1536]{1,0:T(8,128)(2,1)S(1)}, bf16[768,1536]{1,0:T(8,128)(2,1)}, u32[]{:S(2)}) copy-start(bf16[768,1536]{1,0:T(8,128)(2,1)} %refs_0_.5) | copy-start | bytes 7077892
  11.0 7.5 %copy-start.1 = (bf16[768,768]{1,0:T(8,128)(2,1)S(1)}, bf16[768,768]{1,0:T(8,128)(2,1)}, u32[]{:S(2)}) copy-start(bf16[768,768]{1,0:T(8,128)(2,1)} %refs_1_.5) | copy-start | bytes 3538948
  14.3 11.4 %collective-permute-start.3 = (bf16[136,768]{1,0:T(8,128)(2,1)S(1)}, bf16[136,768]{1,0:T(8,128)(2,1)S(1)}, u32[]{:S(2)}, u32[]{:S(2)}) collective-permute-start(bf16[136,768]{1,0:T(8,128)(2,1)S(1)} %aggregate.1.refs_2_), channel_id=1, source_target_pairs={{0,4},{1,5},{2,6},{3,7},{4,0},{5,1},{6,2},{7,3},{8,12},{9,13},{10,... | collective-permute-start | bytes 626696 | tf_op jit(solution)/shard_map/ppermute | solution.py:315
  16.9 8.9 %collective-permute-start.6 = (bf16[136,768]{1,0:T(8,128)(2,1)S(1)}, bf16[136,768]{1,0:T(8,128)(2,1)S(1)}, u32[]{:S(2)}, u32[]{:S(2)}) collective-permute-start(bf16[136,768]{1,0:T(8,128)(2,1)S(1)} %aggregate.1.refs_2_), channel_id=1, source_target_pairs={{0,2},{1,3},{2,0},{3,1},{4,6},{5,7},{6,4},{7,5},{8,10},{9,11},{10,... | collective-permute-start | bytes 626696 | tf_op jit(solution)/shard_map/ppermute | solution.py:315
  21.0 6.3 %collective-permute-start.5 = (bf16[136,768]{1,0:T(8,128)(2,1)S(1)}, bf16[136,768]{1,0:T(8,128)(2,1)S(1)}, u32[]{:S(2)}, u32[]{:S(2)}) collective-permute-start(bf16[136,768]{1,0:T(8,128)(2,1)S(1)} %aggregate.1.refs_2_), channel_id=1, source_target_pairs={{0,1},{1,0},{2,3},{3,2},{4,5},{5,4},{6,7},{7,6},{8,9},{9,8},{10,11... | collective-permute-start | bytes 626696 | tf_op jit(solution)/shard_map/ppermute | solution.py:315
  25.6 1.6 %collective-permute-start.8 = (bf16[136,768]{1,0:T(8,128)(2,1)S(1)}, bf16[136,768]{1,0:T(8,128)(2,1)S(1)}, u32[]{:S(2)}, u32[]{:S(2)}) collective-permute-start(bf16[136,768]{1,0:T(8,128)(2,1)S(1)} %collective-permute-done.3.refs_5_), channel_id=1, source_target_pairs={{0,1},{1,0},{2,3},{3,2},{4,5},{5,4},{6,7},{7,6},{8,9},{9,8},{10,11... | collective-permute-start | bytes 626696 | tf_op jit(solution)/shard_map/ppermute | solution.py:315
  25.8 1.6 %collective-permute-start.7 = (bf16[136,768]{1,0:T(8,128)(2,1)S(1)}, bf16[136,768]{1,0:T(8,128)(2,1)S(1)}, u32[]{:S(2)}, u32[]{:S(2)}) collective-permute-start(bf16[136,768]{1,0:T(8,128)(2,1)S(1)} %collective-permute-done.6.refs_3_), channel_id=1, source_target_pairs={{0,1},{1,0},{2,3},{3,2},{4,5},{5,4},{6,7},{7,6},{8,9},{9,8},{10,11... | collective-permute-start | bytes 626696 | tf_op jit(solution)/shard_map/ppermute | solution.py:315
  26.2 7.3 %collective-permute-start.4 = (bf16[136,768]{1,0:T(8,128)(2,1)S(1)}, bf16[136,768]{1,0:T(8,128)(2,1)S(1)}, u32[]{:S(2)}, u32[]{:S(2)}) collective-permute-start(bf16[136,768]{1,0:T(8,128)(2,1)S(1)} %collective-permute-done.3.refs_5_), channel_id=1, source_target_pairs={{0,2},{1,3},{2,0},{3,1},{4,6},{5,7},{6,4},{7,5},{8,10},{9,11},{10,... | collective-permute-start | bytes 626696 | tf_op jit(solution)/shard_map/ppermute | solution.py:315
  33.4 1.5 %collective-permute-start.9 = (bf16[136,768]{1,0:T(8,128)(2,1)S(1)}, bf16[136,768]{1,0:T(8,128)(2,1)S(1)}, u32[]{:S(2)}, u32[]{:S(2)}) collective-permute-start(bf16[136,768]{1,0:T(8,128)(2,1)S(1)} %collective-permute-done.4.refs_2_), channel_id=1, source_target_pairs={{0,1},{1,0},{2,3},{3,2},{4,5},{5,4},{6,7},{7,6},{8,9},{9,8},{10,11... | collective-permute-start | bytes 626696 | tf_op jit(solution)/shard_map/ppermute | solution.py:315

commit v12 on v10

--- a/solution.py
+++ b/solution.py
@@ -101,7 +101,7 @@
 
 
 def aggregate_kernel(from_ref, extra_ref, masked_ref, *refs):
-    feature_refs, out_ref, held = refs[:-2], refs[-2], refs[-1]
+    feature_refs, out_ref, short_ref, held = refs[:-3], refs[-3], refs[-2], refs[-1]
     rows = feature_refs[0].shape[0]
     for d, ref in enumerate(feature_refs):
         held[d * rows : (d + 1) * rows, :] = ref[...]
@@ -113,9 +113,11 @@
         masked_ref[...], jnp.concatenate(picked, axis=0), preferred_element_type=F32
     )
     mean_square = jnp.mean(total * total, axis=-1, keepdims=True)
-    out_ref[...] = jnp.concatenate(
+    result = jnp.concatenate(
         [total * lax.rsqrt(mean_square + 1e-06), extra_ref[...]], axis=0
     ).astype(BF16)
+    out_ref[...] = result
+    short_ref[...] = result[: short_ref.shape[0], :]
 
 
 def slab_heads(slab):
@@ -127,6 +129,8 @@
     hot_ref, k_ref, v_ref, p_refs, *refs_back = *refs[-6:-3], refs[-3:-1], refs[-1]
     top_ref = refs_back[0]
     refs = refs[:-6]
+    if last:
+        *refs, held_ref, sems = refs
     if first:
         bias_ref, q_ref, shifted_ref, *outs = refs
     else:
@@ -226,13 +230,18 @@
             top = top + old_refs[0][:, cols]
             total = total + old_refs[1][:, cols]
         if last:
-            outs[0][:, cols] = (top / total).astype(BF16)
+            held_ref[:, cols] = (top / total).astype(BF16)
+            send(half * SLABS + slab).start()
         else:
             outs[0][:, cols] = top
             outs[1][:, cols] = total
             if not first:
                 outs[2][:, cols] = jnp.zeros_like(top)
         return total
+
+    def send(step):
+        cols = pl.ds(step * LANES, LANES)
+        return pltpu.make_async_copy(held_ref.at[:, cols], outs[0].at[:, cols], sems.at[step])
 
     steps = [divmod(step, SLABS) for step in range(width // LANES)]
     largest = jnp.zeros((rows, LANES), F32)
@@ -246,6 +255,9 @@
             largest = jnp.maximum(largest, add(*before, p_refs[before[0] % 2]))
         x = ahead
     largest = jnp.maximum(largest, add(*steps[-1], p_refs[steps[-1][0] % 2]))
+    if last:
+        for step in range(len(steps)):
+            send(step).wait()
     if first:
         return
     fine = jnp.max(largest) < SAFE
@@ -268,7 +280,7 @@
                 top = top * share + old_refs[0][:, cols] * old_share
                 total = total * share + old_refs[1][:, cols] * old_share
                 if last:
-                    outs[0][:, cols] = (top / total).astype(BF16)
+                    held_ref[:, cols] = (top / total).astype(BF16)
                 else:
                     outs[0][:, cols] = top
                     outs[1][:, cols] = total
@@ -276,11 +288,16 @@
             return carry
 
         lax.fori_loop(0, width // HALF, careful, 0)
+        if last:
+            for step in range(len(steps)):
+                send(step).start()
+            for step in range(len(steps)):
+                send(step).wait()
 
 
 def attend_part(first, last, w_qk, w_v, blocks, inputs):
     width = w_v.shape[0]
-    rows = blocks[0].shape[0] - EXTRA
+    rows = inputs[0].shape[0]
     keys = rows * len(blocks)
     state = shape(rows, width, dtype=F32)
     if first:
@@ -296,8 +313,11 @@
         lambda *refs: part_kernel(len(blocks), first, last, *refs),
         out_shape=outs,
         in_specs=[vmem()] * len(operands),
-        out_specs=[vmem()] * len(outs),
-        scratch_shapes=[
+        out_specs=[pl.BlockSpec(memory_space=pl.ANY) if last else vmem()] * len(outs),
+        scratch_shapes=(
+            [pltpu.VMEM((rows, width), BF16), pltpu.SemaphoreType.DMA((width // LANES,))] if last else []
+        )
+        + [
             pltpu.VMEM((keys, LANES), BF16),
             pltpu.VMEM((keys, width), BF16),
             pltpu.VMEM((keys, width), BF16),
@@ -306,7 +326,9 @@
             pltpu.VMEM((tall, LANES), F32),
         ],
         compiler_params=limit(need // MIB + 8),
-        cost_estimate=pl.CostEstimate(flops=10**9, bytes_accessed=4_000_000, transcendentals=0),
+        cost_estimate=pl.CostEstimate(
+            flops=1000 if not last else 10**9, bytes_accessed=1000 if not last else 4_000_000, transcendentals=0
+        ),
         name="part",
     )(*operands)
 
@@ -344,25 +366,25 @@
         name="stage",
     )(tile_count, lax.axis_index("group").reshape(1), tile_src, bias_table, own_bucket, features, tiles)
 
-    own = pl.pallas_call(
+    own, short = pl.pallas_call(
         aggregate_kernel,
-        out_shape=shape(rows + EXTRA, width),
+        out_shape=[shape(rows + EXTRA, width), shape(rows + EXTRA // 2, width)],
         in_specs=[vmem()] * (3 + groups),
-        out_specs=vmem(),
+        out_specs=[vmem()] * 2,
         scratch_shapes=[pltpu.VMEM((groups * rows, width), BF16)],
         compiler_params=limit(8),
         cost_estimate=pl.CostEstimate(flops=10**9, bytes_accessed=4_000_000, transcendentals=0),
         name="aggregate",
     )(source, extra, masked, own_features, *received)
 
-    far = [own] + [None] * (chips - 1)
+    far = [short] + [None] * (chips - 1)
     top = 1
     while 2 * top < chips:
         top *= 2
     far[top] = swap(own, "seq", 2 * top)
     step = 1
     while step < top:
-        far[step] = swap(own, "seq", 2 * step)
+        far[step] = swap(short, "seq", 2 * step)
         step *= 2
     for d in range(3, chips):
         if far[d] is None:
@@ -378,7 +400,7 @@
                 block = after(block, *state)
                 near = swap(block, "seq", 1)
             else:
-                near = swap(own, "seq", 1)
+                near = swap(short, "seq", 1)
             blocks += [block, near]
         state = attend_part(
             number == 0, number == len(parts) - 1, w_qk, w_v, blocks, [*queries, *state]

time: 39.9 us -> 38.6 us (0.967)
  waiting for transfers between devices: 12.1 us -> 11.2 us
  starting transfers between devices: 10.2 us -> 9.52 us
    ppermute x10, waiting for transfers between devices: 12.1 us -> 11.2 us  [swap(): lax.ppermute(array, axis, [(i, i ^ distance) for i in range(lax.axis_size...]
    ppermute x10, starting transfers between devices: 10.2 us -> 9.52 us  [swap(): lax.ppermute(array, axis, [(i, i ^ distance) for i in range(lax.axis_size...]
  transfers between devices with their start and end apart: 10 -> 10, of which waited for: 6 -> 5; matrix products, arithmetic and copies ran while one was open for 0% -> 0% of each run, Pallas kernels for 23% -> 24%
where the time goes in v12:
time: 38.6 us; the launch traced here: 38.3 us
  Pallas kernels  12.8 us (33%)
  waiting for transfers between devices  11.2 us (29%)
  starting transfers between devices  9.52 us (25%)
  local copies, waits for them, and re-layouts  3.95 us (10%)
  between operations  0.89 us (2%)
    ppermute x10, waiting for transfers between devices, swap(): lax.ppermute(array, axis, [(i, i ^ distance) for i in range(lax.axis_size...  11.2 us
    pallas_call x3, Pallas kernels, attend_part(): pl.pallas_call(lambda *refs: part_kernel(len(blocks), first, last, *refs)...  10.3 us
    ppermute x10, starting transfers between devices, swap(): lax.ppermute(array, axis, [(i, i ^ distance) for i in range(lax.axis_size...  9.52 us
    unnamed x14, local copies, waits for them, and re-layouts  3.95 us
    pallas_call x1, Pallas kernels, on_device(): pl.pallas_call(stage_kernel, out_shape=[shape(rows, H * LANES), shape(row...  1.95 us
  transfers between devices with their start and end apart: 10, of which 5 were waited for; matrix products, arithmetic and copies ran while one was open for 0% of the time, Pallas kernels for 24%

profile of v12, /device:TPU:0, one launch (start us, length us, event | category | flops | bytes accessed | tf_op | source)
XLA Modules:
  0.0 38.3 jit_solution(16480379019233354413)
XLA Ops:
  0.0 2.9 %collective-permute-start = (bf16[128,768]{1,0:T(8,128)(2,1)}, bf16[128,768]{1,0:T(8,128)(2,1)S(1)}, u32[]{:S(2)}, u32[]{:S(2)}) collective-permute-start(bf16[128,768]{1,0:T(8,128)(2,1)} %features_ref.1), channel_id=1, source_target_pairs={{0,8},{8,0},{16,24},{24,16},{1,9},{9,1},{17,25},{25,17},{2,10},{10... | collective-permute-start | bytes 589832 | tf_op jit(solution)/shard_map/ppermute | solution.py:337
  2.9 1.5 %collective-permute-start.1 = (bf16[128,768]{1,0:T(8,128)(2,1)}, bf16[128,768]{1,0:T(8,128)(2,1)S(1)}, u32[]{:S(2)}, u32[]{:S(2)}) collective-permute-start(bf16[128,768]{1,0:T(8,128)(2,1)} %features_ref.1), channel_id=1, source_target_pairs={{0,16},{8,24},{16,0},{24,8},{1,17},{9,25},{17,1},{25,9},{2,18},{10... | collective-permute-start | bytes 589832 | tf_op jit(solution)/shard_map/ppermute | solution.py:337
  4.5 0.0 collective-permute-start.2
  5.1 0.0 copy-start.2
  5.1 0.9 %copy-done.2 = bf16[128,1024]{1,0:T(8,128)(2,1)S(1)} copy-done((bf16[128,1024]{1,0:T(8,128)(2,1)S(1)}, bf16[128,1024]{1,0:T(8,128)(2,1)}, u32[]{:S(2)}) %copy-start.2) | copy-done | bytes 262168
  6.1 0.0 copy-start.3
  6.1 0.9 %copy-done.3 = bf16[128,768]{1,0:T(8,128)(2,1)S(1)} copy-done((bf16[128,768]{1,0:T(8,128)(2,1)S(1)}, bf16[128,768]{1,0:T(8,128)(2,1)}, u32[]{:S(2)}) %copy-start.3) | copy-done | bytes 196632
  7.0 0.0 copy-start.4
  7.0 0.8 %copy-done.4 = f32[32,256]{1,0:T(8,128)S(1)} copy-done((f32[32,256]{1,0:T(8,128)S(1)}, f32[32,256]{1,0:T(8,128)}, u32[]{:S(2)}) %copy-start.4) | copy-done | bytes 32792
  7.8 0.0 copy-start.5
  7.8 0.7 %copy-done.5 = s32[1,8]{1,0:T(1,128)S(1)} copy-done((s32[1,8]{1,0:T(1,128)S(1)}, s32[1,8]{1,0:T(1,128)}, u32[]{:S(2)}) %copy-start.5) | copy-done | bytes 56
  8.4 0.0 copy-start.6
  8.4 0.7 %copy-done.6 = s32[128]{0:T(128)S(1)} copy-done((s32[128]{0:T(128)S(1)}, s32[128]{0:T(128)}, u32[]{:S(2)}) %copy-start.6) | copy-done | bytes 536
  9.1 1.9 %stage.1 = (bf16[128,4096]{1,0:T(8,128)(2,1)S(1)}, bf16[128,768]{1,0:T(8,128)(2,1)S(1)}, bf16[128,1024]{1,0:T(8,128)(2,1)S(1)}, f32[8,768]{1,0:T(8,128)S(1)}, s32[8,128]{1,0:T(8,128)S(1)}) custom-call(s32[1]{0:T(128)S(6)} %copy.9.count_ref, s32[1]{0:T(128)} %bitcast.me_ref, s32[1,8]{1,0:T(1,128)S(1)} %copy-done.5, f32[32,256]{1,0:T(8,128)S(1)} %copy-done.4, ...), custom_call_target="tpu_custom_call" | custom-call | flops 1000000000 | bytes 4000000 | tf_op jit(solution)/shard_map/stage/pallas_call | solution.py:354
  11.0 0.0 copy-start
  11.0 0.0 copy-start.1
  11.0 0.0 collective-permute-done.refs_1_
  11.1 2.7 %collective-permute-done.1.refs_2_ = bf16[128,768]{1,0:T(8,128)(2,1)S(1)} collective-permute-done((bf16[128,768]{1,0:T(8,128)(2,1)}, bf16[128,768]{1,0:T(8,128)(2,1)S(1)}, u32[]{:S(2)}, u32[]{:S(2)}) %collective-permute-start.1) | collective-permute-done | bytes 196640 | tf_op jit(solution)/shard_map/ppermute | solution.py:337
  13.7 0.0 collective-permute-done.2.refs_3_
  13.7 0.5 %aggregate.1 = (bf16[136,768]{1,0:T(8,128)(2,1)S(1)}, bf16[132,768]{1,0:T(8,128)(2,1)S(1)}) custom-call(s32[8,128]{1,0:T(8,128)S(1)} %get-tuple-element.22.from_ref, f32[8,768]{1,0:T(8,128)S(1)} %get-tuple-element.23.extra_ref, bf16[128,1024]{1,0:T(8,128)(2,1)S(1)} %get-tuple-element.24.masked_ref, bf16[128,768]{1,0:T(8,128)(2,1)S(1)} %get-tuple-element.25.refs_0_, ...), custom_call_target="tpu_custom_call" | custom-call | flops 1000000000 | bytes 4000000 | tf_op jit(solution)/shard_map/aggregate/pallas_call | solution.py:369
  14.3 2.7 %collective-permute-start.3 = (bf16[136,768]{1,0:T(8,128)(2,1)S(1)}, bf16[136,768]{1,0:T(8,128)(2,1)S(1)}, u32[]{:S(2)}, u32[]{:S(2)}) collective-permute-start(bf16[136,768]{1,0:T(8,128)(2,1)S(1)} %get-tuple-element.26), channel_id=1, source_target_pairs={{0,4},{1,5},{2,6},{3,7},{4,0},{5,1},{6,2},{7,3},{8,12},{9,13},{10,... | collective-permute-start | bytes 626696 | tf_op jit(solution)/shard_map/ppermute | solution.py:337
  16.9 0.0 collective-permute-start.6
  16.9 1.6 %collective-permute-start.5 = (bf16[132,768]{1,0:T(8,128)(2,1)S(1)}, bf16[132,768]{1,0:T(8,128)(2,1)S(1)}, u32[]{:S(2)}, u32[]{:S(2)}) collective-permute-start(bf16[132,768]{1,0:T(8,128)(2,1)S(1)} %get-tuple-element.27.refs_2_), channel_id=1, source_target_pairs={{0,2},{1,3},{2,0},{3,1},{4,6},{5,7},{6,4},{7,5},{8,10},{9,11},{10,... | collective-permute-start | bytes 608264 | tf_op jit(solution)/shard_map/ppermute | solution.py:337
  18.5 0.0 collective-permute-done.6.refs_3_
  18.5 0.0 copy-done
  18.5 0.0 copy-done.1
  18.5 3.0 %part.3 = (bf16[128,768]{1,0:T(8,128)(2,1)S(1)}, bf16[128,4096]{1,0:T(8,128)(2,1)S(1)}, f32[128,768]{1,0:T(8,128)S(1)}, f32[128,768]{1,0:T(8,128)S(1)}) custom-call(bf16[768,1536]{1,0:T(8,128)(2,1)S(1)} %copy-done, bf16[768,768]{1,0:T(8,128)(2,1)S(1)} %copy-done.1, bf16[132,768]{1,0:T(8,128)(2,1)S(1)} %get-tuple-element.27.refs_2_, ...), custom_call_target="tpu_custom_call" | custom-call | flops 1000 | bytes 1000 | tf_op jit(solution)/shard_map/part/pallas_call | solution.py:312
  21.5 4.1 %collective-permute-done.3.refs_4_ = bf16[136,768]{1,0:T(8,128)(2,1)S(1)} collective-permute-done((bf16[136,768]{1,0:T(8,128)(2,1)S(1)}, bf16[136,768]{1,0:T(8,128)(2,1)S(1)}, u32[]{:S(2)}, u32[]{:S(2)}) %collective-permute-start.3) | collective-permute-done | bytes 208928 | tf_op jit(solution)/shard_map/ppermute | solution.py:337
  25.6 0.0 collective-permute-start.8
  25.6 0.6 %collective-permute-start.4 = (bf16[136,768]{1,0:T(8,128)(2,1)S(1)}, bf16[136,768]{1,0:T(8,128)(2,1)S(1)}, u32[]{:S(2)}, u32[]{:S(2)}) collective-permute-start(bf16[136,768]{1,0:T(8,128)(2,1)S(1)} %collective-permute-done.3.refs_4_), channel_id=1, source_target_pairs={{0,2},{1,3},{2,0},{3,1},{4,6},{5,7},{6,4},{7,5},{8,10},{9,11},{10,... | collective-permute-start | bytes 626696 | tf_op jit(solution)/shard_map/ppermute | solution.py:337
  26.3 1.6 %collective-permute-done.5.refs_2_ = bf16[132,768]{1,0:T(8,128)(2,1)S(1)} collective-permute-done((bf16[132,768]{1,0:T(8,128)(2,1)S(1)}, bf16[132,768]{1,0:T(8,128)(2,1)S(1)}, u32[]{:S(2)}, u32[]{:S(2)}) %collective-permute-start.5) | collective-permute-done | bytes 202784 | tf_op jit(solution)/shard_map/ppermute | solution.py:337
  27.8 0.0 collective-permute-start.7
  27.9 1.5 %collective-permute-done.7.refs_3_ = bf16[132,768]{1,0:T(8,128)(2,1)S(1)} collective-permute-done((bf16[132,768]{1,0:T(8,128)(2,1)S(1)}, bf16[132,768]{1,0:T(8,128)(2,1)S(1)}, u32[]{:S(2)}, u32[]{:S(2)}) %collective-permute-start.7) | collective-permute-done | bytes 202784 | tf_op jit(solution)/shard_map/ppermute | solution.py:337
  29.3 0.0 collective-permute-done.8.refs_5_
  29.3 4.2 %part.4 = (f32[128,768]{1,0:T(8,128)S(1)}, f32[128,768]{1,0:T(8,128)S(1)}, f32[128,768]{1,0:T(8,128)S(1)}) custom-call(bf16[768,1536]{1,0:T(8,128)(2,1)S(1)} %copy-done, bf16[768,768]{1,0:T(8,128)(2,1)S(1)} %copy-done.1, bf16[132,768]{1,0:T(8,128)(2,1)S(1)} %collective-permute-done.5.refs_2_, bf16[132,768]{1,0:T(8,128)(2,1)S(1)} %collective-permute-done.7.refs_3_, ...), custom_call_target="tpu_custom_call" | custom-call | flops 1000 | bytes 1000 | tf_op jit(solution)/shard_map/part/pallas_call | solution.py:312
  33.5 0.0 collective-permute-done.4.refs_2_
  33.5 0.2 collective-permute-start.9
  33.7 1.3 %collective-permute-done.9.refs_3_ = bf16[136,768]{1,0:T(8,128)(2,1)S(1)} collective-permute-done((bf16[136,768]{1,0:T(8,128)(2,1)S(1)}, bf16[136,768]{1,0:T(8,128)(2,1)S(1)}, u32[]{:S(2)}, u32[]{:S(2)}) %collective-permute-start.9) | collective-permute-done | bytes 208928 | tf_op jit(solution)/shard_map/ppermute | solution.py:337
  35.0 3.1 %part.5 = bf16[128,768]{1,0:T(8,128)(2,1)} custom-call(bf16[768,1536]{1,0:T(8,128)(2,1)S(1)} %copy-done, bf16[768,768]{1,0:T(8,128)(2,1)S(1)} %copy-done.1, bf16[136,768]{1,0:T(8,128)(2,1)S(1)} %collective-permute-done.4.refs_2_, bf16[136,768]{1,0:T(8,128)(2,1)S(1)} %collective-permute-done.9.refs_3_, ...), custom_call_target="tpu_custom_call" | custom-call | flops 1000000000 | bytes 4000000 | tf_op jit(solution)/shard_map/part/pallas_call | solution.py:312
Async XLA Ops:
  0.0 11.0 %collective-permute-start = (bf16[128,768]{1,0:T(8,128)(2,1)}, bf16[128,768]{1,0:T(8,128)(2,1)S(1)}, u32[]{:S(2)}, u32[]{:S(2)}) collective-permute-start(bf16[128,768]{1,0:T(8,128)(2,1)} %features_ref.1), channel_id=1, source_target_pairs={{0,8},{8,0},{16,24},{24,16},{1,9},{9,1},{17,25},{25,17},{2,10},{10... | collective-permute-start | bytes 589832 | tf_op jit(solution)/shard_map/ppermute | solution.py:337
  2.9 10.8 %collective-permute-start.1 = (bf16[128,768]{1,0:T(8,128)(2,1)}, bf16[128,768]{1,0:T(8,128)(2,1)S(1)}, u32[]{:S(2)}, u32[]{:S(2)}) collective-permute-start(bf16[128,768]{1,0:T(8,128)(2,1)} %features_ref.1), channel_id=1, source_target_pairs={{0,16},{8,24},{16,0},{24,8},{1,17},{9,25},{17,1},{25,9},{2,18},{10... | collective-permute-start | bytes 589832 | tf_op jit(solution)/shard_map/ppermute | solution.py:337
  4.5 9.3 %collective-permute-start.2 = (bf16[128,768]{1,0:T(8,128)(2,1)}, bf16[128,768]{1,0:T(8,128)(2,1)S(1)}, u32[]{:S(2)}, u32[]{:S(2)}) collective-permute-start(bf16[128,768]{1,0:T(8,128)(2,1)} %features_ref.1), channel_id=1, source_target_pairs={{0,24},{8,16},{16,8},{24,0},{1,25},{9,17},{17,9},{25,1},{2,26},{10... | collective-permute-start | bytes 589832 | tf_op jit(solution)/shard_map/ppermute | solution.py:337
  5.1 1.0 %copy-start.2 = (bf16[128,1024]{1,0:T(8,128)(2,1)S(1)}, bf16[128,1024]{1,0:T(8,128)(2,1)}, u32[]{:S(2)}) copy-start(bf16[128,1024]{1,0:T(8,128)(2,1)} %tiles_ref.1) | copy-start | bytes 786436
  6.1 0.9 %copy-start.3 = (bf16[128,768]{1,0:T(8,128)(2,1)S(1)}, bf16[128,768]{1,0:T(8,128)(2,1)}, u32[]{:S(2)}) copy-start(bf16[128,768]{1,0:T(8,128)(2,1)} %features_ref.1) | copy-start | bytes 589828
  7.0 0.8 %copy-start.4 = (f32[32,256]{1,0:T(8,128)S(1)}, f32[32,256]{1,0:T(8,128)}, u32[]{:S(2)}) copy-start(f32[32,256]{1,0:T(8,128)} %table_ref.1) | copy-start | bytes 98308
  7.8 0.7 %copy-start.5 = (s32[1,8]{1,0:T(1,128)S(1)}, s32[1,8]{1,0:T(1,128)}, u32[]{:S(2)}) copy-start(s32[1,8]{1,0:T(1,128)} %src_ref.1) | copy-start | bytes 100
  8.4 0.7 %copy-start.6 = (s32[128]{0:T(128)S(1)}, s32[128]{0:T(128)}, u32[]{:S(2)}) copy-start(s32[128]{0:T(128)} %param.12) | copy-start | bytes 1540
  11.0 7.5 %copy-start = (bf16[768,1536]{1,0:T(8,128)(2,1)S(1)}, bf16[768,1536]{1,0:T(8,128)(2,1)}, u32[]{:S(2)}) copy-start(bf16[768,1536]{1,0:T(8,128)(2,1)} %refs_0_.5) | copy-start | bytes 7077892
  11.0 7.5 %copy-start.1 = (bf16[768,768]{1,0:T(8,128)(2,1)S(1)}, bf16[768,768]{1,0:T(8,128)(2,1)}, u32[]{:S(2)}) copy-start(bf16[768,768]{1,0:T(8,128)(2,1)} %refs_1_.5) | copy-start | bytes 3538948
  14.3 11.4 %collective-permute-start.3 = (bf16[136,768]{1,0:T(8,128)(2,1)S(1)}, bf16[136,768]{1,0:T(8,128)(2,1)S(1)}, u32[]{:S(2)}, u32[]{:S(2)}) collective-permute-start(bf16[136,768]{1,0:T(8,128)(2,1)S(1)} %get-tuple-element.26), channel_id=1, source_target_pairs={{0,4},{1,5},{2,6},{3,7},{4,0},{5,1},{6,2},{7,3},{8,12},{9,13},{10,... | collective-permute-start | bytes 626696 | tf_op jit(solution)/shard_map/ppermute | solution.py:337
  16.9 1.6 %collective-permute-start.6 = (bf16[132,768]{1,0:T(8,128)(2,1)S(1)}, bf16[132,768]{1,0:T(8,128)(2,1)S(1)}, u32[]{:S(2)}, u32[]{:S(2)}) collective-permute-start(bf16[132,768]{1,0:T(8,128)(2,1)S(1)} %get-tuple-element.27.refs_2_), channel_id=1, source_target_pairs={{0,1},{1,0},{2,3},{3,2},{4,5},{5,4},{6,7},{7,6},{8,9},{9,8},{10,11... | collective-permute-start | bytes 608264 | tf_op jit(solution)/shard_map/ppermute | solution.py:337
  16.9 10.9 %collective-permute-start.5 = (bf16[132,768]{1,0:T(8,128)(2,1)S(1)}, bf16[132,768]{1,0:T(8,128)(2,1)S(1)}, u32[]{:S(2)}, u32[]{:S(2)}) collective-permute-start(bf16[132,768]{1,0:T(8,128)(2,1)S(1)} %get-tuple-element.27.refs_2_), channel_id=1, source_target_pairs={{0,2},{1,3},{2,0},{3,1},{4,6},{5,7},{6,4},{7,5},{8,10},{9,11},{10,... | collective-permute-start | bytes 608264 | tf_op jit(solution)/shard_map/ppermute | solution.py:337
  25.6 3.7 %collective-permute-start.8 = (bf16[136,768]{1,0:T(8,128)(2,1)S(1)}, bf16[136,768]{1,0:T(8,128)(2,1)S(1)}, u32[]{:S(2)}, u32[]{:S(2)}) collective-permute-start(bf16[136,768]{1,0:T(8,128)(2,1)S(1)} %collective-permute-done.3.refs_4_), channel_id=1, source_target_pairs={{0,1},{1,0},{2,3},{3,2},{4,5},{5,4},{6,7},{7,6},{8,9},{9,8},{10,11... | collective-permute-start | bytes 626696 | tf_op jit(solution)/shard_map/ppermute | solution.py:337
  25.6 7.9 %collective-permute-start.4 = (bf16[136,768]{1,0:T(8,128)(2,1)S(1)}, bf16[136,768]{1,0:T(8,128)(2,1)S(1)}, u32[]{:S(2)}, u32[]{:S(2)}) collective-permute-start(bf16[136,768]{1,0:T(8,128)(2,1)S(1)} %collective-permute-done.3.refs_4_), channel_id=1, source_target_pairs={{0,2},{1,3},{2,0},{3,1},{4,6},{5,7},{6,4},{7,5},{8,10},{9,11},{10,... | collective-permute-start | bytes 626696 | tf_op jit(solution)/shard_map/ppermute | solution.py:337
  27.8 1.5 %collective-permute-start.7 = (bf16[132,768]{1,0:T(8,128)(2,1)S(1)}, bf16[132,768]{1,0:T(8,128)(2,1)S(1)}, u32[]{:S(2)}, u32[]{:S(2)}) collective-permute-start(bf16[132,768]{1,0:T(8,128)(2,1)S(1)} %collective-permute-done.5.refs_2_), channel_id=1, source_target_pairs={{0,1},{1,0},{2,3},{3,2},{4,5},{5,4},{6,7},{7,6},{8,9},{9,8},{10,11... | collective-permute-start | bytes 608264 | tf_op jit(solution)/shard_map/ppermute | solution.py:337
  33.5 1.5 %collective-permute-start.9 = (bf16[136,768]{1,0:T(8,128)(2,1)S(1)}, bf16[136,768]{1,0:T(8,128)(2,1)S(1)}, u32[]{:S(2)}, u32[]{:S(2)}) collective-permute-start(bf16[136,768]{1,0:T(8,128)(2,1)S(1)} %collective-permute-done.4.refs_2_), channel_id=1, source_target_pairs={{0,1},{1,0},{2,3},{3,2},{4,5},{5,4},{6,7},{7,6},{8,9},{9,8},{10,11... | collective-permute-start | bytes 626696 | tf_op jit(solution)/shard_map/ppermute | solution.py:337

commit v13 on v10

--- a/solution.py
+++ b/solution.py
@@ -101,7 +101,7 @@
 
 
 def aggregate_kernel(from_ref, extra_ref, masked_ref, *refs):
-    feature_refs, out_ref, held = refs[:-2], refs[-2], refs[-1]
+    feature_refs, out_ref, short_ref, held = refs[:-3], refs[-3], refs[-2], refs[-1]
     rows = feature_refs[0].shape[0]
     for d, ref in enumerate(feature_refs):
         held[d * rows : (d + 1) * rows, :] = ref[...]
@@ -113,38 +113,24 @@
         masked_ref[...], jnp.concatenate(picked, axis=0), preferred_element_type=F32
     )
     mean_square = jnp.mean(total * total, axis=-1, keepdims=True)
-    out_ref[...] = jnp.concatenate(
+    result = jnp.concatenate(
         [total * lax.rsqrt(mean_square + 1e-06), extra_ref[...]], axis=0
     ).astype(BF16)
+    out_ref[...] = result
+    short_ref[...] = result[: short_ref.shape[0], :]
 
 
 def slab_heads(slab):
     return slab * LANES // HD, ((slab + 1) * LANES - 1) // HD
 
 
-def part_kernel(count, first, last, w_qk_ref, w_v_ref, *refs):
-    block_refs, refs = refs[:count], refs[count:]
-    hot_ref, k_ref, v_ref, p_refs, *refs_back = *refs[-6:-3], refs[-3:-1], refs[-1]
-    top_ref = refs_back[0]
-    refs = refs[:-6]
-    if first:
-        bias_ref, q_ref, shifted_ref, *outs = refs
-    else:
-        q_ref, bias_ref, *refs = refs
-        old_refs, outs = (refs[:2], refs[2:]) if len(refs) in (3, 5) else (refs[:3], refs[3:])
-    rows = q_ref.shape[0]
-    keys = hot_ref.shape[0]
+def project_blocks(block_refs, rows, w_qk_ref, w_v_ref, hot_ref, k_ref, v_ref):
     width = w_v_ref.shape[0]
     arrived = [ref[...] for ref in block_refs]
     for s, item in enumerate(arrived):
         bucket = item[rows:, :rows].astype(F32)[:1, :]
         hot_ref[s * rows : (s + 1) * rows, :] = one_hot_slab(bucket)
     block = jnp.concatenate([item[:rows, :] for item in arrived], axis=0)
-    if first:
-        for n in range(0, width, 256):
-            q_ref[:, n : n + 256] = jnp.dot(
-                block[:rows, :], w_qk_ref[:, n : n + 256], preferred_element_type=F32
-            ).astype(BF16)
     for n in range(0, width, 256):
         k_ref[:, n : n + 256] = jnp.dot(
             block, w_qk_ref[:, width + n : width + n + 256], preferred_element_type=F32
@@ -152,6 +138,42 @@
         v_ref[:, n : n + 256] = jnp.dot(
             block, w_v_ref[:, n : n + 256], preferred_element_type=F32
         ).astype(BF16)
+    return block
+
+
+def project_kernel(w_qk_ref, w_v_ref, *refs):
+    *block_refs, hot_ref, k_ref, v_ref = refs
+    rows = hot_ref.shape[0] // len(block_refs)
+    project_blocks(block_refs, rows, w_qk_ref, w_v_ref, hot_ref, k_ref, v_ref)
+
+
+def part_kernel(count, first, last, w_qk_ref, w_v_ref, *refs):
+    block_refs, refs = refs[:count], refs[count:]
+    hot_refs, k_refs, v_refs = ([ref] for ref in refs[-6:-3])
+    p_refs, top_ref = refs[-3:-1], refs[-1]
+    refs = refs[:-6]
+    if first:
+        bias_ref, q_ref, shifted_ref, *outs = refs
+    else:
+        ready, (q_ref, bias_ref, *refs) = refs[:3], refs[3:]
+        old_refs, outs = (refs[:2], refs[2:]) if len(refs) in (3, 5) else (refs[:3], refs[3:])
+    rows = q_ref.shape[0]
+    width = w_v_ref.shape[0]
+    block = project_blocks(
+        block_refs, rows, w_qk_ref, w_v_ref, hot_refs[0], k_refs[0], v_refs[0]
+    )
+    if first:
+        for n in range(0, width, 256):
+            q_ref[:, n : n + 256] = jnp.dot(
+                block[:rows, :], w_qk_ref[:, n : n + 256], preferred_element_type=F32
+            ).astype(BF16)
+    else:
+        for some, ref in zip((hot_refs, k_refs, v_refs), ready):
+            some.insert(0, ref)
+    keys = sum(ref.shape[0] for ref in hot_refs)
+
+    def every(some, cols=slice(None)):
+        return jnp.concatenate([ref[:, cols] for ref in some], axis=0)
 
     lane = lax.broadcasted_iota(jnp.int32, (rows, LANES), 1)
     ones = jnp.ones((keys, LANES), BF16)
@@ -175,7 +197,7 @@
         query = jnp.concatenate(
             [jnp.concatenate(lefts, axis=0), jnp.concatenate(rights, axis=0)], axis=1
         )
-        key = jnp.concatenate([k_ref[:, cols], hot_ref[...]], axis=1)
+        key = jnp.concatenate([every(k_refs, cols), every(hot_refs)], axis=1)
         return lax.dot_general(query, key, NT, preferred_element_type=F32)
 
     def weigh(half, slab, x, carried, p_ref, local):
@@ -214,7 +236,7 @@
     def mix(half, slab, p_ref):
         cols = span(half * HALF + slab * LANES, LANES)
         begin, end = slab_heads(slab)
-        value = jnp.concatenate([v_ref[:, cols], ones], axis=1)
+        value = jnp.concatenate([every(v_refs, cols), ones], axis=1)
         mixed = jnp.dot(
             p_ref[begin * rows : (end + 1) * rows, :], value, preferred_element_type=F32
         )
@@ -280,8 +302,22 @@
 
 def attend_part(first, last, w_qk, w_v, blocks, inputs):
     width = w_v.shape[0]
-    rows = blocks[0].shape[0] - EXTRA
-    keys = rows * len(blocks)
+    rows = inputs[0].shape[0]
+    ready = []
+    if not first:
+        near, blocks = blocks[::2], blocks[1::2]
+        count = rows * len(near)
+        ready = pl.pallas_call(
+            project_kernel,
+            out_shape=[shape(count, LANES), shape(count, width), shape(count, width)],
+            in_specs=[vmem()] * (2 + len(near)),
+            out_specs=[vmem()] * 3,
+            compiler_params=limit(8),
+            cost_estimate=pl.CostEstimate(flops=1000, bytes_accessed=1000, transcendentals=0),
+            name="project",
+        )(w_qk, w_v, *near)
+    count = rows * len(blocks)
+    keys = count + sum(item.shape[0] for item in ready[:1])
     state = shape(rows, width, dtype=F32)
     if first:
         outs = [shape(rows, width), shape(rows, H * LANES), state, state]
@@ -289,7 +325,7 @@
         outs = [shape(rows, width)]
     else:
         outs = [state] * 3
-    operands = [w_qk, w_v, *blocks, *inputs]
+    operands = [w_qk, w_v, *blocks, *ready, *inputs]
     tall = SET * rows
     need = 4 * tall * keys + 4 * keys * width + 4 * tall * LANES
     return pl.pallas_call(
@@ -298,15 +334,17 @@
         in_specs=[vmem()] * len(operands),
         out_specs=[vmem()] * len(outs),
         scratch_shapes=[
-            pltpu.VMEM((keys, LANES), BF16),
-            pltpu.VMEM((keys, width), BF16),
-            pltpu.VMEM((keys, width), BF16),
+            pltpu.VMEM((count, LANES), BF16),
+            pltpu.VMEM((count, width), BF16),
+            pltpu.VMEM((count, width), BF16),
             pltpu.VMEM((tall, keys), BF16),
             pltpu.VMEM((tall, keys), BF16),
             pltpu.VMEM((tall, LANES), F32),
         ],
         compiler_params=limit(need // MIB + 8),
-        cost_estimate=pl.CostEstimate(flops=10**9, bytes_accessed=4_000_000, transcendentals=0),
+        cost_estimate=pl.CostEstimate(
+            flops=1000 if not last else 10**9, bytes_accessed=1000 if not last else 4_000_000, transcendentals=0
+        ),
         name="part",
     )(*operands)
 
@@ -344,25 +382,25 @@
         name="stage",
     )(tile_count, lax.axis_index("group").reshape(1), tile_src, bias_table, own_bucket, features, tiles)
 
-    own = pl.pallas_call(
+    own, short = pl.pallas_call(
         aggregate_kernel,
-        out_shape=shape(rows + EXTRA, width),
+        out_shape=[shape(rows + EXTRA, width), shape(rows + EXTRA // 2, width)],
         in_specs=[vmem()] * (3 + groups),
-        out_specs=vmem(),
+        out_specs=[vmem()] * 2,
         scratch_shapes=[pltpu.VMEM((groups * rows, width), BF16)],
         compiler_params=limit(8),
         cost_estimate=pl.CostEstimate(flops=10**9, bytes_accessed=4_000_000, transcendentals=0),
         name="aggregate",
     )(source, extra, masked, own_features, *received)
 
-    far = [own] + [None] * (chips - 1)
+    far = [short] + [None] * (chips - 1)
     top = 1
     while 2 * top < chips:
         top *= 2
     far[top] = swap(own, "seq", 2 * top)
     step = 1
     while step < top:
-        far[step] = swap(own, "seq", 2 * step)
+        far[step] = swap(short, "seq", 2 * step)
         step *= 2
     for d in range(3, chips):
         if far[d] is None:
@@ -378,7 +416,7 @@
                 block = after(block, *state)
                 near = swap(block, "seq", 1)
             else:
-                near = swap(own, "seq", 1)
+                near = swap(short, "seq", 1)
             blocks += [block, near]
         state = attend_part(
             number == 0, number == len(parts) - 1, w_qk, w_v, blocks, [*queries, *state]

time: 39.9 us -> 37.7 us (0.945)
  waiting for transfers between devices: 12.1 us -> 10.3 us
  starting transfers between devices: 10.2 us -> 9.31 us
  Pallas kernels: 12.6 us -> 13.2 us
    ppermute x10, waiting for transfers between devices: 12.1 us -> 10.3 us  [swap(): lax.ppermute(array, axis, [(i, i ^ distance) for i in range(lax.axis_size...]
    pallas_call x1 -> x3, Pallas kernels: 0.54 us -> 1.81 us  [the longest x2 1.27 us: attend_part(): pl.pallas_call(project_kernel, out_shape=[shape(count, LANES), shape(coun...]
    ppermute x10, starting transfers between devices: 10.2 us -> 9.31 us  [swap(): lax.ppermute(array, axis, [(i, i ^ distance) for i in range(lax.axis_size...]
    pallas_call x3, Pallas kernels: 10.2 us -> 9.45 us  [attend_part(): pl.pallas_call(lambda *refs: part_kernel(len(blocks), first, last, *refs)...]
  transfers between devices with their start and end apart: 10 -> 10, of which waited for: 6 -> 7; matrix products, arithmetic and copies ran while one was open for 0% -> 0% of each run, Pallas kernels for 23% -> 26%
where the time goes in v13:
time: 37.7 us; the launch traced here: 37.5 us
  Pallas kernels  13.2 us (35%)
  waiting for transfers between devices  10.3 us (27%)
  starting transfers between devices  9.31 us (25%)
  local copies, waits for them, and re-layouts  3.95 us (10%)
  between operations  0.74 us (2%)
    ppermute x10, waiting for transfers between devices, swap(): lax.ppermute(array, axis, [(i, i ^ distance) for i in range(lax.axis_size...  10.3 us
    pallas_call x3, Pallas kernels, attend_part(): pl.pallas_call(lambda *refs: part_kernel(len(blocks), first, last, *refs)...  9.45 us
    ppermute x10, starting transfers between devices, swap(): lax.ppermute(array, axis, [(i, i ^ distance) for i in range(lax.axis_size...  9.31 us
    unnamed x14, local copies, waits for them, and re-layouts  3.95 us
    pallas_call x1, Pallas kernels, on_device(): pl.pallas_call(stage_kernel, out_shape=[shape(rows, H * LANES), shape(row...  1.95 us
    pallas_call x2, Pallas kernels, attend_part(): pl.pallas_call(project_kernel, out_shape=[shape(count, LANES), shape(coun...  1.27 us
  transfers between devices with their start and end apart: 10, of which 7 were waited for; matrix products, arithmetic and copies ran while one was open for 0% of the time, Pallas kernels for 26%

profile of v13, /device:TPU:0, one launch (start us, length us, event | category | flops | bytes accessed | tf_op | source)
XLA Modules:
  0.0 37.5 jit_solution(2343646256899100071)
XLA Ops:
  0.0 2.9 %collective-permute-start = (bf16[128,768]{1,0:T(8,128)(2,1)}, bf16[128,768]{1,0:T(8,128)(2,1)S(1)}, u32[]{:S(2)}, u32[]{:S(2)}) collective-permute-start(bf16[128,768]{1,0:T(8,128)(2,1)} %features_ref.1), channel_id=1, source_target_pairs={{0,8},{8,0},{16,24},{24,16},{1,9},{9,1},{17,25},{25,17},{2,10},{10... | collective-permute-start | bytes 589832 | tf_op jit(solution)/shard_map/ppermute | solution.py:353
  2.9 1.5 %collective-permute-start.2 = (bf16[128,768]{1,0:T(8,128)(2,1)}, bf16[128,768]{1,0:T(8,128)(2,1)S(1)}, u32[]{:S(2)}, u32[]{:S(2)}) collective-permute-start(bf16[128,768]{1,0:T(8,128)(2,1)} %features_ref.1), channel_id=1, source_target_pairs={{0,24},{8,16},{16,8},{24,0},{1,25},{9,17},{17,9},{25,1},{2,26},{10... | collective-permute-start | bytes 589832 | tf_op jit(solution)/shard_map/ppermute | solution.py:353
  4.4 0.0 collective-permute-start.1
  5.1 0.0 copy-start.2
  5.1 0.9 %copy-done.2 = bf16[128,1024]{1,0:T(8,128)(2,1)S(1)} copy-done((bf16[128,1024]{1,0:T(8,128)(2,1)S(1)}, bf16[128,1024]{1,0:T(8,128)(2,1)}, u32[]{:S(2)}) %copy-start.2) | copy-done | bytes 262168
  6.1 0.0 copy-start.3
  6.1 0.9 %copy-done.3 = bf16[128,768]{1,0:T(8,128)(2,1)S(1)} copy-done((bf16[128,768]{1,0:T(8,128)(2,1)S(1)}, bf16[128,768]{1,0:T(8,128)(2,1)}, u32[]{:S(2)}) %copy-start.3) | copy-done | bytes 196632
  7.0 0.0 copy-start.4
  7.0 0.8 %copy-done.4 = f32[32,256]{1,0:T(8,128)S(1)} copy-done((f32[32,256]{1,0:T(8,128)S(1)}, f32[32,256]{1,0:T(8,128)}, u32[]{:S(2)}) %copy-start.4) | copy-done | bytes 32792
  7.8 0.0 copy-start.5
  7.8 0.7 %copy-done.5 = s32[1,8]{1,0:T(1,128)S(1)} copy-done((s32[1,8]{1,0:T(1,128)S(1)}, s32[1,8]{1,0:T(1,128)}, u32[]{:S(2)}) %copy-start.5) | copy-done | bytes 56
  8.4 0.0 copy-start.6
  8.4 0.7 %copy-done.6 = s32[128]{0:T(128)S(1)} copy-done((s32[128]{0:T(128)S(1)}, s32[128]{0:T(128)}, u32[]{:S(2)}) %copy-start.6) | copy-done | bytes 536
  9.1 1.9 %stage.1 = (bf16[128,4096]{1,0:T(8,128)(2,1)S(1)}, bf16[128,768]{1,0:T(8,128)(2,1)S(1)}, bf16[128,1024]{1,0:T(8,128)(2,1)S(1)}, f32[8,768]{1,0:T(8,128)S(1)}, s32[8,128]{1,0:T(8,128)S(1)}) custom-call(s32[1]{0:T(128)S(6)} %copy.9.count_ref, s32[1]{0:T(128)} %bitcast.me_ref, s32[1,8]{1,0:T(1,128)S(1)} %copy-done.5, f32[32,256]{1,0:T(8,128)S(1)} %copy-done.4, ...), custom_call_target="tpu_custom_call" | custom-call | flops 1000000000 | bytes 4000000 | tf_op jit(solution)/shard_map/stage/pallas_call | solution.py:370
  11.0 0.0 copy-start
  11.0 0.0 copy-start.1
  11.0 0.0 collective-permute-done.refs_1_
  11.1 2.5 %collective-permute-done.2.refs_3_ = bf16[128,768]{1,0:T(8,128)(2,1)S(1)} collective-permute-done((bf16[128,768]{1,0:T(8,128)(2,1)}, bf16[128,768]{1,0:T(8,128)(2,1)S(1)}, u32[]{:S(2)}, u32[]{:S(2)}) %collective-permute-start.2) | collective-permute-done | bytes 196640 | tf_op jit(solution)/shard_map/ppermute | solution.py:353
  13.6 1.4 %collective-permute-done.1.refs_2_ = bf16[128,768]{1,0:T(8,128)(2,1)S(1)} collective-permute-done((bf16[128,768]{1,0:T(8,128)(2,1)}, bf16[128,768]{1,0:T(8,128)(2,1)S(1)}, u32[]{:S(2)}, u32[]{:S(2)}) %collective-permute-start.1) | collective-permute-done | bytes 196640 | tf_op jit(solution)/shard_map/ppermute | solution.py:353
  14.9 0.5 %aggregate.1 = (bf16[136,768]{1,0:T(8,128)(2,1)S(1)}, bf16[132,768]{1,0:T(8,128)(2,1)S(1)}) custom-call(s32[8,128]{1,0:T(8,128)S(1)} %get-tuple-element.28.from_ref, f32[8,768]{1,0:T(8,128)S(1)} %get-tuple-element.29.extra_ref, bf16[128,1024]{1,0:T(8,128)(2,1)S(1)} %get-tuple-element.30.masked_ref, bf16[128,768]{1,0:T(8,128)(2,1)S(1)} %get-tuple-element.31.refs_0_, ...), custom_call_target="tpu_custom_call" | custom-call | flops 1000000000 | bytes 4000000 | tf_op jit(solution)/shard_map/aggregate/pallas_call | solution.py:385
  15.5 2.7 %collective-permute-start.3 = (bf16[136,768]{1,0:T(8,128)(2,1)S(1)}, bf16[136,768]{1,0:T(8,128)(2,1)S(1)}, u32[]{:S(2)}, u32[]{:S(2)}) collective-permute-start(bf16[136,768]{1,0:T(8,128)(2,1)S(1)} %get-tuple-element.32), channel_id=1, source_target_pairs={{0,4},{1,5},{2,6},{3,7},{4,0},{5,1},{6,2},{7,3},{8,12},{9,13},{10,... | collective-permute-start | bytes 626696 | tf_op jit(solution)/shard_map/ppermute | solution.py:353
  18.1 0.0 collective-permute-start.6
  18.1 1.6 %collective-permute-start.5 = (bf16[132,768]{1,0:T(8,128)(2,1)S(1)}, bf16[132,768]{1,0:T(8,128)(2,1)S(1)}, u32[]{:S(2)}, u32[]{:S(2)}) collective-permute-start(bf16[132,768]{1,0:T(8,128)(2,1)S(1)} %get-tuple-element.33.refs_2_), channel_id=1, source_target_pairs={{0,2},{1,3},{2,0},{3,1},{4,6},{5,7},{6,4},{7,5},{8,10},{9,11},{10,... | collective-permute-start | bytes 608264 | tf_op jit(solution)/shard_map/ppermute | solution.py:353
  19.7 0.0 collective-permute-done.6.refs_3_
  19.7 0.0 copy-done
  19.7 0.0 copy-done.1
  19.7 3.1 %part.3 = (bf16[128,768]{1,0:T(8,128)(2,1)S(1)}, bf16[128,4096]{1,0:T(8,128)(2,1)S(1)}, f32[128,768]{1,0:T(8,128)S(1)}, f32[128,768]{1,0:T(8,128)S(1)}) custom-call(bf16[768,1536]{1,0:T(8,128)(2,1)S(1)} %copy-done, bf16[768,768]{1,0:T(8,128)(2,1)S(1)} %copy-done.1, bf16[132,768]{1,0:T(8,128)(2,1)S(1)} %get-tuple-element.33.refs_2_, ...), custom_call_target="tpu_custom_call" | custom-call | flops 1000 | bytes 1000 | tf_op jit(solution)/shard_map/part/pallas_call | solution.py:331
  22.8 2.8 %collective-permute-done.3.refs_1_ = bf16[136,768]{1,0:T(8,128)(2,1)S(1)} collective-permute-done((bf16[136,768]{1,0:T(8,128)(2,1)S(1)}, bf16[136,768]{1,0:T(8,128)(2,1)S(1)}, u32[]{:S(2)}, u32[]{:S(2)}) %collective-permute-start.3) | collective-permute-done | bytes 208928 | tf_op jit(solution)/shard_map/ppermute | solution.py:353
  25.6 0.0 collective-permute-start.8
  25.6 0.6 %collective-permute-start.4 = (bf16[136,768]{1,0:T(8,128)(2,1)S(1)}, bf16[136,768]{1,0:T(8,128)(2,1)S(1)}, u32[]{:S(2)}, u32[]{:S(2)}) collective-permute-start(bf16[136,768]{1,0:T(8,128)(2,1)S(1)} %collective-permute-done.3.refs_1_), channel_id=1, source_target_pairs={{0,2},{1,3},{2,0},{3,1},{4,6},{5,7},{6,4},{7,5},{8,10},{9,11},{10,... | collective-permute-start | bytes 626696 | tf_op jit(solution)/shard_map/ppermute | solution.py:353
  26.3 1.6 %collective-permute-done.5.refs_0_ = bf16[132,768]{1,0:T(8,128)(2,1)S(1)} collective-permute-done((bf16[132,768]{1,0:T(8,128)(2,1)S(1)}, bf16[132,768]{1,0:T(8,128)(2,1)S(1)}, u32[]{:S(2)}, u32[]{:S(2)}) %collective-permute-start.5) | collective-permute-done | bytes 202784 | tf_op jit(solution)/shard_map/ppermute | solution.py:353
  27.9 0.0 collective-permute-start.7
  27.9 0.8 %project.2 = (bf16[256,128]{1,0:T(8,128)(2,1)S(1)}, bf16[256,768]{1,0:T(8,128)(2,1)S(1)}, bf16[256,768]{1,0:T(8,128)(2,1)S(1)}) custom-call(bf16[768,1536]{1,0:T(8,128)(2,1)S(1)} %copy-done, bf16[768,768]{1,0:T(8,128)(2,1)S(1)} %copy-done.1, bf16[132,768]{1,0:T(8,128)(2,1)S(1)} %collective-permute-done.5.refs_0_, ...), custom_call_target="tpu_custom_call" | custom-call | flops 1000 | bytes 1000 | tf_op jit(solution)/shard_map/project/pallas_call | solution.py:310
  28.7 0.7 %collective-permute-done.7.refs_2_ = bf16[132,768]{1,0:T(8,128)(2,1)S(1)} collective-permute-done((bf16[132,768]{1,0:T(8,128)(2,1)S(1)}, bf16[132,768]{1,0:T(8,128)(2,1)S(1)}, u32[]{:S(2)}, u32[]{:S(2)}) %collective-permute-start.7) | collective-permute-done | bytes 202784 | tf_op jit(solution)/shard_map/ppermute | solution.py:353
  29.3 0.0 collective-permute-done.8.refs_3_
  29.3 3.6 %part.4 = (f32[128,768]{1,0:T(8,128)S(1)}, f32[128,768]{1,0:T(8,128)S(1)}, f32[128,768]{1,0:T(8,128)S(1)}) custom-call(bf16[768,1536]{1,0:T(8,128)(2,1)S(1)} %copy-done, bf16[768,768]{1,0:T(8,128)(2,1)S(1)} %copy-done.1, bf16[132,768]{1,0:T(8,128)(2,1)S(1)} %collective-permute-done.7.refs_2_, bf16[136,768]{1,0:T(8,128)(2,1)S(1)} %collective-permute-done.8.refs_3_, ...), custom_call_target="tpu_custom_call" | custom-call | flops 1000 | bytes 1000 | tf_op jit(solution)/shard_map/part/pallas_call | solution.py:331
  32.9 0.3 collective-permute-done.4.refs_0_
  33.2 0.0 collective-permute-start.9
  33.2 0.5 %project.3 = (bf16[128,128]{1,0:T(8,128)(2,1)S(1)}, bf16[128,768]{1,0:T(8,128)(2,1)S(1)}, bf16[128,768]{1,0:T(8,128)(2,1)S(1)}) custom-call(bf16[768,1536]{1,0:T(8,128)(2,1)S(1)} %copy-done, bf16[768,768]{1,0:T(8,128)(2,1)S(1)} %copy-done.1, bf16[136,768]{1,0:T(8,128)(2,1)S(1)} %collective-permute-done.4.refs_0_), custom_call_target="tpu_custom_call" | custom-call | flops 1000 | bytes 1000 | tf_op jit(solution)/shard_map/project/pallas_call | solution.py:310
  33.7 1.0 %collective-permute-done.9.refs_2_ = bf16[136,768]{1,0:T(8,128)(2,1)S(1)} collective-permute-done((bf16[136,768]{1,0:T(8,128)(2,1)S(1)}, bf16[136,768]{1,0:T(8,128)(2,1)S(1)}, u32[]{:S(2)}, u32[]{:S(2)}) %collective-permute-start.9) | collective-permute-done | bytes 208928 | tf_op jit(solution)/shard_map/ppermute | solution.py:353
  34.7 2.8 %part.5 = bf16[128,768]{1,0:T(8,128)(2,1)} custom-call(bf16[768,1536]{1,0:T(8,128)(2,1)S(1)} %copy-done, bf16[768,768]{1,0:T(8,128)(2,1)S(1)} %copy-done.1, bf16[136,768]{1,0:T(8,128)(2,1)S(1)} %collective-permute-done.9.refs_2_, bf16[128,128]{1,0:T(8,128)(2,1)S(1)} %get-tuple-element.48.refs_3_, bf16[128,768]{1,0:T(8,128)(2,1)S(1)} %get-tuple-element.49.refs_4_, ...), custom_call_target="tpu_custom_call" | custom-call | flops 1000000000 | bytes 4000000 | tf_op jit(solution)/shard_map/part/pallas_call | solution.py:331
Async XLA Ops:
  0.0 11.0 %collective-permute-start = (bf16[128,768]{1,0:T(8,128)(2,1)}, bf16[128,768]{1,0:T(8,128)(2,1)S(1)}, u32[]{:S(2)}, u32[]{:S(2)}) collective-permute-start(bf16[128,768]{1,0:T(8,128)(2,1)} %features_ref.1), channel_id=1, source_target_pairs={{0,8},{8,0},{16,24},{24,16},{1,9},{9,1},{17,25},{25,17},{2,10},{10... | collective-permute-start | bytes 589832 | tf_op jit(solution)/shard_map/ppermute | solution.py:353
  2.9 10.6 %collective-permute-start.2 = (bf16[128,768]{1,0:T(8,128)(2,1)}, bf16[128,768]{1,0:T(8,128)(2,1)S(1)}, u32[]{:S(2)}, u32[]{:S(2)}) collective-permute-start(bf16[128,768]{1,0:T(8,128)(2,1)} %features_ref.1), channel_id=1, source_target_pairs={{0,24},{8,16},{16,8},{24,0},{1,25},{9,17},{17,9},{25,1},{2,26},{10... | collective-permute-start | bytes 589832 | tf_op jit(solution)/shard_map/ppermute | solution.py:353
  4.4 10.5 %collective-permute-start.1 = (bf16[128,768]{1,0:T(8,128)(2,1)}, bf16[128,768]{1,0:T(8,128)(2,1)S(1)}, u32[]{:S(2)}, u32[]{:S(2)}) collective-permute-start(bf16[128,768]{1,0:T(8,128)(2,1)} %features_ref.1), channel_id=1, source_target_pairs={{0,16},{8,24},{16,0},{24,8},{1,17},{9,25},{17,1},{25,9},{2,18},{10... | collective-permute-start | bytes 589832 | tf_op jit(solution)/shard_map/ppermute | solution.py:353
  5.1 1.0 %copy-start.2 = (bf16[128,1024]{1,0:T(8,128)(2,1)S(1)}, bf16[128,1024]{1,0:T(8,128)(2,1)}, u32[]{:S(2)}) copy-start(bf16[128,1024]{1,0:T(8,128)(2,1)} %tiles_ref.1) | copy-start | bytes 786436
  6.1 0.9 %copy-start.3 = (bf16[128,768]{1,0:T(8,128)(2,1)S(1)}, bf16[128,768]{1,0:T(8,128)(2,1)}, u32[]{:S(2)}) copy-start(bf16[128,768]{1,0:T(8,128)(2,1)} %features_ref.1) | copy-start | bytes 589828
  7.0 0.8 %copy-start.4 = (f32[32,256]{1,0:T(8,128)S(1)}, f32[32,256]{1,0:T(8,128)}, u32[]{:S(2)}) copy-start(f32[32,256]{1,0:T(8,128)} %table_ref.1) | copy-start | bytes 98308
  7.8 0.7 %copy-start.5 = (s32[1,8]{1,0:T(1,128)S(1)}, s32[1,8]{1,0:T(1,128)}, u32[]{:S(2)}) copy-start(s32[1,8]{1,0:T(1,128)} %src_ref.1) | copy-start | bytes 100
  8.4 0.7 %copy-start.6 = (s32[128]{0:T(128)S(1)}, s32[128]{0:T(128)}, u32[]{:S(2)}) copy-start(s32[128]{0:T(128)} %param.12) | copy-start | bytes 1540
  11.0 8.7 %copy-start = (bf16[768,1536]{1,0:T(8,128)(2,1)S(1)}, bf16[768,1536]{1,0:T(8,128)(2,1)}, u32[]{:S(2)}) copy-start(bf16[768,1536]{1,0:T(8,128)(2,1)} %refs_0_.5) | copy-start | bytes 7077892
  11.0 8.7 %copy-start.1 = (bf16[768,768]{1,0:T(8,128)(2,1)S(1)}, bf16[768,768]{1,0:T(8,128)(2,1)}, u32[]{:S(2)}) copy-start(bf16[768,768]{1,0:T(8,128)(2,1)} %refs_1_.5) | copy-start | bytes 3538948
  15.5 10.2 %collective-permute-start.3 = (bf16[136,768]{1,0:T(8,128)(2,1)S(1)}, bf16[136,768]{1,0:T(8,128)(2,1)S(1)}, u32[]{:S(2)}, u32[]{:S(2)}) collective-permute-start(bf16[136,768]{1,0:T(8,128)(2,1)S(1)} %get-tuple-element.32), channel_id=1, source_target_pairs={{0,4},{1,5},{2,6},{3,7},{4,0},{5,1},{6,2},{7,3},{8,12},{9,13},{10,... | collective-permute-start | bytes 626696 | tf_op jit(solution)/shard_map/ppermute | solution.py:353
  18.1 1.6 %collective-permute-start.6 = (bf16[132,768]{1,0:T(8,128)(2,1)S(1)}, bf16[132,768]{1,0:T(8,128)(2,1)S(1)}, u32[]{:S(2)}, u32[]{:S(2)}) collective-permute-start(bf16[132,768]{1,0:T(8,128)(2,1)S(1)} %get-tuple-element.33.refs_2_), channel_id=1, source_target_pairs={{0,1},{1,0},{2,3},{3,2},{4,5},{5,4},{6,7},{7,6},{8,9},{9,8},{10,11... | collective-permute-start | bytes 608264 | tf_op jit(solution)/shard_map/ppermute | solution.py:353
  18.1 9.7 %collective-permute-start.5 = (bf16[132,768]{1,0:T(8,128)(2,1)S(1)}, bf16[132,768]{1,0:T(8,128)(2,1)S(1)}, u32[]{:S(2)}, u32[]{:S(2)}) collective-permute-start(bf16[132,768]{1,0:T(8,128)(2,1)S(1)} %get-tuple-element.33.refs_2_), channel_id=1, source_target_pairs={{0,2},{1,3},{2,0},{3,1},{4,6},{5,7},{6,4},{7,5},{8,10},{9,11},{10,... | collective-permute-start | bytes 608264 | tf_op jit(solution)/shard_map/ppermute | solution.py:353
  25.6 3.7 %collective-permute-start.8 = (bf16[136,768]{1,0:T(8,128)(2,1)S(1)}, bf16[136,768]{1,0:T(8,128)(2,1)S(1)}, u32[]{:S(2)}, u32[]{:S(2)}) collective-permute-start(bf16[136,768]{1,0:T(8,128)(2,1)S(1)} %collective-permute-done.3.refs_1_), channel_id=1, source_target_pairs={{0,1},{1,0},{2,3},{3,2},{4,5},{5,4},{6,7},{7,6},{8,9},{9,8},{10,11... | collective-permute-start | bytes 626696 | tf_op jit(solution)/shard_map/ppermute | solution.py:353
  25.6 7.6 %collective-permute-start.4 = (bf16[136,768]{1,0:T(8,128)(2,1)S(1)}, bf16[136,768]{1,0:T(8,128)(2,1)S(1)}, u32[]{:S(2)}, u32[]{:S(2)}) collective-permute-start(bf16[136,768]{1,0:T(8,128)(2,1)S(1)} %collective-permute-done.3.refs_1_), channel_id=1, source_target_pairs={{0,2},{1,3},{2,0},{3,1},{4,6},{5,7},{6,4},{7,5},{8,10},{9,11},{10,... | collective-permute-start | bytes 626696 | tf_op jit(solution)/shard_map/ppermute | solution.py:353
  27.9 1.5 %collective-permute-start.7 = (bf16[132,768]{1,0:T(8,128)(2,1)S(1)}, bf16[132,768]{1,0:T(8,128)(2,1)S(1)}, u32[]{:S(2)}, u32[]{:S(2)}) collective-permute-start(bf16[132,768]{1,0:T(8,128)(2,1)S(1)} %collective-permute-done.5.refs_0_), channel_id=1, source_target_pairs={{0,1},{1,0},{2,3},{3,2},{4,5},{5,4},{6,7},{7,6},{8,9},{9,8},{10,11... | collective-permute-start | bytes 608264 | tf_op jit(solution)/shard_map/ppermute | solution.py:353
  33.2 1.5 %collective-permute-start.9 = (bf16[136,768]{1,0:T(8,128)(2,1)S(1)}, bf16[136,768]{1,0:T(8,128)(2,1)S(1)}, u32[]{:S(2)}, u32[]{:S(2)}) collective-permute-start(bf16[136,768]{1,0:T(8,128)(2,1)S(1)} %collective-permute-done.4.refs_0_), channel_id=1, source_target_pairs={{0,1},{1,0},{2,3},{3,2},{4,5},{5,4},{6,7},{7,6},{8,9},{9,8},{10,11... | collective-permute-start | bytes 626696 | tf_op jit(solution)/shard_map/ppermute | solution.py:353

commit v14 on v13

--- a/solution.py
+++ b/solution.py
@@ -100,10 +100,10 @@
         )
 
 
-def aggregate_kernel(from_ref, extra_ref, masked_ref, *refs):
+def aggregate_kernel(order, from_ref, extra_ref, masked_ref, *refs):
     feature_refs, out_ref, short_ref, held = refs[:-3], refs[-3], refs[-2], refs[-1]
     rows = feature_refs[0].shape[0]
-    for d, ref in enumerate(feature_refs):
+    for d, ref in zip([0, *order], feature_refs):
         held[d * rows : (d + 1) * rows, :] = ref[...]
     picked = []
     for t in range(TILES):
@@ -364,7 +364,8 @@
     chips = seq_count // 2
     any_space = pl.BlockSpec(memory_space=pl.ANY)
 
-    received = [swap(features, "group", d) for d in range(groups - 1, 0, -1)][::-1]
+    order = [1, *range(groups - 1, 1, -1)]
+    received = [swap(features, "group", d) for d in order]
     own_bucket = node_bucket.reshape(1, rows)
 
     bias, own_features, masked, extra, source = pl.pallas_call(
@@ -383,7 +384,7 @@
     )(tile_count, lax.axis_index("group").reshape(1), tile_src, bias_table, own_bucket, features, tiles)
 
     own, short = pl.pallas_call(
-        aggregate_kernel,
+        lambda *refs: aggregate_kernel(order, *refs),
         out_shape=[shape(rows + EXTRA, width), shape(rows + EXTRA // 2, width)],
         in_specs=[vmem()] * (3 + groups),
         out_specs=[vmem()] * 2,

time: 37.7 us -> 37.7 us (level)
  transfers between devices with their start and end apart: 10 -> 10, of which waited for: 7 -> 6; matrix products, arithmetic and copies ran while one was open for 0% -> 0% of each run, Pallas kernels for 26% -> 26%
where the time goes in v14:
time: 37.7 us; the launch traced here: 37.5 us
  Pallas kernels  13.2 us (35%)
  waiting for transfers between devices  10.3 us (27%)
  starting transfers between devices  9.32 us (25%)
  local copies, waits for them, and re-layouts  3.95 us (10%)
  between operations  0.74 us (2%)
    ppermute x10, waiting for transfers between devices, swap(): lax.ppermute(array, axis, [(i, i ^ distance) for i in range(lax.axis_size...  10.3 us
    pallas_call x3, Pallas kernels, attend_part(): pl.pallas_call(lambda *refs: part_kernel(len(blocks), first, last, *refs)...  9.44 us
    ppermute x10, starting transfers between devices, swap(): lax.ppermute(array, axis, [(i, i ^ distance) for i in range(lax.axis_size...  9.32 us
    unnamed x14, local copies, waits for them, and re-layouts  3.95 us
    pallas_call x1, Pallas kernels, on_device(): pl.pallas_call(stage_kernel, out_shape=[shape(rows, H * LANES), shape(row...  1.95 us
    pallas_call x2, Pallas kernels, attend_part(): pl.pallas_call(project_kernel, out_shape=[shape(count, LANES), shape(coun...  1.27 us
  transfers between devices with their start and end apart: 10, of which 6 were waited for; matrix products, arithmetic and copies ran while one was open for 0% of the time, Pallas kernels for 26%

profile of v14, /device:TPU:0, one launch (start us, length us, event | category | flops | bytes accessed | tf_op | source)
XLA Modules:
  0.0 37.5 jit_solution(6459808773815393873)
XLA Ops:
  0.0 2.9 %collective-permute-start = (bf16[128,768]{1,0:T(8,128)(2,1)}, bf16[128,768]{1,0:T(8,128)(2,1)S(1)}, u32[]{:S(2)}, u32[]{:S(2)}) collective-permute-start(bf16[128,768]{1,0:T(8,128)(2,1)} %features_ref.1), channel_id=1, source_target_pairs={{0,8},{8,0},{16,24},{24,16},{1,9},{9,1},{17,25},{25,17},{2,10},{10... | collective-permute-start | bytes 589832 | tf_op jit(solution)/shard_map/ppermute | solution.py:353
  2.9 1.5 %collective-permute-start.2 = (bf16[128,768]{1,0:T(8,128)(2,1)}, bf16[128,768]{1,0:T(8,128)(2,1)S(1)}, u32[]{:S(2)}, u32[]{:S(2)}) collective-permute-start(bf16[128,768]{1,0:T(8,128)(2,1)} %features_ref.1), channel_id=1, source_target_pairs={{0,16},{8,24},{16,0},{24,8},{1,17},{9,25},{17,1},{25,9},{2,18},{10... | collective-permute-start | bytes 589832 | tf_op jit(solution)/shard_map/ppermute | solution.py:353
  4.5 0.0 collective-permute-start.1
  5.1 0.0 copy-start.2
  5.1 0.9 %copy-done.2 = bf16[128,1024]{1,0:T(8,128)(2,1)S(1)} copy-done((bf16[128,1024]{1,0:T(8,128)(2,1)S(1)}, bf16[128,1024]{1,0:T(8,128)(2,1)}, u32[]{:S(2)}) %copy-start.2) | copy-done | bytes 262168
  6.1 0.0 copy-start.3
  6.1 0.9 %copy-done.3 = bf16[128,768]{1,0:T(8,128)(2,1)S(1)} copy-done((bf16[128,768]{1,0:T(8,128)(2,1)S(1)}, bf16[128,768]{1,0:T(8,128)(2,1)}, u32[]{:S(2)}) %copy-start.3) | copy-done | bytes 196632
  7.0 0.0 copy-start.4
  7.0 0.8 %copy-done.4 = f32[32,256]{1,0:T(8,128)S(1)} copy-done((f32[32,256]{1,0:T(8,128)S(1)}, f32[32,256]{1,0:T(8,128)}, u32[]{:S(2)}) %copy-start.4) | copy-done | bytes 32792
  7.8 0.0 copy-start.5
  7.8 0.7 %copy-done.5 = s32[1,8]{1,0:T(1,128)S(1)} copy-done((s32[1,8]{1,0:T(1,128)S(1)}, s32[1,8]{1,0:T(1,128)}, u32[]{:S(2)}) %copy-start.5) | copy-done | bytes 56
  8.4 0.0 copy-start.6
  8.4 0.7 %copy-done.6 = s32[128]{0:T(128)S(1)} copy-done((s32[128]{0:T(128)S(1)}, s32[128]{0:T(128)}, u32[]{:S(2)}) %copy-start.6) | copy-done | bytes 536
  9.1 1.9 %stage.1 = (bf16[128,4096]{1,0:T(8,128)(2,1)S(1)}, bf16[128,768]{1,0:T(8,128)(2,1)S(1)}, bf16[128,1024]{1,0:T(8,128)(2,1)S(1)}, f32[8,768]{1,0:T(8,128)S(1)}, s32[8,128]{1,0:T(8,128)S(1)}) custom-call(s32[1]{0:T(128)S(6)} %copy.9.count_ref, s32[1]{0:T(128)} %bitcast.me_ref, s32[1,8]{1,0:T(1,128)S(1)} %copy-done.5, f32[32,256]{1,0:T(8,128)S(1)} %copy-done.4, ...), custom_call_target="tpu_custom_call" | custom-call | flops 1000000000 | bytes 4000000 | tf_op jit(solution)/shard_map/stage/pallas_call | solution.py:371
  11.0 0.0 copy-start
  11.0 0.0 copy-start.1
  11.0 0.0 collective-permute-done.refs_4_
  11.1 2.7 %collective-permute-done.2.refs_6_ = bf16[128,768]{1,0:T(8,128)(2,1)S(1)} collective-permute-done((bf16[128,768]{1,0:T(8,128)(2,1)}, bf16[128,768]{1,0:T(8,128)(2,1)S(1)}, u32[]{:S(2)}, u32[]{:S(2)}) %collective-permute-start.2) | collective-permute-done | bytes 196640 | tf_op jit(solution)/shard_map/ppermute | solution.py:353
  13.7 0.0 collective-permute-done.1.refs_5_
  13.7 0.5 %aggregate.1 = (bf16[136,768]{1,0:T(8,128)(2,1)S(1)}, bf16[132,768]{1,0:T(8,128)(2,1)S(1)}) custom-call(s32[8,128]{1,0:T(8,128)S(1)} %get-tuple-element.28.refs_0_, f32[8,768]{1,0:T(8,128)S(1)} %get-tuple-element.29.refs_1_, bf16[128,1024]{1,0:T(8,128)(2,1)S(1)} %get-tuple-element.30.refs_2_, bf16[128,768]{1,0:T(8,128)(2,1)S(1)} %get-tuple-element.31.refs_3_, ...), custom_call_target="tpu_custom_call" | custom-call | flops 1000000000 | bytes 4000000 | tf_op jit(solution)/shard_map/aggregate/pallas_call | solution.py:386
  14.3 2.7 %collective-permute-start.3 = (bf16[136,768]{1,0:T(8,128)(2,1)S(1)}, bf16[136,768]{1,0:T(8,128)(2,1)S(1)}, u32[]{:S(2)}, u32[]{:S(2)}) collective-permute-start(bf16[136,768]{1,0:T(8,128)(2,1)S(1)} %get-tuple-element.32), channel_id=1, source_target_pairs={{0,4},{1,5},{2,6},{3,7},{4,0},{5,1},{6,2},{7,3},{8,12},{9,13},{10,... | collective-permute-start | bytes 626696 | tf_op jit(solution)/shard_map/ppermute | solution.py:353
  16.9 0.0 collective-permute-start.6
  16.9 1.6 %collective-permute-start.5 = (bf16[132,768]{1,0:T(8,128)(2,1)S(1)}, bf16[132,768]{1,0:T(8,128)(2,1)S(1)}, u32[]{:S(2)}, u32[]{:S(2)}) collective-permute-start(bf16[132,768]{1,0:T(8,128)(2,1)S(1)} %get-tuple-element.33.refs_2_), channel_id=1, source_target_pairs={{0,2},{1,3},{2,0},{3,1},{4,6},{5,7},{6,4},{7,5},{8,10},{9,11},{10,... | collective-permute-start | bytes 608264 | tf_op jit(solution)/shard_map/ppermute | solution.py:353
  18.5 0.0 collective-permute-done.6.refs_3_
  18.5 0.0 copy-done
  18.5 0.0 copy-done.1
  18.5 3.1 %part.3 = (bf16[128,768]{1,0:T(8,128)(2,1)S(1)}, bf16[128,4096]{1,0:T(8,128)(2,1)S(1)}, f32[128,768]{1,0:T(8,128)S(1)}, f32[128,768]{1,0:T(8,128)S(1)}) custom-call(bf16[768,1536]{1,0:T(8,128)(2,1)S(1)} %copy-done, bf16[768,768]{1,0:T(8,128)(2,1)S(1)} %copy-done.1, bf16[132,768]{1,0:T(8,128)(2,1)S(1)} %get-tuple-element.33.refs_2_, ...), custom_call_target="tpu_custom_call" | custom-call | flops 1000 | bytes 1000 | tf_op jit(solution)/shard_map/part/pallas_call | solution.py:331
  21.6 4.0 %collective-permute-done.3.refs_1_ = bf16[136,768]{1,0:T(8,128)(2,1)S(1)} collective-permute-done((bf16[136,768]{1,0:T(8,128)(2,1)S(1)}, bf16[136,768]{1,0:T(8,128)(2,1)S(1)}, u32[]{:S(2)}, u32[]{:S(2)}) %collective-permute-start.3) | collective-permute-done | bytes 208928 | tf_op jit(solution)/shard_map/ppermute | solution.py:353
  25.6 0.0 collective-permute-start.8
  25.6 0.6 %collective-permute-start.4 = (bf16[136,768]{1,0:T(8,128)(2,1)S(1)}, bf16[136,768]{1,0:T(8,128)(2,1)S(1)}, u32[]{:S(2)}, u32[]{:S(2)}) collective-permute-start(bf16[136,768]{1,0:T(8,128)(2,1)S(1)} %collective-permute-done.3.refs_1_), channel_id=1, source_target_pairs={{0,2},{1,3},{2,0},{3,1},{4,6},{5,7},{6,4},{7,5},{8,10},{9,11},{10,... | collective-permute-start | bytes 626696 | tf_op jit(solution)/shard_map/ppermute | solution.py:353
  26.3 1.6 %collective-permute-done.5.refs_0_ = bf16[132,768]{1,0:T(8,128)(2,1)S(1)} collective-permute-done((bf16[132,768]{1,0:T(8,128)(2,1)S(1)}, bf16[132,768]{1,0:T(8,128)(2,1)S(1)}, u32[]{:S(2)}, u32[]{:S(2)}) %collective-permute-start.5) | collective-permute-done | bytes 202784 | tf_op jit(solution)/shard_map/ppermute | solution.py:353
  27.8 0.0 collective-permute-start.7
  27.9 0.8 %project.2 = (bf16[256,128]{1,0:T(8,128)(2,1)S(1)}, bf16[256,768]{1,0:T(8,128)(2,1)S(1)}, bf16[256,768]{1,0:T(8,128)(2,1)S(1)}) custom-call(bf16[768,1536]{1,0:T(8,128)(2,1)S(1)} %copy-done, bf16[768,768]{1,0:T(8,128)(2,1)S(1)} %copy-done.1, bf16[132,768]{1,0:T(8,128)(2,1)S(1)} %collective-permute-done.5.refs_0_, ...), custom_call_target="tpu_custom_call" | custom-call | flops 1000 | bytes 1000 | tf_op jit(solution)/shard_map/project/pallas_call | solution.py:310
  28.6 0.7 %collective-permute-done.7.refs_2_ = bf16[132,768]{1,0:T(8,128)(2,1)S(1)} collective-permute-done((bf16[132,768]{1,0:T(8,128)(2,1)S(1)}, bf16[132,768]{1,0:T(8,128)(2,1)S(1)}, u32[]{:S(2)}, u32[]{:S(2)}) %collective-permute-start.7) | collective-permute-done | bytes 202784 | tf_op jit(solution)/shard_map/ppermute | solution.py:353
  29.3 0.0 collective-permute-done.8.refs_3_
  29.3 3.6 %part.4 = (f32[128,768]{1,0:T(8,128)S(1)}, f32[128,768]{1,0:T(8,128)S(1)}, f32[128,768]{1,0:T(8,128)S(1)}) custom-call(bf16[768,1536]{1,0:T(8,128)(2,1)S(1)} %copy-done, bf16[768,768]{1,0:T(8,128)(2,1)S(1)} %copy-done.1, bf16[132,768]{1,0:T(8,128)(2,1)S(1)} %collective-permute-done.7.refs_2_, bf16[136,768]{1,0:T(8,128)(2,1)S(1)} %collective-permute-done.8.refs_3_, ...), custom_call_target="tpu_custom_call" | custom-call | flops 1000 | bytes 1000 | tf_op jit(solution)/shard_map/part/pallas_call | solution.py:331
  32.9 0.3 collective-permute-done.4.refs_0_
  33.2 0.0 collective-permute-start.9
  33.2 0.5 %project.3 = (bf16[128,128]{1,0:T(8,128)(2,1)S(1)}, bf16[128,768]{1,0:T(8,128)(2,1)S(1)}, bf16[128,768]{1,0:T(8,128)(2,1)S(1)}) custom-call(bf16[768,1536]{1,0:T(8,128)(2,1)S(1)} %copy-done, bf16[768,768]{1,0:T(8,128)(2,1)S(1)} %copy-done.1, bf16[136,768]{1,0:T(8,128)(2,1)S(1)} %collective-permute-done.4.refs_0_), custom_call_target="tpu_custom_call" | custom-call | flops 1000 | bytes 1000 | tf_op jit(solution)/shard_map/project/pallas_call | solution.py:310
  33.7 1.0 %collective-permute-done.9.refs_2_ = bf16[136,768]{1,0:T(8,128)(2,1)S(1)} collective-permute-done((bf16[136,768]{1,0:T(8,128)(2,1)S(1)}, bf16[136,768]{1,0:T(8,128)(2,1)S(1)}, u32[]{:S(2)}, u32[]{:S(2)}) %collective-permute-start.9) | collective-permute-done | bytes 208928 | tf_op jit(solution)/shard_map/ppermute | solution.py:353
  34.7 2.8 %part.5 = bf16[128,768]{1,0:T(8,128)(2,1)} custom-call(bf16[768,1536]{1,0:T(8,128)(2,1)S(1)} %copy-done, bf16[768,768]{1,0:T(8,128)(2,1)S(1)} %copy-done.1, bf16[136,768]{1,0:T(8,128)(2,1)S(1)} %collective-permute-done.9.refs_2_, bf16[128,128]{1,0:T(8,128)(2,1)S(1)} %get-tuple-element.48.refs_3_, bf16[128,768]{1,0:T(8,128)(2,1)S(1)} %get-tuple-element.49.refs_4_, ...), custom_call_target="tpu_custom_call" | custom-call | flops 1000000000 | bytes 4000000 | tf_op jit(solution)/shard_map/part/pallas_call | solution.py:331
Async XLA Ops:
  0.0 11.0 %collective-permute-start = (bf16[128,768]{1,0:T(8,128)(2,1)}, bf16[128,768]{1,0:T(8,128)(2,1)S(1)}, u32[]{:S(2)}, u32[]{:S(2)}) collective-permute-start(bf16[128,768]{1,0:T(8,128)(2,1)} %features_ref.1), channel_id=1, source_target_pairs={{0,8},{8,0},{16,24},{24,16},{1,9},{9,1},{17,25},{25,17},{2,10},{10... | collective-permute-start | bytes 589832 | tf_op jit(solution)/shard_map/ppermute | solution.py:353
  2.9 10.8 %collective-permute-start.2 = (bf16[128,768]{1,0:T(8,128)(2,1)}, bf16[128,768]{1,0:T(8,128)(2,1)S(1)}, u32[]{:S(2)}, u32[]{:S(2)}) collective-permute-start(bf16[128,768]{1,0:T(8,128)(2,1)} %features_ref.1), channel_id=1, source_target_pairs={{0,16},{8,24},{16,0},{24,8},{1,17},{9,25},{17,1},{25,9},{2,18},{10... | collective-permute-start | bytes 589832 | tf_op jit(solution)/shard_map/ppermute | solution.py:353
  4.5 9.3 %collective-permute-start.1 = (bf16[128,768]{1,0:T(8,128)(2,1)}, bf16[128,768]{1,0:T(8,128)(2,1)S(1)}, u32[]{:S(2)}, u32[]{:S(2)}) collective-permute-start(bf16[128,768]{1,0:T(8,128)(2,1)} %features_ref.1), channel_id=1, source_target_pairs={{0,24},{8,16},{16,8},{24,0},{1,25},{9,17},{17,9},{25,1},{2,26},{10... | collective-permute-start | bytes 589832 | tf_op jit(solution)/shard_map/ppermute | solution.py:353
  5.1 1.0 %copy-start.2 = (bf16[128,1024]{1,0:T(8,128)(2,1)S(1)}, bf16[128,1024]{1,0:T(8,128)(2,1)}, u32[]{:S(2)}) copy-start(bf16[128,1024]{1,0:T(8,128)(2,1)} %tiles_ref.1) | copy-start | bytes 786436
  6.1 0.9 %copy-start.3 = (bf16[128,768]{1,0:T(8,128)(2,1)S(1)}, bf16[128,768]{1,0:T(8,128)(2,1)}, u32[]{:S(2)}) copy-start(bf16[128,768]{1,0:T(8,128)(2,1)} %features_ref.1) | copy-start | bytes 589828
  7.0 0.8 %copy-start.4 = (f32[32,256]{1,0:T(8,128)S(1)}, f32[32,256]{1,0:T(8,128)}, u32[]{:S(2)}) copy-start(f32[32,256]{1,0:T(8,128)} %table_ref.1) | copy-start | bytes 98308
  7.8 0.7 %copy-start.5 = (s32[1,8]{1,0:T(1,128)S(1)}, s32[1,8]{1,0:T(1,128)}, u32[]{:S(2)}) copy-start(s32[1,8]{1,0:T(1,128)} %src_ref.1) | copy-start | bytes 100
  8.4 0.7 %copy-start.6 = (s32[128]{0:T(128)S(1)}, s32[128]{0:T(128)}, u32[]{:S(2)}) copy-start(s32[128]{0:T(128)} %param.12) | copy-start | bytes 1540
  11.0 7.5 %copy-start = (bf16[768,1536]{1,0:T(8,128)(2,1)S(1)}, bf16[768,1536]{1,0:T(8,128)(2,1)}, u32[]{:S(2)}) copy-start(bf16[768,1536]{1,0:T(8,128)(2,1)} %refs_0_.5) | copy-start | bytes 7077892
  11.0 7.5 %copy-start.1 = (bf16[768,768]{1,0:T(8,128)(2,1)S(1)}, bf16[768,768]{1,0:T(8,128)(2,1)}, u32[]{:S(2)}) copy-start(bf16[768,768]{1,0:T(8,128)(2,1)} %refs_1_.5) | copy-start | bytes 3538948
  14.3 11.4 %collective-permute-start.3 = (bf16[136,768]{1,0:T(8,128)(2,1)S(1)}, bf16[136,768]{1,0:T(8,128)(2,1)S(1)}, u32[]{:S(2)}, u32[]{:S(2)}) collective-permute-start(bf16[136,768]{1,0:T(8,128)(2,1)S(1)} %get-tuple-element.32), channel_id=1, source_target_pairs={{0,4},{1,5},{2,6},{3,7},{4,0},{5,1},{6,2},{7,3},{8,12},{9,13},{10,... | collective-permute-start | bytes 626696 | tf_op jit(solution)/shard_map/ppermute | solution.py:353
  16.9 1.6 %collective-permute-start.6 = (bf16[132,768]{1,0:T(8,128)(2,1)S(1)}, bf16[132,768]{1,0:T(8,128)(2,1)S(1)}, u32[]{:S(2)}, u32[]{:S(2)}) collective-permute-start(bf16[132,768]{1,0:T(8,128)(2,1)S(1)} %get-tuple-element.33.refs_2_), channel_id=1, source_target_pairs={{0,1},{1,0},{2,3},{3,2},{4,5},{5,4},{6,7},{7,6},{8,9},{9,8},{10,11... | collective-permute-start | bytes 608264 | tf_op jit(solution)/shard_map/ppermute | solution.py:353
  16.9 10.9 %collective-permute-start.5 = (bf16[132,768]{1,0:T(8,128)(2,1)S(1)}, bf16[132,768]{1,0:T(8,128)(2,1)S(1)}, u32[]{:S(2)}, u32[]{:S(2)}) collective-permute-start(bf16[132,768]{1,0:T(8,128)(2,1)S(1)} %get-tuple-element.33.refs_2_), channel_id=1, source_target_pairs={{0,2},{1,3},{2,0},{3,1},{4,6},{5,7},{6,4},{7,5},{8,10},{9,11},{10,... | collective-permute-start | bytes 608264 | tf_op jit(solution)/shard_map/ppermute | solution.py:353
  25.6 3.7 %collective-permute-start.8 = (bf16[136,768]{1,0:T(8,128)(2,1)S(1)}, bf16[136,768]{1,0:T(8,128)(2,1)S(1)}, u32[]{:S(2)}, u32[]{:S(2)}) collective-permute-start(bf16[136,768]{1,0:T(8,128)(2,1)S(1)} %collective-permute-done.3.refs_1_), channel_id=1, source_target_pairs={{0,1},{1,0},{2,3},{3,2},{4,5},{5,4},{6,7},{7,6},{8,9},{9,8},{10,11... | collective-permute-start | bytes 626696 | tf_op jit(solution)/shard_map/ppermute | solution.py:353
  25.6 7.6 %collective-permute-start.4 = (bf16[136,768]{1,0:T(8,128)(2,1)S(1)}, bf16[136,768]{1,0:T(8,128)(2,1)S(1)}, u32[]{:S(2)}, u32[]{:S(2)}) collective-permute-start(bf16[136,768]{1,0:T(8,128)(2,1)S(1)} %collective-permute-done.3.refs_1_), channel_id=1, source_target_pairs={{0,2},{1,3},{2,0},{3,1},{4,6},{5,7},{6,4},{7,5},{8,10},{9,11},{10,... | collective-permute-start | bytes 626696 | tf_op jit(solution)/shard_map/ppermute | solution.py:353
  27.8 1.5 %collective-permute-start.7 = (bf16[132,768]{1,0:T(8,128)(2,1)S(1)}, bf16[132,768]{1,0:T(8,128)(2,1)S(1)}, u32[]{:S(2)}, u32[]{:S(2)}) collective-permute-start(bf16[132,768]{1,0:T(8,128)(2,1)S(1)} %collective-permute-done.5.refs_0_), channel_id=1, source_target_pairs={{0,1},{1,0},{2,3},{3,2},{4,5},{5,4},{6,7},{7,6},{8,9},{9,8},{10,11... | collective-permute-start | bytes 608264 | tf_op jit(solution)/shard_map/ppermute | solution.py:353
  33.2 1.5 %collective-permute-start.9 = (bf16[136,768]{1,0:T(8,128)(2,1)S(1)}, bf16[136,768]{1,0:T(8,128)(2,1)S(1)}, u32[]{:S(2)}, u32[]{:S(2)}) collective-permute-start(bf16[136,768]{1,0:T(8,128)(2,1)S(1)} %collective-permute-done.4.refs_0_), channel_id=1, source_target_pairs={{0,1},{1,0},{2,3},{3,2},{4,5},{5,4},{6,7},{7,6},{8,9},{9,8},{10,11... | collective-permute-start | bytes 626696 | tf_op jit(solution)/shard_map/ppermute | solution.py:353

commit v15 on v14

--- a/solution.py
+++ b/solution.py
@@ -398,11 +398,17 @@
     top = 1
     while 2 * top < chips:
         top *= 2
-    far[top] = swap(own, "seq", 2 * top)
-    step = 1
-    while step < top:
-        far[step] = swap(short, "seq", 2 * step)
-        step *= 2
+    if top == 2:
+        lead = [(i, i ^ (2 if i % 2 else 2 * top)) for i in range(seq_count)]
+        other = [(i, i ^ (2 * top if i % 2 else 2)) for i in range(seq_count)]
+        far[top] = lax.ppermute(own, "seq", lead)
+        far[1] = lax.ppermute(short, "seq", other)
+        far[top + 1] = lax.ppermute(far[top], "seq", other)
+    else:
+        step = top
+        while step:
+            far[step] = swap(own, "seq", 2 * step)
+            step //= 2
     for d in range(3, chips):
         if far[d] is None:
             far[d] = swap(far[d & (d - 1)], "seq", 2 * (d & -d))

time: 37.7 us -> 38.9 us (1.032)
  starting transfers between devices: 9.32 us -> 10.6 us
    ppermute x0 -> x3, starting transfers between devices: none -> 6.14 us  [the longest x1 2.65 us: on_device(): far[top] = lax.ppermute(own, 'seq', lead)]
    ppermute x10 -> x7, waiting for transfers between devices: 10.3 us -> 4.31 us  [swap(): lax.ppermute(array, axis, [(i, i ^ distance) for i in range(lax.axis_size...]
    ppermute x0 -> x3, waiting for transfers between devices: none -> 5.87 us  [the longest x1 4.79 us: on_device(): far[top] = lax.ppermute(own, 'seq', lead)]
    ppermute x10 -> x7, starting transfers between devices: 9.32 us -> 4.47 us  [swap(): lax.ppermute(array, axis, [(i, i ^ distance) for i in range(lax.axis_size...]
  transfers between devices with their start and end apart: 10 -> 10, of which waited for: 6 -> 5; matrix products, arithmetic and copies ran while one was open for 0% -> 0% of each run, Pallas kernels for 26% -> 26%
where the time goes in v15:
time: 38.9 us; the launch traced here: 38.7 us
  Pallas kernels  13.2 us (34%)
  starting transfers between devices  10.6 us (27%)
  waiting for transfers between devices  10.2 us (26%)
  local copies, waits for them, and re-layouts  3.95 us (10%)
  between operations  0.74 us (2%)
    pallas_call x3, Pallas kernels, attend_part(): pl.pallas_call(lambda *refs: part_kernel(len(blocks), first, last, *refs)...  9.45 us
    ppermute x1, waiting for transfers between devices, on_device(): far[top] = lax.ppermute(own, 'seq', lead)  4.79 us
    ppermute x7, starting transfers between devices, swap(): lax.ppermute(array, axis, [(i, i ^ distance) for i in range(lax.axis_size...  4.47 us
    ppermute x7, waiting for transfers between devices, swap(): lax.ppermute(array, axis, [(i, i ^ distance) for i in range(lax.axis_size...  4.31 us
    unnamed x14, local copies, waits for them, and re-layouts  3.95 us
    ppermute x1, starting transfers between devices, on_device(): far[top] = lax.ppermute(own, 'seq', lead)  2.65 us
    pallas_call x1, Pallas kernels, on_device(): pl.pallas_call(stage_kernel, out_shape=[shape(rows, H * LANES), shape(row...  1.95 us
    ppermute x1, starting transfers between devices, on_device(): far[top + 1] = lax.ppermute(far[top], 'seq', other)  1.91 us
  transfers between devices with their start and end apart: 10, of which 5 were waited for; matrix products, arithmetic and copies ran while one was open for 0% of the time, Pallas kernels for 26%

profile of v15, /device:TPU:0, one launch (start us, length us, event | category | flops | bytes accessed | tf_op | source)
XLA Modules:
  0.0 38.7 jit_solution(16650024702958522946)
XLA Ops:
  0.0 2.9 %collective-permute-start = (bf16[128,768]{1,0:T(8,128)(2,1)}, bf16[128,768]{1,0:T(8,128)(2,1)S(1)}, u32[]{:S(2)}, u32[]{:S(2)}) collective-permute-start(bf16[128,768]{1,0:T(8,128)(2,1)} %features_ref.1), channel_id=1, source_target_pairs={{0,8},{8,0},{16,24},{24,16},{1,9},{9,1},{17,25},{25,17},{2,10},{10... | collective-permute-start | bytes 589832 | tf_op jit(solution)/shard_map/ppermute | solution.py:353
  2.9 1.5 %collective-permute-start.2 = (bf16[128,768]{1,0:T(8,128)(2,1)}, bf16[128,768]{1,0:T(8,128)(2,1)S(1)}, u32[]{:S(2)}, u32[]{:S(2)}) collective-permute-start(bf16[128,768]{1,0:T(8,128)(2,1)} %features_ref.1), channel_id=1, source_target_pairs={{0,16},{8,24},{16,0},{24,8},{1,17},{9,25},{17,1},{25,9},{2,18},{10... | collective-permute-start | bytes 589832 | tf_op jit(solution)/shard_map/ppermute | solution.py:353
  4.5 0.0 collective-permute-start.1
  5.1 0.0 copy-start.2
  5.1 0.9 %copy-done.2 = bf16[128,1024]{1,0:T(8,128)(2,1)S(1)} copy-done((bf16[128,1024]{1,0:T(8,128)(2,1)S(1)}, bf16[128,1024]{1,0:T(8,128)(2,1)}, u32[]{:S(2)}) %copy-start.2) | copy-done | bytes 262168
  6.1 0.0 copy-start.3
  6.1 0.9 %copy-done.3 = bf16[128,768]{1,0:T(8,128)(2,1)S(1)} copy-done((bf16[128,768]{1,0:T(8,128)(2,1)S(1)}, bf16[128,768]{1,0:T(8,128)(2,1)}, u32[]{:S(2)}) %copy-start.3) | copy-done | bytes 196632
  7.0 0.0 copy-start.4
  7.0 0.8 %copy-done.4 = f32[32,256]{1,0:T(8,128)S(1)} copy-done((f32[32,256]{1,0:T(8,128)S(1)}, f32[32,256]{1,0:T(8,128)}, u32[]{:S(2)}) %copy-start.4) | copy-done | bytes 32792
  7.8 0.0 copy-start.5
  7.8 0.7 %copy-done.5 = s32[1,8]{1,0:T(1,128)S(1)} copy-done((s32[1,8]{1,0:T(1,128)S(1)}, s32[1,8]{1,0:T(1,128)}, u32[]{:S(2)}) %copy-start.5) | copy-done | bytes 56
  8.4 0.0 copy-start.6
  8.4 0.7 %copy-done.6 = s32[128]{0:T(128)S(1)} copy-done((s32[128]{0:T(128)S(1)}, s32[128]{0:T(128)}, u32[]{:S(2)}) %copy-start.6) | copy-done | bytes 536
  9.1 1.9 %stage.1 = (bf16[128,4096]{1,0:T(8,128)(2,1)S(1)}, bf16[128,768]{1,0:T(8,128)(2,1)S(1)}, bf16[128,1024]{1,0:T(8,128)(2,1)S(1)}, f32[8,768]{1,0:T(8,128)S(1)}, s32[8,128]{1,0:T(8,128)S(1)}) custom-call(s32[1]{0:T(128)S(6)} %copy.9.count_ref, s32[1]{0:T(128)} %bitcast.me_ref, s32[1,8]{1,0:T(1,128)S(1)} %copy-done.5, f32[32,256]{1,0:T(8,128)S(1)} %copy-done.4, ...), custom_call_target="tpu_custom_call" | custom-call | flops 1000000000 | bytes 4000000 | tf_op jit(solution)/shard_map/stage/pallas_call | solution.py:371
  11.0 0.0 copy-start
  11.0 0.0 copy-start.1
  11.0 0.0 collective-permute-done.refs_4_
  11.1 2.7 %collective-permute-done.2.refs_6_ = bf16[128,768]{1,0:T(8,128)(2,1)S(1)} collective-permute-done((bf16[128,768]{1,0:T(8,128)(2,1)}, bf16[128,768]{1,0:T(8,128)(2,1)S(1)}, u32[]{:S(2)}, u32[]{:S(2)}) %collective-permute-start.2) | collective-permute-done | bytes 196640 | tf_op jit(solution)/shard_map/ppermute | solution.py:353
  13.7 0.0 collective-permute-done.1.refs_5_
  13.7 0.5 %aggregate.1 = (bf16[136,768]{1,0:T(8,128)(2,1)S(1)}, bf16[132,768]{1,0:T(8,128)(2,1)S(1)}) custom-call(s32[8,128]{1,0:T(8,128)S(1)} %get-tuple-element.28.refs_0_, f32[8,768]{1,0:T(8,128)S(1)} %get-tuple-element.29.refs_1_, bf16[128,1024]{1,0:T(8,128)(2,1)S(1)} %get-tuple-element.30.refs_2_, bf16[128,768]{1,0:T(8,128)(2,1)S(1)} %get-tuple-element.31.refs_3_, ...), custom_call_target="tpu_custom_call" | custom-call | flops 1000000000 | bytes 4000000 | tf_op jit(solution)/shard_map/aggregate/pallas_call | solution.py:386
  14.3 2.7 %collective-permute-start.3 = (bf16[136,768]{1,0:T(8,128)(2,1)S(1)}, bf16[136,768]{1,0:T(8,128)(2,1)S(1)}, u32[]{:S(2)}, u32[]{:S(2)}) collective-permute-start(bf16[136,768]{1,0:T(8,128)(2,1)S(1)} %get-tuple-element.32), channel_id=1, source_target_pairs={{0,4},{1,3},{2,6},{3,1},{4,0},{5,7},{6,2},{7,5},{8,12},{9,11},{10,... | collective-permute-start | bytes 626696 | tf_op jit(solution)/shard_map/ppermute | solution.py:404
  16.9 0.0 collective-permute-start.6
  16.9 1.6 %collective-permute-start.5 = (bf16[132,768]{1,0:T(8,128)(2,1)S(1)}, bf16[132,768]{1,0:T(8,128)(2,1)S(1)}, u32[]{:S(2)}, u32[]{:S(2)}) collective-permute-start(bf16[132,768]{1,0:T(8,128)(2,1)S(1)} %get-tuple-element.33.refs_2_), channel_id=1, source_target_pairs={{0,2},{1,5},{2,0},{3,7},{4,6},{5,1},{6,4},{7,3},{8,10},{9,13},{10,... | collective-permute-start | bytes 608264 | tf_op jit(solution)/shard_map/ppermute | solution.py:405
  18.5 0.0 collective-permute-done.6.refs_3_
  18.5 0.0 copy-done
  18.5 0.0 copy-done.1
  18.5 3.1 %part.3 = (bf16[128,768]{1,0:T(8,128)(2,1)S(1)}, bf16[128,4096]{1,0:T(8,128)(2,1)S(1)}, f32[128,768]{1,0:T(8,128)S(1)}, f32[128,768]{1,0:T(8,128)S(1)}) custom-call(bf16[768,1536]{1,0:T(8,128)(2,1)S(1)} %copy-done, bf16[768,768]{1,0:T(8,128)(2,1)S(1)} %copy-done.1, bf16[132,768]{1,0:T(8,128)(2,1)S(1)} %get-tuple-element.33.refs_2_, ...), custom_call_target="tpu_custom_call" | custom-call | flops 1000 | bytes 1000 | tf_op jit(solution)/shard_map/part/pallas_call | solution.py:331
  21.6 4.8 %collective-permute-done.3.refs_1_ = bf16[136,768]{1,0:T(8,128)(2,1)S(1)} collective-permute-done((bf16[136,768]{1,0:T(8,128)(2,1)S(1)}, bf16[136,768]{1,0:T(8,128)(2,1)S(1)}, u32[]{:S(2)}, u32[]{:S(2)}) %collective-permute-start.3) | collective-permute-done | bytes 208928 | tf_op jit(solution)/shard_map/ppermute | solution.py:404
  26.4 0.0 collective-permute-start.8
  26.4 1.9 %collective-permute-start.4 = (bf16[136,768]{1,0:T(8,128)(2,1)S(1)}, bf16[136,768]{1,0:T(8,128)(2,1)S(1)}, u32[]{:S(2)}, u32[]{:S(2)}) collective-permute-start(bf16[136,768]{1,0:T(8,128)(2,1)S(1)} %collective-permute-done.3.refs_1_), channel_id=1, source_target_pairs={{0,2},{1,5},{2,0},{3,7},{4,6},{5,1},{6,4},{7,3},{8,10},{9,13},{10,... | collective-permute-start | bytes 626696 | tf_op jit(solution)/shard_map/ppermute | solution.py:406
  28.3 0.0 collective-permute-done.5.refs_0_
  28.3 0.0 collective-permute-start.7
  28.3 0.8 %project.2 = (bf16[256,128]{1,0:T(8,128)(2,1)S(1)}, bf16[256,768]{1,0:T(8,128)(2,1)S(1)}, bf16[256,768]{1,0:T(8,128)(2,1)S(1)}) custom-call(bf16[768,1536]{1,0:T(8,128)(2,1)S(1)} %copy-done, bf16[768,768]{1,0:T(8,128)(2,1)S(1)} %copy-done.1, bf16[132,768]{1,0:T(8,128)(2,1)S(1)} %collective-permute-done.5.refs_0_, ...), custom_call_target="tpu_custom_call" | custom-call | flops 1000 | bytes 1000 | tf_op jit(solution)/shard_map/project/pallas_call | solution.py:310
  29.1 0.7 %collective-permute-done.7.refs_2_ = bf16[132,768]{1,0:T(8,128)(2,1)S(1)} collective-permute-done((bf16[132,768]{1,0:T(8,128)(2,1)S(1)}, bf16[132,768]{1,0:T(8,128)(2,1)S(1)}, u32[]{:S(2)}, u32[]{:S(2)}) %collective-permute-start.7) | collective-permute-done | bytes 202784 | tf_op jit(solution)/shard_map/ppermute | solution.py:353
  29.8 0.0 collective-permute-done.8.refs_3_
  29.8 3.6 %part.4 = (f32[128,768]{1,0:T(8,128)S(1)}, f32[128,768]{1,0:T(8,128)S(1)}, f32[128,768]{1,0:T(8,128)S(1)}) custom-call(bf16[768,1536]{1,0:T(8,128)(2,1)S(1)} %copy-done, bf16[768,768]{1,0:T(8,128)(2,1)S(1)} %copy-done.1, bf16[132,768]{1,0:T(8,128)(2,1)S(1)} %collective-permute-done.7.refs_2_, bf16[136,768]{1,0:T(8,128)(2,1)S(1)} %collective-permute-done.8.refs_3_, ...), custom_call_target="tpu_custom_call" | custom-call | flops 1000 | bytes 1000 | tf_op jit(solution)/shard_map/part/pallas_call | solution.py:331
  33.4 1.1 %collective-permute-done.4.refs_0_ = bf16[136,768]{1,0:T(8,128)(2,1)S(1)} collective-permute-done((bf16[136,768]{1,0:T(8,128)(2,1)S(1)}, bf16[136,768]{1,0:T(8,128)(2,1)S(1)}, u32[]{:S(2)}, u32[]{:S(2)}) %collective-permute-start.4) | collective-permute-done | bytes 208928 | tf_op jit(solution)/shard_map/ppermute | solution.py:406
  34.4 0.0 collective-permute-start.9
  34.4 0.5 %project.3 = (bf16[128,128]{1,0:T(8,128)(2,1)S(1)}, bf16[128,768]{1,0:T(8,128)(2,1)S(1)}, bf16[128,768]{1,0:T(8,128)(2,1)S(1)}) custom-call(bf16[768,1536]{1,0:T(8,128)(2,1)S(1)} %copy-done, bf16[768,768]{1,0:T(8,128)(2,1)S(1)} %copy-done.1, bf16[136,768]{1,0:T(8,128)(2,1)S(1)} %collective-permute-done.4.refs_0_), custom_call_target="tpu_custom_call" | custom-call | flops 1000 | bytes 1000 | tf_op jit(solution)/shard_map/project/pallas_call | solution.py:310
  34.9 1.0 %collective-permute-done.9.refs_2_ = bf16[136,768]{1,0:T(8,128)(2,1)S(1)} collective-permute-done((bf16[136,768]{1,0:T(8,128)(2,1)S(1)}, bf16[136,768]{1,0:T(8,128)(2,1)S(1)}, u32[]{:S(2)}, u32[]{:S(2)}) %collective-permute-start.9) | collective-permute-done | bytes 208928 | tf_op jit(solution)/shard_map/ppermute | solution.py:353
  35.9 2.8 %part.5 = bf16[128,768]{1,0:T(8,128)(2,1)} custom-call(bf16[768,1536]{1,0:T(8,128)(2,1)S(1)} %copy-done, bf16[768,768]{1,0:T(8,128)(2,1)S(1)} %copy-done.1, bf16[136,768]{1,0:T(8,128)(2,1)S(1)} %collective-permute-done.9.refs_2_, bf16[128,128]{1,0:T(8,128)(2,1)S(1)} %get-tuple-element.48.refs_3_, bf16[128,768]{1,0:T(8,128)(2,1)S(1)} %get-tuple-element.49.refs_4_, ...), custom_call_target="tpu_custom_call" | custom-call | flops 1000000000 | bytes 4000000 | tf_op jit(solution)/shard_map/part/pallas_call | solution.py:331
Async XLA Ops:
  0.0 11.0 %collective-permute-start = (bf16[128,768]{1,0:T(8,128)(2,1)}, bf16[128,768]{1,0:T(8,128)(2,1)S(1)}, u32[]{:S(2)}, u32[]{:S(2)}) collective-permute-start(bf16[128,768]{1,0:T(8,128)(2,1)} %features_ref.1), channel_id=1, source_target_pairs={{0,8},{8,0},{16,24},{24,16},{1,9},{9,1},{17,25},{25,17},{2,10},{10... | collective-permute-start | bytes 589832 | tf_op jit(solution)/shard_map/ppermute | solution.py:353
  2.9 10.8 %collective-permute-start.2 = (bf16[128,768]{1,0:T(8,128)(2,1)}, bf16[128,768]{1,0:T(8,128)(2,1)S(1)}, u32[]{:S(2)}, u32[]{:S(2)}) collective-permute-start(bf16[128,768]{1,0:T(8,128)(2,1)} %features_ref.1), channel_id=1, source_target_pairs={{0,16},{8,24},{16,0},{24,8},{1,17},{9,25},{17,1},{25,9},{2,18},{10... | collective-permute-start | bytes 589832 | tf_op jit(solution)/shard_map/ppermute | solution.py:353
  4.5 9.3 %collective-permute-start.1 = (bf16[128,768]{1,0:T(8,128)(2,1)}, bf16[128,768]{1,0:T(8,128)(2,1)S(1)}, u32[]{:S(2)}, u32[]{:S(2)}) collective-permute-start(bf16[128,768]{1,0:T(8,128)(2,1)} %features_ref.1), channel_id=1, source_target_pairs={{0,24},{8,16},{16,8},{24,0},{1,25},{9,17},{17,9},{25,1},{2,26},{10... | collective-permute-start | bytes 589832 | tf_op jit(solution)/shard_map/ppermute | solution.py:353
  5.1 1.0 %copy-start.2 = (bf16[128,1024]{1,0:T(8,128)(2,1)S(1)}, bf16[128,1024]{1,0:T(8,128)(2,1)}, u32[]{:S(2)}) copy-start(bf16[128,1024]{1,0:T(8,128)(2,1)} %tiles_ref.1) | copy-start | bytes 786436
  6.1 0.9 %copy-start.3 = (bf16[128,768]{1,0:T(8,128)(2,1)S(1)}, bf16[128,768]{1,0:T(8,128)(2,1)}, u32[]{:S(2)}) copy-start(bf16[128,768]{1,0:T(8,128)(2,1)} %features_ref.1) | copy-start | bytes 589828
  7.0 0.8 %copy-start.4 = (f32[32,256]{1,0:T(8,128)S(1)}, f32[32,256]{1,0:T(8,128)}, u32[]{:S(2)}) copy-start(f32[32,256]{1,0:T(8,128)} %table_ref.1) | copy-start | bytes 98308
  7.8 0.7 %copy-start.5 = (s32[1,8]{1,0:T(1,128)S(1)}, s32[1,8]{1,0:T(1,128)}, u32[]{:S(2)}) copy-start(s32[1,8]{1,0:T(1,128)} %src_ref.1) | copy-start | bytes 100
  8.4 0.7 %copy-start.6 = (s32[128]{0:T(128)S(1)}, s32[128]{0:T(128)}, u32[]{:S(2)}) copy-start(s32[128]{0:T(128)} %param.12) | copy-start | bytes 1540
  11.0 7.5 %copy-start = (bf16[768,1536]{1,0:T(8,128)(2,1)S(1)}, bf16[768,1536]{1,0:T(8,128)(2,1)}, u32[]{:S(2)}) copy-start(bf16[768,1536]{1,0:T(8,128)(2,1)} %refs_0_.5) | copy-start | bytes 7077892
  11.0 7.5 %copy-start.1 = (bf16[768,768]{1,0:T(8,128)(2,1)S(1)}, bf16[768,768]{1,0:T(8,128)(2,1)}, u32[]{:S(2)}) copy-start(bf16[768,768]{1,0:T(8,128)(2,1)} %refs_1_.5) | copy-start | bytes 3538948
  14.3 12.1 %collective-permute-start.3 = (bf16[136,768]{1,0:T(8,128)(2,1)S(1)}, bf16[136,768]{1,0:T(8,128)(2,1)S(1)}, u32[]{:S(2)}, u32[]{:S(2)}) collective-permute-start(bf16[136,768]{1,0:T(8,128)(2,1)S(1)} %get-tuple-element.32), channel_id=1, source_target_pairs={{0,4},{1,3},{2,6},{3,1},{4,0},{5,7},{6,2},{7,5},{8,12},{9,11},{10,... | collective-permute-start | bytes 626696 | tf_op jit(solution)/shard_map/ppermute | solution.py:404
  16.9 1.6 %collective-permute-start.6 = (bf16[132,768]{1,0:T(8,128)(2,1)S(1)}, bf16[132,768]{1,0:T(8,128)(2,1)S(1)}, u32[]{:S(2)}, u32[]{:S(2)}) collective-permute-start(bf16[132,768]{1,0:T(8,128)(2,1)S(1)} %get-tuple-element.33.refs_2_), channel_id=1, source_target_pairs={{0,1},{1,0},{2,3},{3,2},{4,5},{5,4},{6,7},{7,6},{8,9},{9,8},{10,11... | collective-permute-start | bytes 608264 | tf_op jit(solution)/shard_map/ppermute | solution.py:353
  16.9 11.4 %collective-permute-start.5 = (bf16[132,768]{1,0:T(8,128)(2,1)S(1)}, bf16[132,768]{1,0:T(8,128)(2,1)S(1)}, u32[]{:S(2)}, u32[]{:S(2)}) collective-permute-start(bf16[132,768]{1,0:T(8,128)(2,1)S(1)} %get-tuple-element.33.refs_2_), channel_id=1, source_target_pairs={{0,2},{1,5},{2,0},{3,7},{4,6},{5,1},{6,4},{7,3},{8,10},{9,13},{10,... | collective-permute-start | bytes 608264 | tf_op jit(solution)/shard_map/ppermute | solution.py:405
  26.4 3.4 %collective-permute-start.8 = (bf16[136,768]{1,0:T(8,128)(2,1)S(1)}, bf16[136,768]{1,0:T(8,128)(2,1)S(1)}, u32[]{:S(2)}, u32[]{:S(2)}) collective-permute-start(bf16[136,768]{1,0:T(8,128)(2,1)S(1)} %collective-permute-done.3.refs_1_), channel_id=1, source_target_pairs={{0,1},{1,0},{2,3},{3,2},{4,5},{5,4},{6,7},{7,6},{8,9},{9,8},{10,11... | collective-permute-start | bytes 626696 | tf_op jit(solution)/shard_map/ppermute | solution.py:353
  26.4 8.0 %collective-permute-start.4 = (bf16[136,768]{1,0:T(8,128)(2,1)S(1)}, bf16[136,768]{1,0:T(8,128)(2,1)S(1)}, u32[]{:S(2)}, u32[]{:S(2)}) collective-permute-start(bf16[136,768]{1,0:T(8,128)(2,1)S(1)} %collective-permute-done.3.refs_1_), channel_id=1, source_target_pairs={{0,2},{1,5},{2,0},{3,7},{4,6},{5,1},{6,4},{7,3},{8,10},{9,13},{10,... | collective-permute-start | bytes 626696 | tf_op jit(solution)/shard_map/ppermute | solution.py:406
  28.3 1.5 %collective-permute-start.7 = (bf16[132,768]{1,0:T(8,128)(2,1)S(1)}, bf16[132,768]{1,0:T(8,128)(2,1)S(1)}, u32[]{:S(2)}, u32[]{:S(2)}) collective-permute-start(bf16[132,768]{1,0:T(8,128)(2,1)S(1)} %collective-permute-done.5.refs_0_), channel_id=1, source_target_pairs={{0,1},{1,0},{2,3},{3,2},{4,5},{5,4},{6,7},{7,6},{8,9},{9,8},{10,11... | collective-permute-start | bytes 608264 | tf_op jit(solution)/shard_map/ppermute | solution.py:353
  34.4 1.5 %collective-permute-start.9 = (bf16[136,768]{1,0:T(8,128)(2,1)S(1)}, bf16[136,768]{1,0:T(8,128)(2,1)S(1)}, u32[]{:S(2)}, u32[]{:S(2)}) collective-permute-start(bf16[136,768]{1,0:T(8,128)(2,1)S(1)} %collective-permute-done.4.refs_0_), channel_id=1, source_target_pairs={{0,1},{1,0},{2,3},{3,2},{4,5},{5,4},{6,7},{7,6},{8,9},{9,8},{10,11... | collective-permute-start | bytes 626696 | tf_op jit(solution)/shard_map/ppermute | solution.py:353

commit v16 on v14

--- a/solution.py
+++ b/solution.py
@@ -101,7 +101,7 @@
 
 
 def aggregate_kernel(order, from_ref, extra_ref, masked_ref, *refs):
-    feature_refs, out_ref, short_ref, held = refs[:-3], refs[-3], refs[-2], refs[-1]
+    feature_refs, out_ref, short_ref, least_ref, held = refs[:-4], *refs[-4:]
     rows = feature_refs[0].shape[0]
     for d, ref in zip([0, *order], feature_refs):
         held[d * rows : (d + 1) * rows, :] = ref[...]
@@ -118,6 +118,7 @@
     ).astype(BF16)
     out_ref[...] = result
     short_ref[...] = result[: short_ref.shape[0], :]
+    least_ref[...] = result[: least_ref.shape[0], :]
 
 
 def slab_heads(slab):
@@ -383,18 +384,19 @@
         name="stage",
     )(tile_count, lax.axis_index("group").reshape(1), tile_src, bias_table, own_bucket, features, tiles)
 
-    own, short = pl.pallas_call(
+    own, short, least = pl.pallas_call(
         lambda *refs: aggregate_kernel(order, *refs),
-        out_shape=[shape(rows + EXTRA, width), shape(rows + EXTRA // 2, width)],
+        out_shape=[shape(rows + EXTRA, width), shape(rows + EXTRA - 2, width),
+            shape(rows + 1, width)],
         in_specs=[vmem()] * (3 + groups),
-        out_specs=[vmem()] * 2,
+        out_specs=[vmem()] * 3,
         scratch_shapes=[pltpu.VMEM((groups * rows, width), BF16)],
         compiler_params=limit(8),
         cost_estimate=pl.CostEstimate(flops=10**9, bytes_accessed=4_000_000, transcendentals=0),
         name="aggregate",
     )(source, extra, masked, own_features, *received)
 
-    far = [short] + [None] * (chips - 1)
+    far = [least] + [None] * (chips - 1)
     top = 1
     while 2 * top < chips:
         top *= 2
@@ -417,7 +419,7 @@
                 block = after(block, *state)
                 near = swap(block, "seq", 1)
             else:
-                near = swap(short, "seq", 1)
+                near = swap(least, "seq", 1)
             blocks += [block, near]
         state = attend_part(
             number == 0, number == len(parts) - 1, w_qk, w_v, blocks, [*queries, *state]

time: 37.7 us -> 37.7 us (level)
  no operation moved by 1% of the time
where the time goes in v16:
time: 37.7 us; the launch traced here: 37.5 us
  Pallas kernels  13.2 us (35%)
  waiting for transfers between devices  10.1 us (27%)
  starting transfers between devices  9.49 us (25%)
  local copies, waits for them, and re-layouts  3.95 us (10%)
  between operations  0.74 us (2%)
    ppermute x10, waiting for transfers between devices, swap(): lax.ppermute(array, axis, [(i, i ^ distance) for i in range(lax.axis_size...  10.1 us
    ppermute x10, starting transfers between devices, swap(): lax.ppermute(array, axis, [(i, i ^ distance) for i in range(lax.axis_size...  9.49 us
    pallas_call x3, Pallas kernels, attend_part(): pl.pallas_call(lambda *refs: part_kernel(len(blocks), first, last, *refs)...  9.45 us
    unnamed x14, local copies, waits for them, and re-layouts  3.95 us
    pallas_call x1, Pallas kernels, on_device(): pl.pallas_call(stage_kernel, out_shape=[shape(rows, H * LANES), shape(row...  1.95 us
    pallas_call x2, Pallas kernels, attend_part(): pl.pallas_call(project_kernel, out_shape=[shape(count, LANES), shape(coun...  1.27 us
  transfers between devices with their start and end apart: 10, of which 6 were waited for; matrix products, arithmetic and copies ran while one was open for 0% of the time, Pallas kernels for 26%

profile of v16, /device:TPU:0, one launch (start us, length us, event | category | flops | bytes accessed | tf_op | source)
XLA Modules:
  0.0 37.5 jit_solution(8780285867520443097)
XLA Ops:
  0.0 2.9 %collective-permute-start = (bf16[128,768]{1,0:T(8,128)(2,1)}, bf16[128,768]{1,0:T(8,128)(2,1)S(1)}, u32[]{:S(2)}, u32[]{:S(2)}) collective-permute-start(bf16[128,768]{1,0:T(8,128)(2,1)} %features_ref.1), channel_id=1, source_target_pairs={{0,8},{8,0},{16,24},{24,16},{1,9},{9,1},{17,25},{25,17},{2,10},{10... | collective-permute-start | bytes 589832 | tf_op jit(solution)/shard_map/ppermute | solution.py:354
  2.9 1.5 %collective-permute-start.2 = (bf16[128,768]{1,0:T(8,128)(2,1)}, bf16[128,768]{1,0:T(8,128)(2,1)S(1)}, u32[]{:S(2)}, u32[]{:S(2)}) collective-permute-start(bf16[128,768]{1,0:T(8,128)(2,1)} %features_ref.1), channel_id=1, source_target_pairs={{0,16},{8,24},{16,0},{24,8},{1,17},{9,25},{17,1},{25,9},{2,18},{10... | collective-permute-start | bytes 589832 | tf_op jit(solution)/shard_map/ppermute | solution.py:354
  4.5 0.0 collective-permute-start.1
  5.1 0.0 copy-start.2
  5.1 0.9 %copy-done.2 = bf16[128,1024]{1,0:T(8,128)(2,1)S(1)} copy-done((bf16[128,1024]{1,0:T(8,128)(2,1)S(1)}, bf16[128,1024]{1,0:T(8,128)(2,1)}, u32[]{:S(2)}) %copy-start.2) | copy-done | bytes 262168
  6.1 0.0 copy-start.3
  6.1 0.9 %copy-done.3 = bf16[128,768]{1,0:T(8,128)(2,1)S(1)} copy-done((bf16[128,768]{1,0:T(8,128)(2,1)S(1)}, bf16[128,768]{1,0:T(8,128)(2,1)}, u32[]{:S(2)}) %copy-start.3) | copy-done | bytes 196632
  7.0 0.0 copy-start.4
  7.0 0.8 %copy-done.4 = f32[32,256]{1,0:T(8,128)S(1)} copy-done((f32[32,256]{1,0:T(8,128)S(1)}, f32[32,256]{1,0:T(8,128)}, u32[]{:S(2)}) %copy-start.4) | copy-done | bytes 32792
  7.8 0.0 copy-start.5
  7.8 0.7 %copy-done.5 = s32[1,8]{1,0:T(1,128)S(1)} copy-done((s32[1,8]{1,0:T(1,128)S(1)}, s32[1,8]{1,0:T(1,128)}, u32[]{:S(2)}) %copy-start.5) | copy-done | bytes 56
  8.4 0.0 copy-start.6
  8.4 0.7 %copy-done.6 = s32[128]{0:T(128)S(1)} copy-done((s32[128]{0:T(128)S(1)}, s32[128]{0:T(128)}, u32[]{:S(2)}) %copy-start.6) | copy-done | bytes 536
  9.1 1.9 %stage.1 = (bf16[128,4096]{1,0:T(8,128)(2,1)S(1)}, bf16[128,768]{1,0:T(8,128)(2,1)S(1)}, bf16[128,1024]{1,0:T(8,128)(2,1)S(1)}, f32[8,768]{1,0:T(8,128)S(1)}, s32[8,128]{1,0:T(8,128)S(1)}) custom-call(s32[1]{0:T(128)S(6)} %copy.9.count_ref, s32[1]{0:T(128)} %bitcast.me_ref, s32[1,8]{1,0:T(1,128)S(1)} %copy-done.5, f32[32,256]{1,0:T(8,128)S(1)} %copy-done.4, ...), custom_call_target="tpu_custom_call" | custom-call | flops 1000000000 | bytes 4000000 | tf_op jit(solution)/shard_map/stage/pallas_call | solution.py:372
  11.0 0.0 copy-start
  11.0 0.0 copy-start.1
  11.0 0.0 collective-permute-done.refs_4_
  11.1 2.7 %collective-permute-done.2.refs_6_ = bf16[128,768]{1,0:T(8,128)(2,1)S(1)} collective-permute-done((bf16[128,768]{1,0:T(8,128)(2,1)}, bf16[128,768]{1,0:T(8,128)(2,1)S(1)}, u32[]{:S(2)}, u32[]{:S(2)}) %collective-permute-start.2) | collective-permute-done | bytes 196640 | tf_op jit(solution)/shard_map/ppermute | solution.py:354
  13.7 0.0 collective-permute-done.1.refs_5_
  13.7 0.5 %aggregate.1 = (bf16[136,768]{1,0:T(8,128)(2,1)S(1)}, bf16[134,768]{1,0:T(8,128)(2,1)S(1)}, bf16[129,768]{1,0:T(8,128)(2,1)S(1)}) custom-call(s32[8,128]{1,0:T(8,128)S(1)} %get-tuple-element.29.refs_0_, f32[8,768]{1,0:T(8,128)S(1)} %get-tuple-element.30.refs_1_, bf16[128,1024]{1,0:T(8,128)(2,1)S(1)} %get-tuple-element.31.refs_2_, ...), custom_call_target="tpu_custom_call" | custom-call | flops 1000000000 | bytes 4000000 | tf_op jit(solution)/shard_map/aggregate/pallas_call | solution.py:387
  14.3 2.7 %collective-permute-start.3 = (bf16[136,768]{1,0:T(8,128)(2,1)S(1)}, bf16[136,768]{1,0:T(8,128)(2,1)S(1)}, u32[]{:S(2)}, u32[]{:S(2)}) collective-permute-start(bf16[136,768]{1,0:T(8,128)(2,1)S(1)} %get-tuple-element.33), channel_id=1, source_target_pairs={{0,4},{1,5},{2,6},{3,7},{4,0},{5,1},{6,2},{7,3},{8,12},{9,13},{10,... | collective-permute-start | bytes 626696 | tf_op jit(solution)/shard_map/ppermute | solution.py:354
  16.9 1.6 %collective-permute-start.5 = (bf16[134,768]{1,0:T(8,128)(2,1)S(1)}, bf16[134,768]{1,0:T(8,128)(2,1)S(1)}, u32[]{:S(2)}, u32[]{:S(2)}) collective-permute-start(bf16[134,768]{1,0:T(8,128)(2,1)S(1)} %get-tuple-element.34), channel_id=1, source_target_pairs={{0,2},{1,3},{2,0},{3,1},{4,6},{5,7},{6,4},{7,5},{8,10},{9,11},{10,... | collective-permute-start | bytes 617480 | tf_op jit(solution)/shard_map/ppermute | solution.py:354
  18.5 0.0 collective-permute-start.6
  18.5 1.5 %collective-permute-done.6.refs_3_ = bf16[129,768]{1,0:T(8,128)(2,1)S(1)} collective-permute-done((bf16[129,768]{1,0:T(8,128)(2,1)S(1)}, bf16[129,768]{1,0:T(8,128)(2,1)S(1)}, u32[]{:S(2)}, u32[]{:S(2)}) %collective-permute-start.6) | collective-permute-done | bytes 198176 | tf_op jit(solution)/shard_map/ppermute | solution.py:354
  20.0 0.0 copy-done
  20.0 0.0 copy-done.1
  20.0 3.1 %part.3 = (bf16[128,768]{1,0:T(8,128)(2,1)S(1)}, bf16[128,4096]{1,0:T(8,128)(2,1)S(1)}, f32[128,768]{1,0:T(8,128)S(1)}, f32[128,768]{1,0:T(8,128)S(1)}) custom-call(bf16[768,1536]{1,0:T(8,128)(2,1)S(1)} %copy-done, bf16[768,768]{1,0:T(8,128)(2,1)S(1)} %copy-done.1, bf16[129,768]{1,0:T(8,128)(2,1)S(1)} %get-tuple-element.35.refs_2_, ...), custom_call_target="tpu_custom_call" | custom-call | flops 1000 | bytes 1000 | tf_op jit(solution)/shard_map/part/pallas_call | solution.py:332
  23.1 2.6 %collective-permute-done.3.refs_1_ = bf16[136,768]{1,0:T(8,128)(2,1)S(1)} collective-permute-done((bf16[136,768]{1,0:T(8,128)(2,1)S(1)}, bf16[136,768]{1,0:T(8,128)(2,1)S(1)}, u32[]{:S(2)}, u32[]{:S(2)}) %collective-permute-start.3) | collective-permute-done | bytes 208928 | tf_op jit(solution)/shard_map/ppermute | solution.py:354
  25.6 0.0 collective-permute-start.8
  25.7 0.6 %collective-permute-start.4 = (bf16[136,768]{1,0:T(8,128)(2,1)S(1)}, bf16[136,768]{1,0:T(8,128)(2,1)S(1)}, u32[]{:S(2)}, u32[]{:S(2)}) collective-permute-start(bf16[136,768]{1,0:T(8,128)(2,1)S(1)} %collective-permute-done.3.refs_1_), channel_id=1, source_target_pairs={{0,2},{1,3},{2,0},{3,1},{4,6},{5,7},{6,4},{7,5},{8,10},{9,11},{10,... | collective-permute-start | bytes 626696 | tf_op jit(solution)/shard_map/ppermute | solution.py:354
  26.2 0.0 collective-permute-done.5.refs_0_
  26.2 0.2 collective-permute-start.7
  26.4 0.8 %project.2 = (bf16[256,128]{1,0:T(8,128)(2,1)S(1)}, bf16[256,768]{1,0:T(8,128)(2,1)S(1)}, bf16[256,768]{1,0:T(8,128)(2,1)S(1)}) custom-call(bf16[768,1536]{1,0:T(8,128)(2,1)S(1)} %copy-done, bf16[768,768]{1,0:T(8,128)(2,1)S(1)} %copy-done.1, bf16[134,768]{1,0:T(8,128)(2,1)S(1)} %collective-permute-done.5.refs_0_, ...), custom_call_target="tpu_custom_call" | custom-call | flops 1000 | bytes 1000 | tf_op jit(solution)/shard_map/project/pallas_call | solution.py:311
  27.2 0.5 %collective-permute-done.7.refs_2_ = bf16[134,768]{1,0:T(8,128)(2,1)S(1)} collective-permute-done((bf16[134,768]{1,0:T(8,128)(2,1)S(1)}, bf16[134,768]{1,0:T(8,128)(2,1)S(1)}, u32[]{:S(2)}, u32[]{:S(2)}) %collective-permute-start.7) | collective-permute-done | bytes 205856 | tf_op jit(solution)/shard_map/ppermute | solution.py:354
  27.7 0.0 collective-permute-done.8.refs_3_
  27.7 3.6 %part.4 = (f32[128,768]{1,0:T(8,128)S(1)}, f32[128,768]{1,0:T(8,128)S(1)}, f32[128,768]{1,0:T(8,128)S(1)}) custom-call(bf16[768,1536]{1,0:T(8,128)(2,1)S(1)} %copy-done, bf16[768,768]{1,0:T(8,128)(2,1)S(1)} %copy-done.1, bf16[134,768]{1,0:T(8,128)(2,1)S(1)} %collective-permute-done.7.refs_2_, bf16[136,768]{1,0:T(8,128)(2,1)S(1)} %collective-permute-done.8.refs_3_, ...), custom_call_target="tpu_custom_call" | custom-call | flops 1000 | bytes 1000 | tf_op jit(solution)/shard_map/part/pallas_call | solution.py:332
  31.3 1.9 %collective-permute-done.4.refs_0_ = bf16[136,768]{1,0:T(8,128)(2,1)S(1)} collective-permute-done((bf16[136,768]{1,0:T(8,128)(2,1)S(1)}, bf16[136,768]{1,0:T(8,128)(2,1)S(1)}, u32[]{:S(2)}, u32[]{:S(2)}) %collective-permute-start.4) | collective-permute-done | bytes 208928 | tf_op jit(solution)/shard_map/ppermute | solution.py:354
  33.2 0.0 collective-permute-start.9
  33.2 0.5 %project.3 = (bf16[128,128]{1,0:T(8,128)(2,1)S(1)}, bf16[128,768]{1,0:T(8,128)(2,1)S(1)}, bf16[128,768]{1,0:T(8,128)(2,1)S(1)}) custom-call(bf16[768,1536]{1,0:T(8,128)(2,1)S(1)} %copy-done, bf16[768,768]{1,0:T(8,128)(2,1)S(1)} %copy-done.1, bf16[136,768]{1,0:T(8,128)(2,1)S(1)} %collective-permute-done.4.refs_0_), custom_call_target="tpu_custom_call" | custom-call | flops 1000 | bytes 1000 | tf_op jit(solution)/shard_map/project/pallas_call | solution.py:311
  33.7 1.0 %collective-permute-done.9.refs_2_ = bf16[136,768]{1,0:T(8,128)(2,1)S(1)} collective-permute-done((bf16[136,768]{1,0:T(8,128)(2,1)S(1)}, bf16[136,768]{1,0:T(8,128)(2,1)S(1)}, u32[]{:S(2)}, u32[]{:S(2)}) %collective-permute-start.9) | collective-permute-done | bytes 208928 | tf_op jit(solution)/shard_map/ppermute | solution.py:354
  34.7 2.8 %part.5 = bf16[128,768]{1,0:T(8,128)(2,1)} custom-call(bf16[768,1536]{1,0:T(8,128)(2,1)S(1)} %copy-done, bf16[768,768]{1,0:T(8,128)(2,1)S(1)} %copy-done.1, bf16[136,768]{1,0:T(8,128)(2,1)S(1)} %collective-permute-done.9.refs_2_, bf16[128,128]{1,0:T(8,128)(2,1)S(1)} %get-tuple-element.50.refs_3_, bf16[128,768]{1,0:T(8,128)(2,1)S(1)} %get-tuple-element.51.refs_4_, ...), custom_call_target="tpu_custom_call" | custom-call | flops 1000000000 | bytes 4000000 | tf_op jit(solution)/shard_map/part/pallas_call | solution.py:332
Async XLA Ops:
  0.0 11.0 %collective-permute-start = (bf16[128,768]{1,0:T(8,128)(2,1)}, bf16[128,768]{1,0:T(8,128)(2,1)S(1)}, u32[]{:S(2)}, u32[]{:S(2)}) collective-permute-start(bf16[128,768]{1,0:T(8,128)(2,1)} %features_ref.1), channel_id=1, source_target_pairs={{0,8},{8,0},{16,24},{24,16},{1,9},{9,1},{17,25},{25,17},{2,10},{10... | collective-permute-start | bytes 589832 | tf_op jit(solution)/shard_map/ppermute | solution.py:354
  2.9 10.8 %collective-permute-start.2 = (bf16[128,768]{1,0:T(8,128)(2,1)}, bf16[128,768]{1,0:T(8,128)(2,1)S(1)}, u32[]{:S(2)}, u32[]{:S(2)}) collective-permute-start(bf16[128,768]{1,0:T(8,128)(2,1)} %features_ref.1), channel_id=1, source_target_pairs={{0,16},{8,24},{16,0},{24,8},{1,17},{9,25},{17,1},{25,9},{2,18},{10... | collective-permute-start | bytes 589832 | tf_op jit(solution)/shard_map/ppermute | solution.py:354
  4.5 9.3 %collective-permute-start.1 = (bf16[128,768]{1,0:T(8,128)(2,1)}, bf16[128,768]{1,0:T(8,128)(2,1)S(1)}, u32[]{:S(2)}, u32[]{:S(2)}) collective-permute-start(bf16[128,768]{1,0:T(8,128)(2,1)} %features_ref.1), channel_id=1, source_target_pairs={{0,24},{8,16},{16,8},{24,0},{1,25},{9,17},{17,9},{25,1},{2,26},{10... | collective-permute-start | bytes 589832 | tf_op jit(solution)/shard_map/ppermute | solution.py:354
  5.1 1.0 %copy-start.2 = (bf16[128,1024]{1,0:T(8,128)(2,1)S(1)}, bf16[128,1024]{1,0:T(8,128)(2,1)}, u32[]{:S(2)}) copy-start(bf16[128,1024]{1,0:T(8,128)(2,1)} %tiles_ref.1) | copy-start | bytes 786436
  6.1 0.9 %copy-start.3 = (bf16[128,768]{1,0:T(8,128)(2,1)S(1)}, bf16[128,768]{1,0:T(8,128)(2,1)}, u32[]{:S(2)}) copy-start(bf16[128,768]{1,0:T(8,128)(2,1)} %features_ref.1) | copy-start | bytes 589828
  7.0 0.8 %copy-start.4 = (f32[32,256]{1,0:T(8,128)S(1)}, f32[32,256]{1,0:T(8,128)}, u32[]{:S(2)}) copy-start(f32[32,256]{1,0:T(8,128)} %table_ref.1) | copy-start | bytes 98308
  7.8 0.7 %copy-start.5 = (s32[1,8]{1,0:T(1,128)S(1)}, s32[1,8]{1,0:T(1,128)}, u32[]{:S(2)}) copy-start(s32[1,8]{1,0:T(1,128)} %src_ref.1) | copy-start | bytes 100
  8.4 0.7 %copy-start.6 = (s32[128]{0:T(128)S(1)}, s32[128]{0:T(128)}, u32[]{:S(2)}) copy-start(s32[128]{0:T(128)} %param.12) | copy-start | bytes 1540
  11.0 9.0 %copy-start = (bf16[768,1536]{1,0:T(8,128)(2,1)S(1)}, bf16[768,1536]{1,0:T(8,128)(2,1)}, u32[]{:S(2)}) copy-start(bf16[768,1536]{1,0:T(8,128)(2,1)} %refs_0_.5) | copy-start | bytes 7077892
  11.0 8.9 %copy-start.1 = (bf16[768,768]{1,0:T(8,128)(2,1)S(1)}, bf16[768,768]{1,0:T(8,128)(2,1)}, u32[]{:S(2)}) copy-start(bf16[768,768]{1,0:T(8,128)(2,1)} %refs_1_.5) | copy-start | bytes 3538948
  14.3 11.4 %collective-permute-start.3 = (bf16[136,768]{1,0:T(8,128)(2,1)S(1)}, bf16[136,768]{1,0:T(8,128)(2,1)S(1)}, u32[]{:S(2)}, u32[]{:S(2)}) collective-permute-start(bf16[136,768]{1,0:T(8,128)(2,1)S(1)} %get-tuple-element.33), channel_id=1, source_target_pairs={{0,4},{1,5},{2,6},{3,7},{4,0},{5,1},{6,2},{7,3},{8,12},{9,13},{10,... | collective-permute-start | bytes 626696 | tf_op jit(solution)/shard_map/ppermute | solution.py:354
  16.9 9.3 %collective-permute-start.5 = (bf16[134,768]{1,0:T(8,128)(2,1)S(1)}, bf16[134,768]{1,0:T(8,128)(2,1)S(1)}, u32[]{:S(2)}, u32[]{:S(2)}) collective-permute-start(bf16[134,768]{1,0:T(8,128)(2,1)S(1)} %get-tuple-element.34), channel_id=1, source_target_pairs={{0,2},{1,3},{2,0},{3,1},{4,6},{5,7},{6,4},{7,5},{8,10},{9,11},{10,... | collective-permute-start | bytes 617480 | tf_op jit(solution)/shard_map/ppermute | solution.py:354
  18.5 1.5 %collective-permute-start.6 = (bf16[129,768]{1,0:T(8,128)(2,1)S(1)}, bf16[129,768]{1,0:T(8,128)(2,1)S(1)}, u32[]{:S(2)}, u32[]{:S(2)}) collective-permute-start(bf16[129,768]{1,0:T(8,128)(2,1)S(1)} %get-tuple-element.35.refs_2_), channel_id=1, source_target_pairs={{0,1},{1,0},{2,3},{3,2},{4,5},{5,4},{6,7},{7,6},{8,9},{9,8},{10,11... | collective-permute-start | bytes 594440 | tf_op jit(solution)/shard_map/ppermute | solution.py:354
  25.6 2.0 %collective-permute-start.8 = (bf16[136,768]{1,0:T(8,128)(2,1)S(1)}, bf16[136,768]{1,0:T(8,128)(2,1)S(1)}, u32[]{:S(2)}, u32[]{:S(2)}) collective-permute-start(bf16[136,768]{1,0:T(8,128)(2,1)S(1)} %collective-permute-done.3.refs_1_), channel_id=1, source_target_pairs={{0,1},{1,0},{2,3},{3,2},{4,5},{5,4},{6,7},{7,6},{8,9},{9,8},{10,11... | collective-permute-start | bytes 626696 | tf_op jit(solution)/shard_map/ppermute | solution.py:354
  25.7 7.6 %collective-permute-start.4 = (bf16[136,768]{1,0:T(8,128)(2,1)S(1)}, bf16[136,768]{1,0:T(8,128)(2,1)S(1)}, u32[]{:S(2)}, u32[]{:S(2)}) collective-permute-start(bf16[136,768]{1,0:T(8,128)(2,1)S(1)} %collective-permute-done.3.refs_1_), channel_id=1, source_target_pairs={{0,2},{1,3},{2,0},{3,1},{4,6},{5,7},{6,4},{7,5},{8,10},{9,11},{10,... | collective-permute-start | bytes 626696 | tf_op jit(solution)/shard_map/ppermute | solution.py:354
  26.2 1.5 %collective-permute-start.7 = (bf16[134,768]{1,0:T(8,128)(2,1)S(1)}, bf16[134,768]{1,0:T(8,128)(2,1)S(1)}, u32[]{:S(2)}, u32[]{:S(2)}) collective-permute-start(bf16[134,768]{1,0:T(8,128)(2,1)S(1)} %collective-permute-done.5.refs_0_), channel_id=1, source_target_pairs={{0,1},{1,0},{2,3},{3,2},{4,5},{5,4},{6,7},{7,6},{8,9},{9,8},{10,11... | collective-permute-start | bytes 617480 | tf_op jit(solution)/shard_map/ppermute | solution.py:354
  33.2 1.5 %collective-permute-start.9 = (bf16[136,768]{1,0:T(8,128)(2,1)S(1)}, bf16[136,768]{1,0:T(8,128)(2,1)S(1)}, u32[]{:S(2)}, u32[]{:S(2)}) collective-permute-start(bf16[136,768]{1,0:T(8,128)(2,1)S(1)} %collective-permute-done.4.refs_0_), channel_id=1, source_target_pairs={{0,1},{1,0},{2,3},{3,2},{4,5},{5,4},{6,7},{7,6},{8,9},{9,8},{10,11... | collective-permute-start | bytes 626696 | tf_op jit(solution)/shard_map/ppermute | solution.py:354

commit v17 on v16

--- a/solution.py
+++ b/solution.py
@@ -125,27 +125,30 @@
     return slab * LANES // HD, ((slab + 1) * LANES - 1) // HD
 
 
-def project_blocks(block_refs, rows, w_qk_ref, w_v_ref, hot_ref, k_ref, v_ref):
-    width = w_v_ref.shape[0]
+def arrived_rows(block_refs, rows, hot_ref):
     arrived = [ref[...] for ref in block_refs]
     for s, item in enumerate(arrived):
         bucket = item[rows:, :rows].astype(F32)[:1, :]
         hot_ref[s * rows : (s + 1) * rows, :] = one_hot_slab(bucket)
-    block = jnp.concatenate([item[:rows, :] for item in arrived], axis=0)
-    for n in range(0, width, 256):
-        k_ref[:, n : n + 256] = jnp.dot(
-            block, w_qk_ref[:, width + n : width + n + 256], preferred_element_type=F32
-        ).astype(BF16)
-        v_ref[:, n : n + 256] = jnp.dot(
-            block, w_v_ref[:, n : n + 256], preferred_element_type=F32
-        ).astype(BF16)
-    return block
+    return jnp.concatenate([item[:rows, :] for item in arrived], axis=0)
+
+
+def project(block, n, w_qk_ref, w_v_ref, k_ref, v_ref):
+    width = w_v_ref.shape[0]
+    k_ref[:, n : n + 256] = jnp.dot(
+        block, w_qk_ref[:, width + n : width + n + 256], preferred_element_type=F32
+    ).astype(BF16)
+    v_ref[:, n : n + 256] = jnp.dot(
+        block, w_v_ref[:, n : n + 256], preferred_element_type=F32
+    ).astype(BF16)
 
 
 def project_kernel(w_qk_ref, w_v_ref, *refs):
     *block_refs, hot_ref, k_ref, v_ref = refs
     rows = hot_ref.shape[0] // len(block_refs)
-    project_blocks(block_refs, rows, w_qk_ref, w_v_ref, hot_ref, k_ref, v_ref)
+    block = arrived_rows(block_refs, rows, hot_ref)
+    for n in range(0, k_ref.shape[1], 256):
+        project(block, n, w_qk_ref, w_v_ref, k_ref, v_ref)
 
 
 def part_kernel(count, first, last, w_qk_ref, w_v_ref, *refs):
@@ -160,15 +163,20 @@
         old_refs, outs = (refs[:2], refs[2:]) if len(refs) in (3, 5) else (refs[:3], refs[3:])
     rows = q_ref.shape[0]
     width = w_v_ref.shape[0]
-    block = project_blocks(
-        block_refs, rows, w_qk_ref, w_v_ref, hot_refs[0], k_refs[0], v_refs[0]
-    )
-    if first:
-        for n in range(0, width, 256):
+    block = arrived_rows(block_refs, rows, hot_refs[0])
+    raw_k_ref, raw_v_ref = k_refs[0], v_refs[0]
+
+    def prepare(step):
+        n = step * LANES
+        if n % 256:
+            return
+        if first:
             q_ref[:, n : n + 256] = jnp.dot(
                 block[:rows, :], w_qk_ref[:, n : n + 256], preferred_element_type=F32
             ).astype(BF16)
-    else:
+        project(block, n, w_qk_ref, w_v_ref, raw_k_ref, raw_v_ref)
+
+    if not first:
         for some, ref in zip((hot_refs, k_refs, v_refs), ready):
             some.insert(0, ref)
     keys = sum(ref.shape[0] for ref in hot_refs)
@@ -259,10 +267,14 @@
 
     steps = [divmod(step, SLABS) for step in range(width // LANES)]
     largest = jnp.zeros((rows, LANES), F32)
+    prepare(0)
     x = scores(*steps[0])
     carried = None
     for number, (half, slab) in enumerate(steps):
-        ahead = scores(*steps[number + 1]) if number + 1 < len(steps) else None
+        ahead = None
+        if number + 1 < len(steps):
+            prepare(number + 1)
+            ahead = scores(*steps[number + 1])
         carried = weigh(half, slab, x, carried, p_refs[half % 2], first)
         if number:
             before = steps[number - 1]

time: 37.7 us -> 37.7 us (level)
  waiting for transfers between devices: 10.1 us -> 9.68 us
  Pallas kernels: 13.2 us -> 13.6 us
    ppermute x10, waiting for transfers between devices: 10.1 us -> 9.68 us  [swap(): lax.ppermute(array, axis, [(i, i ^ distance) for i in range(lax.axis_size...]
  transfers between devices with their start and end apart: 10 -> 10, of which waited for: 6 -> 6; matrix products, arithmetic and copies ran while one was open for 0% -> 0% of each run, Pallas kernels for 26% -> 28%
where the time goes in v17:
time: 37.7 us; the launch traced here: 37.4 us
  Pallas kernels  13.6 us (36%)
  waiting for transfers between devices  9.68 us (26%)
  starting transfers between devices  9.49 us (25%)
  local copies, waits for them, and re-layouts  3.95 us (10%)
  between operations  0.74 us (2%)
    pallas_call x3, Pallas kernels, attend_part(): pl.pallas_call(lambda *refs: part_kernel(len(blocks), first, last, *refs)...  9.82 us
    ppermute x10, waiting for transfers between devices, swap(): lax.ppermute(array, axis, [(i, i ^ distance) for i in range(lax.axis_size...  9.68 us
    ppermute x10, starting transfers between devices, swap(): lax.ppermute(array, axis, [(i, i ^ distance) for i in range(lax.axis_size...  9.49 us
    unnamed x14, local copies, waits for them, and re-layouts  3.95 us
    pallas_call x1, Pallas kernels, on_device(): pl.pallas_call(stage_kernel, out_shape=[shape(rows, H * LANES), shape(row...  1.95 us
    pallas_call x2, Pallas kernels, attend_part(): pl.pallas_call(project_kernel, out_shape=[shape(count, LANES), shape(coun...  1.27 us
  transfers between devices with their start and end apart: 10, of which 6 were waited for; matrix products, arithmetic and copies ran while one was open for 0% of the time, Pallas kernels for 28%

profile of v17, /device:TPU:0, one launch (start us, length us, event | category | flops | bytes accessed | tf_op | source)
XLA Modules:
  0.0 37.4 jit_solution(8130050327744971812)
XLA Ops:
  0.0 2.9 %collective-permute-start = (bf16[128,768]{1,0:T(8,128)(2,1)}, bf16[128,768]{1,0:T(8,128)(2,1)S(1)}, u32[]{:S(2)}, u32[]{:S(2)}) collective-permute-start(bf16[128,768]{1,0:T(8,128)(2,1)} %features_ref.1), channel_id=1, source_target_pairs={{0,8},{8,0},{16,24},{24,16},{1,9},{9,1},{17,25},{25,17},{2,10},{10... | collective-permute-start | bytes 589832 | tf_op jit(solution)/shard_map/ppermute | solution.py:366
  2.9 1.5 %collective-permute-start.2 = (bf16[128,768]{1,0:T(8,128)(2,1)}, bf16[128,768]{1,0:T(8,128)(2,1)S(1)}, u32[]{:S(2)}, u32[]{:S(2)}) collective-permute-start(bf16[128,768]{1,0:T(8,128)(2,1)} %features_ref.1), channel_id=1, source_target_pairs={{0,16},{8,24},{16,0},{24,8},{1,17},{9,25},{17,1},{25,9},{2,18},{10... | collective-permute-start | bytes 589832 | tf_op jit(solution)/shard_map/ppermute | solution.py:366
  4.5 0.0 collective-permute-start.1
  5.1 0.0 copy-start.2
  5.1 0.9 %copy-done.2 = bf16[128,1024]{1,0:T(8,128)(2,1)S(1)} copy-done((bf16[128,1024]{1,0:T(8,128)(2,1)S(1)}, bf16[128,1024]{1,0:T(8,128)(2,1)}, u32[]{:S(2)}) %copy-start.2) | copy-done | bytes 262168
  6.1 0.0 copy-start.3
  6.1 0.9 %copy-done.3 = bf16[128,768]{1,0:T(8,128)(2,1)S(1)} copy-done((bf16[128,768]{1,0:T(8,128)(2,1)S(1)}, bf16[128,768]{1,0:T(8,128)(2,1)}, u32[]{:S(2)}) %copy-start.3) | copy-done | bytes 196632
  7.0 0.0 copy-start.4
  7.0 0.8 %copy-done.4 = f32[32,256]{1,0:T(8,128)S(1)} copy-done((f32[32,256]{1,0:T(8,128)S(1)}, f32[32,256]{1,0:T(8,128)}, u32[]{:S(2)}) %copy-start.4) | copy-done | bytes 32792
  7.8 0.0 copy-start.5
  7.8 0.7 %copy-done.5 = s32[1,8]{1,0:T(1,128)S(1)} copy-done((s32[1,8]{1,0:T(1,128)S(1)}, s32[1,8]{1,0:T(1,128)}, u32[]{:S(2)}) %copy-start.5) | copy-done | bytes 56
  8.4 0.0 copy-start.6
  8.4 0.7 %copy-done.6 = s32[128]{0:T(128)S(1)} copy-done((s32[128]{0:T(128)S(1)}, s32[128]{0:T(128)}, u32[]{:S(2)}) %copy-start.6) | copy-done | bytes 536
  9.1 1.9 %stage.1 = (bf16[128,4096]{1,0:T(8,128)(2,1)S(1)}, bf16[128,768]{1,0:T(8,128)(2,1)S(1)}, bf16[128,1024]{1,0:T(8,128)(2,1)S(1)}, f32[8,768]{1,0:T(8,128)S(1)}, s32[8,128]{1,0:T(8,128)S(1)}) custom-call(s32[1]{0:T(128)S(6)} %copy.9.count_ref, s32[1]{0:T(128)} %bitcast.me_ref, s32[1,8]{1,0:T(1,128)S(1)} %copy-done.5, f32[32,256]{1,0:T(8,128)S(1)} %copy-done.4, ...), custom_call_target="tpu_custom_call" | custom-call | flops 1000000000 | bytes 4000000 | tf_op jit(solution)/shard_map/stage/pallas_call | solution.py:384
  11.0 0.0 copy-start
  11.0 0.0 copy-start.1
  11.0 0.0 collective-permute-done.refs_4_
  11.1 2.7 %collective-permute-done.2.refs_6_ = bf16[128,768]{1,0:T(8,128)(2,1)S(1)} collective-permute-done((bf16[128,768]{1,0:T(8,128)(2,1)}, bf16[128,768]{1,0:T(8,128)(2,1)S(1)}, u32[]{:S(2)}, u32[]{:S(2)}) %collective-permute-start.2) | collective-permute-done | bytes 196640 | tf_op jit(solution)/shard_map/ppermute | solution.py:366
  13.7 0.0 collective-permute-done.1.refs_5_
  13.7 0.5 %aggregate.1 = (bf16[136,768]{1,0:T(8,128)(2,1)S(1)}, bf16[134,768]{1,0:T(8,128)(2,1)S(1)}, bf16[129,768]{1,0:T(8,128)(2,1)S(1)}) custom-call(s32[8,128]{1,0:T(8,128)S(1)} %get-tuple-element.29.refs_0_, f32[8,768]{1,0:T(8,128)S(1)} %get-tuple-element.30.refs_1_, bf16[128,1024]{1,0:T(8,128)(2,1)S(1)} %get-tuple-element.31.refs_2_, ...), custom_call_target="tpu_custom_call" | custom-call | flops 1000000000 | bytes 4000000 | tf_op jit(solution)/shard_map/aggregate/pallas_call | solution.py:399
  14.3 2.7 %collective-permute-start.3 = (bf16[136,768]{1,0:T(8,128)(2,1)S(1)}, bf16[136,768]{1,0:T(8,128)(2,1)S(1)}, u32[]{:S(2)}, u32[]{:S(2)}) collective-permute-start(bf16[136,768]{1,0:T(8,128)(2,1)S(1)} %get-tuple-element.33), channel_id=1, source_target_pairs={{0,4},{1,5},{2,6},{3,7},{4,0},{5,1},{6,2},{7,3},{8,12},{9,13},{10,... | collective-permute-start | bytes 626696 | tf_op jit(solution)/shard_map/ppermute | solution.py:366
  16.9 1.6 %collective-permute-start.5 = (bf16[134,768]{1,0:T(8,128)(2,1)S(1)}, bf16[134,768]{1,0:T(8,128)(2,1)S(1)}, u32[]{:S(2)}, u32[]{:S(2)}) collective-permute-start(bf16[134,768]{1,0:T(8,128)(2,1)S(1)} %get-tuple-element.34), channel_id=1, source_target_pairs={{0,2},{1,3},{2,0},{3,1},{4,6},{5,7},{6,4},{7,5},{8,10},{9,11},{10,... | collective-permute-start | bytes 617480 | tf_op jit(solution)/shard_map/ppermute | solution.py:366
  18.5 0.0 collective-permute-start.6
  18.5 1.5 %collective-permute-done.6.refs_3_ = bf16[129,768]{1,0:T(8,128)(2,1)S(1)} collective-permute-done((bf16[129,768]{1,0:T(8,128)(2,1)S(1)}, bf16[129,768]{1,0:T(8,128)(2,1)S(1)}, u32[]{:S(2)}, u32[]{:S(2)}) %collective-permute-start.6) | collective-permute-done | bytes 198176 | tf_op jit(solution)/shard_map/ppermute | solution.py:366
  20.0 0.0 copy-done
  20.0 0.0 copy-done.1
  20.0 3.3 %part.3 = (bf16[128,768]{1,0:T(8,128)(2,1)S(1)}, bf16[128,4096]{1,0:T(8,128)(2,1)S(1)}, f32[128,768]{1,0:T(8,128)S(1)}, f32[128,768]{1,0:T(8,128)S(1)}) custom-call(bf16[768,1536]{1,0:T(8,128)(2,1)S(1)} %copy-done, bf16[768,768]{1,0:T(8,128)(2,1)S(1)} %copy-done.1, bf16[129,768]{1,0:T(8,128)(2,1)S(1)} %get-tuple-element.35.refs_2_, ...), custom_call_target="tpu_custom_call" | custom-call | flops 1000 | bytes 1000 | tf_op jit(solution)/shard_map/part/pallas_call | solution.py:344
  23.3 2.4 %collective-permute-done.3.refs_1_ = bf16[136,768]{1,0:T(8,128)(2,1)S(1)} collective-permute-done((bf16[136,768]{1,0:T(8,128)(2,1)S(1)}, bf16[136,768]{1,0:T(8,128)(2,1)S(1)}, u32[]{:S(2)}, u32[]{:S(2)}) %collective-permute-start.3) | collective-permute-done | bytes 208928 | tf_op jit(solution)/shard_map/ppermute | solution.py:366
  25.6 0.0 collective-permute-start.8
  25.7 0.6 %collective-permute-start.4 = (bf16[136,768]{1,0:T(8,128)(2,1)S(1)}, bf16[136,768]{1,0:T(8,128)(2,1)S(1)}, u32[]{:S(2)}, u32[]{:S(2)}) collective-permute-start(bf16[136,768]{1,0:T(8,128)(2,1)S(1)} %collective-permute-done.3.refs_1_), channel_id=1, source_target_pairs={{0,2},{1,3},{2,0},{3,1},{4,6},{5,7},{6,4},{7,5},{8,10},{9,11},{10,... | collective-permute-start | bytes 626696 | tf_op jit(solution)/shard_map/ppermute | solution.py:366
  26.2 0.0 collective-permute-done.5.refs_0_
  26.2 0.2 collective-permute-start.7
  26.4 0.8 %project.2 = (bf16[256,128]{1,0:T(8,128)(2,1)S(1)}, bf16[256,768]{1,0:T(8,128)(2,1)S(1)}, bf16[256,768]{1,0:T(8,128)(2,1)S(1)}) custom-call(bf16[768,1536]{1,0:T(8,128)(2,1)S(1)} %copy-done, bf16[768,768]{1,0:T(8,128)(2,1)S(1)} %copy-done.1, bf16[134,768]{1,0:T(8,128)(2,1)S(1)} %collective-permute-done.5.refs_0_, ...), custom_call_target="tpu_custom_call" | custom-call | flops 1000 | bytes 1000 | tf_op jit(solution)/shard_map/project/pallas_call | solution.py:323
  27.2 0.5 %collective-permute-done.7.refs_2_ = bf16[134,768]{1,0:T(8,128)(2,1)S(1)} collective-permute-done((bf16[134,768]{1,0:T(8,128)(2,1)S(1)}, bf16[134,768]{1,0:T(8,128)(2,1)S(1)}, u32[]{:S(2)}, u32[]{:S(2)}) %collective-permute-start.7) | collective-permute-done | bytes 205856 | tf_op jit(solution)/shard_map/ppermute | solution.py:366
  27.7 0.0 collective-permute-done.8.refs_3_
  27.7 3.8 %part.4 = (f32[128,768]{1,0:T(8,128)S(1)}, f32[128,768]{1,0:T(8,128)S(1)}, f32[128,768]{1,0:T(8,128)S(1)}) custom-call(bf16[768,1536]{1,0:T(8,128)(2,1)S(1)} %copy-done, bf16[768,768]{1,0:T(8,128)(2,1)S(1)} %copy-done.1, bf16[134,768]{1,0:T(8,128)(2,1)S(1)} %collective-permute-done.7.refs_2_, bf16[136,768]{1,0:T(8,128)(2,1)S(1)} %collective-permute-done.8.refs_3_, ...), custom_call_target="tpu_custom_call" | custom-call | flops 1000 | bytes 1000 | tf_op jit(solution)/shard_map/part/pallas_call | solution.py:344
  31.5 1.7 %collective-permute-done.4.refs_0_ = bf16[136,768]{1,0:T(8,128)(2,1)S(1)} collective-permute-done((bf16[136,768]{1,0:T(8,128)(2,1)S(1)}, bf16[136,768]{1,0:T(8,128)(2,1)S(1)}, u32[]{:S(2)}, u32[]{:S(2)}) %collective-permute-start.4) | collective-permute-done | bytes 208928 | tf_op jit(solution)/shard_map/ppermute | solution.py:366
  33.2 0.0 collective-permute-start.9
  33.2 0.5 %project.3 = (bf16[128,128]{1,0:T(8,128)(2,1)S(1)}, bf16[128,768]{1,0:T(8,128)(2,1)S(1)}, bf16[128,768]{1,0:T(8,128)(2,1)S(1)}) custom-call(bf16[768,1536]{1,0:T(8,128)(2,1)S(1)} %copy-done, bf16[768,768]{1,0:T(8,128)(2,1)S(1)} %copy-done.1, bf16[136,768]{1,0:T(8,128)(2,1)S(1)} %collective-permute-done.4.refs_0_), custom_call_target="tpu_custom_call" | custom-call | flops 1000 | bytes 1000 | tf_op jit(solution)/shard_map/project/pallas_call | solution.py:323
  33.7 1.0 %collective-permute-done.9.refs_2_ = bf16[136,768]{1,0:T(8,128)(2,1)S(1)} collective-permute-done((bf16[136,768]{1,0:T(8,128)(2,1)S(1)}, bf16[136,768]{1,0:T(8,128)(2,1)S(1)}, u32[]{:S(2)}, u32[]{:S(2)}) %collective-permute-start.9) | collective-permute-done | bytes 208928 | tf_op jit(solution)/shard_map/ppermute | solution.py:366
  34.7 2.7 %part.5 = bf16[128,768]{1,0:T(8,128)(2,1)} custom-call(bf16[768,1536]{1,0:T(8,128)(2,1)S(1)} %copy-done, bf16[768,768]{1,0:T(8,128)(2,1)S(1)} %copy-done.1, bf16[136,768]{1,0:T(8,128)(2,1)S(1)} %collective-permute-done.9.refs_2_, bf16[128,128]{1,0:T(8,128)(2,1)S(1)} %get-tuple-element.50.refs_3_, bf16[128,768]{1,0:T(8,128)(2,1)S(1)} %get-tuple-element.51.refs_4_, ...), custom_call_target="tpu_custom_call" | custom-call | flops 1000000000 | bytes 4000000 | tf_op jit(solution)/shard_map/part/pallas_call | solution.py:344
Async XLA Ops:
  0.0 11.0 %collective-permute-start = (bf16[128,768]{1,0:T(8,128)(2,1)}, bf16[128,768]{1,0:T(8,128)(2,1)S(1)}, u32[]{:S(2)}, u32[]{:S(2)}) collective-permute-start(bf16[128,768]{1,0:T(8,128)(2,1)} %features_ref.1), channel_id=1, source_target_pairs={{0,8},{8,0},{16,24},{24,16},{1,9},{9,1},{17,25},{25,17},{2,10},{10... | collective-permute-start | bytes 589832 | tf_op jit(solution)/shard_map/ppermute | solution.py:366
  2.9 10.8 %collective-permute-start.2 = (bf16[128,768]{1,0:T(8,128)(2,1)}, bf16[128,768]{1,0:T(8,128)(2,1)S(1)}, u32[]{:S(2)}, u32[]{:S(2)}) collective-permute-start(bf16[128,768]{1,0:T(8,128)(2,1)} %features_ref.1), channel_id=1, source_target_pairs={{0,16},{8,24},{16,0},{24,8},{1,17},{9,25},{17,1},{25,9},{2,18},{10... | collective-permute-start | bytes 589832 | tf_op jit(solution)/shard_map/ppermute | solution.py:366
  4.5 9.3 %collective-permute-start.1 = (bf16[128,768]{1,0:T(8,128)(2,1)}, bf16[128,768]{1,0:T(8,128)(2,1)S(1)}, u32[]{:S(2)}, u32[]{:S(2)}) collective-permute-start(bf16[128,768]{1,0:T(8,128)(2,1)} %features_ref.1), channel_id=1, source_target_pairs={{0,24},{8,16},{16,8},{24,0},{1,25},{9,17},{17,9},{25,1},{2,26},{10... | collective-permute-start | bytes 589832 | tf_op jit(solution)/shard_map/ppermute | solution.py:366
  5.1 1.0 %copy-start.2 = (bf16[128,1024]{1,0:T(8,128)(2,1)S(1)}, bf16[128,1024]{1,0:T(8,128)(2,1)}, u32[]{:S(2)}) copy-start(bf16[128,1024]{1,0:T(8,128)(2,1)} %tiles_ref.1) | copy-start | bytes 786436
  6.1 0.9 %copy-start.3 = (bf16[128,768]{1,0:T(8,128)(2,1)S(1)}, bf16[128,768]{1,0:T(8,128)(2,1)}, u32[]{:S(2)}) copy-start(bf16[128,768]{1,0:T(8,128)(2,1)} %features_ref.1) | copy-start | bytes 589828
  7.0 0.8 %copy-start.4 = (f32[32,256]{1,0:T(8,128)S(1)}, f32[32,256]{1,0:T(8,128)}, u32[]{:S(2)}) copy-start(f32[32,256]{1,0:T(8,128)} %table_ref.1) | copy-start | bytes 98308
  7.8 0.7 %copy-start.5 = (s32[1,8]{1,0:T(1,128)S(1)}, s32[1,8]{1,0:T(1,128)}, u32[]{:S(2)}) copy-start(s32[1,8]{1,0:T(1,128)} %src_ref.1) | copy-start | bytes 100
  8.4 0.7 %copy-start.6 = (s32[128]{0:T(128)S(1)}, s32[128]{0:T(128)}, u32[]{:S(2)}) copy-start(s32[128]{0:T(128)} %param.12) | copy-start | bytes 1540
  11.0 9.0 %copy-start = (bf16[768,1536]{1,0:T(8,128)(2,1)S(1)}, bf16[768,1536]{1,0:T(8,128)(2,1)}, u32[]{:S(2)}) copy-start(bf16[768,1536]{1,0:T(8,128)(2,1)} %refs_0_.5) | copy-start | bytes 7077892
  11.0 8.9 %copy-start.1 = (bf16[768,768]{1,0:T(8,128)(2,1)S(1)}, bf16[768,768]{1,0:T(8,128)(2,1)}, u32[]{:S(2)}) copy-start(bf16[768,768]{1,0:T(8,128)(2,1)} %refs_1_.5) | copy-start | bytes 3538948
  14.3 11.4 %collective-permute-start.3 = (bf16[136,768]{1,0:T(8,128)(2,1)S(1)}, bf16[136,768]{1,0:T(8,128)(2,1)S(1)}, u32[]{:S(2)}, u32[]{:S(2)}) collective-permute-start(bf16[136,768]{1,0:T(8,128)(2,1)S(1)} %get-tuple-element.33), channel_id=1, source_target_pairs={{0,4},{1,5},{2,6},{3,7},{4,0},{5,1},{6,2},{7,3},{8,12},{9,13},{10,... | collective-permute-start | bytes 626696 | tf_op jit(solution)/shard_map/ppermute | solution.py:366
  16.9 9.3 %collective-permute-start.5 = (bf16[134,768]{1,0:T(8,128)(2,1)S(1)}, bf16[134,768]{1,0:T(8,128)(2,1)S(1)}, u32[]{:S(2)}, u32[]{:S(2)}) collective-permute-start(bf16[134,768]{1,0:T(8,128)(2,1)S(1)} %get-tuple-element.34), channel_id=1, source_target_pairs={{0,2},{1,3},{2,0},{3,1},{4,6},{5,7},{6,4},{7,5},{8,10},{9,11},{10,... | collective-permute-start | bytes 617480 | tf_op jit(solution)/shard_map/ppermute | solution.py:366
  18.5 1.5 %collective-permute-start.6 = (bf16[129,768]{1,0:T(8,128)(2,1)S(1)}, bf16[129,768]{1,0:T(8,128)(2,1)S(1)}, u32[]{:S(2)}, u32[]{:S(2)}) collective-permute-start(bf16[129,768]{1,0:T(8,128)(2,1)S(1)} %get-tuple-element.35.refs_2_), channel_id=1, source_target_pairs={{0,1},{1,0},{2,3},{3,2},{4,5},{5,4},{6,7},{7,6},{8,9},{9,8},{10,11... | collective-permute-start | bytes 594440 | tf_op jit(solution)/shard_map/ppermute | solution.py:366
  25.6 2.0 %collective-permute-start.8 = (bf16[136,768]{1,0:T(8,128)(2,1)S(1)}, bf16[136,768]{1,0:T(8,128)(2,1)S(1)}, u32[]{:S(2)}, u32[]{:S(2)}) collective-permute-start(bf16[136,768]{1,0:T(8,128)(2,1)S(1)} %collective-permute-done.3.refs_1_), channel_id=1, source_target_pairs={{0,1},{1,0},{2,3},{3,2},{4,5},{5,4},{6,7},{7,6},{8,9},{9,8},{10,11... | collective-permute-start | bytes 626696 | tf_op jit(solution)/shard_map/ppermute | solution.py:366
  25.7 7.6 %collective-permute-start.4 = (bf16[136,768]{1,0:T(8,128)(2,1)S(1)}, bf16[136,768]{1,0:T(8,128)(2,1)S(1)}, u32[]{:S(2)}, u32[]{:S(2)}) collective-permute-start(bf16[136,768]{1,0:T(8,128)(2,1)S(1)} %collective-permute-done.3.refs_1_), channel_id=1, source_target_pairs={{0,2},{1,3},{2,0},{3,1},{4,6},{5,7},{6,4},{7,5},{8,10},{9,11},{10,... | collective-permute-start | bytes 626696 | tf_op jit(solution)/shard_map/ppermute | solution.py:366
  26.2 1.5 %collective-permute-start.7 = (bf16[134,768]{1,0:T(8,128)(2,1)S(1)}, bf16[134,768]{1,0:T(8,128)(2,1)S(1)}, u32[]{:S(2)}, u32[]{:S(2)}) collective-permute-start(bf16[134,768]{1,0:T(8,128)(2,1)S(1)} %collective-permute-done.5.refs_0_), channel_id=1, source_target_pairs={{0,1},{1,0},{2,3},{3,2},{4,5},{5,4},{6,7},{7,6},{8,9},{9,8},{10,11... | collective-permute-start | bytes 617480 | tf_op jit(solution)/shard_map/ppermute | solution.py:366
  33.2 1.5 %collective-permute-start.9 = (bf16[136,768]{1,0:T(8,128)(2,1)S(1)}, bf16[136,768]{1,0:T(8,128)(2,1)S(1)}, u32[]{:S(2)}, u32[]{:S(2)}) collective-permute-start(bf16[136,768]{1,0:T(8,128)(2,1)S(1)} %collective-permute-done.4.refs_0_), channel_id=1, source_target_pairs={{0,1},{1,0},{2,3},{3,2},{4,5},{5,4},{6,7},{7,6},{8,9},{9,8},{10,11... | collective-permute-start | bytes 626696 | tf_op jit(solution)/shard_map/ppermute | solution.py:366

commit v18 on v17

--- a/solution.py
+++ b/solution.py
@@ -377,7 +377,7 @@
     chips = seq_count // 2
     any_space = pl.BlockSpec(memory_space=pl.ANY)
 
-    order = [1, *range(groups - 1, 1, -1)]
+    order = list(range(1, groups))
     received = [swap(features, "group", d) for d in order]
     own_bucket = node_bucket.reshape(1, rows)
 

time: 37.7 us -> 37.7 us (level)
  transfers between devices with their start and end apart: 10 -> 10, of which waited for: 6 -> 7; matrix products, arithmetic and copies ran while one was open for 0% -> 0% of each run, Pallas kernels for 28% -> 27%
where the time goes in v18:
time: 37.7 us; the launch traced here: 37.5 us
  Pallas kernels  13.6 us (36%)
  waiting for transfers between devices  9.75 us (26%)
  starting transfers between devices  9.45 us (25%)
  local copies, waits for them, and re-layouts  3.95 us (10%)
  between operations  0.74 us (2%)
    pallas_call x3, Pallas kernels, attend_part(): pl.pallas_call(lambda *refs: part_kernel(len(blocks), first, last, *refs)...  9.84 us
    ppermute x10, waiting for transfers between devices, swap(): lax.ppermute(array, axis, [(i, i ^ distance) for i in range(lax.axis_size...  9.75 us
    ppermute x10, starting transfers between devices, swap(): lax.ppermute(array, axis, [(i, i ^ distance) for i in range(lax.axis_size...  9.45 us
    unnamed x14, local copies, waits for them, and re-layouts  3.95 us
    pallas_call x1, Pallas kernels, on_device(): pl.pallas_call(stage_kernel, out_shape=[shape(rows, H * LANES), shape(row...  1.95 us
    pallas_call x2, Pallas kernels, attend_part(): pl.pallas_call(project_kernel, out_shape=[shape(count, LANES), shape(coun...  1.26 us
  transfers between devices with their start and end apart: 10, of which 7 were waited for; matrix products, arithmetic and copies ran while one was open for 0% of the time, Pallas kernels for 27%

profile of v18, /device:TPU:0, one launch (start us, length us, event | category | flops | bytes accessed | tf_op | source)
XLA Modules:
  0.0 37.5 jit_solution(6975889374451634189)
XLA Ops:
  0.0 2.9 %collective-permute-start = (bf16[128,768]{1,0:T(8,128)(2,1)}, bf16[128,768]{1,0:T(8,128)(2,1)S(1)}, u32[]{:S(2)}, u32[]{:S(2)}) collective-permute-start(bf16[128,768]{1,0:T(8,128)(2,1)} %features_ref.1), channel_id=1, source_target_pairs={{0,8},{8,0},{16,24},{24,16},{1,9},{9,1},{17,25},{25,17},{2,10},{10... | collective-permute-start | bytes 589832 | tf_op jit(solution)/shard_map/ppermute | solution.py:366
  2.9 1.5 %collective-permute-start.2 = (bf16[128,768]{1,0:T(8,128)(2,1)}, bf16[128,768]{1,0:T(8,128)(2,1)S(1)}, u32[]{:S(2)}, u32[]{:S(2)}) collective-permute-start(bf16[128,768]{1,0:T(8,128)(2,1)} %features_ref.1), channel_id=1, source_target_pairs={{0,24},{8,16},{16,8},{24,0},{1,25},{9,17},{17,9},{25,1},{2,26},{10... | collective-permute-start | bytes 589832 | tf_op jit(solution)/shard_map/ppermute | solution.py:366
  4.4 0.0 collective-permute-start.1
  5.1 0.0 copy-start.2
  5.1 0.9 %copy-done.2 = bf16[128,1024]{1,0:T(8,128)(2,1)S(1)} copy-done((bf16[128,1024]{1,0:T(8,128)(2,1)S(1)}, bf16[128,1024]{1,0:T(8,128)(2,1)}, u32[]{:S(2)}) %copy-start.2) | copy-done | bytes 262168
  6.1 0.0 copy-start.3
  6.1 0.9 %copy-done.3 = bf16[128,768]{1,0:T(8,128)(2,1)S(1)} copy-done((bf16[128,768]{1,0:T(8,128)(2,1)S(1)}, bf16[128,768]{1,0:T(8,128)(2,1)}, u32[]{:S(2)}) %copy-start.3) | copy-done | bytes 196632
  7.0 0.0 copy-start.4
  7.0 0.8 %copy-done.4 = f32[32,256]{1,0:T(8,128)S(1)} copy-done((f32[32,256]{1,0:T(8,128)S(1)}, f32[32,256]{1,0:T(8,128)}, u32[]{:S(2)}) %copy-start.4) | copy-done | bytes 32792
  7.8 0.0 copy-start.5
  7.8 0.7 %copy-done.5 = s32[1,8]{1,0:T(1,128)S(1)} copy-done((s32[1,8]{1,0:T(1,128)S(1)}, s32[1,8]{1,0:T(1,128)}, u32[]{:S(2)}) %copy-start.5) | copy-done | bytes 56
  8.4 0.0 copy-start.6
  8.4 0.7 %copy-done.6 = s32[128]{0:T(128)S(1)} copy-done((s32[128]{0:T(128)S(1)}, s32[128]{0:T(128)}, u32[]{:S(2)}) %copy-start.6) | copy-done | bytes 536
  9.1 1.9 %stage.1 = (bf16[128,4096]{1,0:T(8,128)(2,1)S(1)}, bf16[128,768]{1,0:T(8,128)(2,1)S(1)}, bf16[128,1024]{1,0:T(8,128)(2,1)S(1)}, f32[8,768]{1,0:T(8,128)S(1)}, s32[8,128]{1,0:T(8,128)S(1)}) custom-call(s32[1]{0:T(128)S(6)} %copy.9.count_ref, s32[1]{0:T(128)} %bitcast.me_ref, s32[1,8]{1,0:T(1,128)S(1)} %copy-done.5, f32[32,256]{1,0:T(8,128)S(1)} %copy-done.4, ...), custom_call_target="tpu_custom_call" | custom-call | flops 1000000000 | bytes 4000000 | tf_op jit(solution)/shard_map/stage/pallas_call | solution.py:384
  11.0 0.0 copy-start
  11.0 0.0 copy-start.1
  11.0 0.0 collective-permute-done.refs_4_
  11.1 2.5 %collective-permute-done.2.refs_6_ = bf16[128,768]{1,0:T(8,128)(2,1)S(1)} collective-permute-done((bf16[128,768]{1,0:T(8,128)(2,1)}, bf16[128,768]{1,0:T(8,128)(2,1)S(1)}, u32[]{:S(2)}, u32[]{:S(2)}) %collective-permute-start.2) | collective-permute-done | bytes 196640 | tf_op jit(solution)/shard_map/ppermute | solution.py:366
  13.6 1.4 %collective-permute-done.1.refs_5_ = bf16[128,768]{1,0:T(8,128)(2,1)S(1)} collective-permute-done((bf16[128,768]{1,0:T(8,128)(2,1)}, bf16[128,768]{1,0:T(8,128)(2,1)S(1)}, u32[]{:S(2)}, u32[]{:S(2)}) %collective-permute-start.1) | collective-permute-done | bytes 196640 | tf_op jit(solution)/shard_map/ppermute | solution.py:366
  14.9 0.5 %aggregate.1 = (bf16[136,768]{1,0:T(8,128)(2,1)S(1)}, bf16[134,768]{1,0:T(8,128)(2,1)S(1)}, bf16[129,768]{1,0:T(8,128)(2,1)S(1)}) custom-call(s32[8,128]{1,0:T(8,128)S(1)} %get-tuple-element.29.refs_0_, f32[8,768]{1,0:T(8,128)S(1)} %get-tuple-element.30.refs_1_, bf16[128,1024]{1,0:T(8,128)(2,1)S(1)} %get-tuple-element.31.refs_2_, ...), custom_call_target="tpu_custom_call" | custom-call | flops 1000000000 | bytes 4000000 | tf_op jit(solution)/shard_map/aggregate/pallas_call | solution.py:399
  15.5 2.7 %collective-permute-start.3 = (bf16[136,768]{1,0:T(8,128)(2,1)S(1)}, bf16[136,768]{1,0:T(8,128)(2,1)S(1)}, u32[]{:S(2)}, u32[]{:S(2)}) collective-permute-start(bf16[136,768]{1,0:T(8,128)(2,1)S(1)} %get-tuple-element.33), channel_id=1, source_target_pairs={{0,4},{1,5},{2,6},{3,7},{4,0},{5,1},{6,2},{7,3},{8,12},{9,13},{10,... | collective-permute-start | bytes 626696 | tf_op jit(solution)/shard_map/ppermute | solution.py:366
  18.1 1.6 %collective-permute-start.5 = (bf16[134,768]{1,0:T(8,128)(2,1)S(1)}, bf16[134,768]{1,0:T(8,128)(2,1)S(1)}, u32[]{:S(2)}, u32[]{:S(2)}) collective-permute-start(bf16[134,768]{1,0:T(8,128)(2,1)S(1)} %get-tuple-element.34), channel_id=1, source_target_pairs={{0,2},{1,3},{2,0},{3,1},{4,6},{5,7},{6,4},{7,5},{8,10},{9,11},{10,... | collective-permute-start | bytes 617480 | tf_op jit(solution)/shard_map/ppermute | solution.py:366
  19.7 0.0 collective-permute-start.6
  19.7 1.5 %collective-permute-done.6.refs_3_ = bf16[129,768]{1,0:T(8,128)(2,1)S(1)} collective-permute-done((bf16[129,768]{1,0:T(8,128)(2,1)S(1)}, bf16[129,768]{1,0:T(8,128)(2,1)S(1)}, u32[]{:S(2)}, u32[]{:S(2)}) %collective-permute-start.6) | collective-permute-done | bytes 198176 | tf_op jit(solution)/shard_map/ppermute | solution.py:366
  21.2 0.0 copy-done
  21.2 0.0 copy-done.1
  21.2 3.3 %part.3 = (bf16[128,768]{1,0:T(8,128)(2,1)S(1)}, bf16[128,4096]{1,0:T(8,128)(2,1)S(1)}, f32[128,768]{1,0:T(8,128)S(1)}, f32[128,768]{1,0:T(8,128)S(1)}) custom-call(bf16[768,1536]{1,0:T(8,128)(2,1)S(1)} %copy-done, bf16[768,768]{1,0:T(8,128)(2,1)S(1)} %copy-done.1, bf16[129,768]{1,0:T(8,128)(2,1)S(1)} %get-tuple-element.35.refs_2_, ...), custom_call_target="tpu_custom_call" | custom-call | flops 1000 | bytes 1000 | tf_op jit(solution)/shard_map/part/pallas_call | solution.py:344
  24.5 1.2 %collective-permute-done.3.refs_1_ = bf16[136,768]{1,0:T(8,128)(2,1)S(1)} collective-permute-done((bf16[136,768]{1,0:T(8,128)(2,1)S(1)}, bf16[136,768]{1,0:T(8,128)(2,1)S(1)}, u32[]{:S(2)}, u32[]{:S(2)}) %collective-permute-start.3) | collective-permute-done | bytes 208928 | tf_op jit(solution)/shard_map/ppermute | solution.py:366
  25.7 0.0 collective-permute-start.8
  25.7 0.5 %collective-permute-start.4 = (bf16[136,768]{1,0:T(8,128)(2,1)S(1)}, bf16[136,768]{1,0:T(8,128)(2,1)S(1)}, u32[]{:S(2)}, u32[]{:S(2)}) collective-permute-start(bf16[136,768]{1,0:T(8,128)(2,1)S(1)} %collective-permute-done.3.refs_1_), channel_id=1, source_target_pairs={{0,2},{1,3},{2,0},{3,1},{4,6},{5,7},{6,4},{7,5},{8,10},{9,11},{10,... | collective-permute-start | bytes 626696 | tf_op jit(solution)/shard_map/ppermute | solution.py:366
  26.2 0.0 collective-permute-done.5.refs_0_
  26.2 0.2 collective-permute-start.7
  26.5 0.8 %project.2 = (bf16[256,128]{1,0:T(8,128)(2,1)S(1)}, bf16[256,768]{1,0:T(8,128)(2,1)S(1)}, bf16[256,768]{1,0:T(8,128)(2,1)S(1)}) custom-call(bf16[768,1536]{1,0:T(8,128)(2,1)S(1)} %copy-done, bf16[768,768]{1,0:T(8,128)(2,1)S(1)} %copy-done.1, bf16[134,768]{1,0:T(8,128)(2,1)S(1)} %collective-permute-done.5.refs_0_, ...), custom_call_target="tpu_custom_call" | custom-call | flops 1000 | bytes 1000 | tf_op jit(solution)/shard_map/project/pallas_call | solution.py:323
  27.2 0.4 %collective-permute-done.7.refs_2_ = bf16[134,768]{1,0:T(8,128)(2,1)S(1)} collective-permute-done((bf16[134,768]{1,0:T(8,128)(2,1)S(1)}, bf16[134,768]{1,0:T(8,128)(2,1)S(1)}, u32[]{:S(2)}, u32[]{:S(2)}) %collective-permute-start.7) | collective-permute-done | bytes 205856 | tf_op jit(solution)/shard_map/ppermute | solution.py:366
  27.7 0.0 collective-permute-done.8.refs_3_
  27.7 3.8 %part.4 = (f32[128,768]{1,0:T(8,128)S(1)}, f32[128,768]{1,0:T(8,128)S(1)}, f32[128,768]{1,0:T(8,128)S(1)}) custom-call(bf16[768,1536]{1,0:T(8,128)(2,1)S(1)} %copy-done, bf16[768,768]{1,0:T(8,128)(2,1)S(1)} %copy-done.1, bf16[134,768]{1,0:T(8,128)(2,1)S(1)} %collective-permute-done.7.refs_2_, bf16[136,768]{1,0:T(8,128)(2,1)S(1)} %collective-permute-done.8.refs_3_, ...), custom_call_target="tpu_custom_call" | custom-call | flops 1000 | bytes 1000 | tf_op jit(solution)/shard_map/part/pallas_call | solution.py:344
  31.5 1.8 %collective-permute-done.4.refs_0_ = bf16[136,768]{1,0:T(8,128)(2,1)S(1)} collective-permute-done((bf16[136,768]{1,0:T(8,128)(2,1)S(1)}, bf16[136,768]{1,0:T(8,128)(2,1)S(1)}, u32[]{:S(2)}, u32[]{:S(2)}) %collective-permute-start.4) | collective-permute-done | bytes 208928 | tf_op jit(solution)/shard_map/ppermute | solution.py:366
  33.3 0.0 collective-permute-start.9
  33.3 0.5 %project.3 = (bf16[128,128]{1,0:T(8,128)(2,1)S(1)}, bf16[128,768]{1,0:T(8,128)(2,1)S(1)}, bf16[128,768]{1,0:T(8,128)(2,1)S(1)}) custom-call(bf16[768,1536]{1,0:T(8,128)(2,1)S(1)} %copy-done, bf16[768,768]{1,0:T(8,128)(2,1)S(1)} %copy-done.1, bf16[136,768]{1,0:T(8,128)(2,1)S(1)} %collective-permute-done.4.refs_0_), custom_call_target="tpu_custom_call" | custom-call | flops 1000 | bytes 1000 | tf_op jit(solution)/shard_map/project/pallas_call | solution.py:323
  33.8 1.0 %collective-permute-done.9.refs_2_ = bf16[136,768]{1,0:T(8,128)(2,1)S(1)} collective-permute-done((bf16[136,768]{1,0:T(8,128)(2,1)S(1)}, bf16[136,768]{1,0:T(8,128)(2,1)S(1)}, u32[]{:S(2)}, u32[]{:S(2)}) %collective-permute-start.9) | collective-permute-done | bytes 208928 | tf_op jit(solution)/shard_map/ppermute | solution.py:366
  34.7 2.7 %part.5 = bf16[128,768]{1,0:T(8,128)(2,1)} custom-call(bf16[768,1536]{1,0:T(8,128)(2,1)S(1)} %copy-done, bf16[768,768]{1,0:T(8,128)(2,1)S(1)} %copy-done.1, bf16[136,768]{1,0:T(8,128)(2,1)S(1)} %collective-permute-done.9.refs_2_, bf16[128,128]{1,0:T(8,128)(2,1)S(1)} %get-tuple-element.50.refs_3_, bf16[128,768]{1,0:T(8,128)(2,1)S(1)} %get-tuple-element.51.refs_4_, ...), custom_call_target="tpu_custom_call" | custom-call | flops 1000000000 | bytes 4000000 | tf_op jit(solution)/shard_map/part/pallas_call | solution.py:344
Async XLA Ops:
  0.0 11.0 %collective-permute-start = (bf16[128,768]{1,0:T(8,128)(2,1)}, bf16[128,768]{1,0:T(8,128)(2,1)S(1)}, u32[]{:S(2)}, u32[]{:S(2)}) collective-permute-start(bf16[128,768]{1,0:T(8,128)(2,1)} %features_ref.1), channel_id=1, source_target_pairs={{0,8},{8,0},{16,24},{24,16},{1,9},{9,1},{17,25},{25,17},{2,10},{10... | collective-permute-start | bytes 589832 | tf_op jit(solution)/shard_map/ppermute | solution.py:366
  2.9 10.6 %collective-permute-start.2 = (bf16[128,768]{1,0:T(8,128)(2,1)}, bf16[128,768]{1,0:T(8,128)(2,1)S(1)}, u32[]{:S(2)}, u32[]{:S(2)}) collective-permute-start(bf16[128,768]{1,0:T(8,128)(2,1)} %features_ref.1), channel_id=1, source_target_pairs={{0,24},{8,16},{16,8},{24,0},{1,25},{9,17},{17,9},{25,1},{2,26},{10... | collective-permute-start | bytes 589832 | tf_op jit(solution)/shard_map/ppermute | solution.py:366
  4.4 10.5 %collective-permute-start.1 = (bf16[128,768]{1,0:T(8,128)(2,1)}, bf16[128,768]{1,0:T(8,128)(2,1)S(1)}, u32[]{:S(2)}, u32[]{:S(2)}) collective-permute-start(bf16[128,768]{1,0:T(8,128)(2,1)} %features_ref.1), channel_id=1, source_target_pairs={{0,16},{8,24},{16,0},{24,8},{1,17},{9,25},{17,1},{25,9},{2,18},{10... | collective-permute-start | bytes 589832 | tf_op jit(solution)/shard_map/ppermute | solution.py:366
  5.1 1.0 %copy-start.2 = (bf16[128,1024]{1,0:T(8,128)(2,1)S(1)}, bf16[128,1024]{1,0:T(8,128)(2,1)}, u32[]{:S(2)}) copy-start(bf16[128,1024]{1,0:T(8,128)(2,1)} %tiles_ref.1) | copy-start | bytes 786436
  6.1 0.9 %copy-start.3 = (bf16[128,768]{1,0:T(8,128)(2,1)S(1)}, bf16[128,768]{1,0:T(8,128)(2,1)}, u32[]{:S(2)}) copy-start(bf16[128,768]{1,0:T(8,128)(2,1)} %features_ref.1) | copy-start | bytes 589828
  7.0 0.8 %copy-start.4 = (f32[32,256]{1,0:T(8,128)S(1)}, f32[32,256]{1,0:T(8,128)}, u32[]{:S(2)}) copy-start(f32[32,256]{1,0:T(8,128)} %table_ref.1) | copy-start | bytes 98308
  7.8 0.7 %copy-start.5 = (s32[1,8]{1,0:T(1,128)S(1)}, s32[1,8]{1,0:T(1,128)}, u32[]{:S(2)}) copy-start(s32[1,8]{1,0:T(1,128)} %src_ref.1) | copy-start | bytes 100
  8.4 0.7 %copy-start.6 = (s32[128]{0:T(128)S(1)}, s32[128]{0:T(128)}, u32[]{:S(2)}) copy-start(s32[128]{0:T(128)} %param.12) | copy-start | bytes 1540
  11.0 10.2 %copy-start = (bf16[768,1536]{1,0:T(8,128)(2,1)S(1)}, bf16[768,1536]{1,0:T(8,128)(2,1)}, u32[]{:S(2)}) copy-start(bf16[768,1536]{1,0:T(8,128)(2,1)} %refs_0_.5) | copy-start | bytes 7077892
  11.0 10.2 %copy-start.1 = (bf16[768,768]{1,0:T(8,128)(2,1)S(1)}, bf16[768,768]{1,0:T(8,128)(2,1)}, u32[]{:S(2)}) copy-start(bf16[768,768]{1,0:T(8,128)(2,1)} %refs_1_.5) | copy-start | bytes 3538948
  15.5 10.2 %collective-permute-start.3 = (bf16[136,768]{1,0:T(8,128)(2,1)S(1)}, bf16[136,768]{1,0:T(8,128)(2,1)S(1)}, u32[]{:S(2)}, u32[]{:S(2)}) collective-permute-start(bf16[136,768]{1,0:T(8,128)(2,1)S(1)} %get-tuple-element.33), channel_id=1, source_target_pairs={{0,4},{1,5},{2,6},{3,7},{4,0},{5,1},{6,2},{7,3},{8,12},{9,13},{10,... | collective-permute-start | bytes 626696 | tf_op jit(solution)/shard_map/ppermute | solution.py:366
  18.1 8.1 %collective-permute-start.5 = (bf16[134,768]{1,0:T(8,128)(2,1)S(1)}, bf16[134,768]{1,0:T(8,128)(2,1)S(1)}, u32[]{:S(2)}, u32[]{:S(2)}) collective-permute-start(bf16[134,768]{1,0:T(8,128)(2,1)S(1)} %get-tuple-element.34), channel_id=1, source_target_pairs={{0,2},{1,3},{2,0},{3,1},{4,6},{5,7},{6,4},{7,5},{8,10},{9,11},{10,... | collective-permute-start | bytes 617480 | tf_op jit(solution)/shard_map/ppermute | solution.py:366
  19.7 1.5 %collective-permute-start.6 = (bf16[129,768]{1,0:T(8,128)(2,1)S(1)}, bf16[129,768]{1,0:T(8,128)(2,1)S(1)}, u32[]{:S(2)}, u32[]{:S(2)}) collective-permute-start(bf16[129,768]{1,0:T(8,128)(2,1)S(1)} %get-tuple-element.35.refs_2_), channel_id=1, source_target_pairs={{0,1},{1,0},{2,3},{3,2},{4,5},{5,4},{6,7},{7,6},{8,9},{9,8},{10,11... | collective-permute-start | bytes 594440 | tf_op jit(solution)/shard_map/ppermute | solution.py:366
  25.7 2.0 %collective-permute-start.8 = (bf16[136,768]{1,0:T(8,128)(2,1)S(1)}, bf16[136,768]{1,0:T(8,128)(2,1)S(1)}, u32[]{:S(2)}, u32[]{:S(2)}) collective-permute-start(bf16[136,768]{1,0:T(8,128)(2,1)S(1)} %collective-permute-done.3.refs_1_), channel_id=1, source_target_pairs={{0,1},{1,0},{2,3},{3,2},{4,5},{5,4},{6,7},{7,6},{8,9},{9,8},{10,11... | collective-permute-start | bytes 626696 | tf_op jit(solution)/shard_map/ppermute | solution.py:366
  25.7 7.6 %collective-permute-start.4 = (bf16[136,768]{1,0:T(8,128)(2,1)S(1)}, bf16[136,768]{1,0:T(8,128)(2,1)S(1)}, u32[]{:S(2)}, u32[]{:S(2)}) collective-permute-start(bf16[136,768]{1,0:T(8,128)(2,1)S(1)} %collective-permute-done.3.refs_1_), channel_id=1, source_target_pairs={{0,2},{1,3},{2,0},{3,1},{4,6},{5,7},{6,4},{7,5},{8,10},{9,11},{10,... | collective-permute-start | bytes 626696 | tf_op jit(solution)/shard_map/ppermute | solution.py:366
  26.2 1.5 %collective-permute-start.7 = (bf16[134,768]{1,0:T(8,128)(2,1)S(1)}, bf16[134,768]{1,0:T(8,128)(2,1)S(1)}, u32[]{:S(2)}, u32[]{:S(2)}) collective-permute-start(bf16[134,768]{1,0:T(8,128)(2,1)S(1)} %collective-permute-done.5.refs_0_), channel_id=1, source_target_pairs={{0,1},{1,0},{2,3},{3,2},{4,5},{5,4},{6,7},{7,6},{8,9},{9,8},{10,11... | collective-permute-start | bytes 617480 | tf_op jit(solution)/shard_map/ppermute | solution.py:366
  33.3 1.5 %collective-permute-start.9 = (bf16[136,768]{1,0:T(8,128)(2,1)S(1)}, bf16[136,768]{1,0:T(8,128)(2,1)S(1)}, u32[]{:S(2)}, u32[]{:S(2)}) collective-permute-start(bf16[136,768]{1,0:T(8,128)(2,1)S(1)} %collective-permute-done.4.refs_0_), channel_id=1, source_target_pairs={{0,1},{1,0},{2,3},{3,2},{4,5},{5,4},{6,7},{7,6},{8,9},{9,8},{10,11... | collective-permute-start | bytes 626696 | tf_op jit(solution)/shard_map/ppermute | solution.py:366

commit v19 on v17

--- a/solution.py
+++ b/solution.py
@@ -417,19 +417,21 @@
     while step < top:
         far[step] = swap(short, "seq", 2 * step)
         step *= 2
-    for d in range(3, chips):
-        if far[d] is None:
-            far[d] = swap(far[d & (d - 1)], "seq", 2 * (d & -d))
     parts = [[0], [1, top]] if top > 1 else [[0, 1]]
     parts += [[d] for d in range(2, chips) if d != top]
     queries, state = [], [bias]
     for number, part in enumerate(parts):
+        if number == 1:
+            for d in range(3, chips):
+                if far[d] is None:
+                    far[d] = swap(after(far[d & (d - 1)], *state), "seq", 2 * (d & -d))
         blocks = []
         for d in part:
             block = far[d]
             if d:
                 block = after(block, *state)
-                near = swap(block, "seq", 1)
+                sent = block[: rows + EXTRA // 2] if d == top else block
+                near = swap(sent, "seq", 1)
             else:
                 near = swap(least, "seq", 1)
             blocks += [block, near]

time: 37.7 us -> 36.3 us (0.963)
  waiting for transfers between devices: 9.68 us -> 7.75 us
  starting transfers between devices: 9.49 us -> 10 us
    ppermute x10, waiting for transfers between devices: 9.68 us -> 7.75 us  [swap(): lax.ppermute(array, axis, [(i, i ^ distance) for i in range(lax.axis_size...]
    ppermute x10, starting transfers between devices: 9.49 us -> 10 us  [swap(): lax.ppermute(array, axis, [(i, i ^ distance) for i in range(lax.axis_size...]
  transfers between devices with their start and end apart: 10 -> 10, of which waited for: 6 -> 5; matrix products, arithmetic and copies ran while one was open for 0% -> 0% of each run, Pallas kernels for 28% -> 29%
where the time goes in v19:
time: 36.3 us; the launch traced here: 36.1 us
  Pallas kernels  13.6 us (37%)
  starting transfers between devices  10 us (28%)
  waiting for transfers between devices  7.75 us (21%)
  local copies, waits for them, and re-layouts  3.95 us (11%)
  between operations  0.75 us (2%)
    ppermute x10, starting transfers between devices, swap(): lax.ppermute(array, axis, [(i, i ^ distance) for i in range(lax.axis_size...  10 us
    pallas_call x3, Pallas kernels, attend_part(): pl.pallas_call(lambda *refs: part_kernel(len(blocks), first, last, *refs)...  9.84 us
    ppermute x10, waiting for transfers between devices, swap(): lax.ppermute(array, axis, [(i, i ^ distance) for i in range(lax.axis_size...  7.75 us
    unnamed x14, local copies, waits for them, and re-layouts  3.95 us
    pallas_call x1, Pallas kernels, on_device(): pl.pallas_call(stage_kernel, out_shape=[shape(rows, H * LANES), shape(row...  1.95 us
    pallas_call x2, Pallas kernels, attend_part(): pl.pallas_call(project_kernel, out_shape=[shape(count, LANES), shape(coun...  1.26 us
  transfers between devices with their start and end apart: 10, of which 5 were waited for; matrix products, arithmetic and copies ran while one was open for 0% of the time, Pallas kernels for 29%

profile of v19, /device:TPU:0, one launch (start us, length us, event | category | flops | bytes accessed | tf_op | source)
XLA Modules:
  0.0 36.1 jit_solution(3866616604436818302)
XLA Ops:
  0.0 2.9 %collective-permute-start = (bf16[128,768]{1,0:T(8,128)(2,1)}, bf16[128,768]{1,0:T(8,128)(2,1)S(1)}, u32[]{:S(2)}, u32[]{:S(2)}) collective-permute-start(bf16[128,768]{1,0:T(8,128)(2,1)} %features_ref.1), channel_id=1, source_target_pairs={{0,8},{8,0},{16,24},{24,16},{1,9},{9,1},{17,25},{25,17},{2,10},{10... | collective-permute-start | bytes 589832 | tf_op jit(solution)/shard_map/ppermute | solution.py:366
  2.9 1.5 %collective-permute-start.2 = (bf16[128,768]{1,0:T(8,128)(2,1)}, bf16[128,768]{1,0:T(8,128)(2,1)S(1)}, u32[]{:S(2)}, u32[]{:S(2)}) collective-permute-start(bf16[128,768]{1,0:T(8,128)(2,1)} %features_ref.1), channel_id=1, source_target_pairs={{0,16},{8,24},{16,0},{24,8},{1,17},{9,25},{17,1},{25,9},{2,18},{10... | collective-permute-start | bytes 589832 | tf_op jit(solution)/shard_map/ppermute | solution.py:366
  4.5 0.0 collective-permute-start.1
  5.1 0.0 copy-start.2
  5.1 0.9 %copy-done.2 = bf16[128,1024]{1,0:T(8,128)(2,1)S(1)} copy-done((bf16[128,1024]{1,0:T(8,128)(2,1)S(1)}, bf16[128,1024]{1,0:T(8,128)(2,1)}, u32[]{:S(2)}) %copy-start.2) | copy-done | bytes 262168
  6.1 0.0 copy-start.3
  6.1 0.9 %copy-done.3 = bf16[128,768]{1,0:T(8,128)(2,1)S(1)} copy-done((bf16[128,768]{1,0:T(8,128)(2,1)S(1)}, bf16[128,768]{1,0:T(8,128)(2,1)}, u32[]{:S(2)}) %copy-start.3) | copy-done | bytes 196632
  7.0 0.0 copy-start.4
  7.0 0.8 %copy-done.4 = f32[32,256]{1,0:T(8,128)S(1)} copy-done((f32[32,256]{1,0:T(8,128)S(1)}, f32[32,256]{1,0:T(8,128)}, u32[]{:S(2)}) %copy-start.4) | copy-done | bytes 32792
  7.8 0.0 copy-start.5
  7.8 0.7 %copy-done.5 = s32[1,8]{1,0:T(1,128)S(1)} copy-done((s32[1,8]{1,0:T(1,128)S(1)}, s32[1,8]{1,0:T(1,128)}, u32[]{:S(2)}) %copy-start.5) | copy-done | bytes 56
  8.4 0.0 copy-start.6
  8.4 0.7 %copy-done.6 = s32[128]{0:T(128)S(1)} copy-done((s32[128]{0:T(128)S(1)}, s32[128]{0:T(128)}, u32[]{:S(2)}) %copy-start.6) | copy-done | bytes 536
  9.1 1.9 %stage.1 = (bf16[128,4096]{1,0:T(8,128)(2,1)S(1)}, bf16[128,768]{1,0:T(8,128)(2,1)S(1)}, bf16[128,1024]{1,0:T(8,128)(2,1)S(1)}, f32[8,768]{1,0:T(8,128)S(1)}, s32[8,128]{1,0:T(8,128)S(1)}) custom-call(s32[1]{0:T(128)S(6)} %copy.9.count_ref, s32[1]{0:T(128)} %bitcast.me_ref, s32[1,8]{1,0:T(1,128)S(1)} %copy-done.5, f32[32,256]{1,0:T(8,128)S(1)} %copy-done.4, ...), custom_call_target="tpu_custom_call" | custom-call | flops 1000000000 | bytes 4000000 | tf_op jit(solution)/shard_map/stage/pallas_call | solution.py:384
  11.0 0.0 copy-start
  11.0 0.0 copy-start.1
  11.0 0.0 collective-permute-done.refs_4_
  11.1 2.7 %collective-permute-done.2.refs_6_ = bf16[128,768]{1,0:T(8,128)(2,1)S(1)} collective-permute-done((bf16[128,768]{1,0:T(8,128)(2,1)}, bf16[128,768]{1,0:T(8,128)(2,1)S(1)}, u32[]{:S(2)}, u32[]{:S(2)}) %collective-permute-start.2) | collective-permute-done | bytes 196640 | tf_op jit(solution)/shard_map/ppermute | solution.py:366
  13.7 0.0 collective-permute-done.1.refs_5_
  13.7 0.5 %aggregate.1 = (bf16[136,768]{1,0:T(8,128)(2,1)S(1)}, bf16[134,768]{1,0:T(8,128)(2,1)S(1)}, bf16[129,768]{1,0:T(8,128)(2,1)S(1)}) custom-call(s32[8,128]{1,0:T(8,128)S(1)} %get-tuple-element.29.refs_0_, f32[8,768]{1,0:T(8,128)S(1)} %get-tuple-element.30.refs_1_, bf16[128,1024]{1,0:T(8,128)(2,1)S(1)} %get-tuple-element.31.refs_2_, ...), custom_call_target="tpu_custom_call" | custom-call | flops 1000000000 | bytes 4000000 | tf_op jit(solution)/shard_map/aggregate/pallas_call | solution.py:399
  14.3 2.7 %collective-permute-start.3 = (bf16[136,768]{1,0:T(8,128)(2,1)S(1)}, bf16[136,768]{1,0:T(8,128)(2,1)S(1)}, u32[]{:S(2)}, u32[]{:S(2)}) collective-permute-start(bf16[136,768]{1,0:T(8,128)(2,1)S(1)} %get-tuple-element.33), channel_id=1, source_target_pairs={{0,4},{1,5},{2,6},{3,7},{4,0},{5,1},{6,2},{7,3},{8,12},{9,13},{10,... | collective-permute-start | bytes 626696 | tf_op jit(solution)/shard_map/ppermute | solution.py:366
  16.9 1.6 %collective-permute-start.6 = (bf16[134,768]{1,0:T(8,128)(2,1)S(1)}, bf16[134,768]{1,0:T(8,128)(2,1)S(1)}, u32[]{:S(2)}, u32[]{:S(2)}) collective-permute-start(bf16[134,768]{1,0:T(8,128)(2,1)S(1)} %get-tuple-element.39), channel_id=1, source_target_pairs={{0,2},{1,3},{2,0},{3,1},{4,6},{5,7},{6,4},{7,5},{8,10},{9,11},{10,... | collective-permute-start | bytes 617480 | tf_op jit(solution)/shard_map/ppermute | solution.py:366
  18.5 0.0 collective-permute-start.4
  18.5 1.5 %collective-permute-done.4.refs_3_ = bf16[129,768]{1,0:T(8,128)(2,1)S(1)} collective-permute-done((bf16[129,768]{1,0:T(8,128)(2,1)S(1)}, bf16[129,768]{1,0:T(8,128)(2,1)S(1)}, u32[]{:S(2)}, u32[]{:S(2)}) %collective-permute-start.4) | collective-permute-done | bytes 198176 | tf_op jit(solution)/shard_map/ppermute | solution.py:366
  20.0 0.0 copy-done
  20.0 0.0 copy-done.1
  20.0 3.3 %part.3 = (bf16[128,768]{1,0:T(8,128)(2,1)S(1)}, bf16[128,4096]{1,0:T(8,128)(2,1)S(1)}, f32[128,768]{1,0:T(8,128)S(1)}, f32[128,768]{1,0:T(8,128)S(1)}) custom-call(bf16[768,1536]{1,0:T(8,128)(2,1)S(1)} %copy-done, bf16[768,768]{1,0:T(8,128)(2,1)S(1)} %copy-done.1, bf16[129,768]{1,0:T(8,128)(2,1)S(1)} %get-tuple-element.34.refs_2_, ...), custom_call_target="tpu_custom_call" | custom-call | flops 1000 | bytes 1000 | tf_op jit(solution)/shard_map/part/pallas_call | solution.py:344
  23.3 2.4 %collective-permute-done.3.refs_1_ = bf16[136,768]{1,0:T(8,128)(2,1)S(1)} collective-permute-done((bf16[136,768]{1,0:T(8,128)(2,1)S(1)}, bf16[136,768]{1,0:T(8,128)(2,1)S(1)}, u32[]{:S(2)}, u32[]{:S(2)}) %collective-permute-start.3) | collective-permute-done | bytes 208928 | tf_op jit(solution)/shard_map/ppermute | solution.py:366
  25.6 0.6 %collective-permute-start.5 = (bf16[136,768]{1,0:T(8,128)(2,1)S(1)}, bf16[136,768]{1,0:T(8,128)(2,1)S(1)}, u32[]{:S(2)}, u32[]{:S(2)}) collective-permute-start(bf16[136,768]{1,0:T(8,128)(2,1)S(1)} %collective-permute-done.3.refs_1_), channel_id=1, source_target_pairs={{0,2},{1,3},{2,0},{3,1},{4,6},{5,7},{6,4},{7,5},{8,10},{9,11},{10,... | collective-permute-start | bytes 626696 | tf_op jit(solution)/shard_map/ppermute | solution.py:366
  26.2 0.0 collective-permute-done.6.refs_0_
  26.2 0.0 collective-permute-start.7
  26.2 0.5 %collective-permute-start.8 = (bf16[132,768]{1,0:T(8,128)(2,1)S(1)}, bf16[132,768]{1,0:T(8,128)(2,1)S(1)}, u32[]{:S(2)}, u32[]{:S(2)}) collective-permute-start(bf16[132,768]{1,0:T(8,128)(2,1)S(1)} %bitcast.3), channel_id=1, source_target_pairs={{0,1},{1,0},{2,3},{3,2},{4,5},{5,4},{6,7},{7,6},{8,9},{9,8},{10,11... | collective-permute-start | bytes 608264 | tf_op jit(solution)/shard_map/ppermute | solution.py:366
  26.7 0.8 %project.2 = (bf16[256,128]{1,0:T(8,128)(2,1)S(1)}, bf16[256,768]{1,0:T(8,128)(2,1)S(1)}, bf16[256,768]{1,0:T(8,128)(2,1)S(1)}) custom-call(bf16[768,1536]{1,0:T(8,128)(2,1)S(1)} %copy-done, bf16[768,768]{1,0:T(8,128)(2,1)S(1)} %copy-done.1, bf16[134,768]{1,0:T(8,128)(2,1)S(1)} %collective-permute-done.6.refs_0_, ...), custom_call_target="tpu_custom_call" | custom-call | flops 1000 | bytes 1000 | tf_op jit(solution)/shard_map/project/pallas_call | solution.py:323
  27.5 0.5 %collective-permute-done.8.refs_3_ = bf16[132,768]{1,0:T(8,128)(2,1)S(1)} collective-permute-done((bf16[132,768]{1,0:T(8,128)(2,1)S(1)}, bf16[132,768]{1,0:T(8,128)(2,1)S(1)}, u32[]{:S(2)}, u32[]{:S(2)}) %collective-permute-start.8) | collective-permute-done | bytes 202784 | tf_op jit(solution)/shard_map/ppermute | solution.py:366
  28.0 0.0 collective-permute-done.7.refs_2_
  28.0 3.8 %part.4 = (f32[128,768]{1,0:T(8,128)S(1)}, f32[128,768]{1,0:T(8,128)S(1)}, f32[128,768]{1,0:T(8,128)S(1)}) custom-call(bf16[768,1536]{1,0:T(8,128)(2,1)S(1)} %copy-done, bf16[768,768]{1,0:T(8,128)(2,1)S(1)} %copy-done.1, bf16[134,768]{1,0:T(8,128)(2,1)S(1)} %collective-permute-done.7.refs_2_, bf16[132,768]{1,0:T(8,128)(2,1)S(1)} %collective-permute-done.8.refs_3_, ...), custom_call_target="tpu_custom_call" | custom-call | flops 1000 | bytes 1000 | tf_op jit(solution)/shard_map/part/pallas_call | solution.py:344
  31.8 0.0 collective-permute-done.5.refs_0_
  31.8 0.3 collective-permute-start.9
  32.1 0.5 %project.3 = (bf16[128,128]{1,0:T(8,128)(2,1)S(1)}, bf16[128,768]{1,0:T(8,128)(2,1)S(1)}, bf16[128,768]{1,0:T(8,128)(2,1)S(1)}) custom-call(bf16[768,1536]{1,0:T(8,128)(2,1)S(1)} %copy-done, bf16[768,768]{1,0:T(8,128)(2,1)S(1)} %copy-done.1, bf16[136,768]{1,0:T(8,128)(2,1)S(1)} %collective-permute-done.5.refs_0_), custom_call_target="tpu_custom_call" | custom-call | flops 1000 | bytes 1000 | tf_op jit(solution)/shard_map/project/pallas_call | solution.py:323
  32.5 0.8 %collective-permute-done.9.refs_2_ = bf16[136,768]{1,0:T(8,128)(2,1)S(1)} collective-permute-done((bf16[136,768]{1,0:T(8,128)(2,1)S(1)}, bf16[136,768]{1,0:T(8,128)(2,1)S(1)}, u32[]{:S(2)}, u32[]{:S(2)}) %collective-permute-start.9) | collective-permute-done | bytes 208928 | tf_op jit(solution)/shard_map/ppermute | solution.py:366
  33.3 2.7 %part.5 = bf16[128,768]{1,0:T(8,128)(2,1)} custom-call(bf16[768,1536]{1,0:T(8,128)(2,1)S(1)} %copy-done, bf16[768,768]{1,0:T(8,128)(2,1)S(1)} %copy-done.1, bf16[136,768]{1,0:T(8,128)(2,1)S(1)} %collective-permute-done.9.refs_2_, bf16[128,128]{1,0:T(8,128)(2,1)S(1)} %get-tuple-element.50.refs_3_, bf16[128,768]{1,0:T(8,128)(2,1)S(1)} %get-tuple-element.51.refs_4_, ...), custom_call_target="tpu_custom_call" | custom-call | flops 1000000000 | bytes 4000000 | tf_op jit(solution)/shard_map/part/pallas_call | solution.py:344
Async XLA Ops:
  0.0 11.0 %collective-permute-start = (bf16[128,768]{1,0:T(8,128)(2,1)}, bf16[128,768]{1,0:T(8,128)(2,1)S(1)}, u32[]{:S(2)}, u32[]{:S(2)}) collective-permute-start(bf16[128,768]{1,0:T(8,128)(2,1)} %features_ref.1), channel_id=1, source_target_pairs={{0,8},{8,0},{16,24},{24,16},{1,9},{9,1},{17,25},{25,17},{2,10},{10... | collective-permute-start | bytes 589832 | tf_op jit(solution)/shard_map/ppermute | solution.py:366
  2.9 10.8 %collective-permute-start.2 = (bf16[128,768]{1,0:T(8,128)(2,1)}, bf16[128,768]{1,0:T(8,128)(2,1)S(1)}, u32[]{:S(2)}, u32[]{:S(2)}) collective-permute-start(bf16[128,768]{1,0:T(8,128)(2,1)} %features_ref.1), channel_id=1, source_target_pairs={{0,16},{8,24},{16,0},{24,8},{1,17},{9,25},{17,1},{25,9},{2,18},{10... | collective-permute-start | bytes 589832 | tf_op jit(solution)/shard_map/ppermute | solution.py:366
  4.5 9.3 %collective-permute-start.1 = (bf16[128,768]{1,0:T(8,128)(2,1)}, bf16[128,768]{1,0:T(8,128)(2,1)S(1)}, u32[]{:S(2)}, u32[]{:S(2)}) collective-permute-start(bf16[128,768]{1,0:T(8,128)(2,1)} %features_ref.1), channel_id=1, source_target_pairs={{0,24},{8,16},{16,8},{24,0},{1,25},{9,17},{17,9},{25,1},{2,26},{10... | collective-permute-start | bytes 589832 | tf_op jit(solution)/shard_map/ppermute | solution.py:366
  5.1 1.0 %copy-start.2 = (bf16[128,1024]{1,0:T(8,128)(2,1)S(1)}, bf16[128,1024]{1,0:T(8,128)(2,1)}, u32[]{:S(2)}) copy-start(bf16[128,1024]{1,0:T(8,128)(2,1)} %tiles_ref.1) | copy-start | bytes 786436
  6.1 0.9 %copy-start.3 = (bf16[128,768]{1,0:T(8,128)(2,1)S(1)}, bf16[128,768]{1,0:T(8,128)(2,1)}, u32[]{:S(2)}) copy-start(bf16[128,768]{1,0:T(8,128)(2,1)} %features_ref.1) | copy-start | bytes 589828
  7.0 0.8 %copy-start.4 = (f32[32,256]{1,0:T(8,128)S(1)}, f32[32,256]{1,0:T(8,128)}, u32[]{:S(2)}) copy-start(f32[32,256]{1,0:T(8,128)} %table_ref.1) | copy-start | bytes 98308
  7.8 0.7 %copy-start.5 = (s32[1,8]{1,0:T(1,128)S(1)}, s32[1,8]{1,0:T(1,128)}, u32[]{:S(2)}) copy-start(s32[1,8]{1,0:T(1,128)} %src_ref.1) | copy-start | bytes 100
  8.4 0.7 %copy-start.6 = (s32[128]{0:T(128)S(1)}, s32[128]{0:T(128)}, u32[]{:S(2)}) copy-start(s32[128]{0:T(128)} %param.12) | copy-start | bytes 1540
  11.0 9.0 %copy-start = (bf16[768,1536]{1,0:T(8,128)(2,1)S(1)}, bf16[768,1536]{1,0:T(8,128)(2,1)}, u32[]{:S(2)}) copy-start(bf16[768,1536]{1,0:T(8,128)(2,1)} %refs_0_.5) | copy-start | bytes 7077892
  11.0 8.9 %copy-start.1 = (bf16[768,768]{1,0:T(8,128)(2,1)S(1)}, bf16[768,768]{1,0:T(8,128)(2,1)}, u32[]{:S(2)}) copy-start(bf16[768,768]{1,0:T(8,128)(2,1)} %refs_1_.5) | copy-start | bytes 3538948
  14.3 11.4 %collective-permute-start.3 = (bf16[136,768]{1,0:T(8,128)(2,1)S(1)}, bf16[136,768]{1,0:T(8,128)(2,1)S(1)}, u32[]{:S(2)}, u32[]{:S(2)}) collective-permute-start(bf16[136,768]{1,0:T(8,128)(2,1)S(1)} %get-tuple-element.33), channel_id=1, source_target_pairs={{0,4},{1,5},{2,6},{3,7},{4,0},{5,1},{6,2},{7,3},{8,12},{9,13},{10,... | collective-permute-start | bytes 626696 | tf_op jit(solution)/shard_map/ppermute | solution.py:366
  16.9 9.3 %collective-permute-start.6 = (bf16[134,768]{1,0:T(8,128)(2,1)S(1)}, bf16[134,768]{1,0:T(8,128)(2,1)S(1)}, u32[]{:S(2)}, u32[]{:S(2)}) collective-permute-start(bf16[134,768]{1,0:T(8,128)(2,1)S(1)} %get-tuple-element.39), channel_id=1, source_target_pairs={{0,2},{1,3},{2,0},{3,1},{4,6},{5,7},{6,4},{7,5},{8,10},{9,11},{10,... | collective-permute-start | bytes 617480 | tf_op jit(solution)/shard_map/ppermute | solution.py:366
  18.5 1.5 %collective-permute-start.4 = (bf16[129,768]{1,0:T(8,128)(2,1)S(1)}, bf16[129,768]{1,0:T(8,128)(2,1)S(1)}, u32[]{:S(2)}, u32[]{:S(2)}) collective-permute-start(bf16[129,768]{1,0:T(8,128)(2,1)S(1)} %get-tuple-element.34.refs_2_), channel_id=1, source_target_pairs={{0,1},{1,0},{2,3},{3,2},{4,5},{5,4},{6,7},{7,6},{8,9},{9,8},{10,11... | collective-permute-start | bytes 594440 | tf_op jit(solution)/shard_map/ppermute | solution.py:366
  25.6 6.1 %collective-permute-start.5 = (bf16[136,768]{1,0:T(8,128)(2,1)S(1)}, bf16[136,768]{1,0:T(8,128)(2,1)S(1)}, u32[]{:S(2)}, u32[]{:S(2)}) collective-permute-start(bf16[136,768]{1,0:T(8,128)(2,1)S(1)} %collective-permute-done.3.refs_1_), channel_id=1, source_target_pairs={{0,2},{1,3},{2,0},{3,1},{4,6},{5,7},{6,4},{7,5},{8,10},{9,11},{10,... | collective-permute-start | bytes 626696 | tf_op jit(solution)/shard_map/ppermute | solution.py:366
  26.2 1.8 %collective-permute-start.7 = (bf16[134,768]{1,0:T(8,128)(2,1)S(1)}, bf16[134,768]{1,0:T(8,128)(2,1)S(1)}, u32[]{:S(2)}, u32[]{:S(2)}) collective-permute-start(bf16[134,768]{1,0:T(8,128)(2,1)S(1)} %collective-permute-done.6.refs_0_), channel_id=1, source_target_pairs={{0,1},{1,0},{2,3},{3,2},{4,5},{5,4},{6,7},{7,6},{8,9},{9,8},{10,11... | collective-permute-start | bytes 617480 | tf_op jit(solution)/shard_map/ppermute | solution.py:366
  26.2 1.8 %collective-permute-start.8 = (bf16[132,768]{1,0:T(8,128)(2,1)S(1)}, bf16[132,768]{1,0:T(8,128)(2,1)S(1)}, u32[]{:S(2)}, u32[]{:S(2)}) collective-permute-start(bf16[132,768]{1,0:T(8,128)(2,1)S(1)} %bitcast.3), channel_id=1, source_target_pairs={{0,1},{1,0},{2,3},{3,2},{4,5},{5,4},{6,7},{7,6},{8,9},{9,8},{10,11... | collective-permute-start | bytes 608264 | tf_op jit(solution)/shard_map/ppermute | solution.py:366
  31.8 1.5 %collective-permute-start.9 = (bf16[136,768]{1,0:T(8,128)(2,1)S(1)}, bf16[136,768]{1,0:T(8,128)(2,1)S(1)}, u32[]{:S(2)}, u32[]{:S(2)}) collective-permute-start(bf16[136,768]{1,0:T(8,128)(2,1)S(1)} %collective-permute-done.5.refs_0_), channel_id=1, source_target_pairs={{0,1},{1,0},{2,3},{3,2},{4,5},{5,4},{6,7},{7,6},{8,9},{9,8},{10,11... | collective-permute-start | bytes 626696 | tf_op jit(solution)/shard_map/ppermute | solution.py:366
